TPU v7x, 128 devices: a whole 4x4x4 slice. The times are simulated.
128 devices in a mesh: ctx: 32 (over z_lo, x, y), wsh: 4 (over z_hi, core).
Axes of the slice: x: 4, y: 4, z: 4 (z_hi: 2, z_lo: 2; z = z_hi * 2 + z_lo), core: 2. Of those that a mesh axis runs over, the one named last changes fastest.
Arguments:
- tokens: bfloat16 [4, 64, 64, 1024], P('wsh', 'ctx'), may hold values from -6 to 6
- w_query: bfloat16 [1024, 1024], P('wsh'), may hold values from -0.1875 to 0.1875
- w_key: bfloat16 [1024, 1024], P('wsh'), may hold values from -0.1875 to 0.1875
- w_value: bfloat16 [1024, 1024], P('wsh'), may hold values from -0.1875 to 0.1875
- w_output: bfloat16 [1024, 1024], P('wsh'), may hold values from -0.5 to 0.5
- w_inner: bfloat16 [1024, 4096], P('wsh'), may hold values from -0.1875 to 0.1875
- w_outer: bfloat16 [4096, 1024], P('wsh'), may hold values from -0.09375 to 0.09375
- ln_gain: float32 [2, 1024], P(None, 'wsh'), may hold values from 0.1 to 1.9
- ln_bias: float32 [2, 1024], P(None, 'wsh'), may hold values from -2 to 2
- block_mask: int32 [4, 64, 64], P('wsh'), may hold values from 0 to 1, as said below
- block_pairs: int32 [32, 2], replicated, may hold values from 0 to 63, as said below
- cotangent: bfloat16 [4, 64, 64, 1024], P('wsh', 'ctx'), may hold values from -6 to 6
Outputs:
- out_tokens: float32 [4, 64, 64, 1024], P('wsh', 'ctx')
- grad_tokens: float32 [4, 64, 64, 1024], P('wsh', 'ctx')
- grad_query: float32 [1024, 1024], P('wsh')
- grad_key: float32 [1024, 1024], P('wsh')
- grad_value: float32 [1024, 1024], P('wsh')
- grad_output: float32 [1024, 1024], P('wsh')
- grad_inner: float32 [1024, 4096], P('wsh')
- grad_outer: float32 [4096, 1024], P('wsh')
- grad_gain: float32 [2, 1024], P(None, 'wsh')
- grad_bias: float32 [2, 1024], P(None, 'wsh')
Inputs may be any that keep to these rules, and one draw needn't show every extreme that they name: block_mask[b, i, j] is 0 for j > i and 1 for j == i. `block_pairs`: row c is the pair of blocks c' and 63 - c' in either order; every number of 0 to 63 appears once.
All inputs are finite; a program needn't handle non-finite values.
Results may differ from a plain program's by a relative error of at most 0.04.
Values may be sent and summed in bfloat16 or wider, within the bound.
A program may use at most 192 MiB of HBM per device.

v0:
```python
import math

import jax
import jax.numpy as jnp
from jax import lax
from jax.sharding import PartitionSpec as P

HD = 64


def layer_norm(values, gain_row, bias_row):
    center = values - jnp.mean(values, axis=-1, keepdims=True)
    spread = jnp.mean(center * center, axis=-1, keepdims=True)
    return center * lax.rsqrt(spread + 1e-05) * gain_row + bias_row


def gelu_exact(values):
    return jax.nn.gelu(values, approximate=False)


def contract_rows(left_mat, right_mat):
    return lax.dot_general(
        left_mat, right_mat, (((0,), (0,)), ((), ())), preferred_element_type=jnp.float32
    )


def contract_cols(left_mat, right_mat):
    return lax.dot_general(
        left_mat, right_mat, (((1,), (1,)), ((), ())), preferred_element_type=jnp.float32
    )


def head_scores(query_part, key_part, allowed):
    raw_scores = jnp.einsum(
        "qhd,khd->hqk", query_part, key_part, preferred_element_type=jnp.float32
    )
    return jnp.where(allowed[None], raw_scores * (1.0 / math.sqrt(HD)), -1e30)


def group_parts(queries, keys_all, values_all, group_index):
    group_width = 4 * HD
    first_col = group_index * group_width
    query_part = lax.dynamic_slice_in_dim(queries, first_col, group_width, 1).reshape(
        queries.shape[0], 4, HD
    )
    key_part = lax.dynamic_slice_in_dim(keys_all, first_col, group_width, 1).reshape(
        keys_all.shape[0], 4, HD
    )
    value_part = lax.dynamic_slice_in_dim(values_all, first_col, group_width, 1).reshape(
        values_all.shape[0], 4, HD
    )
    return (first_col, query_part, key_part, value_part)


def attend_forward(queries, keys_all, values_all, allowed):
    tok_count, model_width = queries.shape
    group_width = 4 * HD

    def one_group(group_index, running):
        outputs, log_sums = running
        first_col, query_part, key_part, value_part = group_parts(
            queries, keys_all, values_all, group_index
        )
        scores = head_scores(query_part, key_part, allowed)
        row_top = jnp.max(scores, axis=-1, keepdims=True)
        exponent = jnp.exp(scores - row_top)
        row_total = jnp.sum(exponent, axis=-1, keepdims=True)
        attn_probs = (exponent / row_total).astype(jnp.bfloat16)
        head_mix = jnp.einsum(
            "hqk,khd->qhd", attn_probs, value_part, preferred_element_type=jnp.float32
        )
        outputs = lax.dynamic_update_slice_in_dim(
            outputs, head_mix.reshape(tok_count, group_width), first_col, 1
        )
        log_sums = lax.dynamic_update_slice_in_dim(
            log_sums, (row_top + jnp.log(row_total))[..., 0], group_index * 4, 0
        )
        return (outputs, log_sums)

    initial = (
        jnp.zeros((tok_count, model_width), jnp.float32),
        jnp.zeros((model_width // HD, tok_count), jnp.float32),
    )
    return lax.fori_loop(0, model_width // group_width, one_group, initial)


def attend_backward(queries, keys_all, values_all, grad_mix, log_sums, allowed):
    tok_count, model_width = queries.shape
    key_count = keys_all.shape[0]
    group_width = 4 * HD
    score_scale = 1.0 / math.sqrt(HD)

    def one_group(group_index, running):
        grad_queries, grad_keys, grad_values = running
        first_col, query_part, key_part, value_part = group_parts(
            queries, keys_all, values_all, group_index
        )
        grad_part = lax.dynamic_slice_in_dim(grad_mix, first_col, group_width, 1).reshape(
            tok_count, 4, HD
        )
        scores = head_scores(query_part, key_part, allowed)
        lse_part = lax.dynamic_slice_in_dim(log_sums, group_index * 4, 4, 0)
        attn_probs = jnp.exp(scores - lse_part[..., None])
        grad_probs = jnp.einsum(
            "qhd,khd->hqk", grad_part, value_part, preferred_element_type=jnp.float32
        )
        row_delta = jnp.sum(grad_probs * attn_probs, axis=-1, keepdims=True)
        grad_scores = (attn_probs * (grad_probs - row_delta)).astype(jnp.bfloat16)
        part_query = (
            jnp.einsum("hqk,khd->qhd", grad_scores, key_part, preferred_element_type=jnp.float32)
            * score_scale
        )
        part_keys = (
            jnp.einsum("hqk,qhd->khd", grad_scores, query_part, preferred_element_type=jnp.float32)
            * score_scale
        )
        part_values = jnp.einsum(
            "hqk,qhd->khd",
            attn_probs.astype(jnp.bfloat16),
            grad_part,
            preferred_element_type=jnp.float32,
        )
        grad_queries = lax.dynamic_update_slice_in_dim(
            grad_queries, part_query.reshape(tok_count, group_width), first_col, 1
        )
        grad_keys = lax.dynamic_update_slice_in_dim(
            grad_keys, part_keys.reshape(key_count, group_width), first_col, 1
        )
        grad_values = lax.dynamic_update_slice_in_dim(
            grad_values, part_values.reshape(key_count, group_width), first_col, 1
        )
        return (grad_queries, grad_keys, grad_values)

    initial = (
        jnp.zeros((tok_count, model_width), jnp.float32),
        jnp.zeros((key_count, model_width), jnp.float32),
        jnp.zeros((key_count, model_width), jnp.float32),
    )
    return lax.fori_loop(0, model_width // group_width, one_group, initial)


def body(
    tokens,
    w_query,
    w_key,
    w_value,
    w_output,
    w_inner,
    w_outer,
    ln_gain,
    ln_bias,
    block_mask,
    block_pairs,
    cotangent,
):
    blk_rows = tokens.shape[2]
    model_width = tokens.shape[3]
    tok_rows = tokens.reshape(2 * blk_rows, model_width)
    wq_full, wk_full, wv_full, wo_full, wi_full, wu_full, gains, biases = (
        lax.all_gather(w_query, "wsh", axis=0, tiled=True),
        lax.all_gather(w_key, "wsh", axis=0, tiled=True),
        lax.all_gather(w_value, "wsh", axis=0, tiled=True),
        lax.all_gather(w_output, "wsh", axis=0, tiled=True),
        lax.all_gather(w_inner, "wsh", axis=0, tiled=True),
        lax.all_gather(w_outer, "wsh", axis=0, tiled=True),
        lax.all_gather(ln_gain.astype(jnp.bfloat16), "wsh", axis=1, tiled=True).astype(
            ln_gain.dtype
        ),
        lax.all_gather(ln_bias.astype(jnp.bfloat16), "wsh", axis=1, tiled=True).astype(
            ln_bias.dtype
        ),
    )
    my_index = lax.axis_index("ctx")
    slot_blocks = block_pairs.reshape(-1)
    block_count = slot_blocks.shape[0]
    my_blocks = lax.dynamic_slice_in_dim(block_pairs, my_index, 1, 0).reshape(2)
    offsets = jnp.arange(blk_rows, dtype=jnp.int32)
    query_pos = (my_blocks[:, None] * blk_rows + offsets[None, :]).reshape(-1)
    key_pos = (slot_blocks[:, None] * blk_rows + offsets[None, :]).reshape(-1)
    block_ids = jnp.arange(block_count, dtype=jnp.int32)
    pick_rows = (my_blocks[:, None] == block_ids[None, :]).astype(jnp.float32)
    pick_keys = (slot_blocks[:, None] == block_ids[None, :]).astype(jnp.float32)
    mask_float = block_mask[0].astype(jnp.float32)
    mask_rows = jnp.dot(pick_rows, mask_float, preferred_element_type=jnp.float32)
    slot_allowed = contract_cols(mask_rows, pick_keys)
    key_allowed = jnp.repeat(jnp.repeat(slot_allowed, blk_rows, axis=0), blk_rows, axis=1) > 0.5
    allowed = key_allowed & (key_pos[None, :] <= query_pos[:, None])
    queries = jnp.dot(tok_rows, wq_full, preferred_element_type=jnp.float32).astype(jnp.bfloat16)
    keys_own = jnp.dot(tok_rows, wk_full, preferred_element_type=jnp.float32).astype(jnp.bfloat16)
    values_own = jnp.dot(tok_rows, wv_full, preferred_element_type=jnp.float32).astype(jnp.bfloat16)
    keys_all, values_all = (
        lax.all_gather(keys_own, "ctx", axis=0, tiled=True),
        lax.all_gather(values_own, "ctx", axis=0, tiled=True),
    )
    head_out, log_sums = attend_forward(queries, keys_all, values_all, allowed)
    attended = head_out.astype(jnp.bfloat16)
    branch = jnp.dot(attended, wo_full, preferred_element_type=jnp.float32)
    normed, norm_one_back = jax.vjp(
        layer_norm, tok_rows.astype(jnp.float32) + branch, gains[0], biases[0]
    )
    normed_low = normed.astype(jnp.bfloat16)
    inner = jnp.dot(normed_low, wi_full, preferred_element_type=jnp.float32)
    activated, gelu_back = jax.vjp(gelu_exact, inner)
    act_low = activated.astype(jnp.bfloat16)
    outer = jnp.dot(act_low, wu_full, preferred_element_type=jnp.float32)
    result, norm_two_back = jax.vjp(layer_norm, normed + outer, gains[1], biases[1])
    cot_rows = cotangent.reshape(2 * blk_rows, model_width).astype(jnp.float32)
    grad_resid_two, gain_two, bias_two = norm_two_back(cot_rows)
    grad_outer_low = grad_resid_two.astype(jnp.bfloat16)
    grad_wu = contract_rows(act_low, grad_outer_low)
    grad_act = contract_cols(grad_outer_low, wu_full)
    grad_inner_low = gelu_back(grad_act)[0].astype(jnp.bfloat16)
    grad_wi = contract_rows(normed_low, grad_inner_low)
    grad_normed = contract_cols(grad_inner_low, wi_full) + grad_resid_two
    grad_resid_one, gain_one, bias_one = norm_one_back(grad_normed)
    grad_branch = grad_resid_one.astype(jnp.bfloat16)
    grad_wo = contract_rows(attended, grad_branch)
    grad_attended = contract_cols(grad_branch, wo_full).astype(jnp.bfloat16)
    keys_back, values_back = (keys_all, values_all)
    grad_queries, grad_keys, grad_values = attend_backward(
        queries, keys_back, values_back, grad_attended, log_sums, allowed
    )
    keys_sum, values_sum = (
        lax.psum_scatter(
            grad_keys.astype(jnp.bfloat16), "ctx", scatter_dimension=0, tiled=True
        ).astype(jnp.float32),
        lax.psum_scatter(
            grad_values.astype(jnp.bfloat16), "ctx", scatter_dimension=0, tiled=True
        ).astype(jnp.float32),
    )
    query_low = grad_queries.astype(jnp.bfloat16)
    key_low = keys_sum.astype(jnp.bfloat16)
    value_low = values_sum.astype(jnp.bfloat16)
    grad_wq = contract_rows(tok_rows, query_low)
    grad_wk = contract_rows(tok_rows, key_low)
    grad_wv = contract_rows(tok_rows, value_low)
    grad_rows = (
        grad_resid_one
        + contract_cols(query_low, wq_full)
        + contract_cols(key_low, wk_full)
        + contract_cols(value_low, wv_full)
    )
    grad_gains = jnp.stack([gain_one, gain_two], axis=0)
    grad_biases = jnp.stack([bias_one, bias_two], axis=0)
    shards = lax.axis_size("wsh")
    ctx_count = lax.axis_size("ctx")
    grad_scale = 1.0 / math.sqrt(shards * 2 * ctx_count * blk_rows)
    shard_q, shard_k, shard_v, shard_o, shard_i, shard_u, shard_g, shard_b = (
        lax.psum_scatter(
            grad_wq.astype(jnp.bfloat16), "wsh", scatter_dimension=0, tiled=True
        ).astype(jnp.float32),
        lax.psum_scatter(
            grad_wk.astype(jnp.bfloat16), "wsh", scatter_dimension=0, tiled=True
        ).astype(jnp.float32),
        lax.psum_scatter(
            grad_wv.astype(jnp.bfloat16), "wsh", scatter_dimension=0, tiled=True
        ).astype(jnp.float32),
        lax.psum_scatter(
            grad_wo.astype(jnp.bfloat16), "wsh", scatter_dimension=0, tiled=True
        ).astype(jnp.float32),
        lax.psum_scatter(
            grad_wi.astype(jnp.bfloat16), "wsh", scatter_dimension=0, tiled=True
        ).astype(jnp.float32),
        lax.psum_scatter(
            grad_wu.astype(jnp.bfloat16), "wsh", scatter_dimension=0, tiled=True
        ).astype(jnp.float32),
        lax.psum_scatter(
            grad_gains.astype(jnp.bfloat16), "wsh", scatter_dimension=1, tiled=True
        ).astype(jnp.float32),
        lax.psum_scatter(
            grad_biases.astype(jnp.bfloat16), "wsh", scatter_dimension=1, tiled=True
        ).astype(jnp.float32),
    )
    summed = (
        lax.psum(shard_q.astype(jnp.bfloat16), "ctx").astype(jnp.float32),
        lax.psum(shard_k.astype(jnp.bfloat16), "ctx").astype(jnp.float32),
        lax.psum(shard_v.astype(jnp.bfloat16), "ctx").astype(jnp.float32),
        lax.psum(shard_o.astype(jnp.bfloat16), "ctx").astype(jnp.float32),
        lax.psum(shard_i.astype(jnp.bfloat16), "ctx").astype(jnp.float32),
        lax.psum(shard_u.astype(jnp.bfloat16), "ctx").astype(jnp.float32),
        lax.psum(shard_g.astype(jnp.bfloat16), "ctx").astype(jnp.float32),
        lax.psum(shard_b.astype(jnp.bfloat16), "ctx").astype(jnp.float32),
    )
    scaled = tuple((gradient * grad_scale for gradient in summed))
    out_shape = tokens.shape
    return (
        result.reshape(out_shape),
        grad_rows.reshape(out_shape),
        scaled[0],
        scaled[1],
        scaled[2],
        scaled[3],
        scaled[4],
        scaled[5],
        scaled[6],
        scaled[7],
    )


def solution(mesh):
    return jax.shard_map(
        body,
        mesh=mesh,
        in_specs=(
            P("wsh", "ctx", None, None),
            P("wsh", None),
            P("wsh", None),
            P("wsh", None),
            P("wsh", None),
            P("wsh", None),
            P("wsh", None),
            P(None, "wsh"),
            P(None, "wsh"),
            P("wsh", None, None),
            P(),
            P("wsh", "ctx", None, None),
        ),
        out_specs=(
            P("wsh", "ctx", None, None),
            P("wsh", "ctx", None, None),
            P("wsh", None),
            P("wsh", None),
            P("wsh", None),
            P("wsh", None),
            P("wsh", None),
            P("wsh", None),
            P(None, "wsh"),
            P(None, "wsh"),
        ),
        check_vma=False,
    )
```

profile of v0, /device:TPU:0, one launch (start us, length us, event | category | flops | bytes accessed | tf_op | source)
XLA Modules:
  0.0 1875.6 jit_solution(10590070522500754527)
XLA Ops:
  9.5 29.5 %all-gather.9.cloned.1.call-done = bf16[1024,1024]{1,0:T(8,128)(2,1)} async-done(((bf16[256,1024]{1,0:T(8,128)(2,1)}), bf16[1024,1024]{1,0:T(8,128)(2,1)}) %all-gather.9.cloned.1.call-update) | async-done | bytes 2097168 | tf_op jit(solution)/shard_map/all_gather | solution.py:162
  41.9 24.8 %all-gather.15.cloned.1.call-done = bf16[1024,1024]{1,0:T(8,128)(2,1)} async-done(((bf16[256,1024]{1,0:T(8,128)(2,1)}), bf16[1024,1024]{1,0:T(8,128)(2,1)}) %all-gather.15.cloned.1.call-update) | async-done | bytes 2097168 | tf_op jit(solution)/shard_map/all_gather | solution.py:161
  85.9 8.4 all-gather.13.cloned.1.call-done
  97.2 165.5 %all-gather.11.cloned.1.call-done = bf16[4096,1024]{1,0:T(8,128)(2,1)} async-done(((bf16[128,1024]{1,0:T(8,128)(2,1)}), bf16[4096,1024]{1,0:T(8,128)(2,1)}) %all-gather.11.cloned.1.call-update) | async-done | bytes 8388624 | tf_op jit(solution)/shard_map/all_gather | solution.py:193
  262.8 11.5 copy.71
  274.3 158.6 %all-gather.17.cloned.1.call-done = bf16[4096,1024]{1,0:T(8,128)(2,1)} async-done(((bf16[128,1024]{1,0:T(8,128)(2,1)}), bf16[4096,1024]{1,0:T(8,128)(2,1)}) %all-gather.17.cloned.1.call-update) | async-done | bytes 8388624 | tf_op jit(solution)/shard_map/all_gather | solution.py:192
  432.9 11.3 copy.73
  444.9 55.8 %while.34 = (s32[]{:T(128)}, bf16[128,1024]{0,1:T(8,128)(2,1)}, f32[16,128]{1,0:T(8,128)S(1)}, bf16[4096,1024]{0,1:T(8,128)(2,1)}, bf16[128,1024]{0,1:T(8,128)(2...) while((s32[]{:T(128)}, bf16[128,1024]{0,1:T(8,128)(2,1)}, ...), condition=%wide.region_3.4_spmd.clone, body=%wide.region_0.3_spmd.clone.sunk | while | flops 563084800 | bytes 49718044 | solution.py:84
  503.2 22.2 %all-gather.21.cloned.1.call-done = bf16[1024,4096]{1,0:T(8,128)(2,1)} async-done(((bf16[256,4096]{1,0:T(8,128)(2,1)}), bf16[1024,4096]{1,0:T(8,128)(2,1)}) %all-gather.21.cloned.1.call-update) | async-done | bytes 8388624 | tf_op jit(solution)/shard_map/all_gather | solution.py:164
  525.5 9.4 multiply_convert_fusion.1
  534.9 54.0 %all-gather.23.cloned.1.call-done = bf16[4096,1024]{1,0:T(8,128)(2,1)} async-done(((bf16[1024,1024]{1,0:T(8,128)(2,1)}), bf16[4096,1024]{1,0:T(8,128)(2,1)}) %all-gather.23.cloned.1.call-update) | async-done | bytes 8388624 | tf_op jit(solution)/shard_map/all_gather | solution.py:165
  615.1 154.2 %while.35 = (s32[]{:T(128)}, bf16[128,1024]{0,1:T(8,128)(2,1)S(1)}, bf16[4096,1024]{0,1:T(8,128)(2,1)}, bf16[4096,1024]{0,1:T(8,128)(2,1)}, bf16[4096,1024]{0,1:...) while((s32[]{:T(128)}, bf16[128,1024]{0,1:T(8,128)(2,1)S(1)}, ...), condition=%wide.region_14.15_spmd.clone, body=%wide.region_12.0_spmd.clone.sunk | while | flops 1364262400 | bytes 95259472 | solution.py:139
  628.9 8.0 multiply_reduce_fusion.6
  637.0 7.9 multiply_convert_fusion.3
  667.4 8.0 multiply_reduce_fusion.6
  675.4 7.9 multiply_convert_fusion.3
  705.9 8.0 multiply_reduce_fusion.6
  744.4 8.0 multiply_reduce_fusion.6
  769.3 12.0 copy.86
  781.3 12.0 copy.88
  811.8 148.6 %reduce-scatter.31.cloned.1.call-done = bf16[128,1024]{1,0:T(8,128)(2,1)} async-done(((bf16[4096,1024]{1,0:T(8,128)(2,1)}), bf16[128,1024]{1,0:T(8,128)(2,1)}) %reduce-scatter.31.cloned.1.call-update) | async-done | bytes 262160
  963.6 175.1 %reduce-scatter.33.cloned.1.call-done = bf16[128,1024]{1,0:T(8,128)(2,1)} async-done(((bf16[4096,1024]{1,0:T(8,128)(2,1)}), bf16[128,1024]{1,0:T(8,128)(2,1)}) %reduce-scatter.33.cloned.1.call-update) | async-done | bytes 262160
  1143.9 33.0 %reduce-scatter.19.cloned.1.call-done = bf16[256,1024]{0,1:T(8,128)(2,1)} async-done(((bf16[1024,1024]{0,1:T(8,128)(2,1)}), bf16[256,1024]{0,1:T(8,128)(2,1)}) %reduce-scatter.19.cloned.1.call-update) | async-done | bytes 524304 | tf_op jit(solution)/shard_map/reduce_scatter | solution.py:249
  1177.0 40.4 %reduce-scatter.25.cloned.1.call-done = bf16[256,1024]{0,1:T(8,128)(2,1)} async-done(((bf16[1024,1024]{0,1:T(8,128)(2,1)}), bf16[256,1024]{0,1:T(8,128)(2,1)}) %reduce-scatter.25.cloned.1.call-update) | async-done | bytes 524304 | tf_op jit(solution)/shard_map/reduce_scatter | solution.py:258
  1217.3 80.7 %reduce-scatter.27.cloned.1.call-done = bf16[256,4096]{1,0:T(8,128)(2,1)} async-done(((bf16[1024,4096]{1,0:T(8,128)(2,1)}), bf16[256,4096]{1,0:T(8,128)(2,1)}) %reduce-scatter.27.cloned.1.call-update) | async-done | bytes 2097168 | tf_op jit(solution)/shard_map/reduce_scatter | solution.py:261
  1298.0 80.8 %reduce-scatter.29.cloned.1.call-done = bf16[1024,1024]{1,0:T(8,128)(2,1)} async-done(((bf16[4096,1024]{1,0:T(8,128)(2,1)}), bf16[1024,1024]{1,0:T(8,128)(2,1)}) %reduce-scatter.29.cloned.1.call-update) | async-done | bytes 2097168 | tf_op jit(solution)/shard_map/reduce_scatter | solution.py:264
  1378.8 40.8 %reduce-scatter.21.cloned.1.call-done = bf16[256,1024]{0,1:T(8,128)(2,1)} async-done(((bf16[1024,1024]{0,1:T(8,128)(2,1)}), bf16[256,1024]{0,1:T(8,128)(2,1)}) %reduce-scatter.21.cloned.1.call-update) | async-done | bytes 524304 | tf_op jit(solution)/shard_map/reduce_scatter | solution.py:252
  1419.6 40.4 %reduce-scatter.23.cloned.1.call-done = bf16[256,1024]{0,1:T(8,128)(2,1)} async-done(((bf16[1024,1024]{0,1:T(8,128)(2,1)}), bf16[256,1024]{0,1:T(8,128)(2,1)}) %reduce-scatter.23.cloned.1.call-update) | async-done | bytes 524304 | tf_op jit(solution)/shard_map/reduce_scatter | solution.py:255
  1462.4 26.8 %reduce-scatter.35.cloned.1.call-done = bf16[256,2]{1,0:T(8,128)(2,1)} async-done(((bf16[1024,2]{1,0:T(8,128)(2,1)}), bf16[256,2]{1,0:T(8,128)(2,1)}) %reduce-scatter.35.cloned.1.call-update) | async-done | bytes 1040
  1490.2 28.6 %reduce-scatter.37.cloned.1.call-done = bf16[256,2]{1,0:T(8,128)(2,1)} async-done(((bf16[1024,2]{1,0:T(8,128)(2,1)}), bf16[256,2]{1,0:T(8,128)(2,1)}) %reduce-scatter.37.cloned.1.call-update) | async-done | bytes 1040
  1519.7 81.9 %all-reduce = (bf16[2,256]{1,0:T(2,128)(2,1)S(1)}, bf16[2,256]{1,0:T(2,128)(2,1)S(1)}) all-reduce(bf16[2,256]{1,0:T(2,128)(2,1)S(1)} %copy.91, bf16[2,256]{1,0:T(2,128)(2,1)S(1)} %copy.93), channel_id=1, replica_groups=mesh['ctx'=32,'wsh'=4] {'ctx'}, use_global_device_ids=true, to_apply=%region_32.33 | all-reduce | flops 1024 | bytes 4096 | tf_op jit(solution)/shard_map/psum | solution.py:281
  1606.3 249.7 %all-reduce.4.cloned.1.call-done = (bf16[256,1024]{0,1:T(8,128)(2,1)}, bf16[256,1024]{0,1:T(8,128)(2,1)}, bf16[256,1024]{0,1:T(8,128)(2,1)}, bf16[256,1024]{0,1:...) async-done(((bf16[256,1024]{0,1:T(8,128)(2,1)}, bf16[256,1024]{0,1:T(8,128)(2,1)}, bf16[256,1024]{0,1:T(8,128)(2,1)}, bf16[256,1024]{0,1:T(8,128)(2,1)}, ...) | async-done | bytes 6291472 | tf_op jit(solution)/shard_map/psum | solution.py:275
  (327 shorter events, 265.8 us)
Async XLA Ops:
  7.2 31.8 %all-gather.9.cloned.1.call-start = ((), (), s32[]{:S(2)}) async-start(), calls=%async_computation.10 | async-start | bytes 2621440 | tf_op jit(solution)/shard_map/all_gather | solution.py:162
  7.9 58.7 %copy-start.3 = (bf16[1,2,64,1024]{3,2,1,0:T(8,128)(2,1)S(1)}, bf16[1,2,64,1024]{3,2,1,0:T(8,128)(2,1)}, u32[]{:S(2)}) copy-start(bf16[1,2,64,1024]{3,2,1,0:T(8,128)(2,1)} %param.16) | copy-start | bytes 786436
  7.9 58.7 %all-gather.15.cloned.1.call-start = ((), (), s32[]{:S(2)}) async-start(), calls=%async_computation.13 | async-start | bytes 2621440 | tf_op jit(solution)/shard_map/all_gather | solution.py:161
  8.7 85.7 %all-gather.13.cloned.1.call-start = ((), (), s32[]{:S(2)}) async-start(), calls=%async_computation.12 | async-start | bytes 2621440 | tf_op jit(solution)/shard_map/all_gather | solution.py:160
  9.4 253.4 %all-gather.11.cloned.1.call-start = ((), (), s32[]{:S(2)}) async-start(), calls=%async_computation.11 | async-start | bytes 8650752 | tf_op jit(solution)/shard_map/all_gather | solution.py:193
  41.8 391.0 %all-gather.17.cloned.1.call-start = ((), (), s32[]{:S(2)}) async-start(), calls=%async_computation.14 | async-start | bytes 8650752 | tf_op jit(solution)/shard_map/all_gather | solution.py:192
  69.4 431.3 %all-gather.19.cloned.1.call-start = ((), (), s32[]{:S(2)}) async-start(), calls=%async_computation.15 | async-start | bytes 2621440 | tf_op jit(solution)/shard_map/all_gather | solution.py:163
  70.0 455.4 %all-gather.21.cloned.1.call-start = ((), (), s32[]{:S(2)}) async-start(), calls=%async_computation.16 | async-start | bytes 10485760 | tf_op jit(solution)/shard_map/all_gather | solution.py:164
  70.8 518.1 %all-gather.23.cloned.1.call-start = ((), (), s32[]{:S(2)}) async-start(), calls=%async_computation.17 | async-start | bytes 10485760 | tf_op jit(solution)/shard_map/all_gather | solution.py:165
  71.5 888.9 %reduce-scatter.31.cloned.1.call-start = ((), (), s32[]{:S(2)}) async-start(), calls=%async_computation.24 | async-start | bytes 8650752
  79.3 509.5 %copy-start.28 = (f32[1,1024]{1,0:T(1,128)}, f32[1,1024]{1,0:T(1,128)S(1)}, u32[]{:S(2)}) copy-start(f32[1,1024]{1,0:T(1,128)S(1)} %get-tuple-element.560) | copy-start | bytes 12292
  85.9 519.3 %copy-start.26 = (f32[1,1024]{1,0:T(1,128)}, f32[1,1024]{1,0:T(1,128)S(1)}, u32[]{:S(2)}) copy-start(f32[1,1024]{1,0:T(1,128)S(1)} %get-tuple-element.558) | copy-start | bytes 12292
  503.0 102.3 %copy-start.1 = (f32[128,1024]{1,0:T(8,128)}, f32[128,1024]{1,0:T(8,128)S(1)}, u32[]{:S(2)}) copy-start(f32[128,1024]{1,0:T(8,128)S(1)} %get-tuple-element.562) | copy-start | bytes 1572868
  503.0 102.3 %copy-start.30 = (f32[128]{0:T(128)}, f32[128]{0:T(128)S(1)}, u32[]{:S(2)}) copy-start(f32[128]{0:T(128)S(1)} %broadcast_multiply_fusion.1) | copy-start | bytes 1540
  503.2 102.1 %copy-start.32 = (f32[128]{0:T(128)}, f32[128]{0:T(128)S(1)}, u32[]{:S(2)}) copy-start(f32[128]{0:T(128)S(1)} %fusion.43) | copy-start | bytes 1540
  534.8 59.0 %copy-start.5 = (bf16[128,4096]{1,0:T(8,128)(2,1)}, bf16[128,4096]{1,0:T(8,128)(2,1)S(1)}, u32[]{:S(2)}) copy-start(bf16[128,4096]{1,0:T(8,128)(2,1)S(1)} %get-tuple-element.546) | copy-start | bytes 3145732
  781.3 357.4 %reduce-scatter.33.cloned.1.call-start = ((), (), s32[]{:S(2)}) async-start(), calls=%async_computation.25 | async-start | bytes 8650752
  793.3 383.6 %reduce-scatter.19.cloned.1.call-start = ((), (), s32[]{:S(2)}) async-start(), calls=%async_computation.18 | async-start | bytes 2621440 | tf_op jit(solution)/shard_map/reduce_scatter | solution.py:249
  796.3 421.0 %reduce-scatter.25.cloned.1.call-start = ((), (), s32[]{:S(2)}) async-start(), calls=%async_computation.21 | async-start | bytes 2621440 | tf_op jit(solution)/shard_map/reduce_scatter | solution.py:258
  798.6 499.4 %reduce-scatter.27.cloned.1.call-start = ((), (), s32[]{:S(2)}) async-start(), calls=%async_computation.22 | async-start | bytes 10485760 | tf_op jit(solution)/shard_map/reduce_scatter | solution.py:261
  804.7 574.1 %reduce-scatter.29.cloned.1.call-start = ((), (), s32[]{:S(2)}) async-start(), calls=%async_computation.23 | async-start | bytes 10485760 | tf_op jit(solution)/shard_map/reduce_scatter | solution.py:264
  811.8 607.8 %reduce-scatter.21.cloned.1.call-start = ((), (), s32[]{:S(2)}) async-start(), calls=%async_computation.19 | async-start | bytes 2621440 | tf_op jit(solution)/shard_map/reduce_scatter | solution.py:252
  963.5 178.4 %copy-start.17 = (bf16[1,2,64,1024]{3,2,1,0:T(8,128)(2,1)S(1)}, bf16[1,2,64,1024]{3,2,1,0:T(8,128)(2,1)}, u32[]{:S(2)}) copy-start(bf16[1,2,64,1024]{3,2,1,0:T(8,128)(2,1)} %param.27) | copy-start | bytes 786436
  963.5 178.4 %copy-start.34 = (bf16[1024]{0:T(1024)(128)(2,1)S(1)}, bf16[1024]{0:T(1024)(128)(2,1)}, u32[]{:S(2)}) copy-start(bf16[1024]{0:T(1024)(128)(2,1)} %get-tuple-element.489) | copy-start | bytes 6148
  963.5 178.4 %copy-start.36 = (bf16[1024]{0:T(1024)(128)(2,1)S(1)}, bf16[1024]{0:T(1024)(128)(2,1)}, u32[]{:S(2)}) copy-start(bf16[1024]{0:T(1024)(128)(2,1)} %get-tuple-element.487) | copy-start | bytes 6148
  963.5 179.4 %copy-start.35 = (bf16[1024]{0:T(1024)(128)(2,1)S(1)}, bf16[1024]{0:T(1024)(128)(2,1)}, u32[]{:S(2)}) copy-start(bf16[1024]{0:T(1024)(128)(2,1)} %get-tuple-element.491) | copy-start | bytes 6148
  963.5 496.5 %reduce-scatter.23.cloned.1.call-start = ((), (), s32[]{:S(2)}) async-start(), calls=%async_computation.20 | async-start | bytes 2621440 | tf_op jit(solution)/shard_map/reduce_scatter | solution.py:255
  1141.8 347.5 %reduce-scatter.35.cloned.1.call-start = ((), (), s32[]{:S(2)}) async-start(), calls=%async_computation.26 | async-start | bytes 327680
  1142.9 375.9 %reduce-scatter.37.cloned.1.call-start = ((), (), s32[]{:S(2)}) async-start(), calls=%async_computation.27 | async-start | bytes 327680
  1143.9 712.2 %all-reduce.4.cloned.1.call-start = ((), (), s32[]{:S(2)}) async-start(), calls=%async_computation.28 | async-start | bytes 12582912 | tf_op jit(solution)/shard_map/psum | solution.py:275
  1462.4 142.3 %copy-start.8 = (bf16[1024,1024]{1,0:T(8,128)(2,1)S(1)}, bf16[1024,1024]{1,0:T(8,128)(2,1)}, u32[]{:S(2)}) copy-start(bf16[1024,1024]{1,0:T(8,128)(2,1)} %all-gather.9.cloned.1.call-done) | copy-start | bytes 6291460
  1462.4 142.3 %copy-start.23 = (bf16[128,1024]{1,0:T(8,128)(2,1)S(1)}, bf16[128,1024]{1,0:T(8,128)(2,1)}, u32[]{:S(2)}) copy-start(bf16[128,1024]{1,0:T(8,128)(2,1)} %reduce-scatter.33.cloned.1.call-done) | copy-start | bytes 786436
  (46 other events, 178.6 us)
Sparse Core Ops, SparseCore 0:
  9.7 29.2 all-gather.8
  40.6 25.9 all-gather.14
  68.3 25.9 all-gather.12
  96.4 166.3 all-gather.10
  264.8 167.9 all-gather.16
  434.4 27.6 all-gather.18
  463.8 61.6 all-gather.20
  527.1 61.6 all-gather.22
  781.4 179.0 reduce-scatter.30
  962.7 175.9 reduce-scatter.32
  1141.9 34.9 reduce-scatter.18
  1179.6 37.6 reduce-scatter.24
  1220.0 77.9 reduce-scatter.26
  1300.8 77.9 reduce-scatter.28
  1381.9 37.6 reduce-scatter.20
  1422.3 37.6 reduce-scatter.22
  1463.0 26.2 reduce-scatter.34
  1492.4 26.2 reduce-scatter.36
  1521.8 334.2 all-reduce.3
where the time goes:
time: 1890 us; the launch traced here: 1880 us
  waiting for transfers between devices  1410 us (75%)
  matrix products  164 us (9%)
  local copies, waits for them, and re-layouts  132 us (7%)
  blocking collectives  95 us (5%)
  other arithmetic  56.4 us (3%)
    unnamed x23, waiting for transfers between devices  383 us
    psum x1, waiting for transfers between devices, body(): lax.psum(shard_q.astype(jnp.bfloat16), 'ctx').astype(jnp.float32)  250 us
    all_gather x1, waiting for transfers between devices, body(): lax.all_gather(values_own, 'ctx', axis=0, tiled=True)  166 us
    all_gather x1, waiting for transfers between devices, body(): lax.all_gather(keys_own, 'ctx', axis=0, tiled=True)  159 us
    psum x1, blocking collectives, body(): lax.psum(shard_g.astype(jnp.bfloat16), 'ctx').astype(jnp.float32)  81.9 us
    reduce_scatter x1, waiting for transfers between devices, body(): lax.psum_scatter(grad_wu.astype(jnp.bfloat16), 'wsh', scatter_dimension=0...  80.8 us
    reduce_scatter x1, waiting for transfers between devices, body(): lax.psum_scatter(grad_wi.astype(jnp.bfloat16), 'wsh', scatter_dimension=0...  80.7 us
    unnamed x109, local copies, waits for them, and re-layouts  61.3 us
  transfers between devices with their start and end apart: 19, of which 18 were waited for; matrix products, arithmetic and copies ran while one was open for 8% of the time, Pallas kernels for 0%

commit v1 on v0

v1 whole, which is shorter than its diff:
```python
import math

import jax
import jax.numpy as jnp
from jax import lax
from jax.experimental import pallas as pl
from jax.experimental.pallas import tpu as pltpu
from jax.sharding import PartitionSpec as P

MESH = pl.DeviceIdType.MESH
BF = jnp.bfloat16
F32 = jnp.float32
ANY = pl.BlockSpec(memory_space=pl.ANY)
VM = pl.BlockSpec(memory_space=pltpu.VMEM)
SM = pl.BlockSpec(memory_space=pltpu.SMEM)
DMA = pltpu.SemaphoreType.DMA
LIMIT = 56 * 1024 * 1024
EPS = 1e-05
NEG = -1e30


def shp(shape, dtype):
    return jax.ShapeDtypeStruct(shape, dtype)


def dot(a, b, dims=((1,), (0,))):
    return lax.dot_general(a, b, (dims, ((), ())), preferred_element_type=F32)


NN = ((1,), (0,))
NT = ((1,), (1,))
TN = ((0,), (0,))


def place():
    c = lax.axis_index("ctx")
    w = lax.axis_index("wsh")
    return c // 16, (c // 4) % 4, c % 4, w // 2, w % 2


def device(zl, x, y, zh, co):
    return {"ctx": zl * 16 + x * 4 + y, "wsh": zh * 2 + co}


def greet(peers):
    bar = pltpu.get_barrier_semaphore()
    for p in peers:
        pl.semaphore_signal(bar, inc=1, device_id=p, device_id_type=MESH)
    pl.semaphore_wait(bar, len(peers))


class Wire:
    def __init__(self, send, recv):
        self.send, self.recv, self.n = send, recv, 0

    def __call__(self, src, dst, peer):
        k = self.n
        self.n += 1
        copy = pltpu.make_async_remote_copy(
            src_ref=src, dst_ref=dst, send_sem=self.send.at[k], recv_sem=self.recv.at[k],
            device_id=peer, device_id_type=MESH,
        )
        copy.start()
        return copy


def gather_kernel(wq, wk, wv, x_ref, ln_ref, wall, xs, lnf, ss, rs, ls):
    zl, x, y, zh, co = place()
    me = zh * 2 + co
    other = (1 - zh) * 2 + co
    core = device(zl, x, y, zh, 1 - co)
    far = device(zl, x, y, 1 - zh, co)
    diag = device(zl, x, y, 1 - zh, 1 - co)
    xp = [device(zl, (x + s) % 4, y, zh, co) for s in (1, 2, 3)]
    yp = [device(zl, x, (y + s) % 4, zh, co) for s in (1, 2, 3)]
    greet([core, far, diag] + xp + yp)
    wire = Wire(ss, rs)
    ws = (wq, wk, wv)
    rows_a = pl.ds(pl.multiple_of(x * 32, 32), 32)
    rows_b = pl.ds(pl.multiple_of(128 + y * 32, 32), 32)
    first_a, first_b = [], []
    for m in range(3):
        first_a.append(wire(ws[m].at[rows_a], wall.at[me, m, rows_a], far))
        first_b.append(wire(ws[m].at[rows_b], wall.at[me, m, rows_b], far))
    rest = []
    for p, idx in ((core, zh * 2 + 1 - co), (far, other), (diag, (1 - zh) * 2 + 1 - co)):
        cols = pl.ds(pl.multiple_of(idx * 256, 256), 256)
        rest.append(wire(x_ref.at[:, cols], xs.at[me], p))
        rest.append(wire(ln_ref, lnf.at[me], p))
    for m in range(3):
        rest.append(wire(ws[m], wall.at[me, m], core))
    local = []
    for m in range(3):
        local.append(pltpu.make_async_copy(ws[m], wall.at[me, m], ls.at[m]))
    own = pl.ds(pl.multiple_of(me * 256, 256), 256)
    local.append(pltpu.make_async_copy(x_ref.at[:, own], xs.at[me], ls.at[3]))
    local.append(pltpu.make_async_copy(ln_ref, lnf.at[me], ls.at[4]))
    for c in local:
        c.start()
    for c in first_a:
        c.wait_recv()
    second = []
    for m in range(3):
        part = wall.at[other, m, rows_a]
        for p in xp:
            second.append(wire(part, part, p))
    for c in first_b:
        c.wait_recv()
    for m in range(3):
        part = wall.at[other, m, rows_b]
        for p in yp:
            second.append(wire(part, part, p))
    for c in second:
        c.wait_recv()
    last = [wire(wall.at[other, m], wall.at[other, m], core) for m in range(3)]
    for c in last:
        c.wait()
    for c in first_a + first_b + second:
        c.wait_send()
    for c in rest:
        c.wait()
    for c in local:
        c.wait()


def gather_weights(wq, wk, wv, tok, lnp):
    n = 6 + 6 + 3 + 18 + 3
    return pl.pallas_call(
        gather_kernel,
        out_shape=[shp((4, 3, 256, 1024), BF), shp((4, 128, 256), BF), shp((4, 8, 256), F32)],
        in_specs=[ANY] * 5,
        out_specs=[ANY] * 3,
        scratch_shapes=[DMA((n,)), DMA((n,)), DMA((5,))],
        compiler_params=pltpu.CompilerParams(collective_id=1, has_side_effects=True),
        name="gather_qkv",
    )(wq, wk, wv, tok, lnp)


def qkv_kernel(x_ref, w_ref, kv_ref, q_ref):
    x = x_ref[...]

    def proj(m):
        return dot(x, w_ref[:, m].reshape(1024, 128)).astype(BF)

    q = (proj(0).astype(F32) * 0.125).astype(BF)
    k = proj(1)
    v = proj(2)
    for u in range(2):
        lanes = slice(64 * u, 64 * u + 64)
        kv_ref[u] = jnp.concatenate([k[:, lanes], v[:, lanes]], axis=1)
        q_ref[u] = jnp.concatenate([q[:64, lanes], q[64:, lanes]], axis=1)


def project(tok, wall):
    return pl.pallas_call(
        qkv_kernel,
        grid=(8,),
        out_shape=[shp((16, 128, 128), BF), shp((16, 64, 128), BF)],
        in_specs=[
            pl.BlockSpec((128, 1024), lambda j: (0, 0)),
            pl.BlockSpec((4, 3, 256, 128), lambda j: (0, 0, 0, j)),
        ],
        out_specs=[
            pl.BlockSpec((2, 128, 128), lambda j: (j, 0, 0)),
            pl.BlockSpec((2, 64, 128), lambda j: (j, 0, 0)),
        ],
        compiler_params=pltpu.CompilerParams(vmem_limit_bytes=LIMIT),
        cost_estimate=pl.CostEstimate(flops=805306368, bytes_accessed=8 << 20, transcendentals=0),
        name="qkv",
    )(tok, wall)


def exchange(wide, narrow, collective):
    has = wide is not None
    n = 32 if has else 16

    def kernel(*refs):
        if has:
            wi, na, wo, no, sw, rw, sn, rn, ls = refs
        else:
            na, no, sn, rn, ls = refs
        me = lax.axis_index("ctx")
        zl = me // 16
        flat = me % 16
        bar = pltpu.get_barrier_semaphore()

        def peer(i):
            if has:
                return (me + i) % 32
            return zl * 16 + (flat + i) % 16

        def greet_one(i, carry):
            pl.semaphore_signal(bar, inc=1, device_id={"ctx": peer(i)}, device_id_type=MESH)
            return carry

        lax.fori_loop(1, n, greet_one, 0)
        pl.semaphore_wait(bar, n - 1)

        def narrow_copy(i):
            p = (flat + i) % 16
            return pltpu.make_async_remote_copy(
                src_ref=na.at[p], dst_ref=no.at[flat], send_sem=sn.at[i], recv_sem=rn.at[i],
                device_id={"ctx": zl * 16 + p}, device_id_type=MESH,
            )

        def wide_copy(i):
            p = (me + i) % 32
            src = p if wide.shape[0] == 32 else p % 16
            return pltpu.make_async_remote_copy(
                src_ref=wi.at[src], dst_ref=wo.at[me], send_sem=sw.at[i], recv_sem=rw.at[i],
                device_id={"ctx": p}, device_id_type=MESH,
            )

        def start(make):
            def one(i, carry):
                make(i).start()
                return carry
            return one

        def wait(make):
            def one(i, carry):
                make(i).wait()
                return carry
            return one

        if has:
            lax.fori_loop(1, 32, start(wide_copy), 0)
        lax.fori_loop(1, 16, start(narrow_copy), 0)
        local = [pltpu.make_async_copy(na.at[flat], no.at[flat], ls.at[0])]
        if has:
            own = me if wide.shape[0] == 32 else flat
            local.append(pltpu.make_async_copy(wi.at[own], wo.at[me], ls.at[1]))
        for c in local:
            c.start()
        for c in local:
            c.wait()
        if has:
            lax.fori_loop(1, 32, wait(wide_copy), 0)
        lax.fori_loop(1, 16, wait(narrow_copy), 0)

    sems = ([DMA((32,)), DMA((32,))] if has else []) + [DMA((16,)), DMA((16,)), DMA((2,))]
    outs = ([shp((32,) + wide.shape[1:], wide.dtype)] if has else []) + [shp(narrow.shape, narrow.dtype)]
    args = ([wide] if has else []) + [narrow]
    return pl.pallas_call(
        kernel,
        out_shape=outs,
        in_specs=[ANY] * len(args),
        out_specs=[ANY] * len(outs),
        scratch_shapes=sems,
        compiler_params=pltpu.CompilerParams(collective_id=collective, has_side_effects=True),
        name=f"exchange_{collective}",
    )(*args)


def attention_setup(blk, mask, kvr, qr, kvs, kaug, kvt, bias, qs, inv, order, oblk):
    first = (lax.axis_index("ctx") // 16) * 32

    def note(s, carry):
        inv[blk[s]] = s
        return carry

    lax.fori_loop(0, 64, note, 0)

    def pick(b, count):
        local = inv[b] - first
        order[count] = local
        oblk[count] = b
        mine = jnp.logical_and(local >= 0, local < 32)
        return count + mine.astype(jnp.int32)

    lax.fori_loop(0, 64, pick, 0)
    for s in range(64):
        at = pl.ds(pl.multiple_of(blk[s] * 64, 64), 64)
        kvs[at, :] = kvr[s // 2, (s % 2) * 64:(s % 2) * 64 + 64, :]
    for j in range(16):
        pair = qr[j]
        qs[2 * j] = pair[:, :64]
        qs[2 * j + 1] = pair[:, 64:]
    rows = lax.broadcasted_iota(jnp.int32, (512, 64), 0) // 64
    lanes = lax.broadcasted_iota(jnp.int32, (512, 64), 1)
    for c in range(8):
        part = kvs[512 * c:512 * c + 512, :]
        hot = jnp.where(rows + 8 * c == lanes, 1.0, 0.0).astype(BF)
        kaug[512 * c:512 * c + 512, :] = jnp.concatenate([part[:, :64], hot], axis=1)
        kvt[c] = part.astype(F32).T.astype(BF)
    qi = lax.broadcasted_iota(jnp.int32, (64, 64), 0)
    ki = lax.broadcasted_iota(jnp.int32, (64, 64), 1)
    bias[...] = jnp.where(jnp.logical_and(mask[0] != 0, ki < qi), 0.0, NEG)


def triangle():
    key = lax.broadcasted_iota(jnp.int32, (64, 256), 0)
    query = lax.broadcasted_iota(jnp.int32, (64, 256), 1) % 64
    return key <= query


def attend_kernel(blk, mask, kvr, qr, o_ref, ot_ref, lse_ref, kvs, kaug, kvt, bias, qs, qa, os, inv, order, oblk):
    attention_setup(blk, mask, kvr, qr, kvs, kaug, kvt, bias, qs, inv, order, oblk)

    def tile(g, carry):
        score, vals = [], []
        for u in range(4):
            i = oblk[4 * g + u]
            q = qs[order[4 * g + u]]
            row = jnp.broadcast_to(bias[pl.ds(i, 1), :], (64, 64)).astype(BF)
            qa[64 * u:64 * u + 64, :] = jnp.concatenate([q, row], axis=1)
            kv = kvs[pl.ds(pl.multiple_of(i * 64, 64), 64), :]
            score.append(dot(kv[:, :64], q, NT))
            vals.append(kv[:, 64:])
        s = jnp.where(triangle(), jnp.concatenate(score, axis=1), NEG)
        top = jnp.max(s, axis=0, keepdims=True)
        p = jnp.exp(s - top)
        total = jnp.sum(p, axis=0, keepdims=True)
        pb = p.astype(BF)
        mix = jnp.concatenate([dot(vals[u], pb[:, 64 * u:64 * u + 64], TN) for u in range(4)], axis=1)
        queries = qa[...]

        def chunk(c, state):
            top, total, mix = state
            keys = kaug[pl.ds(pl.multiple_of(c * 512, 512), 512), :]
            s = dot(keys, queries, NT)
            new = jnp.maximum(top, jnp.max(s, axis=0, keepdims=True))
            shrink = jnp.exp(top - new)
            p = jnp.exp(s - new)
            total = total * shrink + jnp.sum(p, axis=0, keepdims=True)
            mix = mix * shrink + dot(kvt[c, 64:, :], p.astype(BF))
            return new, total, mix

        chunks = (oblk[4 * g + 3] + 7) // 8
        top, total, mix = lax.fori_loop(0, chunks, chunk, (top, total, mix))
        out = mix / total
        ot_ref[g] = out
        lse_ref[g] = top + jnp.log(total)
        back = out.T.astype(BF)
        for u in range(4):
            os[order[4 * g + u]] = back[64 * u:64 * u + 64, :]
        return carry

    lax.fori_loop(0, 8, tile, 0)
    for j in range(16):
        o_ref[j] = jnp.concatenate([os[2 * j], os[2 * j + 1]], axis=1)


def attention_scratch():
    return [
        pltpu.VMEM((4096, 128), BF),
        pltpu.VMEM((4096, 128), BF),
        pltpu.VMEM((8, 128, 512), BF),
        pltpu.VMEM((64, 64), F32),
        pltpu.VMEM((32, 64, 64), BF),
        pltpu.VMEM((256, 128), BF),
        pltpu.VMEM((32, 64, 64), BF),
        pltpu.SMEM((64,), jnp.int32),
        pltpu.SMEM((72,), jnp.int32),
        pltpu.SMEM((72,), jnp.int32),
    ]


def attend(blk, mask, kvr, qr):
    return pl.pallas_call(
        attend_kernel,
        out_shape=[shp((16, 64, 128), BF), shp((8, 64, 256), F32), shp((8, 1, 256), F32)],
        in_specs=[SM, VM, VM, VM],
        out_specs=[VM] * 3,
        scratch_shapes=attention_scratch(),
        compiler_params=pltpu.CompilerParams(vmem_limit_bytes=LIMIT),
        cost_estimate=pl.CostEstimate(flops=10 << 30, bytes_accessed=32 << 20, transcendentals=4 << 20),
        name="attend",
    )(blk, mask, kvr, qr)


def attend_back_kernel(
    blk, mask, kvr, qr, dor, ot_ref, lse_ref, dkv_ref, dq_ref,
    kvs, kaug, kvt, bias, qs, qa, dqs, inv, order, oblk, dos, qz, dz, dkv,
):
    attention_setup(blk, mask, kvr, qr, kvs, kaug, kvt, bias, qs, inv, order, oblk)
    for j in range(16):
        pair = dor[j]
        dos[2 * j] = pair[:, :64]
        dos[2 * j + 1] = pair[:, 64:]
    dkv[...] = jnp.zeros_like(dkv)
    zero = jnp.zeros((64, 64), BF)

    def tile(g, carry):
        score, dprob, places, keys_own, q_own, d_own = [], [], [], [], [], []
        for u in range(4):
            i = oblk[4 * g + u]
            q = qs[order[4 * g + u]]
            do = dos[order[4 * g + u]]
            rows = slice(64 * u, 64 * u + 64)
            row = jnp.broadcast_to(bias[pl.ds(i, 1), :], (64, 64)).astype(BF)
            qa[rows, :] = jnp.concatenate([q, row], axis=1)
            qz[rows, :] = jnp.concatenate([q, zero], axis=1)
            dz[rows, :] = jnp.concatenate([zero, do], axis=1)
            at = pl.ds(pl.multiple_of(i * 64, 64), 64)
            kv = kvs[at, :]
            score.append(dot(kv[:, :64], q, NT))
            dprob.append(dot(kv[:, 64:], do, NT))
            places.append(at)
            keys_own.append(kv[:, :64])
            q_own.append(q)
            d_own.append(do)
        lse = lse_ref[g]
        queries = qa[...]
        qpad = qz[...]
        dpad = dz[...]
        dot_t = dpad[:, 64:].astype(F32).T
        delta = jnp.sum(ot_ref[g] * dot_t, axis=0, keepdims=True)
        s = jnp.where(triangle(), jnp.concatenate(score, axis=1), NEG)
        p = jnp.exp(s - lse)
        ds = (p * (jnp.concatenate(dprob, axis=1) - delta)).astype(BF)
        pb = p.astype(BF)
        dq = []
        for u in range(4):
            lanes = slice(64 * u, 64 * u + 64)
            grad = jnp.concatenate([dot(ds[:, lanes], q_own[u]), dot(pb[:, lanes], d_own[u])], axis=1)
            dkv[places[u], :] += grad
            dq.append(dot(keys_own[u], ds[:, lanes], TN))

        def chunk(c, dq):
            at = pl.ds(pl.multiple_of(c * 512, 512), 512)
            p = jnp.exp(dot(kaug[at, :], queries, NT) - lse)
            dp = dot(kvs[at, :], dpad, NT)
            ds = (p * (dp - delta)).astype(BF)
            dkv[at, :] += dot(ds, qpad) + dot(p.astype(BF), dpad)
            return dq + dot(kvt[c, :64, :], ds)

        chunks = (oblk[4 * g + 3] + 7) // 8
        dq = lax.fori_loop(0, chunks, chunk, jnp.concatenate(dq, axis=1))
        back = (dq * 0.125).T.astype(BF)
        for u in range(4):
            dqs[order[4 * g + u]] = back[64 * u:64 * u + 64, :]
        return carry

    lax.fori_loop(0, 8, tile, 0)
    for j in range(16):
        dq_ref[j] = jnp.concatenate([dqs[2 * j], dqs[2 * j + 1]], axis=1)
    for s in range(64):
        at = pl.ds(pl.multiple_of(blk[s] * 64, 64), 64)
        dkv_ref[s // 2, (s % 2) * 64:(s % 2) * 64 + 64, :] = dkv[at, :].astype(BF)


def attend_back(blk, mask, kvr, qr, dor, ot, lse):
    return pl.pallas_call(
        attend_back_kernel,
        out_shape=[shp((32, 128, 128), BF), shp((16, 64, 128), BF)],
        in_specs=[SM] + [VM] * 6,
        out_specs=[VM] * 2,
        scratch_shapes=attention_scratch()
        + [
            pltpu.VMEM((32, 64, 64), BF),
            pltpu.VMEM((256, 128), BF),
            pltpu.VMEM((256, 128), BF),
            pltpu.VMEM((4096, 128), F32),
        ],
        compiler_params=pltpu.CompilerParams(vmem_limit_bytes=LIMIT),
        cost_estimate=pl.CostEstimate(flops=25 << 30, bytes_accessed=64 << 20, transcendentals=4 << 20),
        name="attend_back",
    )(blk, mask, kvr, qr, dor, ot, lse)


def norm_parts(v):
    center = v - jnp.mean(v, axis=1, keepdims=True)
    r = lax.rsqrt(jnp.mean(center * center, axis=1, keepdims=True) + EPS)
    return center * r, r


def norm_back(e, gain, z, r):
    g = e * gain
    return r * (g - jnp.mean(g, axis=1, keepdims=True) - z * jnp.mean(g * z, axis=1, keepdims=True))


def middle_kernel(
    o_ref, x_ref, e_ref, ln_ref, a0, a1, a2, a3, u0, u1, u2, u3,
    y_ref, dr_ref, do_ref, zpay, cpay, l_ref, gb_ref,
    woi, wu, us, gs, dus, nl, ob, so, si, su,
):
    w = lax.axis_index("wsh")
    zh, co = w // 2, w % 2
    where = [w, zh * 2 + 1 - co, (1 - zh) * 2 + co, (1 - zh) * 2 + 1 - co]
    copies = [[], [], []]
    for r, (a, u) in enumerate(((a0, u0), (a1, u1), (a2, u2), (a3, u3))):
        rows = pl.ds(pl.multiple_of(where[r] * 256, 256), 256)
        copies[0].append(pltpu.make_async_copy(a.at[:, :1024], woi.at[rows, :1024], so.at[r]))
        copies[1].append(pltpu.make_async_copy(a.at[:, 1024:], woi.at[rows, 1024:], si.at[r]))
        rows = pl.ds(pl.multiple_of(where[r] * 1024, 1024), 1024)
        copies[2].append(pltpu.make_async_copy(u, wu.at[rows, :], su.at[r]))
    for group in copies:
        for c in group:
            c.start()

    ln = jnp.concatenate([ln_ref[k] for k in range(4)], axis=1)
    gain0, gain1, bias0, bias1 = (ln[k:k + 1, :] for k in range(4))
    for h in range(16):
        pair = o_ref[h]
        ob[:64, 64 * h:64 * h + 64] = pair[:, :64]
        ob[64:, 64 * h:64 * h + 64] = pair[:, 64:]
    for c in copies[0]:
        c.wait()
    z0, r0 = norm_parts(x_ref[...].astype(F32) + dot(ob[...], woi[:, :1024]))
    n1 = z0 * gain0 + bias0
    nl[...] = n1.astype(BF)
    for c in copies[1]:
        c.wait()

    half = math.sqrt(0.5)

    def up(c, carry):
        cols = pl.ds(pl.multiple_of(1024 + c * 512, 512), 512)
        u = dot(nl[...], woi[:, cols])
        us[c] = u
        gs[:, pl.ds(pl.multiple_of(c * 512, 512), 512)] = (0.5 * u * (1.0 + lax.erf(u * half))).astype(BF)
        return carry

    lax.fori_loop(0, 8, up, 0)
    for c in copies[2]:
        c.wait()

    def down(c, total):
        cols = pl.ds(pl.multiple_of(c * 512, 512), 512)
        return total + dot(gs[:, cols], wu[cols, :])

    r2 = lax.fori_loop(0, 8, down, n1)
    z1, r1 = norm_parts(r2)
    y_ref[...] = z1 * gain1 + bias1
    e = e_ref[...].astype(F32)
    dr2 = norm_back(e, gain1, z1, r1)
    dm = dr2.astype(BF)
    gb_ref[1:2, :] = jnp.sum(e * z1, axis=0, keepdims=True)
    gb_ref[3:4, :] = jnp.sum(e, axis=0, keepdims=True)

    def back(c, total):
        rows = pl.ds(pl.multiple_of(c * 512, 512), 512)
        cols = pl.ds(pl.multiple_of(1024 + c * 512, 512), 512)
        u = us[c]
        dg = dot(dm, wu[rows, :], NT)
        slope = 0.5 * (1.0 + lax.erf(u * half)) + u * (jnp.exp(-0.5 * u * u) * (1.0 / math.sqrt(2 * math.pi)))
        du = (dg * slope).astype(BF)
        dus[:, rows] = du
        return total + dot(du, woi[:, cols], NT)

    dn1 = lax.fori_loop(0, 8, back, dr2)
    gb_ref[0:1, :] = jnp.sum(dn1 * z0, axis=0, keepdims=True)
    gb_ref[2:3, :] = jnp.sum(dn1, axis=0, keepdims=True)
    gb_ref[4:8, :] = jnp.zeros((4, 1024), F32)
    dr1 = norm_back(dn1, gain0, z0, r0)
    dr_ref[...] = dr1
    da = dr1.astype(BF)
    do = dot(da, woi[:, :1024], NT).astype(BF)
    for h in range(16):
        lanes = slice(64 * h, 64 * h + 64)
        do_ref[h] = jnp.concatenate([do[:64, lanes], do[64:, lanes]], axis=1)
    du = dus[...]
    for ref, at in ((zpay, 1536), (cpay, 0)):
        ref[:, at:at + 4096] = du
        ref[:, at + 4096:at + 5120] = dm
        ref[:, at + 5120:at + 6144] = da
    for r, (ref, at) in enumerate(((l_ref, 0), (cpay, 6144), (zpay, 0), (zpay, 7680))):
        few = pl.ds(pl.multiple_of(where[r] * 256, 256), 256)
        many = pl.ds(pl.multiple_of(where[r] * 1024, 1024), 1024)
        ref[:, at:at + 256] = nl[:, few]
        ref[:, at + 256:at + 512] = ob[:, few]
        ref[:, at + 512:at + 1536] = gs[:, many]


def middle(o, tok, cot, lnf, a, u):
    return pl.pallas_call(
        middle_kernel,
        out_shape=[
            shp((128, 1024), F32), shp((128, 1024), F32), shp((16, 64, 128), BF),
            shp((128, 9216), BF), shp((128, 7680), BF), shp((128, 1536), BF), shp((8, 1024), F32),
        ],
        in_specs=[VM] * 4 + [ANY] * 8,
        out_specs=[VM] * 7,
        scratch_shapes=[
            pltpu.VMEM((1024, 5120), BF),
            pltpu.VMEM((4096, 1024), BF),
            pltpu.VMEM((8, 128, 512), F32),
            pltpu.VMEM((128, 4096), BF),
            pltpu.VMEM((128, 4096), BF),
            pltpu.VMEM((128, 1024), BF),
            pltpu.VMEM((128, 1024), BF),
            DMA((4,)), DMA((4,)), DMA((4,)),
        ],
        compiler_params=pltpu.CompilerParams(vmem_limit_bytes=LIMIT),
        cost_estimate=pl.CostEstimate(flops=10 << 30, bytes_accessed=32 << 20, transcendentals=2 << 20),
        name="middle",
    )(o, tok, cot, lnf, *a, *u)


def wgrad_mid_kernel(own_l, own, zr, c1, c2, out, ll, rr, lt, sem):
    copies = []
    for k, (lsrc, rsrc) in enumerate((
        (own_l, own.at[:, :6144]),
        (zr.at[:, :1536], zr.at[:, 1536:7680]),
        (c1.at[:, 6144:], c1.at[:, :6144]),
        (c2.at[:, 6144:], c2.at[:, :6144]),
    )):
        rows = slice(128 * k, 128 * k + 128)
        copies.append(pltpu.make_async_copy(lsrc, ll.at[rows, :], sem.at[2 * k]))
        copies.append(pltpu.make_async_copy(rsrc, rr.at[rows, :], sem.at[2 * k + 1]))
    for c in copies:
        c.start()
    for c in copies:
        c.wait()
    for k in range(6):
        lt[256 * k:256 * k + 256, :] = ll[:, 256 * k:256 * k + 256].astype(F32).T.astype(BF)
    out[0:256, :] = dot(lt[256:512, :], rr[:, 5120:6144]).astype(BF)
    for k in range(4):
        out[256 + 256 * k:512 + 256 * k, :] = dot(lt[0:256, :], rr[:, 1024 * k:1024 * k + 1024]).astype(BF)
    for k in range(4):
        rows = slice(512 + 256 * k, 768 + 256 * k)
        out[1280 + 256 * k:1536 + 256 * k, :] = dot(lt[rows, :], rr[:, 4096:5120]).astype(BF)


def wgrad_mid(own_l, own, zr, c1, c2):
    return pl.pallas_call(
        wgrad_mid_kernel,
        out_shape=shp((2304, 1024), BF),
        in_specs=[ANY] * 5,
        out_specs=VM,
        scratch_shapes=[
            pltpu.VMEM((512, 1536), BF), pltpu.VMEM((512, 6144), BF), pltpu.VMEM((1536, 512), BF), DMA((8,)),
        ],
        compiler_params=pltpu.CompilerParams(vmem_limit_bytes=LIMIT),
        cost_estimate=pl.CostEstimate(flops=2 << 30, bytes_accessed=16 << 20, transcendentals=0),
        name="wgrad_mid",
    )(own_l, own, zr, c1, c2)


def wgrad_tail_kernel(xs, p0, p1, p2, p3, out, vec, ll, rr, sem):
    w = lax.axis_index("wsh")
    zh, co = w // 2, w % 2
    where = [w, zh * 2 + 1 - co, (1 - zh) * 2 + co, (1 - zh) * 2 + 1 - co]
    copies = []
    for k, p in enumerate((p0, p1, p2, p3)):
        rows = slice(128 * k, 128 * k + 128)
        copies.append(pltpu.make_async_copy(xs.at[where[k]], ll.at[rows, :], sem.at[2 * k]))
        copies.append(pltpu.make_async_copy(p, rr.at[k], sem.at[2 * k + 1]))
    for c in copies:
        c.start()
    for c in copies:
        c.wait()
    lt = ll[...].astype(F32).T.astype(BF)
    for m in range(3):
        cols = slice(1024 * m, 1024 * m + 1024)
        total = dot(lt[:, 0:128], rr[0, :128, cols])
        for k in range(1, 4):
            total += dot(lt[:, 128 * k:128 * k + 128], rr[k, :128, cols])
        out[256 * m:256 * m + 256, :] = total.astype(BF)
    mine = pl.ds(pl.multiple_of(w * 256, 256), 256)
    vec[...] = sum(rr[k, 128:144, mine].astype(F32) for k in range(4))[:8]


def wgrad_tail(xs, p0, p1, p2, p3):
    return pl.pallas_call(
        wgrad_tail_kernel,
        out_shape=[shp((768, 1024), BF), shp((8, 256), F32)],
        in_specs=[ANY] * 5,
        out_specs=[VM] * 2,
        scratch_shapes=[pltpu.VMEM((512, 256), BF), pltpu.VMEM((4, 144, 3072), BF), DMA((8,))],
        compiler_params=pltpu.CompilerParams(vmem_limit_bytes=LIMIT),
        cost_estimate=pl.CostEstimate(flops=1 << 30, bytes_accessed=8 << 20, transcendentals=0),
        name="wgrad_tail",
    )(xs, p0, p1, p2, p3)


def tokens_back_kernel(dkv, dqp, w_ref, dr_ref, gb, gt, pay):
    for h in range(16):
        lanes = slice(64 * h, 64 * h + 64)
        pair = dqp[h]
        pay[:64, lanes] = pair[:, :64]
        pay[64:128, lanes] = pair[:, 64:]
        both = (dkv[h].astype(F32) + dkv[16 + h].astype(F32)).astype(BF)
        pay[:128, 1024 + 64 * h:1088 + 64 * h] = both[:, :64]
        pay[:128, 2048 + 64 * h:2112 + 64 * h] = both[:, 64:]
    pay[128:144, :1024] = jnp.concatenate([gb[...], jnp.zeros((8, 1024), F32)], axis=0).astype(BF)
    pay[128:144, 1024:] = jnp.zeros((16, 2048), BF)
    for k in range(4):
        cols = slice(256 * k, 256 * k + 256)
        total = dr_ref[:, cols]
        for m in range(3):
            total += dot(pay[:128, 1024 * m:1024 * m + 1024], w_ref[k, m], NT)
        gt[:, cols] = total


def tokens_back(dkv, dqp, wall, dr, gb):
    return pl.pallas_call(
        tokens_back_kernel,
        out_shape=[shp((128, 1024), F32), shp((144, 3072), BF)],
        in_specs=[VM] * 5,
        out_specs=[VM] * 2,
        compiler_params=pltpu.CompilerParams(vmem_limit_bytes=LIMIT),
        cost_estimate=pl.CostEstimate(flops=1 << 30, bytes_accessed=8 << 20, transcendentals=0),
        name="tokens_back",
    )(dkv, dqp, wall, dr, gb)


def total_kernel(hc, outs_of, with_vec, scale, refs):
    refs = list(refs)
    g = refs.pop(0)
    vec = refs.pop(0) if with_vec else None
    n_out = len(outs_of)
    outs = [refs.pop(0) for _ in range(n_out)]
    vout = refs.pop(0) if with_vec else None
    r1, s1, r2, s2, r3, full, ss, rs = refs[:8]
    if with_vec:
        vx, vy, vz, tx, ty = refs[8:]
    zl, x, y, zh, co = place()
    xp = [device(zl, (x + s) % 4, y, zh, co) for s in (1, 2, 3)]
    yp = [device(zl, x, (y + s) % 4, zh, co) for s in (1, 2, 3)]
    zp = device(1 - zl, x, y, zh, co)
    greet(xp + yp + [zp])
    wire = Wire(ss, rs)
    first = [xp, yp]
    second = [yp, xp]
    at1 = [x, y]
    at2 = [y, x]

    def rows(h, k):
        return pl.ds(pl.multiple_of(h * 4 * hc + k * hc, 16), hc)

    def cols(k, width):
        return pl.ds(pl.multiple_of(k * width, 128), width)

    sends = []
    one = [[], []]
    for s in range(3):
        for h in range(2):
            one[h].append(wire(g.at[rows(h, (at1[h] + s + 1) % 4)], r1.at[h, s], first[h][s]))
    if with_vec:
        vone = [wire(vec, vx.at[s], xp[s]) for s in range(3)]
        sends += vone
    two = [[], []]
    for h in range(2):
        for c in one[h]:
            c.wait_recv()
        total = g[rows(h, at1[h]), :].astype(F32)
        for s in range(3):
            total += r1[h, s].astype(F32)
        s1[h] = total.astype(BF)
        for s in range(3):
            two[h].append(wire(s1.at[h, :, cols((at2[h] + s + 1) % 4, 256)], r2.at[h, s], second[h][s]))
    if with_vec:
        for c in vone:
            c.wait_recv()
        tx[...] = vec[...] + vx[0] + vx[1] + vx[2]
        vtwo = [wire(tx, vy.at[s], yp[s]) for s in range(3)]
        sends += vtwo
    three = []
    for h in range(2):
        for c in two[h]:
            c.wait_recv()
        total = s1[h, :, cols(at2[h], 256)].astype(F32)
        for s in range(3):
            total += r2[h, s].astype(F32)
        s2[h] = total.astype(BF)
        three.append(wire(s2.at[h, :, cols(1 - zl, 128)], r3.at[h], zp))
    if with_vec:
        for c in vtwo:
            c.wait_recv()
        ty[...] = tx[...] + vy[0] + vy[1] + vy[2]
        vthree = wire(ty, vz, zp)
        sends.append(vthree)
    four = []
    for h in range(2):
        three[h].wait_recv()
        total = s2[h, :, cols(zl, 128)].astype(F32) + r3[h].astype(F32)
        spot = full.at[rows(h, at1[h]), cols(at2[h] * 2 + zl, 128)]
        spot[...] = total.astype(BF)
        four.append(wire(spot, spot, zp))
    five = [[], []]
    for h in range(2):
        four[h].wait()
        spot = full.at[rows(h, at1[h]), cols(at2[h], 256)]
        for s in range(3):
            five[h].append(wire(spot, spot, second[h][s]))
    six = [[], []]
    for h in range(2):
        for c in five[h]:
            c.wait()
        spot = full.at[rows(h, at1[h])]
        for s in range(3):
            six[h].append(wire(spot, spot, first[h][s]))
    for c in sends + one[0] + one[1] + two[0] + two[1] + three:
        c.wait_send()
    if with_vec:
        vthree.wait_recv()
        vout[...] = (ty[...] + vz[...]) * scale
    for c in six[0] + six[1]:
        c.wait()
    for ref, spots in zip(outs, outs_of):
        for row, col, start, size in spots:
            ref[row:row + size, col:col + 1024] = full[start:start + size, :].astype(F32) * scale


def total(g, vec, outs_of, shapes, collective, scale):
    rows = g.shape[0]
    hc = rows // 8
    with_vec = vec is not None
    n = 28 + (7 if with_vec else 0)

    def kernel(*refs):
        total_kernel(hc, outs_of, with_vec, scale, refs)

    scratch = [
        pltpu.VMEM((2, 3, hc, 1024), BF),
        pltpu.VMEM((2, hc, 1024), BF),
        pltpu.VMEM((2, 3, hc, 256), BF),
        pltpu.VMEM((2, hc, 256), BF),
        pltpu.VMEM((2, hc, 128), BF),
        pltpu.VMEM((rows, 1024), BF),
        DMA((n,)), DMA((n,)),
    ]
    outs = [shp(s, F32) for s in shapes]
    if with_vec:
        scratch += [
            pltpu.VMEM((3, 8, 256), F32), pltpu.VMEM((3, 8, 256), F32), pltpu.VMEM((8, 256), F32),
            pltpu.VMEM((8, 256), F32), pltpu.VMEM((8, 256), F32),
        ]
        outs.append(shp((8, 256), F32))
    args = [g] + ([vec] if with_vec else [])
    return pl.pallas_call(
        kernel,
        out_shape=outs,
        in_specs=[VM] * len(args),
        out_specs=[VM] * len(outs),
        scratch_shapes=scratch,
        compiler_params=pltpu.CompilerParams(
            collective_id=collective, has_side_effects=True, vmem_limit_bytes=LIMIT
        ),
        name=f"total_{collective}",
    )(*args)


FLIP_CORE = [(0, 1), (1, 0), (2, 3), (3, 2)]
FLIP_FAR = [(0, 2), (2, 0), (1, 3), (3, 1)]


def body(
    tokens, w_query, w_key, w_value, w_output, w_inner, w_outer, ln_gain, ln_bias, block_mask, block_pairs, cotangent,
):
    tok = tokens.reshape(128, 1024)
    cot = cotangent.reshape(128, 1024)
    scale = 1.0 / math.sqrt(16384)
    lnp = jnp.concatenate([ln_gain, ln_bias, jnp.zeros((4, 256), F32)], axis=0)
    blk = block_pairs.reshape(-1)

    wall, xs, lnf = gather_weights(w_query, w_key, w_value, tok, lnp)
    a_own = jnp.concatenate([w_output, w_inner], axis=1)
    a_own, u_own, wall = lax.optimization_barrier((a_own, w_outer, wall))
    a_far = lax.ppermute(a_own, "wsh", FLIP_FAR)
    u_far = lax.ppermute(u_own, "wsh", FLIP_FAR)
    a_core = lax.ppermute(a_own, "wsh", FLIP_CORE)
    u_core = lax.ppermute(u_own, "wsh", FLIP_CORE)
    a_diag = lax.ppermute(a_far, "wsh", FLIP_CORE)
    u_diag = lax.ppermute(u_far, "wsh", FLIP_CORE)

    kvp, qp = project(tok, wall)
    kvr, qr = exchange(kvp, qp, 2)
    o, ot, lse = attend(blk, block_mask, kvr, qr)
    (o_back,) = exchange(None, o, 3)
    y, dr1, do, zpay, cpay, own_l, gb = middle(
        o_back, tok, cot, lnf, (a_own, a_core, a_far, a_diag), (u_own, u_core, u_far, u_diag)
    )
    zr = lax.ppermute(zpay, "wsh", FLIP_FAR)
    c1 = lax.ppermute(cpay, "wsh", FLIP_CORE)
    c2 = lax.ppermute(zr[:, 1536:], "wsh", FLIP_CORE)

    (dor,) = exchange(None, do, 3)
    dkvp, dqp = attend_back(blk, block_mask, kvr, qr, dor, ot, lse)
    dkvr, dqr = exchange(dkvp, dqp, 4)
    grad_tok, pay = tokens_back(dkvr, dqr, wall, dr1, gb)
    t1 = lax.ppermute(pay, "wsh", FLIP_CORE)
    t2 = lax.ppermute(pay, "wsh", FLIP_FAR)
    t3 = lax.ppermute(t2, "wsh", FLIP_CORE)

    gmid = wgrad_mid(own_l, cpay, zr, c1, c2)
    s_o, s_i, s_u = total(
        gmid, None,
        [
            [(0, 0, 0, 256)],
            [(0, 1024 * k, 256 + 256 * k, 256) for k in range(4)],
            [(0, 0, 1280, 1024)],
        ],
        [(256, 1024), (256, 4096), (1024, 1024)], 5, scale,
    )
    gtail, vec = wgrad_tail(xs, pay, t1, t2, t3)
    s_q, s_k, s_v, s_vec = total(
        gtail, vec, [[(0, 0, 256 * k, 256)] for k in range(3)], [(256, 1024)] * 3, 6, scale
    )
    out_shape = tokens.shape
    return (
        y.reshape(out_shape), grad_tok.reshape(out_shape), s_q, s_k, s_v, s_o, s_i, s_u, s_vec[0:2], s_vec[2:4],
    )


def solution(mesh):
    return jax.shard_map(
        body,
        mesh=mesh,
        in_specs=(
            P("wsh", "ctx", None, None),
            P("wsh", None), P("wsh", None), P("wsh", None), P("wsh", None), P("wsh", None), P("wsh", None),
            P(None, "wsh"), P(None, "wsh"),
            P("wsh", None, None),
            P(),
            P("wsh", "ctx", None, None),
        ),
        out_specs=(
            P("wsh", "ctx", None, None), P("wsh", "ctx", None, None),
            P("wsh", None), P("wsh", None), P("wsh", None), P("wsh", None), P("wsh", None), P("wsh", None),
            P(None, "wsh"), P(None, "wsh"),
        ),
        check_vma=False,
    )
```

time: 1890 us -> 516 us (0.27)
  waiting for transfers between devices: 1410 us -> 117 us
  Pallas kernels: 0 us -> 368 us
  matrix products: 164 us -> 0 us
  local copies, waits for them, and re-layouts: 132 us -> 16.6 us
  blocking collectives: 95 us -> 0 us
  other arithmetic: 56.4 us -> 2.65 us
    all_gather x8 -> x0, waiting for transfers between devices: 463 us -> none  [the longest x1 166 us: body(): lax.all_gather(values_own, 'ctx', axis=0, tiled=True)]
    unnamed x23 -> x0, waiting for transfers between devices: 383 us -> none
    pallas_call x0 -> x14, Pallas kernels: none -> 368 us  [the longest x2 126 us: total(): pl.pallas_call(kernel, out_shape=outs, in_specs=[VM] * len(args), out_spe...]
    reduce_scatter x6 -> x0, waiting for transfers between devices: 316 us -> none  [the longest x1 80.8 us: body(): lax.psum_scatter(grad_wu.astype(jnp.bfloat16), 'wsh', scatter_dimension=0...]
    psum x1 -> x0, waiting for transfers between devices: 250 us -> none  [body(): lax.psum(shard_q.astype(jnp.bfloat16), 'ctx').astype(jnp.float32)]
    dot_general x47 -> x0, matrix products: 164 us -> none  [the longest x8 34.8 us: head_scores(): jnp.einsum('qhd,khd->hqk', query_part, key_part, preferred_element_type=j...]
    ppermute x0 -> x12, waiting for transfers between devices: none -> 117 us  [the longest x1 57.8 us: body(): a_far = lax.ppermute(a_own, 'wsh', FLIP_FAR)]
    psum x1 -> x0, blocking collectives: 81.9 us -> none  [body(): lax.psum(shard_g.astype(jnp.bfloat16), 'ctx').astype(jnp.float32)]
  transfers between devices with their start and end apart: 19 -> 12, of which waited for: 18 -> 4; matrix products, arithmetic and copies ran while one was open for 8% -> 1% of each run, Pallas kernels for 0% -> 36%
where the time goes in v1:
time: 516 us; the launch traced here: 515 us
  Pallas kernels  368 us (71%)
  waiting for transfers between devices  117 us (23%)
  local copies, waits for them, and re-layouts  16.6 us (3%)
  starting transfers between devices  9.59 us (2%)
    pallas_call x2, Pallas kernels, total(): pl.pallas_call(kernel, out_shape=outs, in_specs=[VM] * len(args), out_spe...  126 us
    pallas_call x4, Pallas kernels, exchange(): pl.pallas_call(kernel, out_shape=outs, in_specs=[ANY] * len(args), out_sp...  78.8 us
    ppermute x1, waiting for transfers between devices, body(): a_far = lax.ppermute(a_own, 'wsh', FLIP_FAR)  57.8 us
    pallas_call x1, Pallas kernels, gather_weights(): pl.pallas_call(gather_kernel, out_shape=[shp((4, 3, 256, 1024), BF), shp(...  55.6 us
    ppermute x1, waiting for transfers between devices, body(): u_far = lax.ppermute(u_own, 'wsh', FLIP_FAR)  43.6 us
    pallas_call x1, Pallas kernels, attend(): pl.pallas_call(attend_kernel, out_shape=[shp((16, 64, 128), BF), shp((8,...  28.6 us
    pallas_call x1, Pallas kernels, attend_back(): pl.pallas_call(attend_back_kernel, out_shape=[shp((32, 128, 128), BF), sh...  28.4 us
    pallas_call x1, Pallas kernels, middle(): pl.pallas_call(middle_kernel, out_shape=[shp((128, 1024), F32), shp((128,...  23 us
  transfers between devices with their start and end apart: 12, of which 4 were waited for; matrix products, arithmetic and copies ran while one was open for 1% of the time, Pallas kernels for 36%

profile of v1, /device:TPU:0, one launch (start us, length us, event | category | flops | bytes accessed | tf_op | source)
XLA Modules:
  0.0 515.1 jit_solution(10714732782491205457)
XLA Ops:
  0.7 1.9 pad_maximum_fusion.a0
  3.4 55.6 %gather_qkv.1 = (bf16[4,3,256,1024]{3,2,1,0:T(8,128)(2,1)}, bf16[4,128,256]{2,1,0:T(8,128)(2,1)}, f32[4,8,256]{2,1,0:T(8,128)}) custom-call(bf16[256,1024]{1,0:T(8,128)(2,1)} %wq.1, bf16[256,1024]{1,0:T(8,128)(2,1)} %wk.1, bf16[256,1024]{1,0:T(8,128)(2,1)} %wv.1, bf16[128,1024]{1,0:T(8,128)(2,1)} %bitcast.4, f32[8,256]{1,0:T(8,128)} %maximum_maximum_fusion.ln_ref), custom_call_target="tpu_custom_call" | custom-call | tf_op jit(solution)/shard_map/gather_qkv/pallas_call | solution.py:128
  59.1 3.3 collective-permute-start.1
  62.7 57.8 %collective-permute-done.1.a2 = bf16[256,5120]{1,0:T(8,128)(2,1)} collective-permute-done((bf16[256,5120]{1,0:T(8,128)(2,1)S(1)}, bf16[256,5120]{1,0:T(8,128)(2,1)}, u32[]{:S(2)}, u32[]{:S(2)}) %collective-permute-start.1) | collective-permute-done | bytes 2621472 | tf_op jit(solution)/shard_map/ppermute | solution.py:852
  121.0 43.6 %collective-permute-done.4.u2 = bf16[1024,1024]{1,0:T(8,128)(2,1)} collective-permute-done((bf16[1024,1024]{1,0:T(8,128)(2,1)}, bf16[1024,1024]{1,0:T(8,128)(2,1)}, u32[]{:S(2)}, u32[]{:S(2)}) %collective-permute-start.4) | collective-permute-done | bytes 2097184 | tf_op jit(solution)/shard_map/ppermute | solution.py:853
  165.3 7.9 %qkv.1 = (bf16[16,128,128]{2,1,0:T(8,128)(2,1)}, bf16[16,64,128]{2,1,0:T(8,128)(2,1)}) custom-call(bf16[128,1024]{1,0:T(8,128)(2,1)} %bitcast.5, bf16[4,3,256,1024]{3,2,1,0:T(8,128)(2,1)} %get-tuple-element.46.w_ref), custom_call_target="tpu_custom_call" | custom-call | flops 805306368 | bytes 8388608 | tf_op jit(solution)/shard_map/qkv/pallas_call | solution.py:155
  173.2 27.3 %exchange_2.1 = (bf16[32,128,128]{2,1,0:T(8,128)(2,1)}, bf16[16,64,128]{2,1,0:T(8,128)(2,1)}) custom-call(bf16[16,128,128]{2,1,0:T(8,128)(2,1)} %get-tuple-element.47.refs_0_, bf16[16,64,128]{2,1,0:T(8,128)(2,1)} %get-tuple-element.48.refs_1_), custom_call_target="tpu_custom_call" | custom-call | tf_op jit(solution)/shard_map/exchange_2/pallas_call | solution.py:244
  200.5 28.6 %attend.1 = (bf16[16,64,128]{2,1,0:T(8,128)(2,1)}, f32[8,64,256]{2,1,0:T(8,128)}, f32[8,1,256]{2,1,0:T(1,128)}) custom-call(s32[64]{0:T(128)} %reshape.35.blk, s32[1,64,64]{2,1,0:T(8,128)} %mask.3, bf16[32,128,128]{2,1,0:T(8,128)(2,1)} %get-tuple-element.49.kvr, bf16[16,64,128]{2,1,0:T(8,128)(2,1)} %get-tuple-element.50.qr), custom_call_target="tpu_custom_call" | custom-call | flops 10737418240 | bytes 33554432 | tf_op jit(solution)/shard_map/attend/pallas_call | solution.py:360
  229.2 9.2 %exchange_3.2.o_ref = bf16[16,64,128]{2,1,0:T(8,128)(2,1)} custom-call(bf16[16,64,128]{2,1,0:T(8,128)(2,1)} %get-tuple-element.51.refs_0_), custom_call_target="tpu_custom_call" | custom-call | tf_op jit(solution)/shard_map/exchange_3/pallas_call | solution.py:244
  238.4 23.0 %middle.1 = (f32[128,1024]{1,0:T(8,128)}, f32[128,1024]{1,0:T(8,128)}, bf16[16,64,128]{2,1,0:T(8,128)(2,1)}, bf16[128,9216]{1,0:T(8,128)(2,1)}, bf16[128,7680]{1...) custom-call(bf16[16,64,128]{2,1,0:T(8,128)(2,1)} %exchange_3.2.o_ref, bf16[128,1024]{1,0:T(8,128)(2,1)} %bitcast.6, ...), custom_call_target="tpu_custom_call" | custom-call | flops 10737418240 | bytes 33554432 | tf_op jit(solution)/shard_map/middle/pallas_call | solution.py:567
  261.4 9.3 %exchange_3.3.dor = bf16[16,64,128]{2,1,0:T(8,128)(2,1)} custom-call(bf16[16,64,128]{2,1,0:T(8,128)(2,1)} %get-tuple-element.56.refs_0_), custom_call_target="tpu_custom_call" | custom-call | tf_op jit(solution)/shard_map/exchange_3/pallas_call | solution.py:244
  270.7 1.4 collective-permute-start.9
  272.2 28.4 %attend_back.1 = (bf16[32,128,128]{2,1,0:T(8,128)(2,1)}, bf16[16,64,128]{2,1,0:T(8,128)(2,1)}) custom-call(s32[64]{0:T(128)} %reshape.35.blk, s32[1,64,64]{2,1,0:T(8,128)} %mask.3, bf16[32,128,128]{2,1,0:T(8,128)(2,1)} %get-tuple-element.49.kvr, bf16[16,64,128]{2,1,0:T(8,128)(2,1)} %get-tuple-element.50.qr, bf16[16,64,128]{2,1,0:T(8,128)(2,1)} %exchange_3.3.dor, ...), custom_call_target="tpu_custom_call" | custom-call | flops 26843545600 | bytes 67108864 | tf_op jit(solution)/shard_map/attend_back/pallas_call | solution.py:444
  300.5 32.9 %exchange_4.1 = (bf16[32,128,128]{2,1,0:T(8,128)(2,1)}, bf16[16,64,128]{2,1,0:T(8,128)(2,1)}) custom-call(bf16[32,128,128]{2,1,0:T(8,128)(2,1)} %get-tuple-element.59.refs_0_, bf16[16,64,128]{2,1,0:T(8,128)(2,1)} %get-tuple-element.60.refs_1_), custom_call_target="tpu_custom_call" | custom-call | tf_op jit(solution)/shard_map/exchange_4/pallas_call | solution.py:244
  333.4 6.6 %tokens_back.1 = (f32[128,1024]{1,0:T(8,128)}, bf16[144,3072]{1,0:T(8,128)(2,1)}) custom-call(bf16[32,128,128]{2,1,0:T(8,128)(2,1)} %get-tuple-element.61.dkv, bf16[16,64,128]{2,1,0:T(8,128)(2,1)} %get-tuple-element.62.dqp, bf16[4,3,256,1024]{3,2,1,0:T(8,128)(2,1)} %get-tuple-element.46.w_ref, f32[128,1024]{1,0:T(8,128)} %get-tuple-element.63.dr_ref, ...), custom_call_target="tpu_custom_call" | custom-call | flops 1073741824 | bytes 8388608 | tf_op jit(solution)/shard_map/tokens_back/pallas_call | solution.py:688
  340.1 3.5 collective-permute-start.7
  343.6 1.5 slice.12
  345.6 14.5 %collective-permute-done.7.p2 = bf16[144,3072]{1,0:T(8,128)(2,1)S(1)} collective-permute-done((bf16[144,3072]{1,0:T(8,128)(2,1)}, bf16[144,3072]{1,0:T(8,128)(2,1)S(1)}, u32[]{:S(2)}, u32[]{:S(2)}) %collective-permute-start.7) | collective-permute-done | bytes 884768 | tf_op jit(solution)/shard_map/ppermute | solution.py:875
  361.1 1.5 collective-permute-done.8.p3
  363.5 5.1 wgrad_tail.1
  368.6 41.2 %total_6.1 = (f32[256,1024]{1,0:T(8,128)}, f32[256,1024]{1,0:T(8,128)}, f32[256,1024]{1,0:T(8,128)}, f32[8,256]{1,0:T(8,128)}) custom-call(bf16[768,1024]{1,0:T(8,128)(2,1)} %get-tuple-element.68.refs_0_, f32[8,256]{1,0:T(8,128)} %get-tuple-element.69.refs_1_), custom_call_target="tpu_custom_call" | custom-call | tf_op jit(solution)/shard_map/total_6/pallas_call | solution.py:823
  409.8 1.4 fusion
  411.2 1.3 copy-done.5
  412.5 8.2 %wgrad_mid.1.refs_0_ = bf16[2304,1024]{1,0:T(8,128)(2,1)} custom-call(bf16[128,1536]{1,0:T(8,128)(2,1)} %get-tuple-element.73.own_l, bf16[128,7680]{1,0:T(8,128)(2,1)} %get-tuple-element.74.own, bf16[128,9216]{1,0:T(8,128)(2,1)} %copy-done, bf16[128,7680]{1,0:T(8,128)(2,1)} %copy-done.5, bf16[128,7680]{1,0:T(8,128)(2,1)} %collective-permute-done.11.c2), custom_call_target="tpu_custom_call" | custom-call | flops 2147483648 | bytes 16777216 | tf_op jit(solution)/shard_map/wgrad_mid/pallas_call | solution.py:617
  420.7 84.5 %total_5.1 = (f32[256,1024]{1,0:T(8,128)}, f32[256,4096]{1,0:T(8,128)}, f32[1024,1024]{1,0:T(8,128)}) custom-call(bf16[2304,1024]{1,0:T(8,128)(2,1)} %wgrad_mid.1.refs_0_), custom_call_target="tpu_custom_call" | custom-call | tf_op jit(solution)/shard_map/total_5/pallas_call | solution.py:823
  505.3 1.0 copy.30
  506.2 1.0 copy.31
  507.2 1.0 copy.32
  508.2 1.0 copy.33
  509.4 2.1 copy.34
  511.5 1.6 copy-done.1
  513.1 2.0 copy.35
  (54 shorter events, 5.0 us)
Async XLA Ops:
  0.7 1.9 copy-start.10
  0.7 1.9 copy-start.11
  0.7 163.9 %copy-start.12 = (s32[32,2]{0,1:T(2,128)S(1)}, s32[32,2]{0,1:T(2,128)}, u32[]{:S(2)}) copy-start(s32[32,2]{0,1:T(2,128)} %param.22) | copy-start | bytes 772
  2.6 170.5 %copy-start.3 = (bf16[256,5120]{1,0:T(8,128)(2,1)}, bf16[256,5120]{1,0:T(8,128)(2,1)S(1)}, u32[]{:S(2)}) copy-start(bf16[256,5120]{1,0:T(8,128)(2,1)S(1)} %pad_maximum_fusion.a0) | copy-start | bytes 7864324
  59.1 61.4 %collective-permute-start.1 = (bf16[256,5120]{1,0:T(8,128)(2,1)S(1)}, bf16[256,5120]{1,0:T(8,128)(2,1)}, u32[]{:S(2)}, u32[]{:S(2)}) collective-permute-start(bf16[256,5120]{1,0:T(8,128)(2,1)S(1)} %pad_maximum_fusion.a0), channel_id=1, source_target_pairs={{0,2},{2,0},{1,3},{3,1},{4,6},{6,4},{5,7},{7,5},{8,10},{10,8},{9,1... | collective-permute-start | bytes 7864328 | tf_op jit(solution)/shard_map/ppermute | solution.py:852
  62.3 102.3 %collective-permute-start.4 = (bf16[1024,1024]{1,0:T(8,128)(2,1)}, bf16[1024,1024]{1,0:T(8,128)(2,1)}, u32[]{:S(2)}, u32[]{:S(2)}) collective-permute-start(bf16[1024,1024]{1,0:T(8,128)(2,1)} %u0), channel_id=1, source_target_pairs={{0,2},{2,0},{1,3},{3,1},{4,6},{6,4},{5,7},{7,5},{8,10},{10,8},{9,1... | collective-permute-start | bytes 6291464 | tf_op jit(solution)/shard_map/ppermute | solution.py:853
  62.7 175.7 %collective-permute-start = (bf16[256,5120]{1,0:T(8,128)(2,1)S(1)}, bf16[256,5120]{1,0:T(8,128)(2,1)}, u32[]{:S(2)}, u32[]{:S(2)}) collective-permute-start(bf16[256,5120]{1,0:T(8,128)(2,1)S(1)} %pad_maximum_fusion.a0), channel_id=1, source_target_pairs={{0,1},{1,0},{2,3},{3,2},{4,5},{5,4},{6,7},{7,6},{8,9},{9,8},{10,11... | collective-permute-start | bytes 7864328 | tf_op jit(solution)/shard_map/ppermute | solution.py:854
  120.5 117.9 %collective-permute-start.2 = (bf16[256,5120]{1,0:T(8,128)(2,1)}, bf16[256,5120]{1,0:T(8,128)(2,1)}, u32[]{:S(2)}, u32[]{:S(2)}) collective-permute-start(bf16[256,5120]{1,0:T(8,128)(2,1)} %collective-permute-done.1.a2), channel_id=1, source_target_pairs={{0,1},{1,0},{2,3},{3,2},{4,5},{5,4},{6,7},{7,6},{8,9},{9,8},{10,11... | collective-permute-start | bytes 7864328 | tf_op jit(solution)/shard_map/ppermute | solution.py:856
  120.5 117.9 %collective-permute-start.3 = (bf16[1024,1024]{1,0:T(8,128)(2,1)}, bf16[1024,1024]{1,0:T(8,128)(2,1)}, u32[]{:S(2)}, u32[]{:S(2)}) collective-permute-start(bf16[1024,1024]{1,0:T(8,128)(2,1)} %u0), channel_id=1, source_target_pairs={{0,1},{1,0},{2,3},{3,2},{4,5},{5,4},{6,7},{7,6},{8,9},{9,8},{10,11... | collective-permute-start | bytes 6291464 | tf_op jit(solution)/shard_map/ppermute | solution.py:855
  164.6 73.8 %collective-permute-start.5 = (bf16[1024,1024]{1,0:T(8,128)(2,1)}, bf16[1024,1024]{1,0:T(8,128)(2,1)}, u32[]{:S(2)}, u32[]{:S(2)}) collective-permute-start(bf16[1024,1024]{1,0:T(8,128)(2,1)} %collective-permute-done.4.u2), channel_id=1, source_target_pairs={{0,1},{1,0},{2,3},{3,2},{4,5},{5,4},{6,7},{7,6},{8,9},{9,8},{10,11... | collective-permute-start | bytes 6291464 | tf_op jit(solution)/shard_map/ppermute | solution.py:857
  270.7 72.8 %collective-permute-start.9 = (bf16[128,9216]{1,0:T(8,128)(2,1)}, bf16[128,9216]{1,0:T(8,128)(2,1)S(1)}, u32[]{:S(2)}, u32[]{:S(2)}) collective-permute-start(bf16[128,9216]{1,0:T(8,128)(2,1)} %get-tuple-element.75), channel_id=1, source_target_pairs={{0,2},{2,0},{1,3},{3,1},{4,6},{6,4},{5,7},{7,5},{8,10},{10,8},{9,1... | collective-permute-start | bytes 7077896 | tf_op jit(solution)/shard_map/ppermute | solution.py:866
  333.4 10.1 %copy-start.4 = (bf16[128,7680]{1,0:T(8,128)(2,1)S(1)}, bf16[128,7680]{1,0:T(8,128)(2,1)}, u32[]{:S(2)}) copy-start(bf16[128,7680]{1,0:T(8,128)(2,1)} %get-tuple-element.74.own) | copy-start | bytes 5898244
  340.1 5.6 %copy-start.13 = (bf16[144,3072]{1,0:T(8,128)(2,1)S(1)}, bf16[144,3072]{1,0:T(8,128)(2,1)}, u32[]{:S(2)}) copy-start(bf16[144,3072]{1,0:T(8,128)(2,1)} %get-tuple-element.67.p0) | copy-start | bytes 2654212
  340.1 20.1 %collective-permute-start.7 = (bf16[144,3072]{1,0:T(8,128)(2,1)}, bf16[144,3072]{1,0:T(8,128)(2,1)S(1)}, u32[]{:S(2)}, u32[]{:S(2)}) collective-permute-start(bf16[144,3072]{1,0:T(8,128)(2,1)} %get-tuple-element.67.p0), channel_id=1, source_target_pairs={{0,2},{2,0},{1,3},{3,1},{4,6},{6,4},{5,7},{7,5},{8,10},{10,8},{9,1... | collective-permute-start | bytes 2654216 | tf_op jit(solution)/shard_map/ppermute | solution.py:875
  343.6 67.6 %collective-permute-start.10 = (bf16[128,7680]{1,0:T(8,128)(2,1)S(1)}, bf16[128,7680]{1,0:T(8,128)(2,1)S(1)}, u32[]{:S(2)}, u32[]{:S(2)}) collective-permute-start(bf16[128,7680]{1,0:T(8,128)(2,1)S(1)} %copy-done.4), channel_id=1, source_target_pairs={{0,1},{1,0},{2,3},{3,2},{4,5},{5,4},{6,7},{7,6},{8,9},{9,8},{10,11... | collective-permute-start | bytes 5898248 | tf_op jit(solution)/shard_map/ppermute | solution.py:867
  343.6 25.1 %copy-start = (bf16[128,9216]{1,0:T(8,128)(2,1)}, bf16[128,9216]{1,0:T(8,128)(2,1)S(1)}, u32[]{:S(2)}) copy-start(bf16[128,9216]{1,0:T(8,128)(2,1)S(1)} %collective-permute-done.9.zr) | copy-start | bytes 7077892
  345.1 66.1 %collective-permute-start.11 = (bf16[128,7680]{1,0:T(8,128)(2,1)}, bf16[128,7680]{1,0:T(8,128)(2,1)}, u32[]{:S(2)}, u32[]{:S(2)}) collective-permute-start(bf16[128,7680]{1,0:T(8,128)(2,1)} %slice.12), channel_id=1, source_target_pairs={{0,1},{1,0},{2,3},{3,2},{4,5},{5,4},{6,7},{7,6},{8,9},{9,8},{10,11... | collective-permute-start | bytes 5898248 | tf_op jit(solution)/shard_map/ppermute | solution.py:868
  345.6 14.6 %collective-permute-start.6 = (bf16[144,3072]{1,0:T(8,128)(2,1)S(1)}, bf16[144,3072]{1,0:T(8,128)(2,1)S(1)}, u32[]{:S(2)}, u32[]{:S(2)}) collective-permute-start(bf16[144,3072]{1,0:T(8,128)(2,1)S(1)} %copy-done.13), channel_id=1, source_target_pairs={{0,1},{1,0},{2,3},{3,2},{4,5},{5,4},{6,7},{7,6},{8,9},{9,8},{10,11... | collective-permute-start | bytes 2654216 | tf_op jit(solution)/shard_map/ppermute | solution.py:874
  360.2 0.9 copy-start.14
  360.2 2.4 collective-permute-start.8
  361.1 1.5 copy-start.15
  362.6 0.9 copy-start.16
  411.2 1.3 copy-start.5
  420.7 84.6 %copy-start.8 = (f32[256,1024]{1,0:T(8,128)S(1)}, f32[256,1024]{1,0:T(8,128)}, u32[]{:S(2)}) copy-start(f32[256,1024]{1,0:T(8,128)} %get-tuple-element.94) | copy-start | bytes 3145732
  420.7 85.6 %copy-start.7 = (f32[256,1024]{1,0:T(8,128)S(1)}, f32[256,1024]{1,0:T(8,128)}, u32[]{:S(2)}) copy-start(f32[256,1024]{1,0:T(8,128)} %get-tuple-element.95) | copy-start | bytes 3145732
  505.2 2.0 copy-start.6
  505.3 2.9 copy-start.9
  506.2 3.1 copy-start.2
  509.4 3.7 copy-start.1

commit v2 on v1

--- a/solution.py
+++ b/solution.py
@@ -64,7 +64,7 @@
         return copy
 
 
-def gather_kernel(wq, wk, wv, x_ref, ln_ref, wall, xs, lnf, ss, rs, ls):
+def gather_kernel(wq, wk, wv, x_ref, ln_ref, wo, wi, wu, wall, xs, lnf, co_ref, ci_ref, cu_ref, ss, rs):
     zl, x, y, zh, co = place()
     me = zh * 2 + co
     other = (1 - zh) * 2 + co
@@ -83,20 +83,12 @@
         first_a.append(wire(ws[m].at[rows_a], wall.at[me, m, rows_a], far))
         first_b.append(wire(ws[m].at[rows_b], wall.at[me, m, rows_b], far))
     rest = []
+    for m in range(3):
+        rest.append(wire(ws[m], wall.at[me, m], core))
     for p, idx in ((core, zh * 2 + 1 - co), (far, other), (diag, (1 - zh) * 2 + 1 - co)):
         cols = pl.ds(pl.multiple_of(idx * 256, 256), 256)
         rest.append(wire(x_ref.at[:, cols], xs.at[me], p))
         rest.append(wire(ln_ref, lnf.at[me], p))
-    for m in range(3):
-        rest.append(wire(ws[m], wall.at[me, m], core))
-    local = []
-    for m in range(3):
-        local.append(pltpu.make_async_copy(ws[m], wall.at[me, m], ls.at[m]))
-    own = pl.ds(pl.multiple_of(me * 256, 256), 256)
-    local.append(pltpu.make_async_copy(x_ref.at[:, own], xs.at[me], ls.at[3]))
-    local.append(pltpu.make_async_copy(ln_ref, lnf.at[me], ls.at[4]))
-    for c in local:
-        c.start()
     for c in first_a:
         c.wait_recv()
     second = []
@@ -110,6 +102,8 @@
         part = wall.at[other, m, rows_b]
         for p in yp:
             second.append(wire(part, part, p))
+    for src, dst in ((wo, co_ref), (wi, ci_ref), (wu, cu_ref)):
+        rest.append(wire(src, dst, core))
     for c in second:
         c.wait_recv()
     last = [wire(wall.at[other, m], wall.at[other, m], core) for m in range(3)]
@@ -119,55 +113,73 @@
         c.wait_send()
     for c in rest:
         c.wait()
-    for c in local:
-        c.wait()
-
-
-def gather_weights(wq, wk, wv, tok, lnp):
-    n = 6 + 6 + 3 + 18 + 3
+
+
+def gather_weights(wq, wk, wv, tok, lnp, wo, wi, wu):
+    n = 6 + 3 + 6 + 18 + 3 + 3
     return pl.pallas_call(
         gather_kernel,
-        out_shape=[shp((4, 3, 256, 1024), BF), shp((4, 128, 256), BF), shp((4, 8, 256), F32)],
-        in_specs=[ANY] * 5,
-        out_specs=[ANY] * 3,
-        scratch_shapes=[DMA((n,)), DMA((n,)), DMA((5,))],
+        out_shape=[
+            shp((4, 3, 256, 1024), BF), shp((4, 128, 256), BF), shp((4, 8, 256), F32),
+            shp(wo.shape, BF), shp(wi.shape, BF), shp(wu.shape, BF),
+        ],
+        in_specs=[ANY] * 8,
+        out_specs=[ANY] * 6,
+        scratch_shapes=[DMA((n,)), DMA((n,))],
         compiler_params=pltpu.CompilerParams(collective_id=1, has_side_effects=True),
         name="gather_qkv",
-    )(wq, wk, wv, tok, lnp)
-
-
-def qkv_kernel(x_ref, w_ref, kv_ref, q_ref):
-    x = x_ref[...]
-
-    def proj(m):
-        return dot(x, w_ref[:, m].reshape(1024, 128)).astype(BF)
-
-    q = (proj(0).astype(F32) * 0.125).astype(BF)
-    k = proj(1)
-    v = proj(2)
-    for u in range(2):
-        lanes = slice(64 * u, 64 * u + 64)
-        kv_ref[u] = jnp.concatenate([k[:, lanes], v[:, lanes]], axis=1)
-        q_ref[u] = jnp.concatenate([q[:64, lanes], q[64:, lanes]], axis=1)
-
-
-def project(tok, wall):
+    )(wq, wk, wv, tok, lnp, wo, wi, wu)
+
+
+def load_qkv(wall, own, weights, sem):
+    w = lax.axis_index("wsh")
+    copies = [
+        pltpu.make_async_copy(own[m], weights.at[w, m], sem.at[m]) for m in range(3)
+    ]
+    for r in range(1, 4):
+        k = (w + r) % 4
+        copies.append(pltpu.make_async_copy(wall.at[k], weights.at[k], sem.at[2 + r]))
+    for c in copies:
+        c.start()
+    return copies
+
+
+def qkv_kernel(x_ref, wall, wq, wk, wv, kv_ref, q_ref, weights, sem):
+    for c in load_qkv(wall, (wq, wk, wv), weights, sem):
+        c.wait()
+
+    def block(j, carry):
+        lanes = pl.ds(pl.multiple_of(j * 256, 256), 256)
+
+        def proj(m):
+            total = dot(x_ref[:, :256], weights[0, m, :, lanes])
+            for k in range(1, 4):
+                total += dot(x_ref[:, 256 * k:256 * k + 256], weights[k, m, :, lanes])
+            return total.astype(BF)
+
+        q = (proj(0).astype(F32) * 0.125).astype(BF)
+        k = proj(1)
+        v = proj(2)
+        for u in range(4):
+            part = slice(64 * u, 64 * u + 64)
+            kv_ref[4 * j + u] = jnp.concatenate([k[:, part], v[:, part]], axis=1)
+            q_ref[4 * j + u] = jnp.concatenate([q[:64, part], q[64:, part]], axis=1)
+        return carry
+
+    lax.fori_loop(0, 4, block, 0)
+
+
+def project(tok, wall, own):
     return pl.pallas_call(
         qkv_kernel,
-        grid=(8,),
         out_shape=[shp((16, 128, 128), BF), shp((16, 64, 128), BF)],
-        in_specs=[
-            pl.BlockSpec((128, 1024), lambda j: (0, 0)),
-            pl.BlockSpec((4, 3, 256, 128), lambda j: (0, 0, 0, j)),
-        ],
-        out_specs=[
-            pl.BlockSpec((2, 128, 128), lambda j: (j, 0, 0)),
-            pl.BlockSpec((2, 64, 128), lambda j: (j, 0, 0)),
-        ],
+        in_specs=[VM] + [ANY] * 4,
+        out_specs=[VM] * 2,
+        scratch_shapes=[pltpu.VMEM((4, 3, 256, 1024), BF), DMA((6,))],
         compiler_params=pltpu.CompilerParams(vmem_limit_bytes=LIMIT),
         cost_estimate=pl.CostEstimate(flops=805306368, bytes_accessed=8 << 20, transcendentals=0),
         name="qkv",
-    )(tok, wall)
+    )(tok, wall, *own)
 
 
 def exchange(wide, narrow, collective):
@@ -470,26 +482,41 @@
     return r * (g - jnp.mean(g, axis=1, keepdims=True) - z * jnp.mean(g * z, axis=1, keepdims=True))
 
 
-def middle_kernel(
-    o_ref, x_ref, e_ref, ln_ref, a0, a1, a2, a3, u0, u1, u2, u3,
-    y_ref, dr_ref, do_ref, zpay, cpay, l_ref, gb_ref,
-    woi, wu, us, gs, dus, nl, ob, so, si, su,
-):
-    w = lax.axis_index("wsh")
-    zh, co = w // 2, w % 2
+def middle_kernel(*refs):
+    o_ref, x_ref, e_ref, ln_ref, ln_own = refs[:5]
+    shards = (refs[5:8], refs[8:11])
+    pieces = (refs[11:18], refs[18:25])
+    y_ref, dr_ref, do_ref, zpay, cpay, l_ref, gb_ref = refs[25:32]
+    wo, wi, wu, us, gs, dus, nl, ob, sw, sp = refs[32:]
+    zl, x, y, zh, co = place()
+    w = zh * 2 + co
     where = [w, zh * 2 + 1 - co, (1 - zh) * 2 + co, (1 - zh) * 2 + 1 - co]
     copies = [[], [], []]
-    for r, (a, u) in enumerate(((a0, u0), (a1, u1), (a2, u2), (a3, u3))):
+    for r, (a, b, c) in enumerate(shards):
         rows = pl.ds(pl.multiple_of(where[r] * 256, 256), 256)
-        copies[0].append(pltpu.make_async_copy(a.at[:, :1024], woi.at[rows, :1024], so.at[r]))
-        copies[1].append(pltpu.make_async_copy(a.at[:, 1024:], woi.at[rows, 1024:], si.at[r]))
-        rows = pl.ds(pl.multiple_of(where[r] * 1024, 1024), 1024)
-        copies[2].append(pltpu.make_async_copy(u, wu.at[rows, :], su.at[r]))
+        copies[0].append(pltpu.make_async_copy(a, wo.at[rows], sw.at[r, 0]))
+        for k in range(4):
+            cols = slice(1024 * k, 1024 * k + 1024)
+            copies[1].append(pltpu.make_async_copy(b.at[:, cols], wi.at[k, rows], sw.at[r, 1 + k]))
+        groups = pl.ds(where[r] * 8, 8)
+        copies[2].append(pltpu.make_async_copy(c, wu.at[groups], sw.at[r, 5]))
+    for r, parts in enumerate(pieces):
+        t = where[2 + r]
+        own = parts[0]
+        quarters = [(own.at[0], 0, x), (own.at[1], 1, y)]
+        for s in range(3):
+            quarters.append((parts[1 + s].at[0], 0, (x + 3 - s) % 4))
+            quarters.append((parts[4 + s].at[0], 1, (y + 3 - s) % 4))
+        for n, (ref, h, q) in enumerate(quarters):
+            rows = pl.ds(pl.multiple_of(t * 256 + h * 128 + q * 32, 32), 32)
+            copies[0].append(pltpu.make_async_copy(ref.at[0], wo.at[rows], sp.at[r, n, 0]))
+            copies[1].append(pltpu.make_async_copy(ref.at[1:5], wi.at[:, rows], sp.at[r, n, 1]))
+            copies[2].append(pltpu.make_async_copy(ref.at[5:9], wu.at[t * 8 + h * 4 + q], sp.at[r, n, 2]))
     for group in copies:
         for c in group:
             c.start()
 
-    ln = jnp.concatenate([ln_ref[k] for k in range(4)], axis=1)
+    ln = jnp.concatenate([jnp.where(w == k, ln_own[...], ln_ref[k]) for k in range(4)], axis=1)
     gain0, gain1, bias0, bias1 = (ln[k:k + 1, :] for k in range(4))
     for h in range(16):
         pair = o_ref[h]
@@ -497,7 +524,7 @@
         ob[64:, 64 * h:64 * h + 64] = pair[:, 64:]
     for c in copies[0]:
         c.wait()
-    z0, r0 = norm_parts(x_ref[...].astype(F32) + dot(ob[...], woi[:, :1024]))
+    z0, r0 = norm_parts(x_ref[...].astype(F32) + dot(ob[...], wo[...]))
     n1 = z0 * gain0 + bias0
     nl[...] = n1.astype(BF)
     for c in copies[1]:
@@ -506,21 +533,20 @@
     half = math.sqrt(0.5)
 
     def up(c, carry):
-        cols = pl.ds(pl.multiple_of(1024 + c * 512, 512), 512)
-        u = dot(nl[...], woi[:, cols])
+        u = dot(nl[...], wi[c])
         us[c] = u
-        gs[:, pl.ds(pl.multiple_of(c * 512, 512), 512)] = (0.5 * u * (1.0 + lax.erf(u * half))).astype(BF)
+        gs[:, pl.ds(pl.multiple_of(c * 1024, 1024), 1024)] = (0.5 * u * (1.0 + lax.erf(u * half))).astype(BF)
         return carry
 
-    lax.fori_loop(0, 8, up, 0)
+    lax.fori_loop(0, 4, up, 0)
     for c in copies[2]:
         c.wait()
 
     def down(c, total):
-        cols = pl.ds(pl.multiple_of(c * 512, 512), 512)
-        return total + dot(gs[:, cols], wu[cols, :])
-
-    r2 = lax.fori_loop(0, 8, down, n1)
+        cols = pl.ds(pl.multiple_of(c * 1024, 1024), 1024)
+        return total + dot(gs[:, cols], wu[pl.ds(c * 8, 8)].reshape(1024, 1024))
+
+    r2 = lax.fori_loop(0, 4, down, n1)
     z1, r1 = norm_parts(r2)
     y_ref[...] = z1 * gain1 + bias1
     e = e_ref[...].astype(F32)
@@ -530,23 +556,22 @@
     gb_ref[3:4, :] = jnp.sum(e, axis=0, keepdims=True)
 
     def back(c, total):
-        rows = pl.ds(pl.multiple_of(c * 512, 512), 512)
-        cols = pl.ds(pl.multiple_of(1024 + c * 512, 512), 512)
+        rows = pl.ds(pl.multiple_of(c * 1024, 1024), 1024)
         u = us[c]
-        dg = dot(dm, wu[rows, :], NT)
+        dg = dot(dm, wu[pl.ds(c * 8, 8)].reshape(1024, 1024), NT)
         slope = 0.5 * (1.0 + lax.erf(u * half)) + u * (jnp.exp(-0.5 * u * u) * (1.0 / math.sqrt(2 * math.pi)))
         du = (dg * slope).astype(BF)
         dus[:, rows] = du
-        return total + dot(du, woi[:, cols], NT)
-
-    dn1 = lax.fori_loop(0, 8, back, dr2)
+        return total + dot(du, wi[c], NT)
+
+    dn1 = lax.fori_loop(0, 4, back, dr2)
     gb_ref[0:1, :] = jnp.sum(dn1 * z0, axis=0, keepdims=True)
     gb_ref[2:3, :] = jnp.sum(dn1, axis=0, keepdims=True)
     gb_ref[4:8, :] = jnp.zeros((4, 1024), F32)
     dr1 = norm_back(dn1, gain0, z0, r0)
     dr_ref[...] = dr1
     da = dr1.astype(BF)
-    do = dot(da, woi[:, :1024], NT).astype(BF)
+    do = dot(da, wo[...], NT).astype(BF)
     for h in range(16):
         lanes = slice(64 * h, 64 * h + 64)
         do_ref[h] = jnp.concatenate([do[:64, lanes], do[64:, lanes]], axis=1)
@@ -563,29 +588,30 @@
         ref[:, at + 512:at + 1536] = gs[:, many]
 
 
-def middle(o, tok, cot, lnf, a, u):
+def middle(o, tok, cot, lnf, lnp, shards, pieces):
     return pl.pallas_call(
         middle_kernel,
         out_shape=[
             shp((128, 1024), F32), shp((128, 1024), F32), shp((16, 64, 128), BF),
             shp((128, 9216), BF), shp((128, 7680), BF), shp((128, 1536), BF), shp((8, 1024), F32),
         ],
-        in_specs=[VM] * 4 + [ANY] * 8,
+        in_specs=[VM] * 5 + [ANY] * 20,
         out_specs=[VM] * 7,
         scratch_shapes=[
-            pltpu.VMEM((1024, 5120), BF),
-            pltpu.VMEM((4096, 1024), BF),
-            pltpu.VMEM((8, 128, 512), F32),
+            pltpu.VMEM((1024, 1024), BF),
+            pltpu.VMEM((4, 1024, 1024), BF),
+            pltpu.VMEM((32, 4, 32, 1024), BF),
+            pltpu.VMEM((4, 128, 1024), F32),
             pltpu.VMEM((128, 4096), BF),
             pltpu.VMEM((128, 4096), BF),
             pltpu.VMEM((128, 1024), BF),
             pltpu.VMEM((128, 1024), BF),
-            DMA((4,)), DMA((4,)), DMA((4,)),
+            DMA((2, 6)), DMA((2, 8, 3)),
         ],
         compiler_params=pltpu.CompilerParams(vmem_limit_bytes=LIMIT),
         cost_estimate=pl.CostEstimate(flops=10 << 30, bytes_accessed=32 << 20, transcendentals=2 << 20),
         name="middle",
-    )(o, tok, cot, lnf, *a, *u)
+    )(o, tok, cot, lnf, lnp, *shards[0], *shards[1], *pieces[0], *pieces[1])
 
 
 def wgrad_mid_kernel(own_l, own, zr, c1, c2, out, ll, rr, lt, sem):
@@ -628,44 +654,8 @@
     )(own_l, own, zr, c1, c2)
 
 
-def wgrad_tail_kernel(xs, p0, p1, p2, p3, out, vec, ll, rr, sem):
-    w = lax.axis_index("wsh")
-    zh, co = w // 2, w % 2
-    where = [w, zh * 2 + 1 - co, (1 - zh) * 2 + co, (1 - zh) * 2 + 1 - co]
-    copies = []
-    for k, p in enumerate((p0, p1, p2, p3)):
-        rows = slice(128 * k, 128 * k + 128)
-        copies.append(pltpu.make_async_copy(xs.at[where[k]], ll.at[rows, :], sem.at[2 * k]))
-        copies.append(pltpu.make_async_copy(p, rr.at[k], sem.at[2 * k + 1]))
-    for c in copies:
-        c.start()
-    for c in copies:
-        c.wait()
-    lt = ll[...].astype(F32).T.astype(BF)
-    for m in range(3):
-        cols = slice(1024 * m, 1024 * m + 1024)
-        total = dot(lt[:, 0:128], rr[0, :128, cols])
-        for k in range(1, 4):
-            total += dot(lt[:, 128 * k:128 * k + 128], rr[k, :128, cols])
-        out[256 * m:256 * m + 256, :] = total.astype(BF)
-    mine = pl.ds(pl.multiple_of(w * 256, 256), 256)
-    vec[...] = sum(rr[k, 128:144, mine].astype(F32) for k in range(4))[:8]
-
-
-def wgrad_tail(xs, p0, p1, p2, p3):
-    return pl.pallas_call(
-        wgrad_tail_kernel,
-        out_shape=[shp((768, 1024), BF), shp((8, 256), F32)],
-        in_specs=[ANY] * 5,
-        out_specs=[VM] * 2,
-        scratch_shapes=[pltpu.VMEM((512, 256), BF), pltpu.VMEM((4, 144, 3072), BF), DMA((8,))],
-        compiler_params=pltpu.CompilerParams(vmem_limit_bytes=LIMIT),
-        cost_estimate=pl.CostEstimate(flops=1 << 30, bytes_accessed=8 << 20, transcendentals=0),
-        name="wgrad_tail",
-    )(xs, p0, p1, p2, p3)
-
-
-def tokens_back_kernel(dkv, dqp, w_ref, dr_ref, gb, gt, pay):
+def tokens_back_kernel(dkv, dqp, dr_ref, gb, wall, wq, wk, wv, gt, pay, weights, sem):
+    copies = load_qkv(wall, (wq, wk, wv), weights, sem)
     for h in range(16):
         lanes = slice(64 * h, 64 * h + 64)
         pair = dqp[h]
@@ -676,165 +666,234 @@
         pay[:128, 2048 + 64 * h:2112 + 64 * h] = both[:, 64:]
     pay[128:144, :1024] = jnp.concatenate([gb[...], jnp.zeros((8, 1024), F32)], axis=0).astype(BF)
     pay[128:144, 1024:] = jnp.zeros((16, 2048), BF)
+    for c in copies:
+        c.wait()
     for k in range(4):
         cols = slice(256 * k, 256 * k + 256)
         total = dr_ref[:, cols]
         for m in range(3):
-            total += dot(pay[:128, 1024 * m:1024 * m + 1024], w_ref[k, m], NT)
+            total += dot(pay[:128, 1024 * m:1024 * m + 1024], weights[k, m], NT)
         gt[:, cols] = total
 
 
-def tokens_back(dkv, dqp, wall, dr, gb):
+def tokens_back(dkv, dqp, dr, gb, wall, own):
     return pl.pallas_call(
         tokens_back_kernel,
         out_shape=[shp((128, 1024), F32), shp((144, 3072), BF)],
-        in_specs=[VM] * 5,
+        in_specs=[VM] * 4 + [ANY] * 4,
         out_specs=[VM] * 2,
+        scratch_shapes=[pltpu.VMEM((4, 3, 256, 1024), BF), DMA((6,))],
         compiler_params=pltpu.CompilerParams(vmem_limit_bytes=LIMIT),
         cost_estimate=pl.CostEstimate(flops=1 << 30, bytes_accessed=8 << 20, transcendentals=0),
         name="tokens_back",
-    )(dkv, dqp, wall, dr, gb)
-
-
-def total_kernel(hc, outs_of, with_vec, scale, refs):
-    refs = list(refs)
-    g = refs.pop(0)
-    vec = refs.pop(0) if with_vec else None
-    n_out = len(outs_of)
-    outs = [refs.pop(0) for _ in range(n_out)]
-    vout = refs.pop(0) if with_vec else None
-    r1, s1, r2, s2, r3, full, ss, rs = refs[:8]
-    if with_vec:
-        vx, vy, vz, tx, ty = refs[8:]
-    zl, x, y, zh, co = place()
-    xp = [device(zl, (x + s) % 4, y, zh, co) for s in (1, 2, 3)]
-    yp = [device(zl, x, (y + s) % 4, zh, co) for s in (1, 2, 3)]
-    zp = device(1 - zl, x, y, zh, co)
-    greet(xp + yp + [zp])
-    wire = Wire(ss, rs)
-    first = [xp, yp]
-    second = [yp, xp]
-    at1 = [x, y]
-    at2 = [y, x]
-
-    def rows(h, k):
-        return pl.ds(pl.multiple_of(h * 4 * hc + k * hc, 16), hc)
-
-    def cols(k, width):
+    )(dkv, dqp, dr, gb, wall, *own)
+
+
+class Sum:
+    def __init__(self, hc, refs, wire, where, xp, yp, zp):
+        self.hc, self.wire, self.zp = hc, wire, zp
+        self.r1, self.s1, self.r2, self.s2, self.r3, self.full = refs
+        zl, x, y, zh, co = where
+        self.zl = zl
+        self.first, self.second = (xp, yp), (yp, xp)
+        self.at1, self.at2 = (x, y), (y, x)
+        self.sent = []
+
+    def rows(self, h, k):
+        return pl.ds(pl.multiple_of(h * 4 * self.hc + k * self.hc, 16), self.hc)
+
+    def cols(self, k, width):
         return pl.ds(pl.multiple_of(k * width, 128), width)
 
-    sends = []
-    one = [[], []]
-    for s in range(3):
+    def spread(self, g):
+        self.g = g
+        self.one = [[], []]
+        for s in range(3):
+            for h in range(2):
+                src = g.at[self.rows(h, (self.at1[h] + s + 1) % 4)]
+                self.one[h].append(self.wire(src, self.r1.at[h, s], self.first[h][s]))
+
+    def spread_second(self):
+        self.two = [[], []]
         for h in range(2):
-            one[h].append(wire(g.at[rows(h, (at1[h] + s + 1) % 4)], r1.at[h, s], first[h][s]))
-    if with_vec:
-        vone = [wire(vec, vx.at[s], xp[s]) for s in range(3)]
-        sends += vone
-    two = [[], []]
-    for h in range(2):
-        for c in one[h]:
-            c.wait_recv()
-        total = g[rows(h, at1[h]), :].astype(F32)
-        for s in range(3):
-            total += r1[h, s].astype(F32)
-        s1[h] = total.astype(BF)
-        for s in range(3):
-            two[h].append(wire(s1.at[h, :, cols((at2[h] + s + 1) % 4, 256)], r2.at[h, s], second[h][s]))
-    if with_vec:
-        for c in vone:
-            c.wait_recv()
-        tx[...] = vec[...] + vx[0] + vx[1] + vx[2]
-        vtwo = [wire(tx, vy.at[s], yp[s]) for s in range(3)]
-        sends += vtwo
-    three = []
-    for h in range(2):
-        for c in two[h]:
-            c.wait_recv()
-        total = s1[h, :, cols(at2[h], 256)].astype(F32)
-        for s in range(3):
-            total += r2[h, s].astype(F32)
-        s2[h] = total.astype(BF)
-        three.append(wire(s2.at[h, :, cols(1 - zl, 128)], r3.at[h], zp))
-    if with_vec:
-        for c in vtwo:
-            c.wait_recv()
-        ty[...] = tx[...] + vy[0] + vy[1] + vy[2]
-        vthree = wire(ty, vz, zp)
-        sends.append(vthree)
-    four = []
-    for h in range(2):
-        three[h].wait_recv()
-        total = s2[h, :, cols(zl, 128)].astype(F32) + r3[h].astype(F32)
-        spot = full.at[rows(h, at1[h]), cols(at2[h] * 2 + zl, 128)]
-        spot[...] = total.astype(BF)
-        four.append(wire(spot, spot, zp))
-    five = [[], []]
-    for h in range(2):
-        four[h].wait()
-        spot = full.at[rows(h, at1[h]), cols(at2[h], 256)]
-        for s in range(3):
-            five[h].append(wire(spot, spot, second[h][s]))
-    six = [[], []]
-    for h in range(2):
-        for c in five[h]:
+            for c in self.one[h]:
+                c.wait_recv()
+            total = self.g[self.rows(h, self.at1[h]), :].astype(F32)
+            for s in range(3):
+                total += self.r1[h, s].astype(F32)
+            self.s1[h] = total.astype(BF)
+            for s in range(3):
+                src = self.s1.at[h, :, self.cols((self.at2[h] + s + 1) % 4, 256)]
+                self.two[h].append(self.wire(src, self.r2.at[h, s], self.second[h][s]))
+
+    def spread_third(self):
+        self.three = []
+        for h in range(2):
+            for c in self.two[h]:
+                c.wait_recv()
+            total = self.s1[h, :, self.cols(self.at2[h], 256)].astype(F32)
+            for s in range(3):
+                total += self.r2[h, s].astype(F32)
+            self.s2[h] = total.astype(BF)
+            self.three.append(self.wire(self.s2.at[h, :, self.cols(1 - self.zl, 128)], self.r3.at[h], self.zp))
+
+    def collect(self):
+        self.four = []
+        for h in range(2):
+            self.three[h].wait_recv()
+            total = self.s2[h, :, self.cols(self.zl, 128)].astype(F32) + self.r3[h].astype(F32)
+            spot = self.full.at[self.rows(h, self.at1[h]), self.cols(self.at2[h] * 2 + self.zl, 128)]
+            spot[...] = total.astype(BF)
+            self.four.append(self.wire(spot, spot, self.zp))
+
+    def collect_second(self):
+        self.five = [[], []]
+        for h in range(2):
+            self.four[h].wait()
+            spot = self.full.at[self.rows(h, self.at1[h]), self.cols(self.at2[h], 256)]
+            for s in range(3):
+                self.five[h].append(self.wire(spot, spot, self.second[h][s]))
+
+    def collect_third(self):
+        self.six = [[], []]
+        for h in range(2):
+            for c in self.five[h]:
+                c.wait()
+            spot = self.full.at[self.rows(h, self.at1[h])]
+            for s in range(3):
+                self.six[h].append(self.wire(spot, spot, self.first[h][s]))
+
+    def finish(self):
+        for c in self.one[0] + self.one[1] + self.two[0] + self.two[1] + self.three:
+            c.wait_send()
+        for c in self.six[0] + self.six[1]:
             c.wait()
-        spot = full.at[rows(h, at1[h])]
-        for s in range(3):
-            six[h].append(wire(spot, spot, first[h][s]))
-    for c in sends + one[0] + one[1] + two[0] + two[1] + three:
-        c.wait_send()
-    if with_vec:
-        vthree.wait_recv()
-        vout[...] = (ty[...] + vz[...]) * scale
-    for c in six[0] + six[1]:
-        c.wait()
-    for ref, spots in zip(outs, outs_of):
-        for row, col, start, size in spots:
-            ref[row:row + size, col:col + 1024] = full[start:start + size, :].astype(F32) * scale
-
-
-def total(g, vec, outs_of, shapes, collective, scale):
-    rows = g.shape[0]
+
+
+def sum_scratch(rows):
     hc = rows // 8
-    with_vec = vec is not None
-    n = 28 + (7 if with_vec else 0)
-
-    def kernel(*refs):
-        total_kernel(hc, outs_of, with_vec, scale, refs)
-
-    scratch = [
+    return [
         pltpu.VMEM((2, 3, hc, 1024), BF),
         pltpu.VMEM((2, hc, 1024), BF),
         pltpu.VMEM((2, 3, hc, 256), BF),
         pltpu.VMEM((2, hc, 256), BF),
         pltpu.VMEM((2, hc, 128), BF),
         pltpu.VMEM((rows, 1024), BF),
-        DMA((n,)), DMA((n,)),
     ]
-    outs = [shp(s, F32) for s in shapes]
-    if with_vec:
-        scratch += [
-            pltpu.VMEM((3, 8, 256), F32), pltpu.VMEM((3, 8, 256), F32), pltpu.VMEM((8, 256), F32),
-            pltpu.VMEM((8, 256), F32), pltpu.VMEM((8, 256), F32),
-        ]
-        outs.append(shp((8, 256), F32))
-    args = [g] + ([vec] if with_vec else [])
+
+
+def finish_kernel(*refs):
+    mid, pay, xs, x_ref = refs[:4]
+    s_q, s_k, s_v, s_o, s_i, s_u, s_vec = refs[4:11]
+    mid_refs, tail_refs = refs[11:17], refs[17:23]
+    ll, rr, tail, v0, vx, vy, vz, tx, ty, ss, rs, ls = refs[23:]
+    scale = 1.0 / math.sqrt(16384)
+    where = place()
+    zl, x, y, zh, co = where
+    w = zh * 2 + co
+    core = device(zl, x, y, zh, 1 - co)
+    far = device(zl, x, y, 1 - zh, co)
+    xp = [device(zl, (x + s) % 4, y, zh, co) for s in (1, 2, 3)]
+    yp = [device(zl, x, (y + s) % 4, zh, co) for s in (1, 2, 3)]
+    zp = device(1 - zl, x, y, zh, co)
+    greet([core, far, zp] + xp + yp)
+    wire = Wire(ss, rs)
+    big = Sum(288, mid_refs, wire, where, xp, yp, zp)
+    small = Sum(96, tail_refs, wire, where, xp, yp, zp)
+
+    to_far = wire(pay, rr.at[1], far)
+    to_core = wire(pay, rr.at[0], core)
+    big.spread(mid)
+    order = [w, zh * 2 + 1 - co, (1 - zh) * 2 + co, (1 - zh) * 2 + 1 - co]
+    mine = pl.ds(pl.multiple_of(w * 256, 256), 256)
+    local = [pltpu.make_async_copy(x_ref.at[:, mine], ll.at[0:128, :], ls.at[0])]
+    for k in range(1, 4):
+        local.append(pltpu.make_async_copy(xs.at[order[k]], ll.at[128 * k:128 * k + 128, :], ls.at[k]))
+    for c in local:
+        c.start()
+    for c in local:
+        c.wait()
+    lt = ll[...].astype(F32).T.astype(BF)
+    to_far.wait_recv()
+    on_core = wire(rr.at[1], rr.at[2], core)
+    to_core.wait_recv()
+    on_core.wait_recv()
+    for m in range(3):
+        cols = slice(1024 * m, 1024 * m + 1024)
+        total = dot(lt[:, 0:128], pay[:128, cols])
+        for k in range(3):
+            total += dot(lt[:, 128 * k + 128:128 * k + 256], rr[k, :128, cols])
+        tail[256 * m:256 * m + 256, :] = total.astype(BF)
+    small.spread(tail)
+    vec = pay[128:144, mine].astype(F32)
+    for k in range(3):
+        vec += rr[k, 128:144, mine].astype(F32)
+    v0[...] = vec[:8]
+    vone = [wire(v0, vx.at[s], xp[s]) for s in range(3)]
+    big.spread_second()
+    small.spread_second()
+    for c in vone:
+        c.wait_recv()
+    tx[...] = v0[...] + vx[0] + vx[1] + vx[2]
+    vtwo = [wire(tx, vy.at[s], yp[s]) for s in range(3)]
+    big.spread_third()
+    small.spread_third()
+    for c in vtwo:
+        c.wait_recv()
+    ty[...] = tx[...] + vy[0] + vy[1] + vy[2]
+    vthree = wire(ty, vz, zp)
+    big.collect()
+    small.collect()
+    big.collect_second()
+    small.collect_second()
+    big.collect_third()
+    small.collect_third()
+    vthree.wait()
+    s_vec[...] = (ty[...] + vz[...]) * scale
+    for c in vone + vtwo + [to_far, to_core, on_core]:
+        c.wait_send()
+    big.finish()
+    full = big.full
+    s_o[...] = full[:256, :].astype(F32) * scale
+    for k in range(4):
+        s_i[:, 1024 * k:1024 * k + 1024] = full[256 + 256 * k:512 + 256 * k, :].astype(F32) * scale
+    s_u[...] = full[1280:2304, :].astype(F32) * scale
+    small.finish()
+    for k, ref in enumerate((s_q, s_k, s_v)):
+        ref[...] = small.full[256 * k:256 * k + 256, :].astype(F32) * scale
+
+
+def finish(mid, pay, xs, tok):
+    n = 28 * 2 + 3 + 7
     return pl.pallas_call(
-        kernel,
-        out_shape=outs,
-        in_specs=[VM] * len(args),
-        out_specs=[VM] * len(outs),
-        scratch_shapes=scratch,
-        compiler_params=pltpu.CompilerParams(
-            collective_id=collective, has_side_effects=True, vmem_limit_bytes=LIMIT
-        ),
-        name=f"total_{collective}",
-    )(*args)
+        finish_kernel,
+        out_shape=[
+            shp((256, 1024), F32), shp((256, 1024), F32), shp((256, 1024), F32), shp((256, 1024), F32),
+            shp((256, 4096), F32), shp((1024, 1024), F32), shp((8, 256), F32),
+        ],
+        in_specs=[VM, VM, ANY, ANY],
+        out_specs=[VM] * 7,
+        scratch_shapes=sum_scratch(2304) + sum_scratch(768) + [
+            pltpu.VMEM((512, 256), BF), pltpu.VMEM((3, 144, 3072), BF), pltpu.VMEM((768, 1024), BF),
+            pltpu.VMEM((8, 256), F32), pltpu.VMEM((3, 8, 256), F32), pltpu.VMEM((3, 8, 256), F32),
+            pltpu.VMEM((8, 256), F32), pltpu.VMEM((8, 256), F32), pltpu.VMEM((8, 256), F32),
+            DMA((n,)), DMA((n,)), DMA((4,)),
+        ],
+        compiler_params=pltpu.CompilerParams(collective_id=6, has_side_effects=True, vmem_limit_bytes=LIMIT),
+        name="finish",
+    )(mid, pay, xs, tok)
 
 
 FLIP_CORE = [(0, 1), (1, 0), (2, 3), (3, 2)]
 FLIP_FAR = [(0, 2), (2, 0), (1, 3), (3, 1)]
+
+
+def along_x(s):
+    return [(c, c // 16 * 16 + (c // 4 + s) % 4 * 4 + c % 4) for c in range(32)]
+
+
+def along_y(s):
+    return [(c, c // 4 * 4 + (c + s) % 4) for c in range(32)]
 
 
 def body(
@@ -842,56 +901,50 @@
 ):
     tok = tokens.reshape(128, 1024)
     cot = cotangent.reshape(128, 1024)
-    scale = 1.0 / math.sqrt(16384)
     lnp = jnp.concatenate([ln_gain, ln_bias, jnp.zeros((4, 256), F32)], axis=0)
     blk = block_pairs.reshape(-1)
-
-    wall, xs, lnf = gather_weights(w_query, w_key, w_value, tok, lnp)
-    a_own = jnp.concatenate([w_output, w_inner], axis=1)
-    a_own, u_own, wall = lax.optimization_barrier((a_own, w_outer, wall))
-    a_far = lax.ppermute(a_own, "wsh", FLIP_FAR)
-    u_far = lax.ppermute(u_own, "wsh", FLIP_FAR)
-    a_core = lax.ppermute(a_own, "wsh", FLIP_CORE)
-    u_core = lax.ppermute(u_own, "wsh", FLIP_CORE)
-    a_diag = lax.ppermute(a_far, "wsh", FLIP_CORE)
-    u_diag = lax.ppermute(u_far, "wsh", FLIP_CORE)
-
-    kvp, qp = project(tok, wall)
+    own = (w_query, w_key, w_value)
+    outer = w_outer.reshape(8, 4, 32, 1024)
+    zl, x, y, zh, co = place()
+
+    def quarter(k):
+        first = lax.dynamic_slice_in_dim(w_output, 32 * k, 32, 0)[None]
+        second = lax.dynamic_slice_in_dim(w_inner, 32 * k, 32, 0).reshape(32, 4, 1024).transpose(1, 0, 2)
+        third = lax.dynamic_index_in_dim(outer, k, 0, keepdims=False)
+        return jnp.concatenate([first, second, third], axis=0)
+
+    quarters = jnp.stack([quarter(x), quarter(4 + y)])
+    wall, xs, lnf, *core_shard = gather_weights(*own, tok, lnp, w_output, w_inner, outer)
+    quarters, wall = lax.optimization_barrier((quarters, wall))
+    far_own = lax.ppermute(quarters, "wsh", FLIP_FAR)
+
+    kvp, qp = project(tok, wall, own)
     kvr, qr = exchange(kvp, qp, 2)
+    far_own, kvr = lax.optimization_barrier((far_own, kvr))
+    far = [far_own]
+    far += [lax.ppermute(far_own[:1], "ctx", along_x(s)) for s in (1, 2, 3)]
+    far += [lax.ppermute(far_own[1:], "ctx", along_y(s)) for s in (1, 2, 3)]
     o, ot, lse = attend(blk, block_mask, kvr, qr)
+    *far, o = lax.optimization_barrier((*far, o))
+    diag = [lax.ppermute(p, "wsh", FLIP_CORE) for p in far]
     (o_back,) = exchange(None, o, 3)
-    y, dr1, do, zpay, cpay, own_l, gb = middle(
-        o_back, tok, cot, lnf, (a_own, a_core, a_far, a_diag), (u_own, u_core, u_far, u_diag)
+    y_out, dr1, do, zpay, cpay, own_l, gb = middle(
+        o_back, tok, cot, lnf, lnp, ((w_output, w_inner, outer), core_shard), (far, diag)
     )
     zr = lax.ppermute(zpay, "wsh", FLIP_FAR)
     c1 = lax.ppermute(cpay, "wsh", FLIP_CORE)
-    c2 = lax.ppermute(zr[:, 1536:], "wsh", FLIP_CORE)
 
     (dor,) = exchange(None, do, 3)
     dkvp, dqp = attend_back(blk, block_mask, kvr, qr, dor, ot, lse)
     dkvr, dqr = exchange(dkvp, dqp, 4)
-    grad_tok, pay = tokens_back(dkvr, dqr, wall, dr1, gb)
-    t1 = lax.ppermute(pay, "wsh", FLIP_CORE)
-    t2 = lax.ppermute(pay, "wsh", FLIP_FAR)
-    t3 = lax.ppermute(t2, "wsh", FLIP_CORE)
-
+    zr, dkvr = lax.optimization_barrier((zr, dkvr))
+    c2 = lax.ppermute(zr[:, 1536:], "wsh", FLIP_CORE)
+    grad_tok, pay = tokens_back(dkvr, dqr, dr1, gb, wall, own)
     gmid = wgrad_mid(own_l, cpay, zr, c1, c2)
-    s_o, s_i, s_u = total(
-        gmid, None,
-        [
-            [(0, 0, 0, 256)],
-            [(0, 1024 * k, 256 + 256 * k, 256) for k in range(4)],
-            [(0, 0, 1280, 1024)],
-        ],
-        [(256, 1024), (256, 4096), (1024, 1024)], 5, scale,
-    )
-    gtail, vec = wgrad_tail(xs, pay, t1, t2, t3)
-    s_q, s_k, s_v, s_vec = total(
-        gtail, vec, [[(0, 0, 256 * k, 256)] for k in range(3)], [(256, 1024)] * 3, 6, scale
-    )
+    s_q, s_k, s_v, s_o, s_i, s_u, s_vec = finish(gmid, pay, xs, tok)
     out_shape = tokens.shape
     return (
-        y.reshape(out_shape), grad_tok.reshape(out_shape), s_q, s_k, s_v, s_o, s_i, s_u, s_vec[0:2], s_vec[2:4],
+        y_out.reshape(out_shape), grad_tok.reshape(out_shape), s_q, s_k, s_v, s_o, s_i, s_u, s_vec[0:2], s_vec[2:4],
     )
 
 

time: 516 us -> 379 us (0.73)
  waiting for transfers between devices: 117 us -> 11.6 us
  Pallas kernels: 368 us -> 331 us
    ppermute x9 -> x14, waiting for transfers between devices: 117 us -> 11.6 us  [the longest x3 9.12 us: body(): far += [lax.ppermute(far_own[1:], 'ctx', along_y(s)) for s in (1, 2, 3)]]
    pallas_call x1, Pallas kernels: 55.6 us -> 32.1 us  [gather_weights(): pl.pallas_call(gather_kernel, out_shape=[shp((4, 3, 256, 1024), BF), shp(...]
    pallas_call x4 -> x2, Pallas kernels: 139 us -> 116 us  [the longest x1 109 us: finish(): pl.pallas_call(finish_kernel, out_shape=[shp((256, 1024), F32), shp((256,...]
    pallas_call x4, Pallas kernels: 78.8 us -> 89.3 us  [exchange(): pl.pallas_call(kernel, out_shape=outs, in_specs=[ANY] * len(args), out_sp...]
    ppermute x9 -> x14, starting transfers between devices: 7.65 us -> 11.4 us  [the longest x3 4.87 us: body(): far += [lax.ppermute(far_own[:1], 'ctx', along_x(s)) for s in (1, 2, 3)]]
  transfers between devices with their start and end apart: 12 -> 17, of which waited for: 4 -> 3; matrix products, arithmetic and copies ran while one was open for 1% -> 0% of each run, Pallas kernels for 36% -> 40%
where the time goes in v2:
time: 379 us; the launch traced here: 378 us
  Pallas kernels  331 us (87%)
  local copies, waits for them, and re-layouts  20.4 us (5%)
  starting transfers between devices  13.6 us (4%)
  waiting for transfers between devices  11.6 us (3%)
    pallas_call x1, Pallas kernels, finish(): pl.pallas_call(finish_kernel, out_shape=[shp((256, 1024), F32), shp((256,...  109 us
    pallas_call x4, Pallas kernels, exchange(): pl.pallas_call(kernel, out_shape=outs, in_specs=[ANY] * len(args), out_sp...  89.3 us
    pallas_call x1, Pallas kernels, gather_weights(): pl.pallas_call(gather_kernel, out_shape=[shp((4, 3, 256, 1024), BF), shp(...  32.1 us
    pallas_call x1, Pallas kernels, attend(): pl.pallas_call(attend_kernel, out_shape=[shp((16, 64, 128), BF), shp((8,...  28.6 us
    pallas_call x1, Pallas kernels, attend_back(): pl.pallas_call(attend_back_kernel, out_shape=[shp((32, 128, 128), BF), sh...  28.4 us
    pallas_call x1, Pallas kernels, middle(): pl.pallas_call(middle_kernel, out_shape=[shp((128, 1024), F32), shp((128,...  20.5 us
    unnamed x41, local copies, waits for them, and re-layouts  15 us
    ppermute x3, waiting for transfers between devices, body(): far += [lax.ppermute(far_own[1:], 'ctx', along_y(s)) for s in (1, 2, 3)]  9.12 us
  transfers between devices with their start and end apart: 17, of which 3 were waited for; matrix products, arithmetic and copies ran while one was open for 0% of the time, Pallas kernels for 40%

profile of v2, /device:TPU:0, one launch (start us, length us, event | category | flops | bytes accessed | tf_op | source)
XLA Modules:
  0.0 378.3 jit_solution(16078267393886696185)
XLA Ops:
  1.6 1.1 constant_dynamic-slice_fusion.1
  2.8 1.1 dynamic-slice_bitcast_fusion.1
  5.2 32.1 %gather_qkv.1 = (bf16[4,3,256,1024]{3,2,1,0:T(8,128)(2,1)}, bf16[4,128,256]{2,1,0:T(8,128)(2,1)}, f32[4,8,256]{2,1,0:T(8,128)}, bf16[256,1024]{1,0:T(8,128)(2,1)...) custom-call(bf16[256,1024]{1,0:T(8,128)(2,1)} %wq.5, bf16[256,1024]{1,0:T(8,128)(2,1)} %wk.5, ...), custom_call_target="tpu_custom_call" | custom-call | tf_op jit(solution)/shard_map/gather_qkv/pallas_call | solution.py:120
  37.3 1.9 collective-permute-start
  39.2 6.6 %qkv.1 = (bf16[16,128,128]{2,1,0:T(8,128)(2,1)}, bf16[16,64,128]{2,1,0:T(8,128)(2,1)}) custom-call(bf16[128,1024]{1,0:T(8,128)(2,1)} %bitcast.35, bf16[4,3,256,1024]{3,2,1,0:T(8,128)(2,1)} %get-tuple-element.59.wall, bf16[256,1024]{1,0:T(8,128)(2,1)} %wq.5, bf16[256,1024]{1,0:T(8,128)(2,1)} %wk.5, bf16[256,1024]{1,0:T(8,128)(2,1)} %wv.5), custom_call_target="tpu_custom_call" | custom-call | flops 805306368 | bytes 8388608 | tf_op jit(solution)/shard_map/qkv/pallas_call | solution.py:173
  45.8 32.9 %exchange_2.1 = (bf16[32,128,128]{2,1,0:T(8,128)(2,1)}, bf16[16,64,128]{2,1,0:T(8,128)(2,1)}) custom-call(bf16[16,128,128]{2,1,0:T(8,128)(2,1)} %get-tuple-element.60.refs_0_, bf16[16,64,128]{2,1,0:T(8,128)(2,1)} %get-tuple-element.61.refs_1_), custom_call_target="tpu_custom_call" | custom-call | tf_op jit(solution)/shard_map/exchange_2/pallas_call | solution.py:256
  78.9 1.6 collective-permute-start.6
  81.8 1.0 collective-permute-start.4
  82.8 2.5 collective-permute-start.3
  86.1 9.1 %collective-permute-done.6.refs_17_ = bf16[1,9,32,1024]{3,2,1,0:T(8,128)(2,1)S(1)} collective-permute-done((bf16[1,9,32,1024]{3,2,1,0:T(8,128)(2,1)S(1)}, bf16[1,9,32,1024]{3,2,1,0:T(8,128)(2,1)S(1)}, u32[]{:S(2)}, u32[]{:S(2)}) %collective-permute-start.6) | collective-permute-done | bytes 589856 | tf_op jit(solution)/shard_map/ppermute | solution.py:926
  95.2 1.6 collective-permute-start.1
  96.8 28.6 %attend.1 = (bf16[16,64,128]{2,1,0:T(8,128)(2,1)}, f32[8,64,256]{2,1,0:T(8,128)}, f32[8,1,256]{2,1,0:T(1,128)}) custom-call(s32[64]{0:T(128)} %reshape.48.blk, s32[1,64,64]{2,1,0:T(8,128)} %mask.3, bf16[32,128,128]{2,1,0:T(8,128)(2,1)} %get-tuple-element.64.kvr, bf16[16,64,128]{2,1,0:T(8,128)(2,1)} %get-tuple-element.65.qr), custom_call_target="tpu_custom_call" | custom-call | flops 10737418240 | bytes 33554432 | tf_op jit(solution)/shard_map/attend/pallas_call | solution.py:372
  127.7 1.5 collective-permute-done.9.refs_20_
  130.3 10.1 %exchange_3.2.refs_0_ = bf16[16,64,128]{2,1,0:T(8,128)(2,1)} custom-call(bf16[16,64,128]{2,1,0:T(8,128)(2,1)} %get-tuple-element.67.refs_0_), custom_call_target="tpu_custom_call" | custom-call | tf_op jit(solution)/shard_map/exchange_3/pallas_call | solution.py:256
  140.4 1.1 copy-done.11
  141.5 20.5 %middle.1 = (f32[128,1024]{1,0:T(8,128)}, f32[128,1024]{1,0:T(8,128)}, bf16[16,64,128]{2,1,0:T(8,128)(2,1)}, bf16[128,9216]{1,0:T(8,128)(2,1)}, bf16[128,7680]{1...) custom-call(bf16[16,64,128]{2,1,0:T(8,128)(2,1)} %exchange_3.2.refs_0_, bf16[128,1024]{1,0:T(8,128)(2,1)} %bitcast.36, ...), custom_call_target="tpu_custom_call" | custom-call | flops 10737418240 | bytes 33554432 | tf_op jit(solution)/shard_map/middle/pallas_call | solution.py:592
  162.1 9.6 %exchange_3.3.dor = bf16[16,64,128]{2,1,0:T(8,128)(2,1)} custom-call(bf16[16,64,128]{2,1,0:T(8,128)(2,1)} %get-tuple-element.81.refs_0_), custom_call_target="tpu_custom_call" | custom-call | tf_op jit(solution)/shard_map/exchange_3/pallas_call | solution.py:256
  171.8 1.8 collective-permute-start.14
  173.5 28.4 %attend_back.1 = (bf16[32,128,128]{2,1,0:T(8,128)(2,1)}, bf16[16,64,128]{2,1,0:T(8,128)(2,1)}) custom-call(s32[64]{0:T(128)} %reshape.48.blk, s32[1,64,64]{2,1,0:T(8,128)} %mask.3, bf16[32,128,128]{2,1,0:T(8,128)(2,1)} %get-tuple-element.64.kvr, bf16[16,64,128]{2,1,0:T(8,128)(2,1)} %get-tuple-element.65.qr, bf16[16,64,128]{2,1,0:T(8,128)(2,1)} %exchange_3.3.dor, ...), custom_call_target="tpu_custom_call" | custom-call | flops 26843545600 | bytes 67108864 | tf_op jit(solution)/shard_map/attend_back/pallas_call | solution.py:456
  201.9 36.7 %exchange_4.1 = (bf16[32,128,128]{2,1,0:T(8,128)(2,1)}, bf16[16,64,128]{2,1,0:T(8,128)(2,1)}) custom-call(bf16[32,128,128]{2,1,0:T(8,128)(2,1)} %get-tuple-element.84.refs_0_, bf16[16,64,128]{2,1,0:T(8,128)(2,1)} %get-tuple-element.85.refs_1_), custom_call_target="tpu_custom_call" | custom-call | tf_op jit(solution)/shard_map/exchange_4/pallas_call | solution.py:256
  239.0 7.7 %tokens_back.1 = (f32[128,1024]{1,0:T(8,128)}, bf16[144,3072]{1,0:T(8,128)(2,1)}) custom-call(bf16[32,128,128]{2,1,0:T(8,128)(2,1)} %get-tuple-element.87.dkv, bf16[16,64,128]{2,1,0:T(8,128)(2,1)} %get-tuple-element.88.dqp, f32[128,1024]{1,0:T(8,128)} %get-tuple-element.89.dr_ref, f32[8,1024]{1,0:T(8,128)} %get-tuple-element.90.gb, ...), custom_call_target="tpu_custom_call" | custom-call | flops 1073741824 | bytes 8388608 | tf_op jit(solution)/shard_map/tokens_back/pallas_call | solution.py:680
  246.8 1.3 copy-done.3
  248.1 8.2 %wgrad_mid.1.refs_0_ = bf16[2304,1024]{1,0:T(8,128)(2,1)} custom-call(bf16[128,1536]{1,0:T(8,128)(2,1)} %get-tuple-element.92.own_l, bf16[128,7680]{1,0:T(8,128)(2,1)} %get-tuple-element.93.own, bf16[128,9216]{1,0:T(8,128)(2,1)} %copy-done, bf16[128,7680]{1,0:T(8,128)(2,1)} %collective-permute-done.15.c1, bf16[128,7680]{1,0:T(8,128)(2,1)} %copy-done.3), custom_call_target="tpu_custom_call" | custom-call | flops 2147483648 | bytes 16777216 | tf_op jit(solution)/shard_map/wgrad_mid/pallas_call | solution.py:643
  256.3 109.3 %finish.1 = (f32[256,1024]{1,0:T(8,128)}, f32[256,1024]{1,0:T(8,128)}, f32[256,1024]{1,0:T(8,128)}, f32[256,1024]{1,0:T(8,128)}, f32[256,4096]{1,0:T(8,128)}, /*index=5*/f32[1024,1024]{1,0:T(8,128)}, f32[8,256]{1,0:T(8,128)}) custom-call(bf16[2304,1024]{1,0:T(8,128)(2,1)} %wgrad_mid.1.refs_0_, bf16[144,3072]{1,0:T(8,128)(2,1)} %get-tuple-element.95.refs_1_, ...), custom_call_target="tpu_custom_call" | custom-call | tf_op jit(solution)/shard_map/finish/pallas_call | solution.py:868
  365.6 1.4 fusion.1
  367.0 2.5 copy.38
  369.5 1.0 copy.39
  370.5 1.0 copy.40
  371.4 1.0 copy.41
  372.6 2.1 copy.42
  374.7 1.6 copy-done.1
  376.3 2.0 copy.43
  (69 shorter events, 8.5 us)
Async XLA Ops:
  37.3 41.4 %collective-permute-start = (bf16[2,9,32,1024]{3,2,1,0:T(8,128)(2,1)S(1)}, bf16[2,9,32,1024]{3,2,1,0:T(8,128)(2,1)S(1)}, u32[]{:S(2)}, u32[]{:S(2)}) collective-permute-start(bf16[2,9,32,1024]{3,2,1,0:T(8,128)(2,1)S(1)} %pad_maximum_fusion), channel_id=1, source_target_pairs={{0,2},{2,0},{1,3},{3,1},{4,6},{6,4},{5,7},{7,5},{8,10},{10,8},{9,1... | collective-permute-start | bytes 3538952 | tf_op jit(solution)/shard_map/ppermute | solution.py:919
  45.8 34.7 %copy-start.10 = (s32[32,2]{0,1:T(2,128)S(1)}, s32[32,2]{0,1:T(2,128)}, u32[]{:S(2)}) copy-start(s32[32,2]{0,1:T(2,128)} %param.22) | copy-start | bytes 772
  78.7 47.4 %copy-start.4 = (bf16[2,9,32,1024]{3,2,1,0:T(8,128)(2,1)}, bf16[2,9,32,1024]{3,2,1,0:T(8,128)(2,1)S(1)}, u32[]{:S(2)}) copy-start(bf16[2,9,32,1024]{3,2,1,0:T(8,128)(2,1)S(1)} %collective-permute-done.refs_11_) | copy-start | bytes 3538948
  78.9 16.3 %collective-permute-start.6 = (bf16[1,9,32,1024]{3,2,1,0:T(8,128)(2,1)S(1)}, bf16[1,9,32,1024]{3,2,1,0:T(8,128)(2,1)S(1)}, u32[]{:S(2)}, u32[]{:S(2)}) collective-permute-start(bf16[1,9,32,1024]{3,2,1,0:T(8,128)(2,1)S(1)} %get-tuple-element.108), channel_id=1, source_target_pairs={{0,12},{4,0},{8,4},{12,8},{16,28},{20,16},{24,20},{28,24},{32,44},... | collective-permute-start | bytes 1769480 | tf_op jit(solution)/shard_map/ppermute | solution.py:926
  81.2 44.2 %collective-permute-start.5 = (bf16[1,9,32,1024]{3,2,1,0:T(8,128)(2,1)S(1)}, bf16[1,9,32,1024]{3,2,1,0:T(8,128)(2,1)}, u32[]{:S(2)}, u32[]{:S(2)}) collective-permute-start(bf16[1,9,32,1024]{3,2,1,0:T(8,128)(2,1)S(1)} %get-tuple-element.108), channel_id=1, source_target_pairs={{0,8},{4,12},{8,0},{12,4},{16,24},{20,28},{24,16},{28,20},{32,40},... | collective-permute-start | bytes 1769480 | tf_op jit(solution)/shard_map/ppermute | solution.py:926
  81.8 43.6 %collective-permute-start.4 = (bf16[1,9,32,1024]{3,2,1,0:T(8,128)(2,1)S(1)}, bf16[1,9,32,1024]{3,2,1,0:T(8,128)(2,1)}, u32[]{:S(2)}, u32[]{:S(2)}) collective-permute-start(bf16[1,9,32,1024]{3,2,1,0:T(8,128)(2,1)S(1)} %get-tuple-element.108), channel_id=1, source_target_pairs={{0,4},{4,8},{8,12},{12,0},{16,20},{20,24},{24,28},{28,16},{32,36},... | collective-permute-start | bytes 1769480 | tf_op jit(solution)/shard_map/ppermute | solution.py:926
  82.8 42.6 %collective-permute-start.3 = (bf16[1,9,32,1024]{3,2,1,0:T(8,128)(2,1)S(1)}, bf16[1,9,32,1024]{3,2,1,0:T(8,128)(2,1)}, u32[]{:S(2)}, u32[]{:S(2)}) collective-permute-start(bf16[1,9,32,1024]{3,2,1,0:T(8,128)(2,1)S(1)} %get-tuple-element.109), channel_id=1, source_target_pairs={{0,48},{4,52},{8,56},{12,60},{16,0},{20,4},{24,8},{28,12},{32,16},... | collective-permute-start | bytes 1769480 | tf_op jit(solution)/shard_map/ppermute | solution.py:925
  85.3 40.2 %collective-permute-start.2 = (bf16[1,9,32,1024]{3,2,1,0:T(8,128)(2,1)S(1)}, bf16[1,9,32,1024]{3,2,1,0:T(8,128)(2,1)S(1)}, u32[]{:S(2)}, u32[]{:S(2)}) collective-permute-start(bf16[1,9,32,1024]{3,2,1,0:T(8,128)(2,1)S(1)} %get-tuple-element.109), channel_id=1, source_target_pairs={{0,32},{4,36},{8,40},{12,44},{16,48},{20,52},{24,56},{28,60},{32,0... | collective-permute-start | bytes 1769480 | tf_op jit(solution)/shard_map/ppermute | solution.py:925
  95.2 34.1 %copy-start.12 = (bf16[1,9,32,1024]{3,2,1,0:T(8,128)(2,1)}, bf16[1,9,32,1024]{3,2,1,0:T(8,128)(2,1)S(1)}, u32[]{:S(2)}) copy-start(bf16[1,9,32,1024]{3,2,1,0:T(8,128)(2,1)S(1)} %collective-permute-done.6.refs_17_) | copy-start | bytes 1769476
  95.2 30.3 %collective-permute-start.1 = (bf16[1,9,32,1024]{3,2,1,0:T(8,128)(2,1)S(1)}, bf16[1,9,32,1024]{3,2,1,0:T(8,128)(2,1)S(1)}, u32[]{:S(2)}, u32[]{:S(2)}) collective-permute-start(bf16[1,9,32,1024]{3,2,1,0:T(8,128)(2,1)S(1)} %get-tuple-element.109), channel_id=1, source_target_pairs={{0,16},{4,20},{8,24},{12,28},{16,32},{20,36},{24,40},{28,44},{32,4... | collective-permute-start | bytes 1769480 | tf_op jit(solution)/shard_map/ppermute | solution.py:925
  125.5 2.3 copy-start.13
  125.5 3.8 %copy-start.14 = (bf16[1,9,32,1024]{3,2,1,0:T(8,128)(2,1)}, bf16[1,9,32,1024]{3,2,1,0:T(8,128)(2,1)S(1)}, u32[]{:S(2)}) copy-start(bf16[1,9,32,1024]{3,2,1,0:T(8,128)(2,1)S(1)} %collective-permute-done.1.refs_12_) | copy-start | bytes 1769476
  125.5 2.1 collective-permute-start.8
  125.6 3.7 collective-permute-start.9
  126.1 14.3 %collective-permute-start.7 = (bf16[2,9,32,1024]{3,2,1,0:T(8,128)(2,1)S(1)}, bf16[2,9,32,1024]{3,2,1,0:T(8,128)(2,1)S(1)}, u32[]{:S(2)}, u32[]{:S(2)}) collective-permute-start(bf16[2,9,32,1024]{3,2,1,0:T(8,128)(2,1)S(1)} %collective-permute-done.refs_11_), channel_id=1, source_target_pairs={{0,1},{1,0},{2,3},{3,2},{4,5},{5,4},{6,7},{7,6},{8,9},{9,8},{10,11... | collective-permute-start | bytes 3538952 | tf_op jit(solution)/shard_map/ppermute | solution.py:929
  126.2 14.2 %collective-permute-start.10 = (bf16[1,9,32,1024]{3,2,1,0:T(8,128)(2,1)}, bf16[1,9,32,1024]{3,2,1,0:T(8,128)(2,1)}, u32[]{:S(2)}, u32[]{:S(2)}) collective-permute-start(bf16[1,9,32,1024]{3,2,1,0:T(8,128)(2,1)} %collective-permute-done.3.refs_14_), channel_id=1, source_target_pairs={{0,1},{1,0},{2,3},{3,2},{4,5},{5,4},{6,7},{7,6},{8,9},{9,8},{10,11... | collective-permute-start | bytes 1769480 | tf_op jit(solution)/shard_map/ppermute | solution.py:929
  126.6 13.8 %collective-permute-start.11 = (bf16[1,9,32,1024]{3,2,1,0:T(8,128)(2,1)}, bf16[1,9,32,1024]{3,2,1,0:T(8,128)(2,1)}, u32[]{:S(2)}, u32[]{:S(2)}) collective-permute-start(bf16[1,9,32,1024]{3,2,1,0:T(8,128)(2,1)} %collective-permute-done.4.refs_15_), channel_id=1, source_target_pairs={{0,1},{1,0},{2,3},{3,2},{4,5},{5,4},{6,7},{7,6},{8,9},{9,8},{10,11... | collective-permute-start | bytes 1769480 | tf_op jit(solution)/shard_map/ppermute | solution.py:929
  127.6 1.7 copy-start.15
  127.6 12.8 %collective-permute-start.12 = (bf16[1,9,32,1024]{3,2,1,0:T(8,128)(2,1)}, bf16[1,9,32,1024]{3,2,1,0:T(8,128)(2,1)}, u32[]{:S(2)}, u32[]{:S(2)}) collective-permute-start(bf16[1,9,32,1024]{3,2,1,0:T(8,128)(2,1)} %collective-permute-done.5.refs_16_), channel_id=1, source_target_pairs={{0,1},{1,0},{2,3},{3,2},{4,5},{5,4},{6,7},{7,6},{8,9},{9,8},{10,11... | collective-permute-start | bytes 1769480 | tf_op jit(solution)/shard_map/ppermute | solution.py:929
  129.3 0.8 copy-start.16
  130.1 10.3 %collective-permute-start.13 = (bf16[1,9,32,1024]{3,2,1,0:T(8,128)(2,1)S(1)}, bf16[1,9,32,1024]{3,2,1,0:T(8,128)(2,1)}, u32[]{:S(2)}, u32[]{:S(2)}) collective-permute-start(bf16[1,9,32,1024]{3,2,1,0:T(8,128)(2,1)S(1)} %collective-permute-done.6.refs_17_), channel_id=1, source_target_pairs={{0,1},{1,0},{2,3},{3,2},{4,5},{5,4},{6,7},{7,6},{8,9},{9,8},{10,11... | collective-permute-start | bytes 1769480 | tf_op jit(solution)/shard_map/ppermute | solution.py:929
  140.4 1.1 copy-start.11
  171.7 75.1 %collective-permute-start.15 = (bf16[128,7680]{1,0:T(8,128)(2,1)}, bf16[128,7680]{1,0:T(8,128)(2,1)}, u32[]{:S(2)}, u32[]{:S(2)}) collective-permute-start(bf16[128,7680]{1,0:T(8,128)(2,1)} %get-tuple-element.93.own), channel_id=1, source_target_pairs={{0,1},{1,0},{2,3},{3,2},{4,5},{5,4},{6,7},{7,6},{8,9},{9,8},{10,11... | collective-permute-start | bytes 5898248 | tf_op jit(solution)/shard_map/ppermute | solution.py:935
  171.8 66.8 %collective-permute-start.14 = (bf16[128,9216]{1,0:T(8,128)(2,1)}, bf16[128,9216]{1,0:T(8,128)(2,1)S(1)}, u32[]{:S(2)}, u32[]{:S(2)}) collective-permute-start(bf16[128,9216]{1,0:T(8,128)(2,1)} %get-tuple-element.80), channel_id=1, source_target_pairs={{0,2},{2,0},{1,3},{3,1},{4,6},{6,4},{5,7},{7,5},{8,10},{10,8},{9,1... | collective-permute-start | bytes 7077896 | tf_op jit(solution)/shard_map/ppermute | solution.py:934
  238.6 8.2 %copy-start = (bf16[128,9216]{1,0:T(8,128)(2,1)}, bf16[128,9216]{1,0:T(8,128)(2,1)S(1)}, u32[]{:S(2)}) copy-start(bf16[128,9216]{1,0:T(8,128)(2,1)S(1)} %collective-permute-done.14.zr) | copy-start | bytes 7077892
  238.7 8.1 %collective-permute-start.16 = (bf16[128,7680]{1,0:T(8,128)(2,1)S(1)}, bf16[128,7680]{1,0:T(8,128)(2,1)S(1)}, u32[]{:S(2)}, u32[]{:S(2)}) collective-permute-start(bf16[128,7680]{1,0:T(8,128)(2,1)S(1)} %slice.21), channel_id=1, source_target_pairs={{0,1},{1,0},{2,3},{3,2},{4,5},{5,4},{6,7},{7,6},{8,9},{9,8},{10,11... | collective-permute-start | bytes 5898248 | tf_op jit(solution)/shard_map/ppermute | solution.py:941
  246.8 1.3 copy-start.3
  365.6 3.9 %copy-start.7 = (f32[256,1024]{1,0:T(8,128)S(1)}, f32[256,1024]{1,0:T(8,128)}, u32[]{:S(2)}) copy-start(f32[256,1024]{1,0:T(8,128)} %get-tuple-element.129) | copy-start | bytes 3145732
  367.0 3.4 copy-start.6
  367.0 4.4 %copy-start.5 = (f32[256,1024]{1,0:T(8,128)S(1)}, f32[256,1024]{1,0:T(8,128)}, u32[]{:S(2)}) copy-start(f32[256,1024]{1,0:T(8,128)} %get-tuple-element.131) | copy-start | bytes 3145732
  369.5 3.1 copy-start.2
  372.6 3.7 copy-start.1
  (2 other events, 1.4 us)

commit v3 on v2

--- a/solution.py
+++ b/solution.py
@@ -64,7 +64,7 @@
         return copy
 
 
-def gather_kernel(wq, wk, wv, x_ref, ln_ref, wo, wi, wu, wall, xs, lnf, co_ref, ci_ref, cu_ref, ss, rs):
+def gather_kernel(wq, wk, wv, x_ref, ln_ref, wo, wi, wu, wall, xs, lnf, co_ref, ci_ref, cu_ref, qa_ref, qb_ref, ss, rs):
     zl, x, y, zh, co = place()
     me = zh * 2 + co
     other = (1 - zh) * 2 + co
@@ -89,6 +89,15 @@
         cols = pl.ds(pl.multiple_of(idx * 256, 256), 256)
         rest.append(wire(x_ref.at[:, cols], xs.at[me], p))
         rest.append(wire(ln_ref, lnf.at[me], p))
+    quarters = []
+    for ref, k, n in ((qa_ref, x, y), (qb_ref, 4 + y, x)):
+        rows = pl.ds(pl.multiple_of(k * 32, 32), 32)
+        cols = pl.ds(pl.multiple_of(n * 256, 256), 256)
+        quarters.append(wire(wo.at[rows, cols], ref.at[0, :, cols], far))
+        for b in range(4):
+            at = pl.ds(pl.multiple_of(1024 * b + n * 256, 256), 256)
+            quarters.append(wire(wi.at[rows, at], ref.at[1 + b, :, cols], far))
+        quarters.append(wire(wu.at[k, :, :, cols], ref.at[5:9, :, cols], far))
     for c in first_a:
         c.wait_recv()
     second = []
@@ -104,27 +113,33 @@
             second.append(wire(part, part, p))
     for src, dst in ((wo, co_ref), (wi, ci_ref), (wu, cu_ref)):
         rest.append(wire(src, dst, core))
+    for c in quarters:
+        c.wait_recv()
+    for ref, n, peers in ((qa_ref, y, yp), (qb_ref, x, xp)):
+        spot = ref.at[:, :, pl.ds(pl.multiple_of(n * 256, 256), 256)]
+        for p in peers:
+            rest.append(wire(spot, spot, p))
     for c in second:
         c.wait_recv()
     last = [wire(wall.at[other, m], wall.at[other, m], core) for m in range(3)]
     for c in last:
         c.wait()
-    for c in first_a + first_b + second:
+    for c in first_a + first_b + second + quarters:
         c.wait_send()
     for c in rest:
         c.wait()
 
 
 def gather_weights(wq, wk, wv, tok, lnp, wo, wi, wu):
-    n = 6 + 3 + 6 + 18 + 3 + 3
+    n = 6 + 3 + 6 + 12 + 18 + 3 + 6 + 3
     return pl.pallas_call(
         gather_kernel,
         out_shape=[
             shp((4, 3, 256, 1024), BF), shp((4, 128, 256), BF), shp((4, 8, 256), F32),
-            shp(wo.shape, BF), shp(wi.shape, BF), shp(wu.shape, BF),
+            shp(wo.shape, BF), shp(wi.shape, BF), shp(wu.shape, BF), shp((9, 32, 1024), BF), shp((9, 32, 1024), BF),
         ],
         in_specs=[ANY] * 8,
-        out_specs=[ANY] * 6,
+        out_specs=[ANY] * 8,
         scratch_shapes=[DMA((n,)), DMA((n,))],
         compiler_params=pltpu.CompilerParams(collective_id=1, has_side_effects=True),
         name="gather_qkv",
@@ -260,6 +275,7 @@
         out_specs=[ANY] * len(outs),
         scratch_shapes=sems,
         compiler_params=pltpu.CompilerParams(collective_id=collective, has_side_effects=True),
+        cost_estimate=pl.CostEstimate(flops=16 << 30, bytes_accessed=32 << 20, transcendentals=0),
         name=f"exchange_{collective}",
     )(*args)
 
@@ -466,7 +482,7 @@
             pltpu.VMEM((4096, 128), F32),
         ],
         compiler_params=pltpu.CompilerParams(vmem_limit_bytes=LIMIT),
-        cost_estimate=pl.CostEstimate(flops=25 << 30, bytes_accessed=64 << 20, transcendentals=4 << 20),
+        cost_estimate=pl.CostEstimate(flops=1 << 30, bytes_accessed=4 << 20, transcendentals=0),
         name="attend_back",
     )(blk, mask, kvr, qr, dor, ot, lse)
 
@@ -485,9 +501,9 @@
 def middle_kernel(*refs):
     o_ref, x_ref, e_ref, ln_ref, ln_own = refs[:5]
     shards = (refs[5:8], refs[8:11])
-    pieces = (refs[11:18], refs[18:25])
-    y_ref, dr_ref, do_ref, zpay, cpay, l_ref, gb_ref = refs[25:32]
-    wo, wi, wu, us, gs, dus, nl, ob, sw, sp = refs[32:]
+    pieces = (refs[11:19], refs[19:27])
+    y_ref, dr_ref, do_ref, zpay, l_ref, gb_ref = refs[27:33]
+    wo, wi, wu, us, gs, dus, nl, ob, sw, sp = refs[33:]
     zl, x, y, zh, co = place()
     w = zh * 2 + co
     where = [w, zh * 2 + 1 - co, (1 - zh) * 2 + co, (1 - zh) * 2 + 1 - co]
@@ -502,11 +518,8 @@
         copies[2].append(pltpu.make_async_copy(c, wu.at[groups], sw.at[r, 5]))
     for r, parts in enumerate(pieces):
         t = where[2 + r]
-        own = parts[0]
-        quarters = [(own.at[0], 0, x), (own.at[1], 1, y)]
-        for s in range(3):
-            quarters.append((parts[1 + s].at[0], 0, (x + 3 - s) % 4))
-            quarters.append((parts[4 + s].at[0], 1, (y + 3 - s) % 4))
+        quarters = [(parts[s], 0, (x + 4 - s) % 4) for s in range(4)]
+        quarters += [(parts[4 + s], 1, (y + 4 - s) % 4) for s in range(4)]
         for n, (ref, h, q) in enumerate(quarters):
             rows = pl.ds(pl.multiple_of(t * 256 + h * 128 + q * 32, 32), 32)
             copies[0].append(pltpu.make_async_copy(ref.at[0], wo.at[rows], sp.at[r, n, 0]))
@@ -576,11 +589,10 @@
         lanes = slice(64 * h, 64 * h + 64)
         do_ref[h] = jnp.concatenate([do[:64, lanes], do[64:, lanes]], axis=1)
     du = dus[...]
-    for ref, at in ((zpay, 1536), (cpay, 0)):
-        ref[:, at:at + 4096] = du
-        ref[:, at + 4096:at + 5120] = dm
-        ref[:, at + 5120:at + 6144] = da
-    for r, (ref, at) in enumerate(((l_ref, 0), (cpay, 6144), (zpay, 0), (zpay, 7680))):
+    zpay[:, 1536:5632] = du
+    zpay[:, 5632:6656] = dm
+    zpay[:, 6656:7680] = da
+    for r, (ref, at) in enumerate(((l_ref, 0), (l_ref, 1536), (zpay, 0), (zpay, 7680))):
         few = pl.ds(pl.multiple_of(where[r] * 256, 256), 256)
         many = pl.ds(pl.multiple_of(where[r] * 1024, 1024), 1024)
         ref[:, at:at + 256] = nl[:, few]
@@ -593,10 +605,10 @@
         middle_kernel,
         out_shape=[
             shp((128, 1024), F32), shp((128, 1024), F32), shp((16, 64, 128), BF),
-            shp((128, 9216), BF), shp((128, 7680), BF), shp((128, 1536), BF), shp((8, 1024), F32),
+            shp((128, 9216), BF), shp((128, 3072), BF), shp((8, 1024), F32),
         ],
-        in_specs=[VM] * 5 + [ANY] * 20,
-        out_specs=[VM] * 7,
+        in_specs=[VM] * 5 + [ANY] * 22,
+        out_specs=[VM] * 6,
         scratch_shapes=[
             pltpu.VMEM((1024, 1024), BF),
             pltpu.VMEM((4, 1024, 1024), BF),
@@ -614,51 +626,282 @@
     )(o, tok, cot, lnf, lnp, *shards[0], *shards[1], *pieces[0], *pieces[1])
 
 
-def wgrad_mid_kernel(own_l, own, zr, c1, c2, out, ll, rr, lt, sem):
-    copies = []
-    for k, (lsrc, rsrc) in enumerate((
-        (own_l, own.at[:, :6144]),
-        (zr.at[:, :1536], zr.at[:, 1536:7680]),
-        (c1.at[:, 6144:], c1.at[:, :6144]),
-        (c2.at[:, 6144:], c2.at[:, :6144]),
-    )):
-        rows = slice(128 * k, 128 * k + 128)
-        copies.append(pltpu.make_async_copy(lsrc, ll.at[rows, :], sem.at[2 * k]))
-        copies.append(pltpu.make_async_copy(rsrc, rr.at[rows, :], sem.at[2 * k + 1]))
-    for c in copies:
+class Spread:
+    def __init__(self, wire, plus, minus, at, piece, bufs):
+        self.wire, self.plus, self.minus, self.at, self.piece = wire, plus, minus, at, piece
+        self.rp, self.rm, self.m, self.f = bufs
+
+    def part(self, s, u):
+        return self.piece((self.at + s) % 4, u)
+
+    def start(self):
+        self.a = self.wire(self.part(2, 0), self.m.at[0], self.plus)
+        self.b = self.wire(self.part(2, 1), self.m.at[1], self.minus)
+        self.c = self.wire(self.part(1, 1), self.rp.at[1], self.plus)
+        self.d = self.wire(self.part(3, 0), self.rm.at[0], self.minus)
+
+    def relay(self):
+        self.a.wait_recv()
+        self.f[0] = (self.part(1, 0)[...].astype(F32) + self.m[0].astype(F32)).astype(BF)
+        self.e = self.wire(self.f.at[0], self.rp.at[0], self.plus)
+        self.b.wait_recv()
+        self.f[1] = (self.part(3, 1)[...].astype(F32) + self.m[1].astype(F32)).astype(BF)
+        self.g = self.wire(self.f.at[1], self.rm.at[1], self.minus)
+
+    def total(self):
+        for c in (self.c, self.d, self.e, self.g):
+            c.wait_recv()
+        return [
+            self.part(0, u)[...].astype(F32) + self.rp[u].astype(F32) + self.rm[u].astype(F32) for u in range(2)
+        ]
+
+    def sent(self):
+        for c in (self.a, self.b, self.c, self.d, self.e, self.g):
+            c.wait_send()
+
+
+class Gather:
+    def __init__(self, wire, plus, minus, at, block):
+        self.wire, self.plus, self.minus, self.at, self.block = wire, plus, minus, at, block
+
+    def send(self, s, u, peer):
+        spot = self.block((self.at + s) % 4, u)
+        return self.wire(spot, spot, peer)
+
+    def start(self):
+        self.p0 = self.send(0, 0, self.plus)
+        self.m1 = self.send(0, 1, self.minus)
+        self.p1 = self.send(0, 1, self.plus)
+        self.m0 = self.send(0, 0, self.minus)
+
+    def relay(self):
+        self.p0.wait_recv()
+        self.rp = self.send(3, 0, self.plus)
+        self.m1.wait_recv()
+        self.rm = self.send(1, 1, self.minus)
+
+    def done(self):
+        for c in (self.p1, self.m0, self.rp, self.rm):
+            c.wait()
+        for c in (self.p0, self.m1):
+            c.wait_send()
+
+
+class Sum:
+    def __init__(self, g, hc, refs, wire, where, xp, yp, zp):
+        bufs1, s1, bufs2, s2, self.r3, full = refs[:4], refs[4], refs[5:9], refs[9], refs[10], refs[11]
+        zl, x, y, zh, co = where
+        self.wire, self.zp, self.zl, self.hc = wire, zp, zl, hc
+        self.s1, self.s2, self.full = s1, s2, full
+        hh = hc // 2
+        first, second = (xp, yp), (yp, xp)
+        self.at1, self.at2 = (x, y), (y, x)
+
+        def rows(h, k, u):
+            return pl.ds(pl.multiple_of(h * 4 * hc + k * hc + u * hh, 16), hh)
+
+        def cols(k, width):
+            return pl.ds(pl.multiple_of(k * width, 128), width)
+
+        self.cols = cols
+
+        def one(h):
+            return lambda k, u: g.at[rows(h, k, u)]
+
+        def two(h):
+            return lambda k, u: s1.at[h, u, :, cols(k, 256)]
+
+        def five(h):
+            return lambda k, u: full.at[rows(h, self.at1[h], u), cols(k, 256)]
+
+        def six(h):
+            return lambda k, u: full.at[rows(h, k, u)]
+
+        def ends(peers):
+            return wire, peers[0], peers[2]
+
+        self.one = [Spread(*ends(first[h]), self.at1[h], one(h), [r.at[h] for r in bufs1]) for h in range(2)]
+        self.two = [Spread(*ends(second[h]), self.at2[h], two(h), [r.at[h] for r in bufs2]) for h in range(2)]
+        self.five = [Gather(*ends(second[h]), self.at2[h], five(h)) for h in range(2)]
+        self.six = [Gather(*ends(first[h]), self.at1[h], six(h)) for h in range(2)]
+
+    def steps(self):
+        for t in self.one:
+            t.start()
+        yield
+        for t in self.one:
+            t.relay()
+        yield
+        for h in range(2):
+            for u, total in enumerate(self.one[h].total()):
+                self.s1[h, u] = total.astype(BF)
+            self.two[h].start()
+        yield
+        for t in self.two:
+            t.relay()
+        yield
+        three = []
+        for h in range(2):
+            for u, total in enumerate(self.two[h].total()):
+                self.s2[h, u] = total.astype(BF)
+            three.append(self.wire(self.s2.at[h, :, :, self.cols(1 - self.zl, 128)], self.r3.at[h], self.zp))
+        yield
+        four = []
+        for h in range(2):
+            three[h].wait_recv()
+            for u in range(2):
+                total = self.s2[h, u, :, self.cols(self.zl, 128)].astype(F32) + self.r3[h, u].astype(F32)
+                rows = pl.ds(pl.multiple_of(h * 4 * self.hc + self.at1[h] * self.hc + u * (self.hc // 2), 16), self.hc // 2)
+                spot = self.full.at[rows, self.cols(self.at2[h] * 2 + self.zl, 128)]
+                spot[...] = total.astype(BF)
+                four.append(self.wire(spot, spot, self.zp))
+        yield
+        for h in range(2):
+            four[2 * h].wait()
+            four[2 * h + 1].wait()
+            self.five[h].start()
+        yield
+        for t in self.five:
+            t.relay()
+        yield
+        for h in range(2):
+            self.five[h].done()
+            self.six[h].start()
+        yield
+        for t in self.six:
+            t.relay()
+        yield
+        for t in self.one + self.two:
+            t.sent()
+        for c in three:
+            c.wait_send()
+        for t in self.six:
+            t.done()
+        yield
+
+
+SUM_COPIES = 12 + 12 + 2 + 4 + 12 + 12
+
+
+def sum_scratch(rows):
+    hc = rows // 8
+    hh = hc // 2
+    return (
+        [pltpu.VMEM((2, 2, hh, 1024), BF)] * 4
+        + [pltpu.VMEM((2, 2, hh, 1024), BF)]
+        + [pltpu.VMEM((2, 2, hh, 256), BF)] * 4
+        + [pltpu.VMEM((2, 2, hh, 256), BF), pltpu.VMEM((2, 2, hh, 128), BF)]
+    )
+
+
+def finish_kernel(*refs):
+    dkvp, dqp, dr_ref, gb, wall, wq, wk, wv, l_ref, own, zr, xs, x_ref = refs[:13]
+    gt, mid_full, tail_full, s_vec = refs[13:17]
+    mid_refs, tail_refs = list(refs[17:28]) + [mid_full], list(refs[28:39]) + [tail_full]
+    (dkv, dq, weights, ll2, rr2, lt2, mid, pay, ll, rr, tail, v0, vx, vy, vz, tx, ty,
+     sw, rw, sn, rn, ss, rs, ls, lw) = refs[39:]
+    scale = 1.0 / math.sqrt(16384)
+    where = place()
+    zl, x, y, zh, co = where
+    w = zh * 2 + co
+    me = lax.axis_index("ctx")
+    flat = me % 16
+    core = device(zl, x, y, zh, 1 - co)
+    far = device(zl, x, y, 1 - zh, co)
+    xp = [device(zl, (x + s) % 4, y, zh, co) for s in (1, 2, 3)]
+    yp = [device(zl, x, (y + s) % 4, zh, co) for s in (1, 2, 3)]
+    zp = device(1 - zl, x, y, zh, co)
+    bar = pltpu.get_barrier_semaphore()
+
+    def greet_one(i, carry):
+        pl.semaphore_signal(bar, inc=1, device_id={"ctx": (me + i) % 32}, device_id_type=MESH)
+        return carry
+
+    for p in (core, far):
+        pl.semaphore_signal(bar, inc=1, device_id=p, device_id_type=MESH)
+    lax.fori_loop(1, 32, greet_one, 0)
+
+    mine = pl.ds(pl.multiple_of(w * 256, 256), 256)
+    order = [w, zh * 2 + 1 - co, (1 - zh) * 2 + co, (1 - zh) * 2 + 1 - co]
+    local = [
+        pltpu.make_async_copy(l_ref.at[:, :1536], ll2.at[0:128, :], ls.at[0]),
+        pltpu.make_async_copy(own.at[:, 1536:7680], rr2.at[0:128, :], ls.at[1]),
+        pltpu.make_async_copy(zr.at[:, :1536], ll2.at[256:384, :], ls.at[2]),
+        pltpu.make_async_copy(zr.at[:, 1536:7680], rr2.at[256:384, :], ls.at[3]),
+        pltpu.make_async_copy(x_ref.at[:, mine], ll.at[0:128, :], ls.at[4]),
+    ]
+    for k in range(1, 4):
+        local.append(pltpu.make_async_copy(xs.at[order[k]], ll.at[128 * k:128 * k + 128, :], ls.at[4 + k]))
+    for c in local:
         c.start()
-    for c in copies:
+    loads = load_qkv(wall, (wq, wk, wv), weights, lw)
+    pl.semaphore_wait(bar, 33)
+
+    def narrow_copy(i):
+        p = (flat + i) % 16
+        return pltpu.make_async_remote_copy(
+            src_ref=dqp.at[p], dst_ref=dq.at[flat], send_sem=sn.at[i], recv_sem=rn.at[i],
+            device_id={"ctx": zl * 16 + p}, device_id_type=MESH,
+        )
+
+    def wide_copy(i):
+        p = (me + i) % 32
+        return pltpu.make_async_remote_copy(
+            src_ref=dkvp.at[p], dst_ref=dkv.at[me], send_sem=sw.at[i], recv_sem=rw.at[i],
+            device_id={"ctx": p}, device_id_type=MESH,
+        )
+
+    def start(make):
+        def one(i, carry):
+            make(i).start()
+            return carry
+        return one
+
+    def wait(make):
+        def one(i, carry):
+            make(i).wait()
+            return carry
+        return one
+
+    lax.fori_loop(1, 32, start(wide_copy), 0)
+    lax.fori_loop(1, 16, start(narrow_copy), 0)
+    home = [
+        pltpu.make_async_copy(dkvp.at[me], dkv.at[me], ls.at[8]),
+        pltpu.make_async_copy(dqp.at[flat], dq.at[flat], ls.at[9]),
+    ]
+    for c in home:
+        c.start()
+    wire = Wire(ss, rs)
+    near = [
+        wire(l_ref.at[:, 1536:], ll2.at[128:256, :], core),
+        wire(own.at[:, 1536:7680], rr2.at[128:256, :], core),
+        wire(zr.at[:, 7680:], ll2.at[384:512, :], core),
+        wire(zr.at[:, 1536:7680], rr2.at[384:512, :], core),
+    ]
+    big = Sum(mid, 288, mid_refs, wire, where, xp, yp, zp).steps()
+    small = Sum(tail, 96, tail_refs, wire, where, xp, yp, zp).steps()
+    for c in local:
+        c.wait()
+    lt = ll[...].astype(F32).T.astype(BF)
+    for c in near:
         c.wait()
     for k in range(6):
-        lt[256 * k:256 * k + 256, :] = ll[:, 256 * k:256 * k + 256].astype(F32).T.astype(BF)
-    out[0:256, :] = dot(lt[256:512, :], rr[:, 5120:6144]).astype(BF)
+        lt2[256 * k:256 * k + 256, :] = ll2[:, 256 * k:256 * k + 256].astype(F32).T.astype(BF)
+    mid[0:256, :] = dot(lt2[256:512, :], rr2[:, 5120:6144]).astype(BF)
     for k in range(4):
-        out[256 + 256 * k:512 + 256 * k, :] = dot(lt[0:256, :], rr[:, 1024 * k:1024 * k + 1024]).astype(BF)
+        mid[256 + 256 * k:512 + 256 * k, :] = dot(lt2[0:256, :], rr2[:, 1024 * k:1024 * k + 1024]).astype(BF)
     for k in range(4):
         rows = slice(512 + 256 * k, 768 + 256 * k)
-        out[1280 + 256 * k:1536 + 256 * k, :] = dot(lt[rows, :], rr[:, 4096:5120]).astype(BF)
-
-
-def wgrad_mid(own_l, own, zr, c1, c2):
-    return pl.pallas_call(
-        wgrad_mid_kernel,
-        out_shape=shp((2304, 1024), BF),
-        in_specs=[ANY] * 5,
-        out_specs=VM,
-        scratch_shapes=[
-            pltpu.VMEM((512, 1536), BF), pltpu.VMEM((512, 6144), BF), pltpu.VMEM((1536, 512), BF), DMA((8,)),
-        ],
-        compiler_params=pltpu.CompilerParams(vmem_limit_bytes=LIMIT),
-        cost_estimate=pl.CostEstimate(flops=2 << 30, bytes_accessed=16 << 20, transcendentals=0),
-        name="wgrad_mid",
-    )(own_l, own, zr, c1, c2)
-
-
-def tokens_back_kernel(dkv, dqp, dr_ref, gb, wall, wq, wk, wv, gt, pay, weights, sem):
-    copies = load_qkv(wall, (wq, wk, wv), weights, sem)
+        mid[1280 + 256 * k:1536 + 256 * k, :] = dot(lt2[rows, :], rr2[:, 4096:5120]).astype(BF)
+    next(big)
+
+    for c in home:
+        c.wait()
+    lax.fori_loop(1, 32, wait(wide_copy), 0)
+    lax.fori_loop(1, 16, wait(narrow_copy), 0)
     for h in range(16):
         lanes = slice(64 * h, 64 * h + 64)
-        pair = dqp[h]
+        pair = dq[h]
         pay[:64, lanes] = pair[:, :64]
         pay[64:128, lanes] = pair[:, 64:]
         both = (dkv[h].astype(F32) + dkv[16 + h].astype(F32)).astype(BF)
@@ -666,7 +909,10 @@
         pay[:128, 2048 + 64 * h:2112 + 64 * h] = both[:, 64:]
     pay[128:144, :1024] = jnp.concatenate([gb[...], jnp.zeros((8, 1024), F32)], axis=0).astype(BF)
     pay[128:144, 1024:] = jnp.zeros((16, 2048), BF)
-    for c in copies:
+    to_far = wire(pay, rr.at[1], far)
+    to_core = wire(pay, rr.at[0], core)
+    next(big)
+    for c in loads:
         c.wait()
     for k in range(4):
         cols = slice(256 * k, 256 * k + 256)
@@ -674,148 +920,9 @@
         for m in range(3):
             total += dot(pay[:128, 1024 * m:1024 * m + 1024], weights[k, m], NT)
         gt[:, cols] = total
-
-
-def tokens_back(dkv, dqp, dr, gb, wall, own):
-    return pl.pallas_call(
-        tokens_back_kernel,
-        out_shape=[shp((128, 1024), F32), shp((144, 3072), BF)],
-        in_specs=[VM] * 4 + [ANY] * 4,
-        out_specs=[VM] * 2,
-        scratch_shapes=[pltpu.VMEM((4, 3, 256, 1024), BF), DMA((6,))],
-        compiler_params=pltpu.CompilerParams(vmem_limit_bytes=LIMIT),
-        cost_estimate=pl.CostEstimate(flops=1 << 30, bytes_accessed=8 << 20, transcendentals=0),
-        name="tokens_back",
-    )(dkv, dqp, dr, gb, wall, *own)
-
-
-class Sum:
-    def __init__(self, hc, refs, wire, where, xp, yp, zp):
-        self.hc, self.wire, self.zp = hc, wire, zp
-        self.r1, self.s1, self.r2, self.s2, self.r3, self.full = refs
-        zl, x, y, zh, co = where
-        self.zl = zl
-        self.first, self.second = (xp, yp), (yp, xp)
-        self.at1, self.at2 = (x, y), (y, x)
-        self.sent = []
-
-    def rows(self, h, k):
-        return pl.ds(pl.multiple_of(h * 4 * self.hc + k * self.hc, 16), self.hc)
-
-    def cols(self, k, width):
-        return pl.ds(pl.multiple_of(k * width, 128), width)
-
-    def spread(self, g):
-        self.g = g
-        self.one = [[], []]
-        for s in range(3):
-            for h in range(2):
-                src = g.at[self.rows(h, (self.at1[h] + s + 1) % 4)]
-                self.one[h].append(self.wire(src, self.r1.at[h, s], self.first[h][s]))
-
-    def spread_second(self):
-        self.two = [[], []]
-        for h in range(2):
-            for c in self.one[h]:
-                c.wait_recv()
-            total = self.g[self.rows(h, self.at1[h]), :].astype(F32)
-            for s in range(3):
-                total += self.r1[h, s].astype(F32)
-            self.s1[h] = total.astype(BF)
-            for s in range(3):
-                src = self.s1.at[h, :, self.cols((self.at2[h] + s + 1) % 4, 256)]
-                self.two[h].append(self.wire(src, self.r2.at[h, s], self.second[h][s]))
-
-    def spread_third(self):
-        self.three = []
-        for h in range(2):
-            for c in self.two[h]:
-                c.wait_recv()
-            total = self.s1[h, :, self.cols(self.at2[h], 256)].astype(F32)
-            for s in range(3):
-                total += self.r2[h, s].astype(F32)
-            self.s2[h] = total.astype(BF)
-            self.three.append(self.wire(self.s2.at[h, :, self.cols(1 - self.zl, 128)], self.r3.at[h], self.zp))
-
-    def collect(self):
-        self.four = []
-        for h in range(2):
-            self.three[h].wait_recv()
-            total = self.s2[h, :, self.cols(self.zl, 128)].astype(F32) + self.r3[h].astype(F32)
-            spot = self.full.at[self.rows(h, self.at1[h]), self.cols(self.at2[h] * 2 + self.zl, 128)]
-            spot[...] = total.astype(BF)
-            self.four.append(self.wire(spot, spot, self.zp))
-
-    def collect_second(self):
-        self.five = [[], []]
-        for h in range(2):
-            self.four[h].wait()
-            spot = self.full.at[self.rows(h, self.at1[h]), self.cols(self.at2[h], 256)]
-            for s in range(3):
-                self.five[h].append(self.wire(spot, spot, self.second[h][s]))
-
-    def collect_third(self):
-        self.six = [[], []]
-        for h in range(2):
-            for c in self.five[h]:
-                c.wait()
-            spot = self.full.at[self.rows(h, self.at1[h])]
-            for s in range(3):
-                self.six[h].append(self.wire(spot, spot, self.first[h][s]))
-
-    def finish(self):
-        for c in self.one[0] + self.one[1] + self.two[0] + self.two[1] + self.three:
-            c.wait_send()
-        for c in self.six[0] + self.six[1]:
-            c.wait()
-
-
-def sum_scratch(rows):
-    hc = rows // 8
-    return [
-        pltpu.VMEM((2, 3, hc, 1024), BF),
-        pltpu.VMEM((2, hc, 1024), BF),
-        pltpu.VMEM((2, 3, hc, 256), BF),
-        pltpu.VMEM((2, hc, 256), BF),
-        pltpu.VMEM((2, hc, 128), BF),
-        pltpu.VMEM((rows, 1024), BF),
-    ]
-
-
-def finish_kernel(*refs):
-    mid, pay, xs, x_ref = refs[:4]
-    s_q, s_k, s_v, s_o, s_i, s_u, s_vec = refs[4:11]
-    mid_refs, tail_refs = refs[11:17], refs[17:23]
-    ll, rr, tail, v0, vx, vy, vz, tx, ty, ss, rs, ls = refs[23:]
-    scale = 1.0 / math.sqrt(16384)
-    where = place()
-    zl, x, y, zh, co = where
-    w = zh * 2 + co
-    core = device(zl, x, y, zh, 1 - co)
-    far = device(zl, x, y, 1 - zh, co)
-    xp = [device(zl, (x + s) % 4, y, zh, co) for s in (1, 2, 3)]
-    yp = [device(zl, x, (y + s) % 4, zh, co) for s in (1, 2, 3)]
-    zp = device(1 - zl, x, y, zh, co)
-    greet([core, far, zp] + xp + yp)
-    wire = Wire(ss, rs)
-    big = Sum(288, mid_refs, wire, where, xp, yp, zp)
-    small = Sum(96, tail_refs, wire, where, xp, yp, zp)
-
-    to_far = wire(pay, rr.at[1], far)
-    to_core = wire(pay, rr.at[0], core)
-    big.spread(mid)
-    order = [w, zh * 2 + 1 - co, (1 - zh) * 2 + co, (1 - zh) * 2 + 1 - co]
-    mine = pl.ds(pl.multiple_of(w * 256, 256), 256)
-    local = [pltpu.make_async_copy(x_ref.at[:, mine], ll.at[0:128, :], ls.at[0])]
-    for k in range(1, 4):
-        local.append(pltpu.make_async_copy(xs.at[order[k]], ll.at[128 * k:128 * k + 128, :], ls.at[k]))
-    for c in local:
-        c.start()
-    for c in local:
-        c.wait()
-    lt = ll[...].astype(F32).T.astype(BF)
     to_far.wait_recv()
     on_core = wire(rr.at[1], rr.at[2], core)
+    next(big)
     to_core.wait_recv()
     on_core.wait_recv()
     for m in range(3):
@@ -824,64 +931,86 @@
         for k in range(3):
             total += dot(lt[:, 128 * k + 128:128 * k + 256], rr[k, :128, cols])
         tail[256 * m:256 * m + 256, :] = total.astype(BF)
-    small.spread(tail)
+    next(small)
     vec = pay[128:144, mine].astype(F32)
     for k in range(3):
         vec += rr[k, 128:144, mine].astype(F32)
     v0[...] = vec[:8]
     vone = [wire(v0, vx.at[s], xp[s]) for s in range(3)]
-    big.spread_second()
-    small.spread_second()
+    next(big)
+    next(small)
+    next(big)
+    next(small)
     for c in vone:
         c.wait_recv()
     tx[...] = v0[...] + vx[0] + vx[1] + vx[2]
     vtwo = [wire(tx, vy.at[s], yp[s]) for s in range(3)]
-    big.spread_third()
-    small.spread_third()
+    next(big)
+    next(small)
+    next(big)
+    next(small)
     for c in vtwo:
         c.wait_recv()
     ty[...] = tx[...] + vy[0] + vy[1] + vy[2]
     vthree = wire(ty, vz, zp)
-    big.collect()
-    small.collect()
-    big.collect_second()
-    small.collect_second()
-    big.collect_third()
-    small.collect_third()
+    next(big)
+    next(small)
+    next(big)
+    next(small)
+    next(big)
+    next(small)
     vthree.wait()
     s_vec[...] = (ty[...] + vz[...]) * scale
     for c in vone + vtwo + [to_far, to_core, on_core]:
         c.wait_send()
-    big.finish()
-    full = big.full
-    s_o[...] = full[:256, :].astype(F32) * scale
-    for k in range(4):
-        s_i[:, 1024 * k:1024 * k + 1024] = full[256 + 256 * k:512 + 256 * k, :].astype(F32) * scale
-    s_u[...] = full[1280:2304, :].astype(F32) * scale
-    small.finish()
-    for k, ref in enumerate((s_q, s_k, s_v)):
-        ref[...] = small.full[256 * k:256 * k + 256, :].astype(F32) * scale
-
-
-def finish(mid, pay, xs, tok):
-    n = 28 * 2 + 3 + 7
+    next(small)
+    next(small)
+    next(big)
+    next(small)
+
+
+def finish(dkvp, dqp, dr, gb, wall, own, l01, zpay, zr, xs, tok):
+    n = SUM_COPIES * 2 + 4 + 3 + 7
     return pl.pallas_call(
         finish_kernel,
-        out_shape=[
-            shp((256, 1024), F32), shp((256, 1024), F32), shp((256, 1024), F32), shp((256, 1024), F32),
-            shp((256, 4096), F32), shp((1024, 1024), F32), shp((8, 256), F32),
-        ],
-        in_specs=[VM, VM, ANY, ANY],
-        out_specs=[VM] * 7,
+        out_shape=[shp((128, 1024), F32), shp((2304, 1024), BF), shp((768, 1024), BF), shp((8, 256), F32)],
+        in_specs=[ANY, ANY, VM, VM] + [ANY] * 9,
+        out_specs=[VM] * 4,
         scratch_shapes=sum_scratch(2304) + sum_scratch(768) + [
+            pltpu.VMEM((32, 128, 128), BF), pltpu.VMEM((16, 64, 128), BF), pltpu.VMEM((4, 3, 256, 1024), BF),
+            pltpu.VMEM((512, 1536), BF), pltpu.VMEM((512, 6144), BF), pltpu.VMEM((1536, 512), BF),
+            pltpu.VMEM((2304, 1024), BF), pltpu.VMEM((144, 3072), BF),
             pltpu.VMEM((512, 256), BF), pltpu.VMEM((3, 144, 3072), BF), pltpu.VMEM((768, 1024), BF),
             pltpu.VMEM((8, 256), F32), pltpu.VMEM((3, 8, 256), F32), pltpu.VMEM((3, 8, 256), F32),
             pltpu.VMEM((8, 256), F32), pltpu.VMEM((8, 256), F32), pltpu.VMEM((8, 256), F32),
-            DMA((n,)), DMA((n,)), DMA((4,)),
+            DMA((32,)), DMA((32,)), DMA((16,)), DMA((16,)), DMA((n,)), DMA((n,)), DMA((10,)), DMA((6,)),
         ],
         compiler_params=pltpu.CompilerParams(collective_id=6, has_side_effects=True, vmem_limit_bytes=LIMIT),
         name="finish",
-    )(mid, pay, xs, tok)
+    )(dkvp, dqp, dr, gb, wall, *own, l01, zpay, zr, xs, tok)
+
+
+def scale_kernel(o, i0, i1, i2, i3, u, q, k, v, out_q, out_k, out_v, out_o, out_i, out_u):
+    scale = 1.0 / math.sqrt(16384)
+    for src, dst in ((q, out_q), (k, out_k), (v, out_v), (o, out_o), (u, out_u)):
+        dst[...] = src[...].astype(F32) * scale
+    for n, src in enumerate((i0, i1, i2, i3)):
+        out_i[:, 1024 * n:1024 * n + 1024] = src[...].astype(F32) * scale
+
+
+def scaled(mid, tail):
+    def rows(first, n=32):
+        return pl.BlockSpec((n, 1024), lambda j: (first // n + j, 0))
+
+    return pl.pallas_call(
+        scale_kernel,
+        grid=(8,),
+        out_shape=[shp((256, 1024), F32)] * 4 + [shp((256, 4096), F32), shp((1024, 1024), F32)],
+        in_specs=[rows(0)] + [rows(256 + 256 * k) for k in range(4)] + [rows(1280, 128)] + [rows(256 * k) for k in range(3)],
+        out_specs=[rows(0)] * 4 + [pl.BlockSpec((32, 4096), lambda j: (j, 0)), rows(0, 128)],
+        compiler_params=pltpu.CompilerParams(vmem_limit_bytes=LIMIT),
+        name="scaled",
+    )(*[mid] * 6, *[tail] * 3)
 
 
 FLIP_CORE = [(0, 1), (1, 0), (2, 3), (3, 2)]
@@ -905,43 +1034,34 @@
     blk = block_pairs.reshape(-1)
     own = (w_query, w_key, w_value)
     outer = w_outer.reshape(8, 4, 32, 1024)
-    zl, x, y, zh, co = place()
-
-    def quarter(k):
-        first = lax.dynamic_slice_in_dim(w_output, 32 * k, 32, 0)[None]
-        second = lax.dynamic_slice_in_dim(w_inner, 32 * k, 32, 0).reshape(32, 4, 1024).transpose(1, 0, 2)
-        third = lax.dynamic_index_in_dim(outer, k, 0, keepdims=False)
-        return jnp.concatenate([first, second, third], axis=0)
-
-    quarters = jnp.stack([quarter(x), quarter(4 + y)])
-    wall, xs, lnf, *core_shard = gather_weights(*own, tok, lnp, w_output, w_inner, outer)
-    quarters, wall = lax.optimization_barrier((quarters, wall))
-    far_own = lax.ppermute(quarters, "wsh", FLIP_FAR)
+    wall, xs, lnf, *core_shard, qa, qb = gather_weights(*own, tok, lnp, w_output, w_inner, outer)
+    qa, qb, wall = lax.optimization_barrier((qa, qb, wall))
+    x2 = lax.ppermute(qa, "ctx", along_x(2))
+    y2 = lax.ppermute(qb, "ctx", along_y(2))
+    diag_a = lax.ppermute(qa, "wsh", FLIP_CORE)
+    diag_b = lax.ppermute(qb, "wsh", FLIP_CORE)
 
     kvp, qp = project(tok, wall, own)
     kvr, qr = exchange(kvp, qp, 2)
-    far_own, kvr = lax.optimization_barrier((far_own, kvr))
-    far = [far_own]
-    far += [lax.ppermute(far_own[:1], "ctx", along_x(s)) for s in (1, 2, 3)]
-    far += [lax.ppermute(far_own[1:], "ctx", along_y(s)) for s in (1, 2, 3)]
+    qa, qb, x2, y2, diag_a, diag_b, kvr = lax.optimization_barrier((qa, qb, x2, y2, diag_a, diag_b, kvr))
+    x1, x3 = (lax.ppermute(qa, "ctx", along_x(s)) for s in (1, 3))
+    y1, y3 = (lax.ppermute(qb, "ctx", along_y(s)) for s in (1, 3))
     o, ot, lse = attend(blk, block_mask, kvr, qr)
-    *far, o = lax.optimization_barrier((*far, o))
-    diag = [lax.ppermute(p, "wsh", FLIP_CORE) for p in far]
+    x1, x2, x3, y1, y2, y3, o = lax.optimization_barrier((x1, x2, x3, y1, y2, y3, o))
+    far = [qa, x1, x2, x3, qb, y1, y2, y3]
+    d1, d2, d3, e1, e2, e3 = (lax.ppermute(p, "wsh", FLIP_CORE) for p in (x1, x2, x3, y1, y2, y3))
+    diag = [diag_a, d1, d2, d3, diag_b, e1, e2, e3]
     (o_back,) = exchange(None, o, 3)
-    y_out, dr1, do, zpay, cpay, own_l, gb = middle(
+    y_out, dr1, do, zpay, l01, gb = middle(
         o_back, tok, cot, lnf, lnp, ((w_output, w_inner, outer), core_shard), (far, diag)
     )
     zr = lax.ppermute(zpay, "wsh", FLIP_FAR)
-    c1 = lax.ppermute(cpay, "wsh", FLIP_CORE)
 
     (dor,) = exchange(None, do, 3)
     dkvp, dqp = attend_back(blk, block_mask, kvr, qr, dor, ot, lse)
-    dkvr, dqr = exchange(dkvp, dqp, 4)
-    zr, dkvr = lax.optimization_barrier((zr, dkvr))
-    c2 = lax.ppermute(zr[:, 1536:], "wsh", FLIP_CORE)
-    grad_tok, pay = tokens_back(dkvr, dqr, dr1, gb, wall, own)
-    gmid = wgrad_mid(own_l, cpay, zr, c1, c2)
-    s_q, s_k, s_v, s_o, s_i, s_u, s_vec = finish(gmid, pay, xs, tok)
+    zr, dkvp = lax.optimization_barrier((zr, dkvp))
+    grad_tok, mid, tail, s_vec = finish(dkvp, dqp, dr1, gb, wall, own, l01, zpay, zr, xs, tok)
+    s_q, s_k, s_v, s_o, s_i, s_u = scaled(mid, tail)
     out_shape = tokens.shape
     return (
         y_out.reshape(out_shape), grad_tok.reshape(out_shape), s_q, s_k, s_v, s_o, s_i, s_u, s_vec[0:2], s_vec[2:4],

time: 379 us -> 318 us (0.84)
  Pallas kernels: 331 us -> 283 us
  local copies, waits for them, and re-layouts: 20.4 us -> 5.71 us
    pallas_call x4 -> x3, Pallas kernels: 89.3 us -> 45.5 us  [exchange(): pl.pallas_call(kernel, out_shape=outs, in_specs=[ANY] * len(args), out_sp...]
    ppermute x1, waiting for transfers between devices: 0.01 us -> 12.7 us  [body(): zr = lax.ppermute(zpay, 'wsh', FLIP_FAR)]
    unnamed x41 -> x28, local copies, waits for them, and re-layouts: 15 us -> 3.65 us
    ppermute x16 -> x14, waiting for transfers between devices: 11.6 us -> 0.82 us  [the longest x6 0.8 us: body(): lax.ppermute(p, 'wsh', FLIP_CORE)]
    pallas_call x3 -> x2, Pallas kernels: 125 us -> 117 us  [the longest x1 109 us: finish(): pl.pallas_call(finish_kernel, out_shape=[shp((128, 1024), F32), shp((2304...]
    pallas_call x1, Pallas kernels: 32.1 us -> 36.3 us  [gather_weights(): pl.pallas_call(gather_kernel, out_shape=[shp((4, 3, 256, 1024), BF), shp(...]
    ppermute x16 -> x14, starting transfers between devices: 11.8 us -> 9.78 us  [the longest x2 2.51 us: body(): y1, y3 = (lax.ppermute(qb, 'ctx', along_y(s)) for s in (1, 3))]
  transfers between devices with their start and end apart: 17 -> 15, of which waited for: 3 -> 2; matrix products, arithmetic and copies ran while one was open for 0% -> 0% of each run, Pallas kernels for 40% -> 34%
where the time goes in v3:
time: 318 us; the launch traced here: 317 us
  Pallas kernels  283 us (89%)
  waiting for transfers between devices  13.5 us (4%)
  starting transfers between devices  13.2 us (4%)
  local copies, waits for them, and re-layouts  5.71 us (2%)
    pallas_call x1, Pallas kernels, finish(): pl.pallas_call(finish_kernel, out_shape=[shp((128, 1024), F32), shp((2304...  109 us
    pallas_call x3, Pallas kernels, exchange(): pl.pallas_call(kernel, out_shape=outs, in_specs=[ANY] * len(args), out_sp...  45.5 us
    pallas_call x1, Pallas kernels, gather_weights(): pl.pallas_call(gather_kernel, out_shape=[shp((4, 3, 256, 1024), BF), shp(...  36.3 us
    pallas_call x1, Pallas kernels, attend(): pl.pallas_call(attend_kernel, out_shape=[shp((16, 64, 128), BF), shp((8,...  28.6 us
    pallas_call x1, Pallas kernels, attend_back(): pl.pallas_call(attend_back_kernel, out_shape=[shp((32, 128, 128), BF), sh...  28.4 us
    pallas_call x1, Pallas kernels, middle(): pl.pallas_call(middle_kernel, out_shape=[shp((128, 1024), F32), shp((128,...  19.9 us
    ppermute x1, waiting for transfers between devices, body(): zr = lax.ppermute(zpay, 'wsh', FLIP_FAR)  12.7 us
    pallas_call x1, Pallas kernels, scaled(): pl.pallas_call(scale_kernel, grid=(8,), out_shape=[shp((256, 1024), F32)]...  8.42 us
  transfers between devices with their start and end apart: 15, of which 2 were waited for; matrix products, arithmetic and copies ran while one was open for 0% of the time, Pallas kernels for 34%

profile of v3, /device:TPU:0, one launch (start us, length us, event | category | flops | bytes accessed | tf_op | source)
XLA Modules:
  0.0 317.4 jit_solution(1149176302046775073)
XLA Ops:
  0.7 1.4 maximum_maximum_fusion.ln_ref.refs_4_
  2.1 36.3 %gather_qkv.1 = (bf16[4,3,256,1024]{3,2,1,0:T(8,128)(2,1)}, bf16[4,128,256]{2,1,0:T(8,128)(2,1)}, f32[4,8,256]{2,1,0:T(8,128)}, bf16[256,1024]{1,0:T(8,128)(2,1)...) custom-call(bf16[256,1024]{1,0:T(8,128)(2,1)} %refs_5_.3, ...), custom_call_target="tpu_custom_call" | custom-call | tf_op jit(solution)/shard_map/gather_qkv/pallas_call | solution.py:135
  38.5 1.4 collective-permute-start
  39.8 0.2 collective-permute-start.3
  40.0 2.3 collective-permute-start.1
  42.2 6.6 %qkv.1 = (bf16[16,128,128]{2,1,0:T(8,128)(2,1)}, bf16[16,64,128]{2,1,0:T(8,128)(2,1)}) custom-call(bf16[128,1024]{1,0:T(8,128)(2,1)} %bitcast.6, bf16[4,3,256,1024]{3,2,1,0:T(8,128)(2,1)} %get-tuple-element.67.wall.refs_4_, bf16[256,1024]{1,0:T(8,128)(2,1)} %refs_5_.3, bf16[256,1024]{1,0:T(8,128)(2,1)} %refs_6_.3, bf16[256,1024]{1,0:T(8,128)(2,1)} %refs_7_.1), custom_call_target="tpu_custom_call" | custom-call | flops 805306368 | bytes 8388608 | tf_op jit(solution)/shard_map/qkv/pallas_call | solution.py:188
  48.9 24.9 %exchange_2.1 = (bf16[32,128,128]{2,1,0:T(8,128)(2,1)}, bf16[16,64,128]{2,1,0:T(8,128)(2,1)}) custom-call(bf16[16,128,128]{2,1,0:T(8,128)(2,1)} %get-tuple-element.68.refs_0_, bf16[16,64,128]{2,1,0:T(8,128)(2,1)} %get-tuple-element.69.refs_1_), custom_call_target="tpu_custom_call" | custom-call | flops 17179869184 | bytes 33554432 | tf_op jit(solution)/shard_map/exchange_2/pallas_call | solution.py:271
  73.8 0.1 copy.23
  73.9 0.6 reshape.40.blk
  74.6 2.2 collective-permute-start.5
  76.8 2.5 collective-permute-start.7
  79.3 28.6 %attend.1 = (bf16[16,64,128]{2,1,0:T(8,128)(2,1)}, f32[8,64,256]{2,1,0:T(8,128)}, f32[8,1,256]{2,1,0:T(1,128)}) custom-call(s32[64]{0:T(128)} %reshape.40.blk, s32[1,64,64]{2,1,0:T(8,128)} %mask.3, bf16[32,128,128]{2,1,0:T(8,128)(2,1)} %get-tuple-element.75.kvr, bf16[16,64,128]{2,1,0:T(8,128)(2,1)} %get-tuple-element.76.qr), custom_call_target="tpu_custom_call" | custom-call | flops 10737418240 | bytes 33554432 | tf_op jit(solution)/shard_map/attend/pallas_call | solution.py:388
  108.0 0.1 collective-permute-start.8
  108.1 0.5 collective-permute-start.9
  108.6 0.2 copy-done.8
  108.7 0.5 collective-permute-start.11
  109.3 0.8 collective-permute-done.8.refs_20_
  110.0 0.1 collective-permute-start.13
  110.2 11.1 %exchange_3.2.refs_0_ = bf16[16,64,128]{2,1,0:T(8,128)(2,1)} custom-call(bf16[16,64,128]{2,1,0:T(8,128)(2,1)} %get-tuple-element.78.refs_0_), custom_call_target="tpu_custom_call" | custom-call | flops 17179869184 | bytes 33554432 | tf_op jit(solution)/shard_map/exchange_3/pallas_call | solution.py:271
  121.4 0.8 copy-done.10
  122.2 0.2 copy-done.11
  122.3 0.2 copy-done.12
  122.5 19.9 %middle.1 = (f32[128,1024]{1,0:T(8,128)}, f32[128,1024]{1,0:T(8,128)}, bf16[16,64,128]{2,1,0:T(8,128)(2,1)}, bf16[128,9216]{1,0:T(8,128)(2,1)}, bf16[128,3072]{1,0:T(8,128)(2,1)}, /*index=5*/f32[8,1024]{1,0:T(8,128)}) custom-call(bf16[16,64,128]{2,1,0:T(8,128)(2,1)} %exchange_3.2.refs_0_, bf16[128,1024]{1,0:T(8,128)(2,1)} %bitcast.7, ...), custom_call_target="tpu_custom_call" | custom-call | flops 10737418240 | bytes 33554432 | tf_op jit(solution)/shard_map/middle/pallas_call | solution.py:604
  142.5 3.5 %collective-permute-start.14 = (bf16[128,9216]{1,0:T(8,128)(2,1)}, bf16[128,9216]{1,0:T(8,128)(2,1)S(1)}, u32[]{:S(2)}, u32[]{:S(2)}) collective-permute-start(bf16[128,9216]{1,0:T(8,128)(2,1)} %get-tuple-element.92.refs_9_), channel_id=1, source_target_pairs={{0,2},{2,0},{1,3},{3,1},{4,6},{6,4},{5,7},{7,5},{8,10},{10,8},{9,1... | collective-permute-start | bytes 7077896 | tf_op jit(solution)/shard_map/ppermute | solution.py:1058
  145.9 9.5 %exchange_3.3.dor = bf16[16,64,128]{2,1,0:T(8,128)(2,1)} custom-call(bf16[16,64,128]{2,1,0:T(8,128)(2,1)} %get-tuple-element.93.refs_0_), custom_call_target="tpu_custom_call" | custom-call | flops 17179869184 | bytes 33554432 | tf_op jit(solution)/shard_map/exchange_3/pallas_call | solution.py:271
  155.4 28.4 %attend_back.1 = (bf16[32,128,128]{2,1,0:T(8,128)(2,1)}, bf16[16,64,128]{2,1,0:T(8,128)(2,1)}) custom-call(s32[64]{0:T(128)} %reshape.40.blk, s32[1,64,64]{2,1,0:T(8,128)} %mask.3, bf16[32,128,128]{2,1,0:T(8,128)(2,1)} %get-tuple-element.75.kvr, bf16[16,64,128]{2,1,0:T(8,128)(2,1)} %get-tuple-element.76.qr, bf16[16,64,128]{2,1,0:T(8,128)(2,1)} %exchange_3.3.dor, ...), custom_call_target="tpu_custom_call" | custom-call | flops 1073741824 | bytes 4194304 | tf_op jit(solution)/shard_map/attend_back/pallas_call | solution.py:472
  183.8 12.7 %collective-permute-done.14.refs_10_ = bf16[128,9216]{1,0:T(8,128)(2,1)S(1)} collective-permute-done((bf16[128,9216]{1,0:T(8,128)(2,1)}, bf16[128,9216]{1,0:T(8,128)(2,1)S(1)}, u32[]{:S(2)}, u32[]{:S(2)}) %collective-permute-start.14) | collective-permute-done | bytes 2359328 | tf_op jit(solution)/shard_map/ppermute | solution.py:1058
  196.5 1.4 copy-done
  197.9 108.9 %finish.1 = (f32[128,1024]{1,0:T(8,128)}, bf16[2304,1024]{1,0:T(8,128)(2,1)}, bf16[768,1024]{1,0:T(8,128)(2,1)}, f32[8,256]{1,0:T(8,128)}) custom-call(bf16[32,128,128]{2,1,0:T(8,128)(2,1)} %get-tuple-element.97.refs_0_, bf16[16,64,128]{2,1,0:T(8,128)(2,1)} %get-tuple-element.98.refs_1_, f32[128,1024]{1,0:T(8,128)} %get-tuple-element.99.refs_2_, ...), custom_call_target="tpu_custom_call" | custom-call | tf_op jit(solution)/shard_map/finish/pallas_call | solution.py:974
  306.8 1.4 fusion
  308.1 8.4 %scaled.1 = (f32[256,1024]{1,0:T(8,128)}, f32[256,1024]{1,0:T(8,128)}, f32[256,1024]{1,0:T(8,128)}, f32[256,1024]{1,0:T(8,128)}, f32[256,4096]{1,0:T(8,128)}, /*index=5*/f32[1024,1024]{1,0:T(8,128)}) custom-call(bf16[2304,1024]{1,0:T(8,128)(2,1)} %get-tuple-element.105.o.i0.i1.i2.i3.u, bf16[2304,1024]{1,0:T(8,128)(2,1)} %get-tuple-element.105.o.i0.i1.i2.i3.u, ...), custom_call_target="tpu_custom_call" | custom-call | tf_op jit(solution)/shard_map/scaled/pallas_call | solution.py:1005
  316.6 0.8 copy.25
  (41 shorter events, 0.3 us)
Async XLA Ops:
  38.4 36.1 %collective-permute-start.2 = (bf16[9,32,1024]{2,1,0:T(8,128)(2,1)}, bf16[9,32,1024]{2,1,0:T(8,128)(2,1)S(1)}, u32[]{:S(2)}, u32[]{:S(2)}) collective-permute-start(bf16[9,32,1024]{2,1,0:T(8,128)(2,1)} %get-tuple-element.71.refs_11_), channel_id=1, source_target_pairs={{0,1},{1,0},{2,3},{3,2},{4,5},{5,4},{6,7},{7,6},{8,9},{9,8},{10,11... | collective-permute-start | bytes 1769480 | tf_op jit(solution)/shard_map/ppermute | solution.py:1041
  38.5 36.0 %collective-permute-start = (bf16[9,32,1024]{2,1,0:T(8,128)(2,1)}, bf16[9,32,1024]{2,1,0:T(8,128)(2,1)S(1)}, u32[]{:S(2)}, u32[]{:S(2)}) collective-permute-start(bf16[9,32,1024]{2,1,0:T(8,128)(2,1)} %get-tuple-element.71.refs_11_), channel_id=1, source_target_pairs={{0,32},{4,36},{8,40},{12,44},{16,48},{20,52},{24,56},{28,60},{32,0... | collective-permute-start | bytes 1769480 | tf_op jit(solution)/shard_map/ppermute | solution.py:1039
  39.8 34.7 %collective-permute-start.3 = (bf16[9,32,1024]{2,1,0:T(8,128)(2,1)}, bf16[9,32,1024]{2,1,0:T(8,128)(2,1)S(1)}, u32[]{:S(2)}, u32[]{:S(2)}) collective-permute-start(bf16[9,32,1024]{2,1,0:T(8,128)(2,1)} %get-tuple-element.73.refs_15_), channel_id=1, source_target_pairs={{0,1},{1,0},{2,3},{3,2},{4,5},{5,4},{6,7},{7,6},{8,9},{9,8},{10,11... | collective-permute-start | bytes 1769480 | tf_op jit(solution)/shard_map/ppermute | solution.py:1042
  40.0 34.6 %collective-permute-start.1 = (bf16[9,32,1024]{2,1,0:T(8,128)(2,1)}, bf16[9,32,1024]{2,1,0:T(8,128)(2,1)}, u32[]{:S(2)}, u32[]{:S(2)}) collective-permute-start(bf16[9,32,1024]{2,1,0:T(8,128)(2,1)} %get-tuple-element.73.refs_15_), channel_id=1, source_target_pairs={{0,8},{4,12},{8,0},{12,4},{16,24},{20,28},{24,16},{28,20},{32,40},... | collective-permute-start | bytes 1769480 | tf_op jit(solution)/shard_map/ppermute | solution.py:1040
  48.9 24.9 %copy-start.2 = (s32[32,2]{0,1:T(2,128)S(1)}, s32[32,2]{0,1:T(2,128)}, u32[]{:S(2)}) copy-start(s32[32,2]{0,1:T(2,128)} %param.22) | copy-start | bytes 772
  48.9 25.7 %copy-start.3 = (bf16[9,32,1024]{2,1,0:T(8,128)(2,1)S(1)}, bf16[9,32,1024]{2,1,0:T(8,128)(2,1)}, u32[]{:S(2)}) copy-start(bf16[9,32,1024]{2,1,0:T(8,128)(2,1)} %get-tuple-element.71.refs_11_) | copy-start | bytes 1769476
  48.9 27.9 %copy-start.4 = (bf16[9,32,1024]{2,1,0:T(8,128)(2,1)S(1)}, bf16[9,32,1024]{2,1,0:T(8,128)(2,1)}, u32[]{:S(2)}) copy-start(bf16[9,32,1024]{2,1,0:T(8,128)(2,1)} %get-tuple-element.73.refs_15_) | copy-start | bytes 1769476
  74.5 33.4 %copy-start.5 = (bf16[9,32,1024]{2,1,0:T(8,128)(2,1)}, bf16[9,32,1024]{2,1,0:T(8,128)(2,1)S(1)}, u32[]{:S(2)}) copy-start(bf16[9,32,1024]{2,1,0:T(8,128)(2,1)S(1)} %collective-permute-done.2.refs_19_) | copy-start | bytes 1769476
  74.5 33.5 %copy-start.6 = (bf16[9,32,1024]{2,1,0:T(8,128)(2,1)}, bf16[9,32,1024]{2,1,0:T(8,128)(2,1)S(1)}, u32[]{:S(2)}) copy-start(bf16[9,32,1024]{2,1,0:T(8,128)(2,1)S(1)} %collective-permute-done.refs_13_) | copy-start | bytes 1769476
  74.5 33.4 %copy-start.7 = (bf16[9,32,1024]{2,1,0:T(8,128)(2,1)}, bf16[9,32,1024]{2,1,0:T(8,128)(2,1)S(1)}, u32[]{:S(2)}) copy-start(bf16[9,32,1024]{2,1,0:T(8,128)(2,1)S(1)} %collective-permute-done.3.refs_23_) | copy-start | bytes 1769476
  74.6 33.3 %collective-permute-start.5 = (bf16[9,32,1024]{2,1,0:T(8,128)(2,1)S(1)}, bf16[9,32,1024]{2,1,0:T(8,128)(2,1)}, u32[]{:S(2)}, u32[]{:S(2)}) collective-permute-start(bf16[9,32,1024]{2,1,0:T(8,128)(2,1)S(1)} %copy-done.3), channel_id=1, source_target_pairs={{0,48},{4,52},{8,56},{12,60},{16,0},{20,4},{24,8},{28,12},{32,16},... | collective-permute-start | bytes 1769480 | tf_op jit(solution)/shard_map/ppermute | solution.py:1047
  76.8 31.2 %collective-permute-start.4 = (bf16[9,32,1024]{2,1,0:T(8,128)(2,1)S(1)}, bf16[9,32,1024]{2,1,0:T(8,128)(2,1)S(1)}, u32[]{:S(2)}, u32[]{:S(2)}) collective-permute-start(bf16[9,32,1024]{2,1,0:T(8,128)(2,1)S(1)} %copy-done.3), channel_id=1, source_target_pairs={{0,16},{4,20},{8,24},{12,28},{16,32},{20,36},{24,40},{28,44},{32,4... | collective-permute-start | bytes 1769480 | tf_op jit(solution)/shard_map/ppermute | solution.py:1047
  76.8 31.2 %collective-permute-start.7 = (bf16[9,32,1024]{2,1,0:T(8,128)(2,1)S(1)}, bf16[9,32,1024]{2,1,0:T(8,128)(2,1)}, u32[]{:S(2)}, u32[]{:S(2)}) collective-permute-start(bf16[9,32,1024]{2,1,0:T(8,128)(2,1)S(1)} %copy-done.4), channel_id=1, source_target_pairs={{0,12},{4,0},{8,4},{12,8},{16,28},{20,16},{24,20},{28,24},{32,44},... | collective-permute-start | bytes 1769480 | tf_op jit(solution)/shard_map/ppermute | solution.py:1048
  79.3 28.7 %collective-permute-start.6 = (bf16[9,32,1024]{2,1,0:T(8,128)(2,1)S(1)}, bf16[9,32,1024]{2,1,0:T(8,128)(2,1)}, u32[]{:S(2)}, u32[]{:S(2)}) collective-permute-start(bf16[9,32,1024]{2,1,0:T(8,128)(2,1)S(1)} %copy-done.4), channel_id=1, source_target_pairs={{0,4},{4,8},{8,12},{12,0},{16,20},{20,24},{24,28},{28,16},{32,36},... | collective-permute-start | bytes 1769480 | tf_op jit(solution)/shard_map/ppermute | solution.py:1048
  107.9 0.8 copy-start.8
  108.0 2.1 collective-permute-start.8
  108.1 13.3 %collective-permute-start.9 = (bf16[9,32,1024]{2,1,0:T(8,128)(2,1)S(1)}, bf16[9,32,1024]{2,1,0:T(8,128)(2,1)S(1)}, u32[]{:S(2)}, u32[]{:S(2)}) collective-permute-start(bf16[9,32,1024]{2,1,0:T(8,128)(2,1)S(1)} %collective-permute-done.refs_13_), channel_id=1, source_target_pairs={{0,1},{1,0},{2,3},{3,2},{4,5},{5,4},{6,7},{7,6},{8,9},{9,8},{10,11... | collective-permute-start | bytes 1769480 | tf_op jit(solution)/shard_map/ppermute | solution.py:1052
  108.7 12.6 %collective-permute-start.10 = (bf16[9,32,1024]{2,1,0:T(8,128)(2,1)}, bf16[9,32,1024]{2,1,0:T(8,128)(2,1)S(1)}, u32[]{:S(2)}, u32[]{:S(2)}) collective-permute-start(bf16[9,32,1024]{2,1,0:T(8,128)(2,1)} %collective-permute-done.5.refs_14_), channel_id=1, source_target_pairs={{0,1},{1,0},{2,3},{3,2},{4,5},{5,4},{6,7},{7,6},{8,9},{9,8},{10,11... | collective-permute-start | bytes 1769480 | tf_op jit(solution)/shard_map/ppermute | solution.py:1052
  108.7 12.6 %collective-permute-start.11 = (bf16[9,32,1024]{2,1,0:T(8,128)(2,1)}, bf16[9,32,1024]{2,1,0:T(8,128)(2,1)S(1)}, u32[]{:S(2)}, u32[]{:S(2)}) collective-permute-start(bf16[9,32,1024]{2,1,0:T(8,128)(2,1)} %collective-permute-done.6.refs_16_), channel_id=1, source_target_pairs={{0,1},{1,0},{2,3},{3,2},{4,5},{5,4},{6,7},{7,6},{8,9},{9,8},{10,11... | collective-permute-start | bytes 1769480 | tf_op jit(solution)/shard_map/ppermute | solution.py:1052
  109.3 12.1 %collective-permute-start.12 = (bf16[9,32,1024]{2,1,0:T(8,128)(2,1)}, bf16[9,32,1024]{2,1,0:T(8,128)(2,1)}, u32[]{:S(2)}, u32[]{:S(2)}) collective-permute-start(bf16[9,32,1024]{2,1,0:T(8,128)(2,1)} %collective-permute-done.1.refs_17_), channel_id=1, source_target_pairs={{0,1},{1,0},{2,3},{3,2},{4,5},{5,4},{6,7},{7,6},{8,9},{9,8},{10,11... | collective-permute-start | bytes 1769480 | tf_op jit(solution)/shard_map/ppermute | solution.py:1052
  110.0 11.3 %copy-start.9 = (bf16[9,32,1024]{2,1,0:T(8,128)(2,1)}, bf16[9,32,1024]{2,1,0:T(8,128)(2,1)S(1)}, u32[]{:S(2)}) copy-start(bf16[9,32,1024]{2,1,0:T(8,128)(2,1)S(1)} %collective-permute-done.8.refs_20_) | copy-start | bytes 1769476
  110.0 11.3 %collective-permute-start.13 = (bf16[9,32,1024]{2,1,0:T(8,128)(2,1)}, bf16[9,32,1024]{2,1,0:T(8,128)(2,1)}, u32[]{:S(2)}, u32[]{:S(2)}) collective-permute-start(bf16[9,32,1024]{2,1,0:T(8,128)(2,1)} %collective-permute-done.7.refs_18_), channel_id=1, source_target_pairs={{0,1},{1,0},{2,3},{3,2},{4,5},{5,4},{6,7},{7,6},{8,9},{9,8},{10,11... | collective-permute-start | bytes 1769480 | tf_op jit(solution)/shard_map/ppermute | solution.py:1052
  121.3 0.8 copy-start.10
  121.3 1.0 copy-start.11
  121.4 1.2 copy-start.12
  142.5 54.0 %collective-permute-start.14 = (bf16[128,9216]{1,0:T(8,128)(2,1)}, bf16[128,9216]{1,0:T(8,128)(2,1)S(1)}, u32[]{:S(2)}, u32[]{:S(2)}) collective-permute-start(bf16[128,9216]{1,0:T(8,128)(2,1)} %get-tuple-element.92.refs_9_), channel_id=1, source_target_pairs={{0,2},{2,0},{1,3},{3,1},{4,6},{6,4},{5,7},{7,5},{8,10},{10,8},{9,1... | collective-permute-start | bytes 7077896 | tf_op jit(solution)/shard_map/ppermute | solution.py:1058
  196.5 1.4 copy-start
  308.1 8.4 %copy-start.1 = (f32[128,1024]{1,0:T(8,128)S(1)}, f32[128,1024]{1,0:T(8,128)}, u32[]{:S(2)}) copy-start(f32[128,1024]{1,0:T(8,128)} %get-tuple-element.104) | copy-start | bytes 1572868

commit v4 on v3

--- a/solution.py
+++ b/solution.py
@@ -85,10 +85,10 @@
     rest = []
     for m in range(3):
         rest.append(wire(ws[m], wall.at[me, m], core))
-    for p, idx in ((core, zh * 2 + 1 - co), (far, other), (diag, (1 - zh) * 2 + 1 - co)):
-        cols = pl.ds(pl.multiple_of(idx * 256, 256), 256)
-        rest.append(wire(x_ref.at[:, cols], xs.at[me], p))
+    for p in (core, far, diag):
         rest.append(wire(ln_ref, lnf.at[me], p))
+    for n, idx in enumerate((zh * 2 + 1 - co, (1 - zh) * 2 + 1 - co)):
+        rest.append(wire(x_ref.at[:, pl.ds(pl.multiple_of(idx * 256, 256), 256)], xs.at[n], core))
     quarters = []
     for ref, k, n in ((qa_ref, x, y), (qb_ref, 4 + y, x)):
         rows = pl.ds(pl.multiple_of(k * 32, 32), 32)
@@ -131,11 +131,11 @@
 
 
 def gather_weights(wq, wk, wv, tok, lnp, wo, wi, wu):
-    n = 6 + 3 + 6 + 12 + 18 + 3 + 6 + 3
+    n = 6 + 3 + 5 + 12 + 18 + 3 + 6 + 3
     return pl.pallas_call(
         gather_kernel,
         out_shape=[
-            shp((4, 3, 256, 1024), BF), shp((4, 128, 256), BF), shp((4, 8, 256), F32),
+            shp((4, 3, 256, 1024), BF), shp((2, 128, 256), BF), shp((4, 8, 256), F32),
             shp(wo.shape, BF), shp(wi.shape, BF), shp(wu.shape, BF), shp((9, 32, 1024), BF), shp((9, 32, 1024), BF),
         ],
         in_specs=[ANY] * 8,
@@ -355,7 +355,22 @@
             return new, total, mix
 
         chunks = (oblk[4 * g + 3] + 7) // 8
-        top, total, mix = lax.fori_loop(0, chunks, chunk, (top, total, mix))
+        def pair(c, state):
+            top, total, mix = state
+            parts = [dot(kaug[pl.ds(pl.multiple_of(c * 1024 + 512 * k, 512), 512), :], queries, NT) for k in range(2)]
+            new = top
+            for s in parts:
+                new = jnp.maximum(new, jnp.max(s, axis=0, keepdims=True))
+            shrink = jnp.exp(top - new)
+            total, mix = total * shrink, mix * shrink
+            for k, s in enumerate(parts):
+                p = jnp.exp(s - new)
+                total += jnp.sum(p, axis=0, keepdims=True)
+                mix += dot(kvt[2 * c + k, 64:, :], p.astype(BF))
+            return new, total, mix
+
+        top, total, mix = lax.fori_loop(0, chunks // 2, pair, (top, total, mix))
+        top, total, mix = lax.fori_loop(chunks // 2 * 2, chunks, chunk, (top, total, mix))
         out = mix / total
         ot_ref[g] = out
         lse_ref[g] = top + jnp.log(total)
@@ -454,7 +469,8 @@
             return dq + dot(kvt[c, :64, :], ds)
 
         chunks = (oblk[4 * g + 3] + 7) // 8
-        dq = lax.fori_loop(0, chunks, chunk, jnp.concatenate(dq, axis=1))
+        dq = lax.fori_loop(0, chunks // 2, lambda c, dq: chunk(2 * c + 1, chunk(2 * c, dq)), jnp.concatenate(dq, axis=1))
+        dq = lax.fori_loop(chunks // 2 * 2, chunks, chunk, dq)
         back = (dq * 0.125).T.astype(BF)
         for u in range(4):
             dqs[order[4 * g + u]] = back[64 * u:64 * u + 64, :]
@@ -502,8 +518,8 @@
     o_ref, x_ref, e_ref, ln_ref, ln_own = refs[:5]
     shards = (refs[5:8], refs[8:11])
     pieces = (refs[11:19], refs[19:27])
-    y_ref, dr_ref, do_ref, zpay, l_ref, gb_ref = refs[27:33]
-    wo, wi, wu, us, gs, dus, nl, ob, sw, sp = refs[33:]
+    y_ref, dr_ref, do_ref, zpay, gpay, cpay, lown, gb_ref = refs[27:35]
+    wo, wi, wu, us, gs, nl, ob, sw, sp = refs[35:]
     zl, x, y, zh, co = place()
     w = zh * 2 + co
     where = [w, zh * 2 + 1 - co, (1 - zh) * 2 + co, (1 - zh) * 2 + 1 - co]
@@ -574,7 +590,7 @@
         dg = dot(dm, wu[pl.ds(c * 8, 8)].reshape(1024, 1024), NT)
         slope = 0.5 * (1.0 + lax.erf(u * half)) + u * (jnp.exp(-0.5 * u * u) * (1.0 / math.sqrt(2 * math.pi)))
         du = (dg * slope).astype(BF)
-        dus[:, rows] = du
+        cpay[:, rows] = du
         return total + dot(du, wi[c], NT)
 
     dn1 = lax.fori_loop(0, 4, back, dr2)
@@ -588,16 +604,16 @@
     for h in range(16):
         lanes = slice(64 * h, 64 * h + 64)
         do_ref[h] = jnp.concatenate([do[:64, lanes], do[64:, lanes]], axis=1)
-    du = dus[...]
-    zpay[:, 1536:5632] = du
-    zpay[:, 5632:6656] = dm
-    zpay[:, 6656:7680] = da
-    for r, (ref, at) in enumerate(((l_ref, 0), (l_ref, 1536), (zpay, 0), (zpay, 7680))):
+    cpay[:, 4096:5120] = da
+    zpay[:, 1024:2048] = dm
+    for r, (ref, at, gref, gat) in enumerate((
+        (lown, 0, gpay, 0), (cpay, 5120, gpay, 1024), (lown, 512, zpay, 0), (cpay, 5632, zpay, 2048)
+    )):
         few = pl.ds(pl.multiple_of(where[r] * 256, 256), 256)
         many = pl.ds(pl.multiple_of(where[r] * 1024, 1024), 1024)
         ref[:, at:at + 256] = nl[:, few]
         ref[:, at + 256:at + 512] = ob[:, few]
-        ref[:, at + 512:at + 1536] = gs[:, many]
+        gref[:, gat:gat + 1024] = gs[:, many]
 
 
 def middle(o, tok, cot, lnf, lnp, shards, pieces):
@@ -605,16 +621,15 @@
         middle_kernel,
         out_shape=[
             shp((128, 1024), F32), shp((128, 1024), F32), shp((16, 64, 128), BF),
-            shp((128, 9216), BF), shp((128, 3072), BF), shp((8, 1024), F32),
+            shp((128, 3072), BF), shp((128, 2048), BF), shp((128, 6144), BF), shp((128, 1024), BF), shp((8, 1024), F32),
         ],
         in_specs=[VM] * 5 + [ANY] * 22,
-        out_specs=[VM] * 6,
+        out_specs=[VM] * 8,
         scratch_shapes=[
             pltpu.VMEM((1024, 1024), BF),
             pltpu.VMEM((4, 1024, 1024), BF),
             pltpu.VMEM((32, 4, 32, 1024), BF),
             pltpu.VMEM((4, 128, 1024), F32),
-            pltpu.VMEM((128, 4096), BF),
             pltpu.VMEM((128, 4096), BF),
             pltpu.VMEM((128, 1024), BF),
             pltpu.VMEM((128, 1024), BF),
@@ -626,6 +641,94 @@
     )(o, tok, cot, lnf, lnp, *shards[0], *shards[1], *pieces[0], *pieces[1])
 
 
+def turn_kernel(do, cpay, lown, dor, own_a, plus_a, minus_a, own_b, plus_b, minus_b, rr, ll, lt, mid, sn, rn, ss, rs, ls, lo):
+    zl, x, y, zh, co = place()
+    flat = lax.axis_index("ctx") % 16
+    core = device(zl, x, y, zh, 1 - co)
+    bar = pltpu.get_barrier_semaphore()
+
+    def greet_one(i, carry):
+        pl.semaphore_signal(bar, inc=1, device_id={"ctx": zl * 16 + (flat + i) % 16}, device_id_type=MESH)
+        return carry
+
+    pl.semaphore_signal(bar, inc=1, device_id=core, device_id_type=MESH)
+    lax.fori_loop(1, 16, greet_one, 0)
+    local = [
+        pltpu.make_async_copy(cpay.at[:, :5120], rr.at[0:128, :], ls.at[0]),
+        pltpu.make_async_copy(lown, ll.at[0:128, :], ls.at[1]),
+    ]
+    for c in local:
+        c.start()
+    pl.semaphore_wait(bar, 16)
+
+    def narrow_copy(i):
+        p = (flat + i) % 16
+        return pltpu.make_async_remote_copy(
+            src_ref=do.at[p], dst_ref=dor.at[flat], send_sem=sn.at[i], recv_sem=rn.at[i],
+            device_id={"ctx": zl * 16 + p}, device_id_type=MESH,
+        )
+
+    def start_one(i, carry):
+        narrow_copy(i).start()
+        return carry
+
+    def wait_one(i, carry):
+        narrow_copy(i).wait()
+        return carry
+
+    wire = Wire(ss, rs)
+    near = [wire(cpay.at[:, 5120:], ll.at[128:256, :], core), wire(cpay.at[:, :5120], rr.at[128:256, :], core)]
+    lax.fori_loop(1, 16, start_one, 0)
+    home = pltpu.make_async_copy(do.at[flat], dor.at[flat], ls.at[2])
+    home.start()
+    for c in local:
+        c.wait()
+    for c in near:
+        c.wait()
+    for k in range(4):
+        lt[256 * k:256 * k + 256, :] = ll[:, 256 * k:256 * k + 256].astype(F32).T.astype(BF)
+    for z in range(2):
+        mid[z, 0:256, :] = dot(lt[512 * z + 256:512 * z + 512, :], rr[:, 4096:5120]).astype(BF)
+        for k in range(4):
+            rows = slice(256 + 256 * k, 512 + 256 * k)
+            mid[z, rows, :] = dot(lt[512 * z:512 * z + 256, :], rr[:, 1024 * k:1024 * k + 1024]).astype(BF)
+    out = []
+    for h, (at, own, plus, minus) in enumerate(((x, own_a, plus_a, minus_a), (y, own_b, plus_b, minus_b))):
+
+        def rows(s, first, size):
+            return pl.ds(pl.multiple_of(h * 640 + (at + s) % 4 * 160 + first, 16), size)
+
+        for src, dst in (
+            (rows(0, 0, 160), own),
+            (rows(1, 0, 160), plus.at[:, :160]), (rows(2, 0, 80), plus.at[:, 160:]),
+            (rows(3, 0, 160), minus.at[:, :160]), (rows(2, 80, 80), minus.at[:, 160:]),
+        ):
+            out.append(pltpu.make_async_copy(mid.at[:, src], dst, lo.at[len(out)]))
+    for c in out:
+        c.start()
+    home.wait()
+    lax.fori_loop(1, 16, wait_one, 0)
+    for c in out:
+        c.wait()
+
+
+def turn(do, cpay, lown):
+    return pl.pallas_call(
+        turn_kernel,
+        out_shape=[shp(do.shape, BF)] + [shp((2, 160, 1024), BF), shp((2, 240, 1024), BF), shp((2, 240, 1024), BF)] * 2,
+        in_specs=[ANY] * 3,
+        out_specs=[ANY] * 7,
+        scratch_shapes=[
+            pltpu.VMEM((256, 5120), BF), pltpu.VMEM((256, 1024), BF), pltpu.VMEM((1024, 256), BF),
+            pltpu.VMEM((2, 1280, 1024), BF),
+            DMA((16,)), DMA((16,)), DMA((2,)), DMA((2,)), DMA((3,)), DMA((10,)),
+        ],
+        compiler_params=pltpu.CompilerParams(collective_id=5, has_side_effects=True, vmem_limit_bytes=LIMIT),
+        cost_estimate=pl.CostEstimate(flops=16 << 30, bytes_accessed=32 << 20, transcendentals=0),
+        name="turn",
+    )(do, cpay, lown)
+
+
 class Spread:
     def __init__(self, wire, plus, minus, at, piece, bufs):
         self.wire, self.plus, self.minus, self.at, self.piece = wire, plus, minus, at, piece
@@ -687,15 +790,70 @@
             c.wait_send()
 
 
+class DirectSpread:
+    def __init__(self, wire, peers, at, piece, bufs):
+        self.wire, self.peers, self.at, self.piece, self.bufs = wire, peers, at, piece, bufs
+
+    def start(self):
+        self.copies = []
+        for s in range(3):
+            for u in range(2):
+                src = self.piece((self.at + s + 1) % 4, u)
+                self.copies.append(self.wire(src, self.bufs[s].at[u], self.peers[s]))
+
+    def relay(self):
+        pass
+
+    def total(self):
+        for c in self.copies:
+            c.wait_recv()
+        out = []
+        for u in range(2):
+            total = self.piece(self.at, u)[...].astype(F32)
+            for s in range(3):
+                total += self.bufs[s][u].astype(F32)
+            out.append(total)
+        return out
+
+    def sent(self):
+        for c in self.copies:
+            c.wait_send()
+
+
+class DirectGather:
+    def __init__(self, wire, peers, at, block):
+        self.wire, self.peers, self.at, self.block = wire, peers, at, block
+
+    def start(self):
+        self.copies = []
+        for u in range(2):
+            spot = self.block(self.at, u)
+            for p in self.peers:
+                self.copies.append(self.wire(spot, spot, p))
+
+    def relay(self):
+        pass
+
+    def done(self):
+        for c in self.copies:
+            c.wait()
+
+
 class Sum:
+    direct = False
+
+    def cut(self, g, rows):
+        return g.at[rows]
+
     def __init__(self, g, hc, refs, wire, where, xp, yp, zp):
         bufs1, s1, bufs2, s2, self.r3, full = refs[:4], refs[4], refs[5:9], refs[9], refs[10], refs[11]
         zl, x, y, zh, co = where
-        self.wire, self.zp, self.zl, self.hc = wire, zp, zl, hc
-        self.s1, self.s2, self.full = s1, s2, full
+        self.wire, self.zp, self.zl = wire, zp, zl
+        self.s1, self.s2, self.last, self.full = s1, s2, s2, full
         hh = hc // 2
         first, second = (xp, yp), (yp, xp)
         self.at1, self.at2 = (x, y), (y, x)
+        self.peers = [(first[h][0], first[h][2]) for h in range(2)]
 
         def rows(h, k, u):
             return pl.ds(pl.multiple_of(h * 4 * hc + k * hc + u * hh, 16), hh)
@@ -703,10 +861,10 @@
         def cols(k, width):
             return pl.ds(pl.multiple_of(k * width, 128), width)
 
-        self.cols = cols
+        self.rows, self.cols = rows, cols
 
         def one(h):
-            return lambda k, u: g.at[rows(h, k, u)]
+            return lambda k, u: self.cut(g, rows(h, k, u))
 
         def two(h):
             return lambda k, u: s1.at[h, u, :, cols(k, 256)]
@@ -720,39 +878,63 @@
         def ends(peers):
             return wire, peers[0], peers[2]
 
-        self.one = [Spread(*ends(first[h]), self.at1[h], one(h), [r.at[h] for r in bufs1]) for h in range(2)]
-        self.two = [Spread(*ends(second[h]), self.at2[h], two(h), [r.at[h] for r in bufs2]) for h in range(2)]
-        self.five = [Gather(*ends(second[h]), self.at2[h], five(h)) for h in range(2)]
+        if g is not None:
+            self.one = [Spread(*ends(first[h]), self.at1[h], one(h), [r.at[h] for r in bufs1]) for h in range(2)]
+        if self.direct:
+            self.two = [DirectSpread(wire, second[h], self.at2[h], two(h), [r.at[h] for r in bufs2]) for h in range(2)]
+            self.five = [DirectGather(wire, second[h], self.at2[h], five(h)) for h in range(2)]
+        else:
+            self.two = [Spread(*ends(second[h]), self.at2[h], two(h), [r.at[h] for r in bufs2]) for h in range(2)]
+            self.five = [Gather(*ends(second[h]), self.at2[h], five(h)) for h in range(2)]
         self.six = [Gather(*ends(first[h]), self.at1[h], six(h)) for h in range(2)]
 
-    def steps(self):
+    def begin(self):
         for t in self.one:
             t.start()
-        yield
+
+    def relay(self):
         for t in self.one:
             t.relay()
+
+    def totals(self, h):
+        return self.one[h].total()
+
+    def across(self):
+        pass
+
+    def settle(self):
+        for t in self.one:
+            t.sent()
+
+    def steps(self):
+        self.begin()
+        yield
+        self.relay()
         yield
         for h in range(2):
-            for u, total in enumerate(self.one[h].total()):
+            for u, total in enumerate(self.totals(h)):
                 self.s1[h, u] = total.astype(BF)
             self.two[h].start()
         yield
         for t in self.two:
             t.relay()
         yield
-        three = []
         for h in range(2):
             for u, total in enumerate(self.two[h].total()):
                 self.s2[h, u] = total.astype(BF)
-            three.append(self.wire(self.s2.at[h, :, :, self.cols(1 - self.zl, 128)], self.r3.at[h], self.zp))
+        self.across()
+        yield
+        three = []
+        for h in range(2):
+            self.ready(h)
+            three.append(self.wire(self.last.at[h, :, :, self.cols(1 - self.zl, 128)], self.r3.at[h], self.zp))
         yield
         four = []
         for h in range(2):
             three[h].wait_recv()
             for u in range(2):
-                total = self.s2[h, u, :, self.cols(self.zl, 128)].astype(F32) + self.r3[h, u].astype(F32)
-                rows = pl.ds(pl.multiple_of(h * 4 * self.hc + self.at1[h] * self.hc + u * (self.hc // 2), 16), self.hc // 2)
-                spot = self.full.at[rows, self.cols(self.at2[h] * 2 + self.zl, 128)]
+                total = self.last[h, u, :, self.cols(self.zl, 128)].astype(F32) + self.r3[h, u].astype(F32)
+                spot = self.full.at[self.rows(h, self.at1[h], u), self.cols(self.at2[h] * 2 + self.zl, 128)]
                 spot[...] = total.astype(BF)
                 four.append(self.wire(spot, spot, self.zp))
         yield
@@ -771,21 +953,98 @@
         for t in self.six:
             t.relay()
         yield
-        for t in self.one + self.two:
+        for t in self.two:
             t.sent()
         for c in three:
             c.wait_send()
+        self.settle()
         for t in self.six:
             t.done()
         yield
 
+    def ready(self, h):
+        pass
+
+
+class PairSum(Sum):
+    direct = True
+
+    def cut(self, g, rows):
+        return g.at[:, rows]
+
+    def __init__(self, g, hc, refs, wire, where, xp, yp, zp, far):
+        self.rf, self.s3 = refs[:2]
+        super().__init__(g, hc, refs[2:], wire, where, xp, yp, zp)
+        self.far, self.hh, self.last = far, hc // 2, self.s3
+
+    def totals(self, h):
+        return [t.reshape(2 * self.hh, 1024) for t in self.one[h].total()]
+
+    def across(self):
+        self.crossed = [self.wire(self.s2.at[h, :, self.hh:], self.rf.at[h], self.far) for h in range(2)]
+
+    def ready(self, h):
+        self.crossed[h].wait_recv()
+        for u in range(2):
+            self.s3[h, u] = (self.s2[h, u, :self.hh].astype(F32) + self.rf[h, u].astype(F32)).astype(BF)
+
+    def settle(self):
+        for t in self.one:
+            t.sent()
+        for c in self.crossed:
+            c.wait_send()
+
+
+class BegunSum(PairSum):
+    direct = False
+
+    def __init__(self, hc, refs, wire, where, xp, yp, zp, far, own, plus, minus):
+        self.own, self.fwd = refs[:2]
+        super().__init__(None, hc, list(refs[2:4]) + [None] * 4 + list(refs[4:]), wire, where, xp, yp, zp, far)
+        self.plus, self.minus = plus, minus
+
+    def begin(self):
+        hc = 2 * self.hh
+        self.passed = []
+        for h in range(2):
+            plus, minus = self.peers[h]
+            self.passed.append((
+                self.wire(self.plus[h].at[:, hc:], self.fwd.at[h, 0], plus),
+                self.wire(self.minus[h].at[:, hc:], self.fwd.at[h, 1], minus),
+            ))
+
+    def relay(self):
+        pass
+
+    def totals(self, h):
+        hh = self.hh
+        for c in self.passed[h]:
+            c.wait_recv()
+        out = []
+        for u in range(2):
+            rows = slice(u * hh, u * hh + hh)
+            total = self.own[h, 0, :, rows].astype(F32) + self.own[h, 1, :, rows].astype(F32)
+            total += self.own[h, 2, :, rows].astype(F32) + self.fwd[h, u].astype(F32)
+            out.append(total.reshape(2 * hh, 1024))
+        return out
+
+    def settle(self):
+        for c in self.crossed:
+            c.wait_send()
+        for pair in self.passed:
+            for c in pair:
+                c.wait_send()
+
 
 SUM_COPIES = 12 + 12 + 2 + 4 + 12 + 12
 
 
+BEGUN_COPIES = 4 + 12 + 2 + 2 + 4 + 12 + 12
+PAIR_COPIES = 12 + 12 + 2 + 2 + 4 + 12 + 12
+
+
 def sum_scratch(rows):
-    hc = rows // 8
-    hh = hc // 2
+    hh = rows // 16
     return (
         [pltpu.VMEM((2, 2, hh, 1024), BF)] * 4
         + [pltpu.VMEM((2, 2, hh, 1024), BF)]
@@ -794,12 +1053,28 @@
     )
 
 
+def pair_scratch(rows, begun):
+    hh = rows // 16
+    begin = [pltpu.VMEM((2, 3, 2, 2 * hh, 1024), BF), pltpu.VMEM((2, 2, 2, hh, 1024), BF)]
+    first = [pltpu.VMEM((2, 2, 2, hh, 1024), BF)] * 4
+    return (
+        (begin if begun else [])
+        + [pltpu.VMEM((2, 2, hh, 256), BF)] * 2
+        + ([] if begun else first)
+        + [pltpu.VMEM((2, 2, 2 * hh, 1024), BF)]
+        + [pltpu.VMEM((2, 2, 2 * hh, 256), BF)] * 4
+        + [pltpu.VMEM((2, 2, 2 * hh, 256), BF), pltpu.VMEM((2, 2, hh, 128), BF)]
+    )
+
+
 def finish_kernel(*refs):
-    dkvp, dqp, dr_ref, gb, wall, wq, wk, wv, l_ref, own, zr, xs, x_ref = refs[:13]
-    gt, mid_full, tail_full, s_vec = refs[13:17]
-    mid_refs, tail_refs = list(refs[17:28]) + [mid_full], list(refs[28:39]) + [tail_full]
-    (dkv, dq, weights, ll2, rr2, lt2, mid, pay, ll, rr, tail, v0, vx, vy, vz, tx, ty,
-     sw, rw, sn, rn, ss, rs, ls, lw) = refs[39:]
+    dkvp, dqp, dr_ref, gb, wall, wq, wk, wv, gpay, zpay, zr, xs, x_ref = refs[:13]
+    got = ((refs[13], refs[16]), (refs[14], refs[17]), (refs[15], refs[18]))
+    gt, io_full, u_full, tail_full, s_vec = refs[19:24]
+    io_refs = list(refs[24:35]) + [io_full]
+    u_refs, tail_refs = list(refs[35:46]) + [u_full], list(refs[46:59]) + [tail_full]
+    (dkv, dq, weights, ll2, rr2, lt2, mid, pay, ll, rr, tail, v0, vf, v1, vx, vy, vz, tx, ty,
+     sw, rw, sn, rn, ss, rs, ls, lw) = refs[59:]
     scale = 1.0 / math.sqrt(16384)
     where = place()
     zl, x, y, zh, co = where
@@ -821,18 +1096,22 @@
         pl.semaphore_signal(bar, inc=1, device_id=p, device_id_type=MESH)
     lax.fori_loop(1, 32, greet_one, 0)
 
-    mine = pl.ds(pl.multiple_of(w * 256, 256), 256)
-    order = [w, zh * 2 + 1 - co, (1 - zh) * 2 + co, (1 - zh) * 2 + 1 - co]
+    mine = [pl.ds(pl.multiple_of(k * 256, 256), 256) for k in (w, (1 - zh) * 2 + co)]
+    parts = []
+    for h in range(2):
+        for n in range(3):
+            parts.append(pltpu.make_async_copy(got[n][h].at[:, :160], io_refs[0].at[h, n], ls.at[10 + 3 * h + n]))
     local = [
-        pltpu.make_async_copy(l_ref.at[:, :1536], ll2.at[0:128, :], ls.at[0]),
-        pltpu.make_async_copy(own.at[:, 1536:7680], rr2.at[0:128, :], ls.at[1]),
-        pltpu.make_async_copy(zr.at[:, :1536], ll2.at[256:384, :], ls.at[2]),
-        pltpu.make_async_copy(zr.at[:, 1536:7680], rr2.at[256:384, :], ls.at[3]),
-        pltpu.make_async_copy(x_ref.at[:, mine], ll.at[0:128, :], ls.at[4]),
+        pltpu.make_async_copy(gpay.at[:, :1024], ll2.at[0:128, :], ls.at[0]),
+        pltpu.make_async_copy(zpay.at[:, 1024:2048], rr2.at[0:128, :], ls.at[1]),
+        pltpu.make_async_copy(zr.at[:, :1024], ll2.at[256:384, :], ls.at[2]),
+        pltpu.make_async_copy(zr.at[:, 1024:2048], rr2.at[256:384, :], ls.at[3]),
     ]
-    for k in range(1, 4):
-        local.append(pltpu.make_async_copy(xs.at[order[k]], ll.at[128 * k:128 * k + 128, :], ls.at[4 + k]))
-    for c in local:
+    for k in range(2):
+        cols = slice(256 * k, 256 * k + 256)
+        local.append(pltpu.make_async_copy(x_ref.at[:, mine[k]], ll.at[0:128, cols], ls.at[4 + k]))
+        local.append(pltpu.make_async_copy(xs.at[k], ll.at[128:256, cols], ls.at[6 + k]))
+    for c in local + parts:
         c.start()
     loads = load_qkv(wall, (wq, wk, wv), weights, lw)
     pl.semaphore_wait(bar, 33)
@@ -873,27 +1152,30 @@
         c.start()
     wire = Wire(ss, rs)
     near = [
-        wire(l_ref.at[:, 1536:], ll2.at[128:256, :], core),
-        wire(own.at[:, 1536:7680], rr2.at[128:256, :], core),
-        wire(zr.at[:, 7680:], ll2.at[384:512, :], core),
-        wire(zr.at[:, 1536:7680], rr2.at[384:512, :], core),
+        wire(gpay.at[:, 1024:], ll2.at[128:256, :], core),
+        wire(zpay.at[:, 1024:2048], rr2.at[128:256, :], core),
+        wire(zr.at[:, 2048:], ll2.at[384:512, :], core),
+        wire(zr.at[:, 1024:2048], rr2.at[384:512, :], core),
     ]
-    big = Sum(mid, 288, mid_refs, wire, where, xp, yp, zp).steps()
-    small = Sum(tail, 96, tail_refs, wire, where, xp, yp, zp).steps()
+    io = BegunSum(160, io_refs, wire, where, xp, yp, zp, far, *got).steps()
+    big = Sum(mid, 128, u_refs, wire, where, xp, yp, zp).steps()
+    small = PairSum(tail, 96, tail_refs, wire, where, xp, yp, zp, far).steps()
+    next(io)
+    next(io)
     for c in local:
         c.wait()
     lt = ll[...].astype(F32).T.astype(BF)
     for c in near:
         c.wait()
-    for k in range(6):
+    for k in range(4):
         lt2[256 * k:256 * k + 256, :] = ll2[:, 256 * k:256 * k + 256].astype(F32).T.astype(BF)
-    mid[0:256, :] = dot(lt2[256:512, :], rr2[:, 5120:6144]).astype(BF)
     for k in range(4):
-        mid[256 + 256 * k:512 + 256 * k, :] = dot(lt2[0:256, :], rr2[:, 1024 * k:1024 * k + 1024]).astype(BF)
-    for k in range(4):
-        rows = slice(512 + 256 * k, 768 + 256 * k)
-        mid[1280 + 256 * k:1536 + 256 * k, :] = dot(lt2[rows, :], rr2[:, 4096:5120]).astype(BF)
+        rows = slice(256 * k, 256 * k + 256)
+        mid[rows, :] = dot(lt2[rows, :], rr2[...]).astype(BF)
     next(big)
+    for c in parts:
+        c.wait()
+    next(io)
 
     for c in home:
         c.wait()
@@ -909,9 +1191,9 @@
         pay[:128, 2048 + 64 * h:2112 + 64 * h] = both[:, 64:]
     pay[128:144, :1024] = jnp.concatenate([gb[...], jnp.zeros((8, 1024), F32)], axis=0).astype(BF)
     pay[128:144, 1024:] = jnp.zeros((16, 2048), BF)
-    to_far = wire(pay, rr.at[1], far)
-    to_core = wire(pay, rr.at[0], core)
+    to_core = wire(pay, rr, core)
     next(big)
+    next(io)
     for c in loads:
         c.wait()
     for k in range(4):
@@ -920,39 +1202,47 @@
         for m in range(3):
             total += dot(pay[:128, 1024 * m:1024 * m + 1024], weights[k, m], NT)
         gt[:, cols] = total
-    to_far.wait_recv()
-    on_core = wire(rr.at[1], rr.at[2], core)
-    next(big)
     to_core.wait_recv()
-    on_core.wait_recv()
-    for m in range(3):
-        cols = slice(1024 * m, 1024 * m + 1024)
-        total = dot(lt[:, 0:128], pay[:128, cols])
-        for k in range(3):
-            total += dot(lt[:, 128 * k + 128:128 * k + 256], rr[k, :128, cols])
-        tail[256 * m:256 * m + 256, :] = total.astype(BF)
+    for z in range(2):
+        for m in range(3):
+            cols = slice(1024 * m, 1024 * m + 1024)
+            total = dot(lt[256 * z:256 * z + 256, :128], pay[:128, cols])
+            total += dot(lt[256 * z:256 * z + 256, 128:], rr[:128, cols])
+            tail[z, 256 * m:256 * m + 256, :] = total.astype(BF)
     next(small)
-    vec = pay[128:144, mine].astype(F32)
-    for k in range(3):
-        vec += rr[k, 128:144, mine].astype(F32)
-    v0[...] = vec[:8]
-    vone = [wire(v0, vx.at[s], xp[s]) for s in range(3)]
+    for z in range(2):
+        v0[z] = (pay[128:144, mine[z]].astype(F32) + rr[128:144, mine[z]].astype(F32))[:8]
+    vfar = wire(v0.at[1], vf, far)
+    next(io)
     next(big)
     next(small)
+    next(io)
+    next(big)
+    next(small)
+    vfar.wait_recv()
+    v1[...] = v0[0] + vf[...]
+    vone = [wire(v1, vx.at[s], xp[s]) for s in range(3)]
+    next(io)
+    next(big)
+    next(small)
+    next(io)
     next(big)
     next(small)
     for c in vone:
         c.wait_recv()
-    tx[...] = v0[...] + vx[0] + vx[1] + vx[2]
+    tx[...] = v1[...] + vx[0] + vx[1] + vx[2]
     vtwo = [wire(tx, vy.at[s], yp[s]) for s in range(3)]
+    next(io)
     next(big)
     next(small)
+    next(io)
     next(big)
     next(small)
     for c in vtwo:
         c.wait_recv()
     ty[...] = tx[...] + vy[0] + vy[1] + vy[2]
     vthree = wire(ty, vz, zp)
+    next(io)
     next(big)
     next(small)
     next(big)
@@ -961,33 +1251,36 @@
     next(small)
     vthree.wait()
     s_vec[...] = (ty[...] + vz[...]) * scale
-    for c in vone + vtwo + [to_far, to_core, on_core]:
+    for c in vone + vtwo + [to_core, vfar]:
         c.wait_send()
     next(small)
-    next(small)
+    next(io)
     next(big)
     next(small)
 
 
-def finish(dkvp, dqp, dr, gb, wall, own, l01, zpay, zr, xs, tok):
-    n = SUM_COPIES * 2 + 4 + 3 + 7
+def finish(dkvp, dqp, dr, gb, wall, own, gpay, zpay, zr, xs, tok, parts):
+    n = SUM_COPIES + BEGUN_COPIES + PAIR_COPIES + 4 + 2 + 7
     return pl.pallas_call(
         finish_kernel,
-        out_shape=[shp((128, 1024), F32), shp((2304, 1024), BF), shp((768, 1024), BF), shp((8, 256), F32)],
-        in_specs=[ANY, ANY, VM, VM] + [ANY] * 9,
-        out_specs=[VM] * 4,
-        scratch_shapes=sum_scratch(2304) + sum_scratch(768) + [
+        out_shape=[
+            shp((128, 1024), F32), shp((1280, 1024), BF), shp((1024, 1024), BF), shp((768, 1024), BF), shp((8, 256), F32),
+        ],
+        in_specs=[ANY, ANY, VM, VM] + [ANY] * 15,
+        out_specs=[VM] * 5,
+        scratch_shapes=pair_scratch(1280, True) + sum_scratch(1024) + pair_scratch(768, False) + [
             pltpu.VMEM((32, 128, 128), BF), pltpu.VMEM((16, 64, 128), BF), pltpu.VMEM((4, 3, 256, 1024), BF),
-            pltpu.VMEM((512, 1536), BF), pltpu.VMEM((512, 6144), BF), pltpu.VMEM((1536, 512), BF),
-            pltpu.VMEM((2304, 1024), BF), pltpu.VMEM((144, 3072), BF),
-            pltpu.VMEM((512, 256), BF), pltpu.VMEM((3, 144, 3072), BF), pltpu.VMEM((768, 1024), BF),
-            pltpu.VMEM((8, 256), F32), pltpu.VMEM((3, 8, 256), F32), pltpu.VMEM((3, 8, 256), F32),
+            pltpu.VMEM((512, 1024), BF), pltpu.VMEM((512, 1024), BF), pltpu.VMEM((1024, 512), BF),
+            pltpu.VMEM((1024, 1024), BF), pltpu.VMEM((144, 3072), BF),
+            pltpu.VMEM((256, 512), BF), pltpu.VMEM((144, 3072), BF), pltpu.VMEM((2, 768, 1024), BF),
+            pltpu.VMEM((2, 8, 256), F32), pltpu.VMEM((8, 256), F32), pltpu.VMEM((8, 256), F32),
+            pltpu.VMEM((3, 8, 256), F32), pltpu.VMEM((3, 8, 256), F32),
             pltpu.VMEM((8, 256), F32), pltpu.VMEM((8, 256), F32), pltpu.VMEM((8, 256), F32),
-            DMA((32,)), DMA((32,)), DMA((16,)), DMA((16,)), DMA((n,)), DMA((n,)), DMA((10,)), DMA((6,)),
+            DMA((32,)), DMA((32,)), DMA((16,)), DMA((16,)), DMA((n,)), DMA((n,)), DMA((16,)), DMA((6,)),
         ],
         compiler_params=pltpu.CompilerParams(collective_id=6, has_side_effects=True, vmem_limit_bytes=LIMIT),
         name="finish",
-    )(dkvp, dqp, dr, gb, wall, *own, l01, zpay, zr, xs, tok)
+    )(dkvp, dqp, dr, gb, wall, *own, gpay, zpay, zr, xs, tok, *parts)
 
 
 def scale_kernel(o, i0, i1, i2, i3, u, q, k, v, out_q, out_k, out_v, out_o, out_i, out_u):
@@ -998,7 +1291,7 @@
         out_i[:, 1024 * n:1024 * n + 1024] = src[...].astype(F32) * scale
 
 
-def scaled(mid, tail):
+def scaled(io, u, tail):
     def rows(first, n=32):
         return pl.BlockSpec((n, 1024), lambda j: (first // n + j, 0))
 
@@ -1006,11 +1299,11 @@
         scale_kernel,
         grid=(8,),
         out_shape=[shp((256, 1024), F32)] * 4 + [shp((256, 4096), F32), shp((1024, 1024), F32)],
-        in_specs=[rows(0)] + [rows(256 + 256 * k) for k in range(4)] + [rows(1280, 128)] + [rows(256 * k) for k in range(3)],
+        in_specs=[rows(0)] + [rows(256 + 256 * k) for k in range(4)] + [rows(0, 128)] + [rows(256 * k) for k in range(3)],
         out_specs=[rows(0)] * 4 + [pl.BlockSpec((32, 4096), lambda j: (j, 0)), rows(0, 128)],
         compiler_params=pltpu.CompilerParams(vmem_limit_bytes=LIMIT),
         name="scaled",
-    )(*[mid] * 6, *[tail] * 3)
+    )(*[io] * 5, u, *[tail] * 3)
 
 
 FLIP_CORE = [(0, 1), (1, 0), (2, 3), (3, 2)]
@@ -1052,16 +1345,21 @@
     d1, d2, d3, e1, e2, e3 = (lax.ppermute(p, "wsh", FLIP_CORE) for p in (x1, x2, x3, y1, y2, y3))
     diag = [diag_a, d1, d2, d3, diag_b, e1, e2, e3]
     (o_back,) = exchange(None, o, 3)
-    y_out, dr1, do, zpay, l01, gb = middle(
+    y_out, dr1, do, zpay, gpay, cpay, lown, gb = middle(
         o_back, tok, cot, lnf, lnp, ((w_output, w_inner, outer), core_shard), (far, diag)
     )
     zr = lax.ppermute(zpay, "wsh", FLIP_FAR)
-
-    (dor,) = exchange(None, do, 3)
+    dor, own_a, plus_a, minus_a, own_b, plus_b, minus_b = turn(do, cpay, lown)
+    plus_a = lax.ppermute(plus_a, "ctx", along_x(1))
+    minus_a = lax.ppermute(minus_a, "ctx", along_x(3))
+    plus_b = lax.ppermute(plus_b, "ctx", along_y(1))
+    minus_b = lax.ppermute(minus_b, "ctx", along_y(3))
     dkvp, dqp = attend_back(blk, block_mask, kvr, qr, dor, ot, lse)
-    zr, dkvp = lax.optimization_barrier((zr, dkvp))
-    grad_tok, mid, tail, s_vec = finish(dkvp, dqp, dr1, gb, wall, own, l01, zpay, zr, xs, tok)
-    s_q, s_k, s_v, s_o, s_i, s_u = scaled(mid, tail)
+    zr, plus_a, minus_a, plus_b, minus_b, dkvp = lax.optimization_barrier((zr, plus_a, minus_a, plus_b, minus_b, dkvp))
+    grad_tok, io, u, tail, s_vec = finish(
+        dkvp, dqp, dr1, gb, wall, own, gpay, zpay, zr, xs, tok, (own_a, plus_a, minus_a, own_b, plus_b, minus_b)
+    )
+    s_q, s_k, s_v, s_o, s_i, s_u = scaled(io, u, tail)
     out_shape = tokens.shape
     return (
         y_out.reshape(out_shape), grad_tok.reshape(out_shape), s_q, s_k, s_v, s_o, s_i, s_u, s_vec[0:2], s_vec[2:4],

time: 318 us -> 303 us (0.953)
  waiting for transfers between devices: 13.5 us -> 0.83 us
  Pallas kernels: 283 us -> 274 us
  starting transfers between devices: 13.2 us -> 18.4 us
    ppermute x1, waiting for transfers between devices: 12.7 us -> 0.01 us  [body(): zr = lax.ppermute(zpay, 'wsh', FLIP_FAR)]
    pallas_call x3 -> x2, Pallas kernels: 45.5 us -> 36.2 us  [exchange(): pl.pallas_call(kernel, out_shape=outs, in_specs=[ANY] * len(args), out_sp...]
    pallas_call x1 -> x2, Pallas kernels: 109 us -> 116 us  [the longest x1 105 us: finish(): pl.pallas_call(finish_kernel, out_shape=[shp((128, 1024), F32), shp((1280...]
    ppermute x0 -> x4, starting transfers between devices: none -> 6.56 us  [the longest x1 2.68 us: body(): minus_a = lax.ppermute(minus_a, 'ctx', along_x(3))]
    pallas_call x1, Pallas kernels: 28.6 us -> 24.2 us  [attend(): pl.pallas_call(attend_kernel, out_shape=[shp((16, 64, 128), BF), shp((8,...]
  transfers between devices with their start and end apart: 15 -> 19, of which waited for: 2 -> 1; matrix products, arithmetic and copies ran while one was open for 0% -> 0% of each run, Pallas kernels for 34% -> 31%
where the time goes in v4:
time: 303 us
  Pallas kernels  274 us (90%)
  starting transfers between devices  18.4 us (6%)
  local copies, waits for them, and re-layouts  6.43 us (2%)
    pallas_call x1, Pallas kernels, finish(): pl.pallas_call(finish_kernel, out_shape=[shp((128, 1024), F32), shp((1280...  105 us
    pallas_call x2, Pallas kernels, exchange(): pl.pallas_call(kernel, out_shape=outs, in_specs=[ANY] * len(args), out_sp...  36.2 us
    pallas_call x1, Pallas kernels, gather_weights(): pl.pallas_call(gather_kernel, out_shape=[shp((4, 3, 256, 1024), BF), shp(...  35.3 us
    pallas_call x1, Pallas kernels, attend_back(): pl.pallas_call(attend_back_kernel, out_shape=[shp((32, 128, 128), BF), sh...  27.6 us
    pallas_call x1, Pallas kernels, attend(): pl.pallas_call(attend_kernel, out_shape=[shp((16, 64, 128), BF), shp((8,...  24.2 us
    pallas_call x1, Pallas kernels, middle(): pl.pallas_call(middle_kernel, out_shape=[shp((128, 1024), F32), shp((128,...  19.8 us
    pallas_call x1, Pallas kernels, turn(): pl.pallas_call(turn_kernel, out_shape=[shp(do.shape, BF)] + [shp((2, 160,...  11.5 us
    pallas_call x1, Pallas kernels, scaled(): pl.pallas_call(scale_kernel, grid=(8,), out_shape=[shp((256, 1024), F32)]...  8.42 us
  transfers between devices with their start and end apart: 19, of which 1 were waited for; matrix products, arithmetic and copies ran while one was open for 0% of the time, Pallas kernels for 31%

profile of v4, /device:TPU:0, one launch (start us, length us, event | category | flops | bytes accessed | tf_op | source)
XLA Modules:
  0.0 302.5 jit_solution(11897127918538177817)
XLA Ops:
  0.7 1.4 maximum_maximum_fusion.ln_ref.refs_4_
  2.1 35.3 %gather_qkv.1 = (bf16[4,3,256,1024]{3,2,1,0:T(8,128)(2,1)}, bf16[2,128,256]{2,1,0:T(8,128)(2,1)}, f32[4,8,256]{2,1,0:T(8,128)}, bf16[256,1024]{1,0:T(8,128)(2,1)...) custom-call(bf16[256,1024]{1,0:T(8,128)(2,1)} %refs_5_.3, ...), custom_call_target="tpu_custom_call" | custom-call | tf_op jit(solution)/shard_map/gather_qkv/pallas_call | solution.py:135
  37.4 1.4 collective-permute-start
  39.0 2.3 collective-permute-start.1
  41.2 6.6 %qkv.1 = (bf16[16,128,128]{2,1,0:T(8,128)(2,1)}, bf16[16,64,128]{2,1,0:T(8,128)(2,1)}) custom-call(bf16[128,1024]{1,0:T(8,128)(2,1)} %bitcast.6, bf16[4,3,256,1024]{3,2,1,0:T(8,128)(2,1)} %get-tuple-element.81.wall.refs_4_, bf16[256,1024]{1,0:T(8,128)(2,1)} %refs_5_.3, bf16[256,1024]{1,0:T(8,128)(2,1)} %refs_6_.3, bf16[256,1024]{1,0:T(8,128)(2,1)} %refs_7_.1), custom_call_target="tpu_custom_call" | custom-call | flops 805306368 | bytes 8388608 | tf_op jit(solution)/shard_map/qkv/pallas_call | solution.py:188
  47.9 25.2 %exchange_2.1 = (bf16[32,128,128]{2,1,0:T(8,128)(2,1)}, bf16[16,64,128]{2,1,0:T(8,128)(2,1)}) custom-call(bf16[16,128,128]{2,1,0:T(8,128)(2,1)} %get-tuple-element.82.refs_0_, bf16[16,64,128]{2,1,0:T(8,128)(2,1)} %get-tuple-element.83.refs_1_), custom_call_target="tpu_custom_call" | custom-call | flops 17179869184 | bytes 33554432 | tf_op jit(solution)/shard_map/exchange_2/pallas_call | solution.py:271
  73.2 0.6 reshape.40.blk
  73.9 1.3 collective-permute-start.5
  75.1 0.8 collective-permute-start.4
  76.0 2.6 collective-permute-start.7
  78.5 24.2 %attend.1 = (bf16[16,64,128]{2,1,0:T(8,128)(2,1)}, f32[8,64,256]{2,1,0:T(8,128)}, f32[8,1,256]{2,1,0:T(1,128)}) custom-call(s32[64]{0:T(128)} %reshape.40.blk, s32[1,64,64]{2,1,0:T(8,128)} %mask.3, bf16[32,128,128]{2,1,0:T(8,128)(2,1)} %get-tuple-element.89.kvr, bf16[16,64,128]{2,1,0:T(8,128)(2,1)} %get-tuple-element.90.qr), custom_call_target="tpu_custom_call" | custom-call | flops 10737418240 | bytes 33554432 | tf_op jit(solution)/shard_map/attend/pallas_call | solution.py:403
  102.9 0.5 collective-permute-start.9
  103.6 0.5 collective-permute-start.11
  104.1 0.8 collective-permute-done.8.refs_20_
  105.0 11.0 %exchange_3.1.refs_0_ = bf16[16,64,128]{2,1,0:T(8,128)(2,1)} custom-call(bf16[16,64,128]{2,1,0:T(8,128)(2,1)} %get-tuple-element.92.refs_0_), custom_call_target="tpu_custom_call" | custom-call | flops 17179869184 | bytes 33554432 | tf_op jit(solution)/shard_map/exchange_3/pallas_call | solution.py:271
  116.1 0.8 copy-done.15
  117.3 19.8 %middle.1 = (f32[128,1024]{1,0:T(8,128)}, f32[128,1024]{1,0:T(8,128)}, bf16[16,64,128]{2,1,0:T(8,128)(2,1)}, bf16[128,3072]{1,0:T(8,128)(2,1)}, bf16[128,2048]{1...) custom-call(bf16[16,64,128]{2,1,0:T(8,128)(2,1)} %exchange_3.1.refs_0_, ...), custom_call_target="tpu_custom_call" | custom-call | flops 10737418240 | bytes 33554432 | tf_op jit(solution)/shard_map/middle/pallas_call | solution.py:620
  137.2 11.5 %turn.1 = (bf16[16,64,128]{2,1,0:T(8,128)(2,1)}, bf16[2,160,1024]{2,1,0:T(8,128)(2,1)}, bf16[2,240,1024]{2,1,0:T(8,128)(2,1)}, bf16[2,240,1024]{2,1,0:T(8,128)(2...) custom-call(bf16[16,64,128]{2,1,0:T(8,128)(2,1)} %get-tuple-element.107.do, ...), custom_call_target="tpu_custom_call" | custom-call | flops 17179869184 | bytes 33554432 | tf_op jit(solution)/shard_map/turn/pallas_call | solution.py:716
  148.6 0.6 collective-permute-start.15
  149.3 2.7 collective-permute-start.16
  152.0 0.9 collective-permute-start.17
  152.8 2.4 collective-permute-start.18
  155.2 2.1 collective-permute-start.14
  157.3 27.6 %attend_back.1 = (bf16[32,128,128]{2,1,0:T(8,128)(2,1)}, bf16[16,64,128]{2,1,0:T(8,128)(2,1)}) custom-call(s32[64]{0:T(128)} %reshape.40.blk, s32[1,64,64]{2,1,0:T(8,128)} %mask.3, bf16[32,128,128]{2,1,0:T(8,128)(2,1)} %get-tuple-element.89.kvr, bf16[16,64,128]{2,1,0:T(8,128)(2,1)} %get-tuple-element.90.qr, bf16[16,64,128]{2,1,0:T(8,128)(2,1)} %get-tuple-element.114.dor, ...), custom_call_target="tpu_custom_call" | custom-call | flops 1073741824 | bytes 4194304 | tf_op jit(solution)/shard_map/attend_back/pallas_call | solution.py:488
  185.1 0.8 copy-done.5
  186.2 0.3 copy-done.1
  186.5 0.3 copy-done.2
  186.8 0.3 copy-done.3
  187.2 104.8 %finish.1 = (f32[128,1024]{1,0:T(8,128)}, bf16[1280,1024]{1,0:T(8,128)(2,1)}, bf16[1024,1024]{1,0:T(8,128)(2,1)}, bf16[768,1024]{1,0:T(8,128)(2,1)}, f32[8,256]{1,0:T(8,128)}) custom-call(bf16[32,128,128]{2,1,0:T(8,128)(2,1)} %get-tuple-element.118.refs_0_, bf16[16,64,128]{2,1,0:T(8,128)(2,1)} %get-tuple-element.119.refs_1_, ...), custom_call_target="tpu_custom_call" | custom-call | tf_op jit(solution)/shard_map/finish/pallas_call | solution.py:1264
  292.0 1.4 fusion
  293.3 8.4 %scaled.1 = (f32[256,1024]{1,0:T(8,128)}, f32[256,1024]{1,0:T(8,128)}, f32[256,1024]{1,0:T(8,128)}, f32[256,1024]{1,0:T(8,128)}, f32[256,4096]{1,0:T(8,128)}, /*index=5*/f32[1024,1024]{1,0:T(8,128)}) custom-call(bf16[1280,1024]{1,0:T(8,128)(2,1)} %get-tuple-element.132.o.i0.i1.i2.i3, bf16[1280,1024]{1,0:T(8,128)(2,1)} %get-tuple-element.132.o.i0.i1.i2.i3, ...), custom_call_target="tpu_custom_call" | custom-call | tf_op jit(solution)/shard_map/scaled/pallas_call | solution.py:1298
  301.7 0.8 copy.25
  (59 shorter events, 1.6 us)
Async XLA Ops:
  37.3 36.5 %collective-permute-start.2 = (bf16[9,32,1024]{2,1,0:T(8,128)(2,1)}, bf16[9,32,1024]{2,1,0:T(8,128)(2,1)S(1)}, u32[]{:S(2)}, u32[]{:S(2)}) collective-permute-start(bf16[9,32,1024]{2,1,0:T(8,128)(2,1)} %get-tuple-element.85.refs_11_), channel_id=1, source_target_pairs={{0,1},{1,0},{2,3},{3,2},{4,5},{5,4},{6,7},{7,6},{8,9},{9,8},{10,11... | collective-permute-start | bytes 1769480 | tf_op jit(solution)/shard_map/ppermute | solution.py:1334
  37.4 36.4 %collective-permute-start = (bf16[9,32,1024]{2,1,0:T(8,128)(2,1)}, bf16[9,32,1024]{2,1,0:T(8,128)(2,1)S(1)}, u32[]{:S(2)}, u32[]{:S(2)}) collective-permute-start(bf16[9,32,1024]{2,1,0:T(8,128)(2,1)} %get-tuple-element.85.refs_11_), channel_id=1, source_target_pairs={{0,32},{4,36},{8,40},{12,44},{16,48},{20,52},{24,56},{28,60},{32,0... | collective-permute-start | bytes 1769480 | tf_op jit(solution)/shard_map/ppermute | solution.py:1332
  38.8 35.0 %collective-permute-start.3 = (bf16[9,32,1024]{2,1,0:T(8,128)(2,1)}, bf16[9,32,1024]{2,1,0:T(8,128)(2,1)S(1)}, u32[]{:S(2)}, u32[]{:S(2)}) collective-permute-start(bf16[9,32,1024]{2,1,0:T(8,128)(2,1)} %get-tuple-element.87.refs_15_), channel_id=1, source_target_pairs={{0,1},{1,0},{2,3},{3,2},{4,5},{5,4},{6,7},{7,6},{8,9},{9,8},{10,11... | collective-permute-start | bytes 1769480 | tf_op jit(solution)/shard_map/ppermute | solution.py:1335
  39.0 34.9 %collective-permute-start.1 = (bf16[9,32,1024]{2,1,0:T(8,128)(2,1)}, bf16[9,32,1024]{2,1,0:T(8,128)(2,1)}, u32[]{:S(2)}, u32[]{:S(2)}) collective-permute-start(bf16[9,32,1024]{2,1,0:T(8,128)(2,1)} %get-tuple-element.87.refs_15_), channel_id=1, source_target_pairs={{0,8},{4,12},{8,0},{12,4},{16,24},{20,28},{24,16},{28,20},{32,40},... | collective-permute-start | bytes 1769480 | tf_op jit(solution)/shard_map/ppermute | solution.py:1333
  47.8 25.3 %copy-start.7 = (s32[32,2]{0,1:T(2,128)S(1)}, s32[32,2]{0,1:T(2,128)}, u32[]{:S(2)}) copy-start(s32[32,2]{0,1:T(2,128)} %param.22) | copy-start | bytes 772
  47.8 26.0 %copy-start.8 = (bf16[9,32,1024]{2,1,0:T(8,128)(2,1)S(1)}, bf16[9,32,1024]{2,1,0:T(8,128)(2,1)}, u32[]{:S(2)}) copy-start(bf16[9,32,1024]{2,1,0:T(8,128)(2,1)} %get-tuple-element.85.refs_11_) | copy-start | bytes 1769476
  47.8 28.1 %copy-start.9 = (bf16[9,32,1024]{2,1,0:T(8,128)(2,1)S(1)}, bf16[9,32,1024]{2,1,0:T(8,128)(2,1)}, u32[]{:S(2)}) copy-start(bf16[9,32,1024]{2,1,0:T(8,128)(2,1)} %get-tuple-element.87.refs_15_) | copy-start | bytes 1769476
  73.8 28.9 %copy-start.10 = (bf16[9,32,1024]{2,1,0:T(8,128)(2,1)}, bf16[9,32,1024]{2,1,0:T(8,128)(2,1)S(1)}, u32[]{:S(2)}) copy-start(bf16[9,32,1024]{2,1,0:T(8,128)(2,1)S(1)} %collective-permute-done.2.refs_19_) | copy-start | bytes 1769476
  73.8 29.1 %copy-start.11 = (bf16[9,32,1024]{2,1,0:T(8,128)(2,1)}, bf16[9,32,1024]{2,1,0:T(8,128)(2,1)S(1)}, u32[]{:S(2)}) copy-start(bf16[9,32,1024]{2,1,0:T(8,128)(2,1)S(1)} %collective-permute-done.refs_13_) | copy-start | bytes 1769476
  73.8 28.9 %copy-start.12 = (bf16[9,32,1024]{2,1,0:T(8,128)(2,1)}, bf16[9,32,1024]{2,1,0:T(8,128)(2,1)S(1)}, u32[]{:S(2)}) copy-start(bf16[9,32,1024]{2,1,0:T(8,128)(2,1)S(1)} %collective-permute-done.3.refs_23_) | copy-start | bytes 1769476
  73.9 28.9 %collective-permute-start.5 = (bf16[9,32,1024]{2,1,0:T(8,128)(2,1)S(1)}, bf16[9,32,1024]{2,1,0:T(8,128)(2,1)}, u32[]{:S(2)}, u32[]{:S(2)}) collective-permute-start(bf16[9,32,1024]{2,1,0:T(8,128)(2,1)S(1)} %copy-done.8), channel_id=1, source_target_pairs={{0,48},{4,52},{8,56},{12,60},{16,0},{20,4},{24,8},{28,12},{32,16},... | collective-permute-start | bytes 1769480 | tf_op jit(solution)/shard_map/ppermute | solution.py:1340
  75.1 27.6 %collective-permute-start.4 = (bf16[9,32,1024]{2,1,0:T(8,128)(2,1)S(1)}, bf16[9,32,1024]{2,1,0:T(8,128)(2,1)S(1)}, u32[]{:S(2)}, u32[]{:S(2)}) collective-permute-start(bf16[9,32,1024]{2,1,0:T(8,128)(2,1)S(1)} %copy-done.8), channel_id=1, source_target_pairs={{0,16},{4,20},{8,24},{12,28},{16,32},{20,36},{24,40},{28,44},{32,4... | collective-permute-start | bytes 1769480 | tf_op jit(solution)/shard_map/ppermute | solution.py:1340
  76.0 26.8 %collective-permute-start.7 = (bf16[9,32,1024]{2,1,0:T(8,128)(2,1)S(1)}, bf16[9,32,1024]{2,1,0:T(8,128)(2,1)}, u32[]{:S(2)}, u32[]{:S(2)}) collective-permute-start(bf16[9,32,1024]{2,1,0:T(8,128)(2,1)S(1)} %copy-done.9), channel_id=1, source_target_pairs={{0,12},{4,0},{8,4},{12,8},{16,28},{20,16},{24,20},{28,24},{32,44},... | collective-permute-start | bytes 1769480 | tf_op jit(solution)/shard_map/ppermute | solution.py:1341
  78.5 24.3 %collective-permute-start.6 = (bf16[9,32,1024]{2,1,0:T(8,128)(2,1)S(1)}, bf16[9,32,1024]{2,1,0:T(8,128)(2,1)}, u32[]{:S(2)}, u32[]{:S(2)}) collective-permute-start(bf16[9,32,1024]{2,1,0:T(8,128)(2,1)S(1)} %copy-done.9), channel_id=1, source_target_pairs={{0,4},{4,8},{8,12},{12,0},{16,20},{20,24},{24,28},{28,16},{32,36},... | collective-permute-start | bytes 1769480 | tf_op jit(solution)/shard_map/ppermute | solution.py:1341
  102.8 2.1 collective-permute-start.8
  102.9 13.1 %collective-permute-start.9 = (bf16[9,32,1024]{2,1,0:T(8,128)(2,1)S(1)}, bf16[9,32,1024]{2,1,0:T(8,128)(2,1)S(1)}, u32[]{:S(2)}, u32[]{:S(2)}) collective-permute-start(bf16[9,32,1024]{2,1,0:T(8,128)(2,1)S(1)} %collective-permute-done.refs_13_), channel_id=1, source_target_pairs={{0,1},{1,0},{2,3},{3,2},{4,5},{5,4},{6,7},{7,6},{8,9},{9,8},{10,11... | collective-permute-start | bytes 1769480 | tf_op jit(solution)/shard_map/ppermute | solution.py:1345
  103.6 12.5 %collective-permute-start.10 = (bf16[9,32,1024]{2,1,0:T(8,128)(2,1)}, bf16[9,32,1024]{2,1,0:T(8,128)(2,1)S(1)}, u32[]{:S(2)}, u32[]{:S(2)}) collective-permute-start(bf16[9,32,1024]{2,1,0:T(8,128)(2,1)} %collective-permute-done.5.refs_14_), channel_id=1, source_target_pairs={{0,1},{1,0},{2,3},{3,2},{4,5},{5,4},{6,7},{7,6},{8,9},{9,8},{10,11... | collective-permute-start | bytes 1769480 | tf_op jit(solution)/shard_map/ppermute | solution.py:1345
  103.6 12.5 %collective-permute-start.11 = (bf16[9,32,1024]{2,1,0:T(8,128)(2,1)}, bf16[9,32,1024]{2,1,0:T(8,128)(2,1)S(1)}, u32[]{:S(2)}, u32[]{:S(2)}) collective-permute-start(bf16[9,32,1024]{2,1,0:T(8,128)(2,1)} %collective-permute-done.6.refs_16_), channel_id=1, source_target_pairs={{0,1},{1,0},{2,3},{3,2},{4,5},{5,4},{6,7},{7,6},{8,9},{9,8},{10,11... | collective-permute-start | bytes 1769480 | tf_op jit(solution)/shard_map/ppermute | solution.py:1345
  104.1 12.0 %collective-permute-start.12 = (bf16[9,32,1024]{2,1,0:T(8,128)(2,1)}, bf16[9,32,1024]{2,1,0:T(8,128)(2,1)}, u32[]{:S(2)}, u32[]{:S(2)}) collective-permute-start(bf16[9,32,1024]{2,1,0:T(8,128)(2,1)} %collective-permute-done.1.refs_17_), channel_id=1, source_target_pairs={{0,1},{1,0},{2,3},{3,2},{4,5},{5,4},{6,7},{7,6},{8,9},{9,8},{10,11... | collective-permute-start | bytes 1769480 | tf_op jit(solution)/shard_map/ppermute | solution.py:1345
  104.9 11.2 %copy-start.14 = (bf16[9,32,1024]{2,1,0:T(8,128)(2,1)}, bf16[9,32,1024]{2,1,0:T(8,128)(2,1)S(1)}, u32[]{:S(2)}) copy-start(bf16[9,32,1024]{2,1,0:T(8,128)(2,1)S(1)} %collective-permute-done.8.refs_20_) | copy-start | bytes 1769476
  104.9 11.2 %collective-permute-start.13 = (bf16[9,32,1024]{2,1,0:T(8,128)(2,1)}, bf16[9,32,1024]{2,1,0:T(8,128)(2,1)}, u32[]{:S(2)}, u32[]{:S(2)}) collective-permute-start(bf16[9,32,1024]{2,1,0:T(8,128)(2,1)} %collective-permute-done.7.refs_18_), channel_id=1, source_target_pairs={{0,1},{1,0},{2,3},{3,2},{4,5},{5,4},{6,7},{7,6},{8,9},{9,8},{10,11... | collective-permute-start | bytes 1769480 | tf_op jit(solution)/shard_map/ppermute | solution.py:1345
  137.1 18.1 %copy-start.4 = (bf16[128,3072]{1,0:T(8,128)(2,1)S(1)}, bf16[128,3072]{1,0:T(8,128)(2,1)}, u32[]{:S(2)}) copy-start(bf16[128,3072]{1,0:T(8,128)(2,1)} %get-tuple-element.106.refs_9_) | copy-start | bytes 2359300
  148.6 36.3 %collective-permute-start.15 = (bf16[2,240,1024]{2,1,0:T(8,128)(2,1)}, bf16[2,240,1024]{2,1,0:T(8,128)(2,1)S(1)}, u32[]{:S(2)}, u32[]{:S(2)}) collective-permute-start(bf16[2,240,1024]{2,1,0:T(8,128)(2,1)} %get-tuple-element.110), channel_id=1, source_target_pairs={{0,16},{4,20},{8,24},{12,28},{16,32},{20,36},{24,40},{28,44},{32,4... | collective-permute-start | bytes 2949128 | tf_op jit(solution)/shard_map/ppermute | solution.py:1353
  149.3 35.7 %collective-permute-start.16 = (bf16[2,240,1024]{2,1,0:T(8,128)(2,1)}, bf16[2,240,1024]{2,1,0:T(8,128)(2,1)S(1)}, u32[]{:S(2)}, u32[]{:S(2)}) collective-permute-start(bf16[2,240,1024]{2,1,0:T(8,128)(2,1)} %get-tuple-element.111), channel_id=1, source_target_pairs={{0,48},{4,52},{8,56},{12,60},{16,0},{20,4},{24,8},{28,12},{32,16},... | collective-permute-start | bytes 2949128 | tf_op jit(solution)/shard_map/ppermute | solution.py:1354
  152.0 33.1 %collective-permute-start.17 = (bf16[2,240,1024]{2,1,0:T(8,128)(2,1)}, bf16[2,240,1024]{2,1,0:T(8,128)(2,1)S(1)}, u32[]{:S(2)}, u32[]{:S(2)}) collective-permute-start(bf16[2,240,1024]{2,1,0:T(8,128)(2,1)} %get-tuple-element.112), channel_id=1, source_target_pairs={{0,4},{4,8},{8,12},{12,0},{16,20},{20,24},{24,28},{28,16},{32,36},... | collective-permute-start | bytes 2949128 | tf_op jit(solution)/shard_map/ppermute | solution.py:1355
  152.8 32.2 %collective-permute-start.18 = (bf16[2,240,1024]{2,1,0:T(8,128)(2,1)}, bf16[2,240,1024]{2,1,0:T(8,128)(2,1)S(1)}, u32[]{:S(2)}, u32[]{:S(2)}) collective-permute-start(bf16[2,240,1024]{2,1,0:T(8,128)(2,1)} %get-tuple-element.113), channel_id=1, source_target_pairs={{0,12},{4,0},{8,4},{12,8},{16,28},{20,16},{24,20},{28,24},{32,44},... | collective-permute-start | bytes 2949128 | tf_op jit(solution)/shard_map/ppermute | solution.py:1356
  155.2 29.8 %collective-permute-start.14 = (bf16[128,3072]{1,0:T(8,128)(2,1)S(1)}, bf16[128,3072]{1,0:T(8,128)(2,1)S(1)}, u32[]{:S(2)}, u32[]{:S(2)}) collective-permute-start(bf16[128,3072]{1,0:T(8,128)(2,1)S(1)} %copy-done.4), channel_id=1, source_target_pairs={{0,2},{2,0},{1,3},{3,1},{4,6},{6,4},{5,7},{7,5},{8,10},{10,8},{9,1... | collective-permute-start | bytes 2359304 | tf_op jit(solution)/shard_map/ppermute | solution.py:1351
  185.0 1.2 copy-start
  185.0 1.5 copy-start.1
  185.0 1.8 copy-start.2
  185.1 2.1 copy-start.3
  293.3 8.4 %copy-start.6 = (f32[128,1024]{1,0:T(8,128)S(1)}, f32[128,1024]{1,0:T(8,128)}, u32[]{:S(2)}) copy-start(f32[128,1024]{1,0:T(8,128)} %get-tuple-element.131) | copy-start | bytes 1572868
  (5 other events, 4.7 us)

commit v5 on v4

--- a/solution.py
+++ b/solution.py
@@ -64,31 +64,43 @@
         return copy
 
 
-def gather_kernel(wq, wk, wv, x_ref, ln_ref, wo, wi, wu, wall, xs, lnf, co_ref, ci_ref, cu_ref, qa_ref, qb_ref, ss, rs):
+def front_kernel(*refs):
+    x_ref, wq, wk, wv, x_any, ln_ref, wo, wi, wu = refs[:9]
+    wall, xs, lnf, co_ref, ci_ref, cu_ref, qa_ref, qb_ref, x2_ref, y2_ref, da_ref, db_ref, kvr, qr = refs[9:23]
+    weights, acc, kvp, qp, ss, rs, sw, rw, sf, rf, sn, rn, ls = refs[23:]
     zl, x, y, zh, co = place()
     me = zh * 2 + co
-    other = (1 - zh) * 2 + co
+    slots = [me, zh * 2 + 1 - co, (1 - zh) * 2 + co, (1 - zh) * 2 + 1 - co]
+    here = lax.axis_index("ctx")
+    flat = here % 16
     core = device(zl, x, y, zh, 1 - co)
     far = device(zl, x, y, 1 - zh, co)
     diag = device(zl, x, y, 1 - zh, 1 - co)
+    zp = device(1 - zl, x, y, zh, co)
     xp = [device(zl, (x + s) % 4, y, zh, co) for s in (1, 2, 3)]
     yp = [device(zl, x, (y + s) % 4, zh, co) for s in (1, 2, 3)]
-    greet([core, far, diag] + xp + yp)
+    bar = pltpu.get_barrier_semaphore()
+
+    def greet_one(i, carry):
+        pl.semaphore_signal(bar, inc=1, device_id={"ctx": zl * 16 + (flat + i) % 16}, device_id_type=MESH)
+        return carry
+
+    for p in (far, core, diag, zp):
+        pl.semaphore_signal(bar, inc=1, device_id=p, device_id_type=MESH)
+    lax.fori_loop(1, 16, greet_one, 0)
+    ws = (wq, wk, wv)
+    local = [pltpu.make_async_copy(ws[m], weights.at[me, m], ls.at[m]) for m in range(3)]
+    for c in local:
+        c.start()
+    pl.semaphore_wait(bar, 19)
     wire = Wire(ss, rs)
-    ws = (wq, wk, wv)
     rows_a = pl.ds(pl.multiple_of(x * 32, 32), 32)
     rows_b = pl.ds(pl.multiple_of(128 + y * 32, 32), 32)
     first_a, first_b = [], []
     for m in range(3):
-        first_a.append(wire(ws[m].at[rows_a], wall.at[me, m, rows_a], far))
-        first_b.append(wire(ws[m].at[rows_b], wall.at[me, m, rows_b], far))
-    rest = []
-    for m in range(3):
-        rest.append(wire(ws[m], wall.at[me, m], core))
-    for p in (core, far, diag):
-        rest.append(wire(ln_ref, lnf.at[me], p))
-    for n, idx in enumerate((zh * 2 + 1 - co, (1 - zh) * 2 + 1 - co)):
-        rest.append(wire(x_ref.at[:, pl.ds(pl.multiple_of(idx * 256, 256), 256)], xs.at[n], core))
+        first_a.append(wire(ws[m].at[rows_a], weights.at[me, m, rows_a], far))
+        first_b.append(wire(ws[m].at[rows_b], weights.at[me, m, rows_b], far))
+    near = [wire(ws[m], weights.at[me, m], core) for m in range(3)]
     quarters = []
     for ref, k, n in ((qa_ref, x, y), (qb_ref, 4 + y, x)):
         rows = pl.ds(pl.multiple_of(k * 32, 32), 32)
@@ -98,103 +110,149 @@
             at = pl.ds(pl.multiple_of(1024 * b + n * 256, 256), 256)
             quarters.append(wire(wi.at[rows, at], ref.at[1 + b, :, cols], far))
         quarters.append(wire(wu.at[k, :, :, cols], ref.at[5:9, :, cols], far))
+    rest = []
+    for p in (core, far, diag):
+        rest.append(wire(ln_ref, lnf.at[me], p))
+    for n, idx in enumerate((slots[1], slots[3])):
+        rest.append(wire(x_any.at[:, pl.ds(pl.multiple_of(idx * 256, 256), 256)], xs.at[n], core))
+
+    def add(k, fresh):
+        cols = x_ref[:, pl.ds(pl.multiple_of(slots[k] * 256, 256), 256)]
+        for m in range(3):
+            part = dot(cols, weights[slots[k], m])
+            acc[m] = part if fresh else acc[m] + part
+
     for c in first_a:
         c.wait_recv()
     second = []
     for m in range(3):
-        part = wall.at[other, m, rows_a]
+        part = weights.at[slots[2], m, rows_a]
         for p in xp:
             second.append(wire(part, part, p))
     for c in first_b:
         c.wait_recv()
     for m in range(3):
-        part = wall.at[other, m, rows_b]
+        part = weights.at[slots[2], m, rows_b]
         for p in yp:
             second.append(wire(part, part, p))
-    for src, dst in ((wo, co_ref), (wi, ci_ref), (wu, cu_ref)):
-        rest.append(wire(src, dst, core))
+    for c in local:
+        c.wait()
+    add(0, True)
+    for c in near:
+        c.wait_recv()
+    add(1, False)
+    for c in second:
+        c.wait_recv()
+    last = [wire(weights.at[slots[2], m], weights.at[slots[2], m], core) for m in range(3)]
+    add(2, False)
+    for c in last:
+        c.wait_recv()
+    add(3, False)
+    keep = pltpu.make_async_copy(weights, wall, ls.at[0])
+    keep.start()
+    for j in range(8):
+        lanes = slice(128 * j, 128 * j + 128)
+        q = (acc[0, :, lanes].astype(BF).astype(F32) * 0.125).astype(BF)
+        k = acc[1, :, lanes].astype(BF)
+        v = acc[2, :, lanes].astype(BF)
+        for u in range(2):
+            part = slice(64 * u, 64 * u + 64)
+            kvp[2 * j + u] = jnp.concatenate([k[:, part], v[:, part]], axis=1)
+            qp[2 * j + u] = jnp.concatenate([q[:64, part], q[64:, part]], axis=1)
+
+    def plane(i):
+        return {"ctx": zl * 16 + (flat + i) % 16}
+
+    def wide_copy(i):
+        return pltpu.make_async_remote_copy(
+            src_ref=kvp.at[(flat + i) % 16], dst_ref=kvr.at[here], send_sem=sw.at[i], recv_sem=rw.at[i],
+            device_id=plane(i), device_id_type=MESH,
+        )
+
+    def narrow_copy(i):
+        return pltpu.make_async_remote_copy(
+            src_ref=qp.at[(flat + i) % 16], dst_ref=qr.at[flat], send_sem=sn.at[i], recv_sem=rn.at[i],
+            device_id=plane(i), device_id_type=MESH,
+        )
+
+    def pass_copy(i):
+        spot = kvr.at[zl * 16 + (flat + 16 - i) % 16]
+        return pltpu.make_async_remote_copy(
+            src_ref=spot, dst_ref=spot, send_sem=sf.at[i], recv_sem=rf.at[i], device_id=zp, device_id_type=MESH,
+        )
+
+    def start_wide(i, carry):
+        wide_copy(i).start()
+        return carry
+
+    def start_narrow(i, carry):
+        narrow_copy(i).start()
+        return carry
+
+    def pass_on(i, carry):
+        wide_copy(i).wait_recv()
+        pass_copy(i).start()
+        return carry
+
+    def wait_all(i, carry):
+        wide_copy(i).wait_send()
+        narrow_copy(i).wait()
+        pass_copy(i).wait()
+        return carry
+
+    to_z = wire(kvp.at[flat], kvr.at[here], zp)
+    lax.fori_loop(1, 16, start_wide, 0)
+    lax.fori_loop(1, 16, start_narrow, 0)
+    home = [
+        pltpu.make_async_copy(kvp.at[flat], kvr.at[here], ls.at[1]),
+        pltpu.make_async_copy(qp.at[flat], qr.at[flat], ls.at[2]),
+    ]
+    for c in home:
+        c.start()
     for c in quarters:
         c.wait_recv()
+    subs = []
     for ref, n, peers in ((qa_ref, y, yp), (qb_ref, x, xp)):
         spot = ref.at[:, :, pl.ds(pl.multiple_of(n * 256, 256), 256)]
         for p in peers:
-            rest.append(wire(spot, spot, p))
-    for c in second:
+            subs.append(wire(spot, spot, p))
+    for src, dst in ((wo, co_ref), (wi, ci_ref), (wu, cu_ref)):
+        rest.append(wire(src, dst, core))
+    lax.fori_loop(1, 16, pass_on, 0)
+    for c in subs:
         c.wait_recv()
-    last = [wire(wall.at[other, m], wall.at[other, m], core) for m in range(3)]
-    for c in last:
+    for src, dst, p in ((qa_ref, x2_ref, xp[1]), (qb_ref, y2_ref, yp[1]), (qa_ref, da_ref, core), (qb_ref, db_ref, core)):
+        rest.append(wire(src, dst, p))
+    for c in home:
         c.wait()
-    for c in first_a + first_b + second + quarters:
+    keep.wait()
+    lax.fori_loop(1, 16, wait_all, 0)
+    to_z.wait()
+    for c in first_a + first_b + near + second + last + quarters + subs:
         c.wait_send()
     for c in rest:
         c.wait()
 
 
-def gather_weights(wq, wk, wv, tok, lnp, wo, wi, wu):
-    n = 6 + 3 + 5 + 12 + 18 + 3 + 6 + 3
+def front(tok, own, lnp, wo, wi, wu):
+    n = 6 + 3 + 12 + 3 + 2 + 18 + 3 + 1 + 6 + 3 + 4
+    piece = shp((9, 32, 1024), BF)
     return pl.pallas_call(
-        gather_kernel,
-        out_shape=[
-            shp((4, 3, 256, 1024), BF), shp((2, 128, 256), BF), shp((4, 8, 256), F32),
-            shp(wo.shape, BF), shp(wi.shape, BF), shp(wu.shape, BF), shp((9, 32, 1024), BF), shp((9, 32, 1024), BF),
+        front_kernel,
+        out_shape=[shp((4, 3, 256, 1024), BF), shp((2, 128, 256), BF), shp((4, 8, 256), F32)]
+        + [shp(wo.shape, BF), shp(wi.shape, BF), shp(wu.shape, BF)] + [piece] * 6
+        + [shp((32, 128, 128), BF), shp((16, 64, 128), BF)],
+        in_specs=[VM] + [ANY] * 8,
+        out_specs=[ANY] * 14,
+        scratch_shapes=[
+            pltpu.VMEM((4, 3, 256, 1024), BF), pltpu.VMEM((3, 128, 1024), F32),
+            pltpu.VMEM((16, 128, 128), BF), pltpu.VMEM((16, 64, 128), BF),
+            DMA((n,)), DMA((n,)), DMA((16,)), DMA((16,)), DMA((16,)), DMA((16,)), DMA((16,)), DMA((16,)), DMA((3,)),
         ],
-        in_specs=[ANY] * 8,
-        out_specs=[ANY] * 8,
-        scratch_shapes=[DMA((n,)), DMA((n,))],
-        compiler_params=pltpu.CompilerParams(collective_id=1, has_side_effects=True),
-        name="gather_qkv",
-    )(wq, wk, wv, tok, lnp, wo, wi, wu)
-
-
-def load_qkv(wall, own, weights, sem):
-    w = lax.axis_index("wsh")
-    copies = [
-        pltpu.make_async_copy(own[m], weights.at[w, m], sem.at[m]) for m in range(3)
-    ]
-    for r in range(1, 4):
-        k = (w + r) % 4
-        copies.append(pltpu.make_async_copy(wall.at[k], weights.at[k], sem.at[2 + r]))
-    for c in copies:
-        c.start()
-    return copies
-
-
-def qkv_kernel(x_ref, wall, wq, wk, wv, kv_ref, q_ref, weights, sem):
-    for c in load_qkv(wall, (wq, wk, wv), weights, sem):
-        c.wait()
-
-    def block(j, carry):
-        lanes = pl.ds(pl.multiple_of(j * 256, 256), 256)
-
-        def proj(m):
-            total = dot(x_ref[:, :256], weights[0, m, :, lanes])
-            for k in range(1, 4):
-                total += dot(x_ref[:, 256 * k:256 * k + 256], weights[k, m, :, lanes])
-            return total.astype(BF)
-
-        q = (proj(0).astype(F32) * 0.125).astype(BF)
-        k = proj(1)
-        v = proj(2)
-        for u in range(4):
-            part = slice(64 * u, 64 * u + 64)
-            kv_ref[4 * j + u] = jnp.concatenate([k[:, part], v[:, part]], axis=1)
-            q_ref[4 * j + u] = jnp.concatenate([q[:64, part], q[64:, part]], axis=1)
-        return carry
-
-    lax.fori_loop(0, 4, block, 0)
-
-
-def project(tok, wall, own):
-    return pl.pallas_call(
-        qkv_kernel,
-        out_shape=[shp((16, 128, 128), BF), shp((16, 64, 128), BF)],
-        in_specs=[VM] + [ANY] * 4,
-        out_specs=[VM] * 2,
-        scratch_shapes=[pltpu.VMEM((4, 3, 256, 1024), BF), DMA((6,))],
-        compiler_params=pltpu.CompilerParams(vmem_limit_bytes=LIMIT),
-        cost_estimate=pl.CostEstimate(flops=805306368, bytes_accessed=8 << 20, transcendentals=0),
-        name="qkv",
-    )(tok, wall, *own)
+        compiler_params=pltpu.CompilerParams(collective_id=1, has_side_effects=True, vmem_limit_bytes=LIMIT),
+        cost_estimate=pl.CostEstimate(flops=16 << 30, bytes_accessed=32 << 20, transcendentals=0),
+        name="front",
+    )(tok, *own, tok, lnp, wo, wi, wu)
 
 
 def exchange(wide, narrow, collective):
@@ -1068,13 +1126,14 @@
 
 
 def finish_kernel(*refs):
-    dkvp, dqp, dr_ref, gb, wall, wq, wk, wv, gpay, zpay, zr, xs, x_ref = refs[:13]
-    got = ((refs[13], refs[16]), (refs[14], refs[17]), (refs[15], refs[18]))
-    gt, io_full, u_full, tail_full, s_vec = refs[19:24]
-    io_refs = list(refs[24:35]) + [io_full]
-    u_refs, tail_refs = list(refs[35:46]) + [u_full], list(refs[46:59]) + [tail_full]
+    dkvp, dqp, dr_ref, gb, wall, gpay, zpay, zr, xs, x_ref = refs[:10]
+    got = ((refs[10], refs[13]), (refs[11], refs[14]), (refs[12], refs[15]))
+
+    gt, io_full, u_full, tail_full, s_vec = refs[16:21]
+    io_refs = list(refs[21:32]) + [io_full]
+    u_refs, tail_refs = list(refs[32:43]) + [u_full], list(refs[43:56]) + [tail_full]
     (dkv, dq, weights, ll2, rr2, lt2, mid, pay, ll, rr, tail, v0, vf, v1, vx, vy, vz, tx, ty,
-     sw, rw, sn, rn, ss, rs, ls, lw) = refs[59:]
+     sw, rw, sn, rn, ss, rs, ls, lw) = refs[56:]
     scale = 1.0 / math.sqrt(16384)
     where = place()
     zl, x, y, zh, co = where
@@ -1113,7 +1172,8 @@
         local.append(pltpu.make_async_copy(xs.at[k], ll.at[128:256, cols], ls.at[6 + k]))
     for c in local + parts:
         c.start()
-    loads = load_qkv(wall, (wq, wk, wv), weights, lw)
+    loads = [pltpu.make_async_copy(wall, weights, lw.at[0])]
+    loads[0].start()
     pl.semaphore_wait(bar, 33)
 
     def narrow_copy(i):
@@ -1259,14 +1319,14 @@
     next(small)
 
 
-def finish(dkvp, dqp, dr, gb, wall, own, gpay, zpay, zr, xs, tok, parts):
+def finish(dkvp, dqp, dr, gb, wall, gpay, zpay, zr, xs, tok, parts):
     n = SUM_COPIES + BEGUN_COPIES + PAIR_COPIES + 4 + 2 + 7
     return pl.pallas_call(
         finish_kernel,
         out_shape=[
             shp((128, 1024), F32), shp((1280, 1024), BF), shp((1024, 1024), BF), shp((768, 1024), BF), shp((8, 256), F32),
         ],
-        in_specs=[ANY, ANY, VM, VM] + [ANY] * 15,
+        in_specs=[ANY, ANY, VM, VM] + [ANY] * 12,
         out_specs=[VM] * 5,
         scratch_shapes=pair_scratch(1280, True) + sum_scratch(1024) + pair_scratch(768, False) + [
             pltpu.VMEM((32, 128, 128), BF), pltpu.VMEM((16, 64, 128), BF), pltpu.VMEM((4, 3, 256, 1024), BF),
@@ -1276,11 +1336,11 @@
             pltpu.VMEM((2, 8, 256), F32), pltpu.VMEM((8, 256), F32), pltpu.VMEM((8, 256), F32),
             pltpu.VMEM((3, 8, 256), F32), pltpu.VMEM((3, 8, 256), F32),
             pltpu.VMEM((8, 256), F32), pltpu.VMEM((8, 256), F32), pltpu.VMEM((8, 256), F32),
-            DMA((32,)), DMA((32,)), DMA((16,)), DMA((16,)), DMA((n,)), DMA((n,)), DMA((16,)), DMA((6,)),
+            DMA((32,)), DMA((32,)), DMA((16,)), DMA((16,)), DMA((n,)), DMA((n,)), DMA((16,)), DMA((1,)),
         ],
         compiler_params=pltpu.CompilerParams(collective_id=6, has_side_effects=True, vmem_limit_bytes=LIMIT),
         name="finish",
-    )(dkvp, dqp, dr, gb, wall, *own, gpay, zpay, zr, xs, tok, *parts)
+    )(dkvp, dqp, dr, gb, wall, gpay, zpay, zr, xs, tok, *parts)
 
 
 def scale_kernel(o, i0, i1, i2, i3, u, q, k, v, out_q, out_k, out_v, out_o, out_i, out_u):
@@ -1327,16 +1387,8 @@
     blk = block_pairs.reshape(-1)
     own = (w_query, w_key, w_value)
     outer = w_outer.reshape(8, 4, 32, 1024)
-    wall, xs, lnf, *core_shard, qa, qb = gather_weights(*own, tok, lnp, w_output, w_inner, outer)
-    qa, qb, wall = lax.optimization_barrier((qa, qb, wall))
-    x2 = lax.ppermute(qa, "ctx", along_x(2))
-    y2 = lax.ppermute(qb, "ctx", along_y(2))
-    diag_a = lax.ppermute(qa, "wsh", FLIP_CORE)
-    diag_b = lax.ppermute(qb, "wsh", FLIP_CORE)
-
-    kvp, qp = project(tok, wall, own)
-    kvr, qr = exchange(kvp, qp, 2)
-    qa, qb, x2, y2, diag_a, diag_b, kvr = lax.optimization_barrier((qa, qb, x2, y2, diag_a, diag_b, kvr))
+    wall, xs, lnf, *rest = front(tok, own, lnp, w_output, w_inner, outer)
+    core_shard, (qa, qb, x2, y2, diag_a, diag_b, kvr, qr) = rest[:3], rest[3:]
     x1, x3 = (lax.ppermute(qa, "ctx", along_x(s)) for s in (1, 3))
     y1, y3 = (lax.ppermute(qb, "ctx", along_y(s)) for s in (1, 3))
     o, ot, lse = attend(blk, block_mask, kvr, qr)
@@ -1357,7 +1409,7 @@
     dkvp, dqp = attend_back(blk, block_mask, kvr, qr, dor, ot, lse)
     zr, plus_a, minus_a, plus_b, minus_b, dkvp = lax.optimization_barrier((zr, plus_a, minus_a, plus_b, minus_b, dkvp))
     grad_tok, io, u, tail, s_vec = finish(
-        dkvp, dqp, dr1, gb, wall, own, gpay, zpay, zr, xs, tok, (own_a, plus_a, minus_a, own_b, plus_b, minus_b)
+        dkvp, dqp, dr1, gb, wall, gpay, zpay, zr, xs, tok, (own_a, plus_a, minus_a, own_b, plus_b, minus_b)
     )
     s_q, s_k, s_v, s_o, s_i, s_u = scaled(io, u, tail)
     out_shape = tokens.shape

time: 303 us -> 298 us (0.983)
    pallas_call x2 -> x1, Pallas kernels: 36.2 us -> 11.2 us  [exchange(): pl.pallas_call(kernel, out_shape=outs, in_specs=[ANY] * len(args), out_sp...]
    pallas_call x2 -> x1, Pallas kernels: 41.9 us -> 65 us  [front(): pl.pallas_call(front_kernel, out_shape=[shp((4, 3, 256, 1024), BF), shp((...]
    ppermute x4 -> x0, starting transfers between devices: 3.86 us -> none  [the longest x1 2.26 us: body(): y2 = lax.ppermute(qb, 'ctx', along_y(2))]
  transfers between devices with their start and end apart: 19 -> 15, of which waited for: 1 -> 1; matrix products, arithmetic and copies ran while one was open for 0% -> 0% of each run, Pallas kernels for 31% -> 21%
where the time goes in v5:
time: 298 us; the launch traced here: 297 us
  Pallas kernels  272 us (91%)
  starting transfers between devices  15.9 us (5%)
  local copies, waits for them, and re-layouts  5.88 us (2%)
    pallas_call x1, Pallas kernels, finish(): pl.pallas_call(finish_kernel, out_shape=[shp((128, 1024), F32), shp((1280...  105 us
    pallas_call x1, Pallas kernels, front(): pl.pallas_call(front_kernel, out_shape=[shp((4, 3, 256, 1024), BF), shp((...  65 us
    pallas_call x1, Pallas kernels, attend_back(): pl.pallas_call(attend_back_kernel, out_shape=[shp((32, 128, 128), BF), sh...  27.4 us
    pallas_call x1, Pallas kernels, attend(): pl.pallas_call(attend_kernel, out_shape=[shp((16, 64, 128), BF), shp((8,...  24.3 us
    pallas_call x1, Pallas kernels, middle(): pl.pallas_call(middle_kernel, out_shape=[shp((128, 1024), F32), shp((128,...  19.9 us
    pallas_call x1, Pallas kernels, turn(): pl.pallas_call(turn_kernel, out_shape=[shp(do.shape, BF)] + [shp((2, 160,...  11.2 us
    pallas_call x1, Pallas kernels, exchange(): pl.pallas_call(kernel, out_shape=outs, in_specs=[ANY] * len(args), out_sp...  11.2 us
    pallas_call x1, Pallas kernels, scaled(): pl.pallas_call(scale_kernel, grid=(8,), out_shape=[shp((256, 1024), F32)]...  8.42 us
  transfers between devices with their start and end apart: 15, of which 1 were waited for; matrix products, arithmetic and copies ran while one was open for 0% of the time, Pallas kernels for 21%

profile of v5, /device:TPU:0, one launch (start us, length us, event | category | flops | bytes accessed | tf_op | source)
XLA Modules:
  0.0 296.9 jit_solution(11548264085666211473)
XLA Ops:
  0.7 1.4 maximum_maximum_fusion.refs_5_.refs_4_
  2.1 65.0 %front.1 = (bf16[4,3,256,1024]{3,2,1,0:T(8,128)(2,1)}, bf16[2,128,256]{2,1,0:T(8,128)(2,1)}, f32[4,8,256]{2,1,0:T(8,128)}, bf16[256,1024]{1,0:T(8,128)(2,1)}, bf...) custom-call(bf16[128,1024]{1,0:T(8,128)(2,1)} %bitcast.6, ...), custom_call_target="tpu_custom_call" | custom-call | flops 17179869184 | bytes 33554432 | tf_op jit(solution)/shard_map/front/pallas_call | solution.py:240
  67.1 2.8 collective-permute-start.1
  69.9 1.4 collective-permute-start.3
  71.3 0.6 collective-permute-start.2
  72.0 0.6 reshape.40.blk
  72.6 24.3 %attend.1 = (bf16[16,64,128]{2,1,0:T(8,128)(2,1)}, f32[8,64,256]{2,1,0:T(8,128)}, f32[8,1,256]{2,1,0:T(1,128)}) custom-call(s32[64]{0:T(128)} %reshape.40.blk, s32[1,64,64]{2,1,0:T(8,128)} %mask.3, bf16[32,128,128]{2,1,0:T(8,128)(2,1)} %get-tuple-element.72.kvr, bf16[16,64,128]{2,1,0:T(8,128)(2,1)} %get-tuple-element.73.qr), custom_call_target="tpu_custom_call" | custom-call | flops 10737418240 | bytes 33554432 | tf_op jit(solution)/shard_map/attend/pallas_call | solution.py:461
  97.1 0.5 collective-permute-start.5
  97.6 0.1 collective-permute-start.6
  97.7 0.4 collective-permute-start.7
  98.1 0.1 collective-permute-start.8
  98.2 0.9 collective-permute-done.4.refs_20_
  99.1 0.8 copy-done.14
  99.9 0.1 collective-permute-start.9
  100.0 11.2 %exchange_3.1.refs_0_ = bf16[16,64,128]{2,1,0:T(8,128)(2,1)} custom-call(bf16[16,64,128]{2,1,0:T(8,128)(2,1)} %get-tuple-element.75.refs_0_), custom_call_target="tpu_custom_call" | custom-call | flops 17179869184 | bytes 33554432 | tf_op jit(solution)/shard_map/exchange_3/pallas_call | solution.py:329
  111.3 19.9 %middle.1 = (f32[128,1024]{1,0:T(8,128)}, f32[128,1024]{1,0:T(8,128)}, bf16[16,64,128]{2,1,0:T(8,128)(2,1)}, bf16[128,3072]{1,0:T(8,128)(2,1)}, bf16[128,2048]{1...) custom-call(bf16[16,64,128]{2,1,0:T(8,128)(2,1)} %exchange_3.1.refs_0_, ...), custom_call_target="tpu_custom_call" | custom-call | flops 10737418240 | bytes 33554432 | tf_op jit(solution)/shard_map/middle/pallas_call | solution.py:678
  131.2 11.2 %turn.1 = (bf16[16,64,128]{2,1,0:T(8,128)(2,1)}, bf16[2,160,1024]{2,1,0:T(8,128)(2,1)}, bf16[2,240,1024]{2,1,0:T(8,128)(2,1)}, bf16[2,240,1024]{2,1,0:T(8,128)(2...) custom-call(bf16[16,64,128]{2,1,0:T(8,128)(2,1)} %get-tuple-element.90.do, ...), custom_call_target="tpu_custom_call" | custom-call | flops 17179869184 | bytes 33554432 | tf_op jit(solution)/shard_map/turn/pallas_call | solution.py:774
  142.4 0.6 collective-permute-start.11
  143.0 2.7 collective-permute-start.12
  145.7 0.9 collective-permute-start.13
  146.6 2.4 collective-permute-start.14
  149.0 3.2 %collective-permute-start.10 = (bf16[128,3072]{1,0:T(8,128)(2,1)S(1)}, bf16[128,3072]{1,0:T(8,128)(2,1)S(1)}, u32[]{:S(2)}, u32[]{:S(2)}) collective-permute-start(bf16[128,3072]{1,0:T(8,128)(2,1)S(1)} %copy-done.4), channel_id=1, source_target_pairs={{0,2},{2,0},{1,3},{3,1},{4,6},{6,4},{5,7},{7,5},{8,10},{10,8},{9,1... | collective-permute-start | bytes 2359304 | tf_op jit(solution)/shard_map/ppermute | solution.py:1403
  152.2 27.4 %attend_back.1 = (bf16[32,128,128]{2,1,0:T(8,128)(2,1)}, bf16[16,64,128]{2,1,0:T(8,128)(2,1)}) custom-call(s32[64]{0:T(128)} %reshape.40.blk, s32[1,64,64]{2,1,0:T(8,128)} %mask.3, bf16[32,128,128]{2,1,0:T(8,128)(2,1)} %get-tuple-element.72.kvr, bf16[16,64,128]{2,1,0:T(8,128)(2,1)} %get-tuple-element.73.qr, bf16[16,64,128]{2,1,0:T(8,128)(2,1)} %get-tuple-element.97.dor, ...), custom_call_target="tpu_custom_call" | custom-call | flops 1073741824 | bytes 4194304 | tf_op jit(solution)/shard_map/attend_back/pallas_call | solution.py:546
  179.7 0.8 copy-done.5
  180.5 0.3 copy-done
  180.8 0.3 copy-done.1
  181.1 0.3 copy-done.2
  181.4 0.3 copy-done.3
  181.8 104.6 %finish.1 = (f32[128,1024]{1,0:T(8,128)}, bf16[1280,1024]{1,0:T(8,128)(2,1)}, bf16[1024,1024]{1,0:T(8,128)(2,1)}, bf16[768,1024]{1,0:T(8,128)(2,1)}, f32[8,256]{1,0:T(8,128)}) custom-call(bf16[32,128,128]{2,1,0:T(8,128)(2,1)} %get-tuple-element.101.refs_0_, bf16[16,64,128]{2,1,0:T(8,128)(2,1)} %get-tuple-element.102.refs_1_, ...), custom_call_target="tpu_custom_call" | custom-call | tf_op jit(solution)/shard_map/finish/pallas_call | solution.py:1324
  286.4 1.4 fusion
  287.7 8.4 %scaled.1 = (f32[256,1024]{1,0:T(8,128)}, f32[256,1024]{1,0:T(8,128)}, f32[256,1024]{1,0:T(8,128)}, f32[256,1024]{1,0:T(8,128)}, f32[256,4096]{1,0:T(8,128)}, /*index=5*/f32[1024,1024]{1,0:T(8,128)}) custom-call(bf16[1280,1024]{1,0:T(8,128)(2,1)} %get-tuple-element.116.o.i0.i1.i2.i3, bf16[1280,1024]{1,0:T(8,128)(2,1)} %get-tuple-element.116.o.i0.i1.i2.i3, ...), custom_call_target="tpu_custom_call" | custom-call | tf_op jit(solution)/shard_map/scaled/pallas_call | solution.py:1358
  296.2 0.8 copy.25
  (43 shorter events, 0.4 us)
Async XLA Ops:
  2.1 69.8 %copy-start.7 = (s32[32,2]{0,1:T(2,128)S(1)}, s32[32,2]{0,1:T(2,128)}, u32[]{:S(2)}) copy-start(s32[32,2]{0,1:T(2,128)} %param.22) | copy-start | bytes 772
  67.1 29.9 %collective-permute-start.1 = (bf16[9,32,1024]{2,1,0:T(8,128)(2,1)}, bf16[9,32,1024]{2,1,0:T(8,128)(2,1)S(1)}, u32[]{:S(2)}, u32[]{:S(2)}) collective-permute-start(bf16[9,32,1024]{2,1,0:T(8,128)(2,1)} %get-tuple-element.68.refs_11_), channel_id=1, source_target_pairs={{0,48},{4,52},{8,56},{12,60},{16,0},{20,4},{24,8},{28,12},{32,16},... | collective-permute-start | bytes 1769480 | tf_op jit(solution)/shard_map/ppermute | solution.py:1392
  69.9 27.1 %collective-permute-start = (bf16[9,32,1024]{2,1,0:T(8,128)(2,1)}, bf16[9,32,1024]{2,1,0:T(8,128)(2,1)S(1)}, u32[]{:S(2)}, u32[]{:S(2)}) collective-permute-start(bf16[9,32,1024]{2,1,0:T(8,128)(2,1)} %get-tuple-element.68.refs_11_), channel_id=1, source_target_pairs={{0,16},{4,20},{8,24},{12,28},{16,32},{20,36},{24,40},{28,44},{32,4... | collective-permute-start | bytes 1769480 | tf_op jit(solution)/shard_map/ppermute | solution.py:1392
  69.9 27.1 %collective-permute-start.3 = (bf16[9,32,1024]{2,1,0:T(8,128)(2,1)}, bf16[9,32,1024]{2,1,0:T(8,128)(2,1)S(1)}, u32[]{:S(2)}, u32[]{:S(2)}) collective-permute-start(bf16[9,32,1024]{2,1,0:T(8,128)(2,1)} %get-tuple-element.70.refs_15_), channel_id=1, source_target_pairs={{0,12},{4,0},{8,4},{12,8},{16,28},{20,16},{24,20},{28,24},{32,44},... | collective-permute-start | bytes 1769480 | tf_op jit(solution)/shard_map/ppermute | solution.py:1393
  71.3 25.7 %collective-permute-start.2 = (bf16[9,32,1024]{2,1,0:T(8,128)(2,1)}, bf16[9,32,1024]{2,1,0:T(8,128)(2,1)S(1)}, u32[]{:S(2)}, u32[]{:S(2)}) collective-permute-start(bf16[9,32,1024]{2,1,0:T(8,128)(2,1)} %get-tuple-element.70.refs_15_), channel_id=1, source_target_pairs={{0,4},{4,8},{8,12},{12,0},{16,20},{20,24},{24,28},{28,16},{32,36},... | collective-permute-start | bytes 1769480 | tf_op jit(solution)/shard_map/ppermute | solution.py:1393
  72.6 24.5 %copy-start.8 = (bf16[9,32,1024]{2,1,0:T(8,128)(2,1)S(1)}, bf16[9,32,1024]{2,1,0:T(8,128)(2,1)}, u32[]{:S(2)}) copy-start(bf16[9,32,1024]{2,1,0:T(8,128)(2,1)} %get-tuple-element.81.refs_13_) | copy-start | bytes 1769476
  72.6 25.5 %copy-start.9 = (bf16[9,32,1024]{2,1,0:T(8,128)(2,1)S(1)}, bf16[9,32,1024]{2,1,0:T(8,128)(2,1)}, u32[]{:S(2)}) copy-start(bf16[9,32,1024]{2,1,0:T(8,128)(2,1)} %get-tuple-element.84.refs_17_) | copy-start | bytes 1769476
  96.9 14.3 %copy-start.10 = (bf16[9,32,1024]{2,1,0:T(8,128)(2,1)}, bf16[9,32,1024]{2,1,0:T(8,128)(2,1)S(1)}, u32[]{:S(2)}) copy-start(bf16[9,32,1024]{2,1,0:T(8,128)(2,1)S(1)} %collective-permute-done.1.refs_14_) | copy-start | bytes 1769476
  96.9 14.3 %copy-start.11 = (bf16[9,32,1024]{2,1,0:T(8,128)(2,1)}, bf16[9,32,1024]{2,1,0:T(8,128)(2,1)S(1)}, u32[]{:S(2)}) copy-start(bf16[9,32,1024]{2,1,0:T(8,128)(2,1)S(1)} %collective-permute-done.refs_12_) | copy-start | bytes 1769476
  97.0 14.3 %copy-start.12 = (bf16[9,32,1024]{2,1,0:T(8,128)(2,1)}, bf16[9,32,1024]{2,1,0:T(8,128)(2,1)S(1)}, u32[]{:S(2)}) copy-start(bf16[9,32,1024]{2,1,0:T(8,128)(2,1)S(1)} %collective-permute-done.3.refs_18_) | copy-start | bytes 1769476
  97.0 14.3 %copy-start.13 = (bf16[9,32,1024]{2,1,0:T(8,128)(2,1)}, bf16[9,32,1024]{2,1,0:T(8,128)(2,1)S(1)}, u32[]{:S(2)}) copy-start(bf16[9,32,1024]{2,1,0:T(8,128)(2,1)S(1)} %collective-permute-done.2.refs_16_) | copy-start | bytes 1769476
  97.0 2.1 collective-permute-start.4
  97.1 14.1 %collective-permute-start.5 = (bf16[9,32,1024]{2,1,0:T(8,128)(2,1)S(1)}, bf16[9,32,1024]{2,1,0:T(8,128)(2,1)}, u32[]{:S(2)}, u32[]{:S(2)}) collective-permute-start(bf16[9,32,1024]{2,1,0:T(8,128)(2,1)S(1)} %copy-done.8), channel_id=1, source_target_pairs={{0,1},{1,0},{2,3},{3,2},{4,5},{5,4},{6,7},{7,6},{8,9},{9,8},{10,11... | collective-permute-start | bytes 1769480 | tf_op jit(solution)/shard_map/ppermute | solution.py:1397
  97.6 13.7 %collective-permute-start.6 = (bf16[9,32,1024]{2,1,0:T(8,128)(2,1)S(1)}, bf16[9,32,1024]{2,1,0:T(8,128)(2,1)}, u32[]{:S(2)}, u32[]{:S(2)}) collective-permute-start(bf16[9,32,1024]{2,1,0:T(8,128)(2,1)S(1)} %collective-permute-done.1.refs_14_), channel_id=1, source_target_pairs={{0,1},{1,0},{2,3},{3,2},{4,5},{5,4},{6,7},{7,6},{8,9},{9,8},{10,11... | collective-permute-start | bytes 1769480 | tf_op jit(solution)/shard_map/ppermute | solution.py:1397
  97.7 13.6 %collective-permute-start.7 = (bf16[9,32,1024]{2,1,0:T(8,128)(2,1)S(1)}, bf16[9,32,1024]{2,1,0:T(8,128)(2,1)}, u32[]{:S(2)}, u32[]{:S(2)}) collective-permute-start(bf16[9,32,1024]{2,1,0:T(8,128)(2,1)S(1)} %collective-permute-done.2.refs_16_), channel_id=1, source_target_pairs={{0,1},{1,0},{2,3},{3,2},{4,5},{5,4},{6,7},{7,6},{8,9},{9,8},{10,11... | collective-permute-start | bytes 1769480 | tf_op jit(solution)/shard_map/ppermute | solution.py:1397
  98.1 13.2 %collective-permute-start.8 = (bf16[9,32,1024]{2,1,0:T(8,128)(2,1)S(1)}, bf16[9,32,1024]{2,1,0:T(8,128)(2,1)}, u32[]{:S(2)}, u32[]{:S(2)}) collective-permute-start(bf16[9,32,1024]{2,1,0:T(8,128)(2,1)S(1)} %copy-done.9), channel_id=1, source_target_pairs={{0,1},{1,0},{2,3},{3,2},{4,5},{5,4},{6,7},{7,6},{8,9},{9,8},{10,11... | collective-permute-start | bytes 1769480 | tf_op jit(solution)/shard_map/ppermute | solution.py:1397
  99.1 0.8 copy-start.14
  99.9 11.4 %collective-permute-start.9 = (bf16[9,32,1024]{2,1,0:T(8,128)(2,1)S(1)}, bf16[9,32,1024]{2,1,0:T(8,128)(2,1)}, u32[]{:S(2)}, u32[]{:S(2)}) collective-permute-start(bf16[9,32,1024]{2,1,0:T(8,128)(2,1)S(1)} %collective-permute-done.3.refs_18_), channel_id=1, source_target_pairs={{0,1},{1,0},{2,3},{3,2},{4,5},{5,4},{6,7},{7,6},{8,9},{9,8},{10,11... | collective-permute-start | bytes 1769480 | tf_op jit(solution)/shard_map/ppermute | solution.py:1397
  131.2 17.8 %copy-start.4 = (bf16[128,3072]{1,0:T(8,128)(2,1)S(1)}, bf16[128,3072]{1,0:T(8,128)(2,1)}, u32[]{:S(2)}) copy-start(bf16[128,3072]{1,0:T(8,128)(2,1)} %get-tuple-element.89.refs_6_) | copy-start | bytes 2359300
  142.4 37.2 %collective-permute-start.11 = (bf16[2,240,1024]{2,1,0:T(8,128)(2,1)}, bf16[2,240,1024]{2,1,0:T(8,128)(2,1)S(1)}, u32[]{:S(2)}, u32[]{:S(2)}) collective-permute-start(bf16[2,240,1024]{2,1,0:T(8,128)(2,1)} %get-tuple-element.93), channel_id=1, source_target_pairs={{0,16},{4,20},{8,24},{12,28},{16,32},{20,36},{24,40},{28,44},{32,4... | collective-permute-start | bytes 2949128 | tf_op jit(solution)/shard_map/ppermute | solution.py:1405
  143.0 36.6 %collective-permute-start.12 = (bf16[2,240,1024]{2,1,0:T(8,128)(2,1)}, bf16[2,240,1024]{2,1,0:T(8,128)(2,1)S(1)}, u32[]{:S(2)}, u32[]{:S(2)}) collective-permute-start(bf16[2,240,1024]{2,1,0:T(8,128)(2,1)} %get-tuple-element.94), channel_id=1, source_target_pairs={{0,48},{4,52},{8,56},{12,60},{16,0},{20,4},{24,8},{28,12},{32,16},... | collective-permute-start | bytes 2949128 | tf_op jit(solution)/shard_map/ppermute | solution.py:1406
  145.7 33.9 %collective-permute-start.13 = (bf16[2,240,1024]{2,1,0:T(8,128)(2,1)}, bf16[2,240,1024]{2,1,0:T(8,128)(2,1)S(1)}, u32[]{:S(2)}, u32[]{:S(2)}) collective-permute-start(bf16[2,240,1024]{2,1,0:T(8,128)(2,1)} %get-tuple-element.95), channel_id=1, source_target_pairs={{0,4},{4,8},{8,12},{12,0},{16,20},{20,24},{24,28},{28,16},{32,36},... | collective-permute-start | bytes 2949128 | tf_op jit(solution)/shard_map/ppermute | solution.py:1407
  146.6 33.1 %collective-permute-start.14 = (bf16[2,240,1024]{2,1,0:T(8,128)(2,1)}, bf16[2,240,1024]{2,1,0:T(8,128)(2,1)S(1)}, u32[]{:S(2)}, u32[]{:S(2)}) collective-permute-start(bf16[2,240,1024]{2,1,0:T(8,128)(2,1)} %get-tuple-element.96), channel_id=1, source_target_pairs={{0,12},{4,0},{8,4},{12,8},{16,28},{20,16},{24,20},{28,24},{32,44},... | collective-permute-start | bytes 2949128 | tf_op jit(solution)/shard_map/ppermute | solution.py:1408
  149.0 30.6 %collective-permute-start.10 = (bf16[128,3072]{1,0:T(8,128)(2,1)S(1)}, bf16[128,3072]{1,0:T(8,128)(2,1)S(1)}, u32[]{:S(2)}, u32[]{:S(2)}) collective-permute-start(bf16[128,3072]{1,0:T(8,128)(2,1)S(1)} %copy-done.4), channel_id=1, source_target_pairs={{0,2},{2,0},{1,3},{3,1},{4,6},{6,4},{5,7},{7,5},{8,10},{10,8},{9,1... | collective-permute-start | bytes 2359304 | tf_op jit(solution)/shard_map/ppermute | solution.py:1403
  179.6 0.9 copy-start.5
  179.6 1.2 copy-start
  179.6 1.5 copy-start.1
  179.7 1.8 copy-start.2
  179.7 2.1 copy-start.3
  287.7 8.4 %copy-start.6 = (f32[128,1024]{1,0:T(8,128)S(1)}, f32[128,1024]{1,0:T(8,128)}, u32[]{:S(2)}) copy-start(f32[128,1024]{1,0:T(8,128)} %get-tuple-element.115) | copy-start | bytes 1572868

commit v6 on v5

--- a/solution.py
+++ b/solution.py
@@ -1094,20 +1094,100 @@
                 c.wait_send()
 
 
-SUM_COPIES = 12 + 12 + 2 + 4 + 12 + 12
+class FirstSum:
+    def __init__(self, g, refs, wire, where, xp, yp, zp):
+        bufs1, s1, bufs2, rz, half, full = refs[:4], refs[4], refs[5:9], refs[9], refs[10], refs[11]
+        zl, x, y, zh, co = where
+        self.g, self.wire, self.zp, self.zl = g, wire, zp, zl
+        self.s1, self.rz, self.half, self.full = s1, rz, half, full
+        first, second = (xp, yp), (yp, xp)
+        self.at1, self.at2 = (x, y), (y, x)
+
+        def cols(k):
+            return pl.ds(pl.multiple_of(k * 256, 128), 256)
+
+        def one(h):
+            return lambda k, u: half.at[pl.ds(pl.multiple_of(h * 256 + k * 64 + u * 32, 32), 32)]
+
+        def two(h):
+            return lambda k, u: s1.at[h, u, :, cols(k)]
+
+        def rows(h, k, z):
+            return pl.ds(pl.multiple_of(z * 512 + h * 256 + k * 64, 64), 64)
+
+        def five(h):
+            return lambda k, z: full.at[rows(h, self.at1[h], z), cols(k)]
+
+        def six(h):
+            return lambda k, z: full.at[rows(h, k, z)]
+
+        self.spot = lambda h: full.at[rows(h, self.at1[h], zl), cols(self.at2[h])]
+        self.one = [Spread(wire, first[h][0], first[h][2], self.at1[h], one(h), [r.at[h] for r in bufs1]) for h in range(2)]
+        self.two = [DirectSpread(wire, second[h], self.at2[h], two(h), [r.at[h] for r in bufs2]) for h in range(2)]
+        self.five = [Gather(wire, second[h][0], second[h][2], self.at2[h], five(h)) for h in range(2)]
+        self.six = [Gather(wire, first[h][0], first[h][2], self.at1[h], six(h)) for h in range(2)]
+
+    def steps(self):
+        zs = []
+        for h in range(2):
+            src = self.g.at[pl.ds(pl.multiple_of((1 - self.zl) * 512 + h * 256, 256), 256)]
+            zs.append(self.wire(src, self.rz.at[h], self.zp))
+        yield
+        for h in range(2):
+            zs[h].wait_recv()
+            mine = self.g[pl.ds(pl.multiple_of(self.zl * 512 + h * 256, 256), 256), :]
+            self.half[256 * h:256 * h + 256, :] = (mine.astype(F32) + self.rz[h].astype(F32)).astype(BF)
+            self.one[h].start()
+        yield
+        for t in self.one:
+            t.relay()
+        yield
+        for h in range(2):
+            for u, total in enumerate(self.one[h].total()):
+                self.s1[h, u] = total.astype(BF)
+            self.two[h].start()
+        yield
+        four = []
+        for h in range(2):
+            spot = self.spot(h)
+            spot[...] = jnp.concatenate(self.two[h].total(), axis=0).astype(BF)
+            four.append(self.wire(spot, spot, self.zp))
+        yield
+        for h in range(2):
+            four[h].wait()
+            self.five[h].start()
+        yield
+        for t in self.five:
+            t.relay()
+        yield
+        for h in range(2):
+            self.five[h].done()
+            self.six[h].start()
+        yield
+        for t in self.six:
+            t.relay()
+        yield
+        for t in self.one + self.two:
+            t.sent()
+        for c in zs:
+            c.wait_send()
+        for t in self.six:
+            t.done()
+        yield
+
+
+SUM_COPIES = 2 + 12 + 12 + 2 + 12 + 12
 
 
 BEGUN_COPIES = 4 + 12 + 2 + 2 + 4 + 12 + 12
 PAIR_COPIES = 12 + 12 + 2 + 2 + 4 + 12 + 12
 
 
-def sum_scratch(rows):
-    hh = rows // 16
+def first_scratch():
     return (
-        [pltpu.VMEM((2, 2, hh, 1024), BF)] * 4
-        + [pltpu.VMEM((2, 2, hh, 1024), BF)]
-        + [pltpu.VMEM((2, 2, hh, 256), BF)] * 4
-        + [pltpu.VMEM((2, 2, hh, 256), BF), pltpu.VMEM((2, 2, hh, 128), BF)]
+        [pltpu.VMEM((2, 2, 32, 1024), BF)] * 5
+        + [pltpu.VMEM((2, 2, 32, 256), BF)] * 4
+        + [pltpu.VMEM((2, 256, 1024), BF), pltpu.VMEM((512, 1024), BF)]
     )
 
 
@@ -1132,8 +1212,8 @@
     gt, io_full, u_full, tail_full, s_vec = refs[16:21]
     io_refs = list(refs[21:32]) + [io_full]
     u_refs, tail_refs = list(refs[32:43]) + [u_full], list(refs[43:56]) + [tail_full]
-    (dkv, dq, weights, ll2, rr2, lt2, mid, pay, ll, rr, tail, v0, vf, v1, vx, vy, vz, tx, ty,
-     sw, rw, sn, rn, ss, rs, ls, lw) = refs[56:]
+    (dkv, zb, sb, dq, weights, ll2, rr2, lt2, mid, pay, ll, rr, tail, v0, vf, v1, vx, vy, vz, tx, ty,
+     sz, rz, sw, rw, sn, rn, ss, rs, ls, lw) = refs[56:]
     scale = 1.0 / math.sqrt(16384)
     where = place()
     zl, x, y, zh, co = where
@@ -1148,12 +1228,12 @@
     bar = pltpu.get_barrier_semaphore()
 
     def greet_one(i, carry):
-        pl.semaphore_signal(bar, inc=1, device_id={"ctx": (me + i) % 32}, device_id_type=MESH)
+        pl.semaphore_signal(bar, inc=1, device_id={"ctx": zl * 16 + (flat + i) % 16}, device_id_type=MESH)
         return carry
 
-    for p in (core, far):
+    for p in (core, far, zp):
         pl.semaphore_signal(bar, inc=1, device_id=p, device_id_type=MESH)
-    lax.fori_loop(1, 32, greet_one, 0)
+    lax.fori_loop(1, 16, greet_one, 0)
 
     mine = [pl.ds(pl.multiple_of(k * 256, 256), 256) for k in (w, (1 - zh) * 2 + co)]
     parts = []
@@ -1174,7 +1254,7 @@
         c.start()
     loads = [pltpu.make_async_copy(wall, weights, lw.at[0])]
     loads[0].start()
-    pl.semaphore_wait(bar, 33)
+    pl.semaphore_wait(bar, 18)
 
     def narrow_copy(i):
         p = (flat + i) % 16
@@ -1183,11 +1263,17 @@
             device_id={"ctx": zl * 16 + p}, device_id_type=MESH,
         )
 
+    def z_copy(i):
+        return pltpu.make_async_remote_copy(
+            src_ref=dkvp.at[(1 - zl) * 16 + (flat + i) % 16], dst_ref=zb.at[i], send_sem=sz.at[i], recv_sem=rz.at[i],
+            device_id=zp, device_id_type=MESH,
+        )
+
     def wide_copy(i):
-        p = (me + i) % 32
+        p = (flat + i) % 16
         return pltpu.make_async_remote_copy(
-            src_ref=dkvp.at[p], dst_ref=dkv.at[me], send_sem=sw.at[i], recv_sem=rw.at[i],
-            device_id={"ctx": p}, device_id_type=MESH,
+            src_ref=sb.at[i], dst_ref=dkv.at[flat], send_sem=sw.at[i], recv_sem=rw.at[i],
+            device_id={"ctx": zl * 16 + p}, device_id_type=MESH,
         )
 
     def start(make):
@@ -1202,12 +1288,23 @@
             return carry
         return one
 
-    lax.fori_loop(1, 32, start(wide_copy), 0)
+    def both(i):
+        z_copy(i).wait_recv()
+        return (dkvp[zl * 16 + (flat + i) % 16].astype(F32) + zb[i].astype(F32)).astype(BF)
+
+    def pass_on(i, carry):
+        sb[i] = both(i)
+        wide_copy(i).start()
+        return carry
+
+    def sent(i, carry):
+        z_copy(i).wait_send()
+        return carry
+
+    lax.fori_loop(1, 16, start(z_copy), 0)
+    z_copy(0).start()
     lax.fori_loop(1, 16, start(narrow_copy), 0)
-    home = [
-        pltpu.make_async_copy(dkvp.at[me], dkv.at[me], ls.at[8]),
-        pltpu.make_async_copy(dqp.at[flat], dq.at[flat], ls.at[9]),
-    ]
+    home = [pltpu.make_async_copy(dqp.at[flat], dq.at[flat], ls.at[9])]
     for c in home:
         c.start()
     wire = Wire(ss, rs)
@@ -1218,7 +1315,7 @@
         wire(zr.at[:, 1024:2048], rr2.at[384:512, :], core),
     ]
     io = BegunSum(160, io_refs, wire, where, xp, yp, zp, far, *got).steps()
-    big = Sum(mid, 128, u_refs, wire, where, xp, yp, zp).steps()
+    big = FirstSum(mid, u_refs, wire, where, xp, yp, zp).steps()
     small = PairSum(tail, 96, tail_refs, wire, where, xp, yp, zp, far).steps()
     next(io)
     next(io)
@@ -1233,26 +1330,28 @@
         rows = slice(256 * k, 256 * k + 256)
         mid[rows, :] = dot(lt2[rows, :], rr2[...]).astype(BF)
     next(big)
+    lax.fori_loop(1, 16, pass_on, 0)
+    dkv[flat] = both(0)
     for c in parts:
         c.wait()
     next(io)
 
     for c in home:
         c.wait()
-    lax.fori_loop(1, 32, wait(wide_copy), 0)
+    lax.fori_loop(1, 16, wait(wide_copy), 0)
     lax.fori_loop(1, 16, wait(narrow_copy), 0)
+    lax.fori_loop(0, 16, sent, 0)
     for h in range(16):
         lanes = slice(64 * h, 64 * h + 64)
         pair = dq[h]
         pay[:64, lanes] = pair[:, :64]
         pay[64:128, lanes] = pair[:, 64:]
-        both = (dkv[h].astype(F32) + dkv[16 + h].astype(F32)).astype(BF)
-        pay[:128, 1024 + 64 * h:1088 + 64 * h] = both[:, :64]
-        pay[:128, 2048 + 64 * h:2112 + 64 * h] = both[:, 64:]
+        pair = dkv[h]
+        pay[:128, 1024 + 64 * h:1088 + 64 * h] = pair[:, :64]
+        pay[:128, 2048 + 64 * h:2112 + 64 * h] = pair[:, 64:]
     pay[128:144, :1024] = jnp.concatenate([gb[...], jnp.zeros((8, 1024), F32)], axis=0).astype(BF)
     pay[128:144, 1024:] = jnp.zeros((16, 2048), BF)
     to_core = wire(pay, rr, core)
-    next(big)
     next(io)
     for c in loads:
         c.wait()
@@ -1262,6 +1361,7 @@
         for m in range(3):
             total += dot(pay[:128, 1024 * m:1024 * m + 1024], weights[k, m], NT)
         gt[:, cols] = total
+    next(io)
     to_core.wait_recv()
     for z in range(2):
         for m in range(3):
@@ -1273,42 +1373,40 @@
     for z in range(2):
         v0[z] = (pay[128:144, mine[z]].astype(F32) + rr[128:144, mine[z]].astype(F32))[:8]
     vfar = wire(v0.at[1], vf, far)
+    next(big)
+    next(io)
+    next(small)
+    next(big)
+    next(io)
+    vfar.wait_recv()
+    v1[...] = v0[0] + vf[...]
+    vone = [wire(v1, vx.at[s], xp[s]) for s in range(3)]
+    next(small)
     next(io)
     next(big)
     next(small)
     next(io)
-    next(big)
-    next(small)
-    vfar.wait_recv()
-    v1[...] = v0[0] + vf[...]
-    vone = [wire(v1, vx.at[s], xp[s]) for s in range(3)]
-    next(io)
-    next(big)
-    next(small)
-    next(io)
-    next(big)
-    next(small)
     for c in vone:
         c.wait_recv()
     tx[...] = v1[...] + vx[0] + vx[1] + vx[2]
     vtwo = [wire(tx, vy.at[s], yp[s]) for s in range(3)]
+    next(small)
+    next(big)
     next(io)
+    next(small)
     next(big)
-    next(small)
-    next(io)
-    next(big)
-    next(small)
     for c in vtwo:
         c.wait_recv()
     ty[...] = tx[...] + vy[0] + vy[1] + vy[2]
     vthree = wire(ty, vz, zp)
-    next(io)
-    next(big)
     next(small)
     next(big)
     next(small)
     next(big)
+    next(io)
     next(small)
+    next(small)
+    next(big)
     vthree.wait()
     s_vec[...] = (ty[...] + vz[...]) * scale
     for c in vone + vtwo + [to_core, vfar]:
@@ -1326,17 +1424,19 @@
         out_shape=[
             shp((128, 1024), F32), shp((1280, 1024), BF), shp((1024, 1024), BF), shp((768, 1024), BF), shp((8, 256), F32),
         ],
-        in_specs=[ANY, ANY, VM, VM] + [ANY] * 12,
+        in_specs=[VM, ANY, VM, VM] + [ANY] * 12,
         out_specs=[VM] * 5,
-        scratch_shapes=pair_scratch(1280, True) + sum_scratch(1024) + pair_scratch(768, False) + [
-            pltpu.VMEM((32, 128, 128), BF), pltpu.VMEM((16, 64, 128), BF), pltpu.VMEM((4, 3, 256, 1024), BF),
+        scratch_shapes=pair_scratch(1280, True) + first_scratch() + pair_scratch(768, False) + [
+            pltpu.VMEM((16, 128, 128), BF), pltpu.VMEM((16, 128, 128), BF), pltpu.VMEM((16, 128, 128), BF),
+            pltpu.VMEM((16, 64, 128), BF), pltpu.VMEM((4, 3, 256, 1024), BF),
             pltpu.VMEM((512, 1024), BF), pltpu.VMEM((512, 1024), BF), pltpu.VMEM((1024, 512), BF),
             pltpu.VMEM((1024, 1024), BF), pltpu.VMEM((144, 3072), BF),
             pltpu.VMEM((256, 512), BF), pltpu.VMEM((144, 3072), BF), pltpu.VMEM((2, 768, 1024), BF),
             pltpu.VMEM((2, 8, 256), F32), pltpu.VMEM((8, 256), F32), pltpu.VMEM((8, 256), F32),
             pltpu.VMEM((3, 8, 256), F32), pltpu.VMEM((3, 8, 256), F32),
             pltpu.VMEM((8, 256), F32), pltpu.VMEM((8, 256), F32), pltpu.VMEM((8, 256), F32),
-            DMA((32,)), DMA((32,)), DMA((16,)), DMA((16,)), DMA((n,)), DMA((n,)), DMA((16,)), DMA((1,)),
+            DMA((16,)), DMA((16,)), DMA((16,)), DMA((16,)), DMA((16,)), DMA((16,)),
+            DMA((n,)), DMA((n,)), DMA((16,)), DMA((1,)),
         ],
         compiler_params=pltpu.CompilerParams(collective_id=6, has_side_effects=True, vmem_limit_bytes=LIMIT),
         name="finish",

time: 298 us -> 288 us (0.966)
  Pallas kernels: 272 us -> 263 us
    pallas_call x1, Pallas kernels: 105 us -> 95.5 us  [finish(): pl.pallas_call(finish_kernel, out_shape=[shp((128, 1024), F32), shp((1280...]
  transfers between devices with their start and end apart: 15 -> 15, of which waited for: 1 -> 1; matrix products, arithmetic and copies ran while one was open for 0% -> 0% of each run, Pallas kernels for 21% -> 22%
where the time goes in v6:
time: 288 us
  Pallas kernels  263 us (91%)
  starting transfers between devices  15.9 us (6%)
  local copies, waits for them, and re-layouts  5.88 us (2%)
    pallas_call x1, Pallas kernels, finish(): pl.pallas_call(finish_kernel, out_shape=[shp((128, 1024), F32), shp((1280...  95.5 us
    pallas_call x1, Pallas kernels, front(): pl.pallas_call(front_kernel, out_shape=[shp((4, 3, 256, 1024), BF), shp((...  65 us
    pallas_call x1, Pallas kernels, attend_back(): pl.pallas_call(attend_back_kernel, out_shape=[shp((32, 128, 128), BF), sh...  27.4 us
    pallas_call x1, Pallas kernels, attend(): pl.pallas_call(attend_kernel, out_shape=[shp((16, 64, 128), BF), shp((8,...  24.3 us
    pallas_call x1, Pallas kernels, middle(): pl.pallas_call(middle_kernel, out_shape=[shp((128, 1024), F32), shp((128,...  19.9 us
    pallas_call x1, Pallas kernels, exchange(): pl.pallas_call(kernel, out_shape=outs, in_specs=[ANY] * len(args), out_sp...  11.2 us
    pallas_call x1, Pallas kernels, turn(): pl.pallas_call(turn_kernel, out_shape=[shp(do.shape, BF)] + [shp((2, 160,...  11.2 us
    pallas_call x1, Pallas kernels, scaled(): pl.pallas_call(scale_kernel, grid=(8,), out_shape=[shp((256, 1024), F32)]...  8.42 us
  transfers between devices with their start and end apart: 15, of which 1 were waited for; matrix products, arithmetic and copies ran while one was open for 0% of the time, Pallas kernels for 22%

profile of v6, /device:TPU:0, one launch (start us, length us, event | category | flops | bytes accessed | tf_op | source)
XLA Modules:
  0.0 287.9 jit_solution(2909137285651567940)
XLA Ops:
  0.7 1.4 maximum_maximum_fusion.refs_5_.refs_4_
  2.1 65.0 %front.1 = (bf16[4,3,256,1024]{3,2,1,0:T(8,128)(2,1)}, bf16[2,128,256]{2,1,0:T(8,128)(2,1)}, f32[4,8,256]{2,1,0:T(8,128)}, bf16[256,1024]{1,0:T(8,128)(2,1)}, bf...) custom-call(bf16[128,1024]{1,0:T(8,128)(2,1)} %bitcast.6, ...), custom_call_target="tpu_custom_call" | custom-call | flops 17179869184 | bytes 33554432 | tf_op jit(solution)/shard_map/front/pallas_call | solution.py:240
  67.1 2.8 collective-permute-start.1
  69.9 1.4 collective-permute-start.3
  71.3 0.6 collective-permute-start.2
  72.0 0.6 reshape.40.blk
  72.6 24.3 %attend.1 = (bf16[16,64,128]{2,1,0:T(8,128)(2,1)}, f32[8,64,256]{2,1,0:T(8,128)}, f32[8,1,256]{2,1,0:T(1,128)}) custom-call(s32[64]{0:T(128)} %reshape.40.blk, s32[1,64,64]{2,1,0:T(8,128)} %mask.3, bf16[32,128,128]{2,1,0:T(8,128)(2,1)} %get-tuple-element.72.kvr, bf16[16,64,128]{2,1,0:T(8,128)(2,1)} %get-tuple-element.73.qr), custom_call_target="tpu_custom_call" | custom-call | flops 10737418240 | bytes 33554432 | tf_op jit(solution)/shard_map/attend/pallas_call | solution.py:461
  97.1 0.5 collective-permute-start.5
  97.6 0.1 collective-permute-start.6
  97.7 0.4 collective-permute-start.7
  98.1 0.1 collective-permute-start.8
  98.2 0.9 collective-permute-done.4.refs_20_
  99.1 0.8 copy-done.14
  99.9 0.1 collective-permute-start.9
  100.0 11.2 %exchange_3.1.refs_0_ = bf16[16,64,128]{2,1,0:T(8,128)(2,1)} custom-call(bf16[16,64,128]{2,1,0:T(8,128)(2,1)} %get-tuple-element.75.refs_0_), custom_call_target="tpu_custom_call" | custom-call | flops 17179869184 | bytes 33554432 | tf_op jit(solution)/shard_map/exchange_3/pallas_call | solution.py:329
  111.3 19.9 %middle.1 = (f32[128,1024]{1,0:T(8,128)}, f32[128,1024]{1,0:T(8,128)}, bf16[16,64,128]{2,1,0:T(8,128)(2,1)}, bf16[128,3072]{1,0:T(8,128)(2,1)}, bf16[128,2048]{1...) custom-call(bf16[16,64,128]{2,1,0:T(8,128)(2,1)} %exchange_3.1.refs_0_, ...), custom_call_target="tpu_custom_call" | custom-call | flops 10737418240 | bytes 33554432 | tf_op jit(solution)/shard_map/middle/pallas_call | solution.py:678
  131.2 11.2 %turn.1 = (bf16[16,64,128]{2,1,0:T(8,128)(2,1)}, bf16[2,160,1024]{2,1,0:T(8,128)(2,1)}, bf16[2,240,1024]{2,1,0:T(8,128)(2,1)}, bf16[2,240,1024]{2,1,0:T(8,128)(2...) custom-call(bf16[16,64,128]{2,1,0:T(8,128)(2,1)} %get-tuple-element.90.do, ...), custom_call_target="tpu_custom_call" | custom-call | flops 17179869184 | bytes 33554432 | tf_op jit(solution)/shard_map/turn/pallas_call | solution.py:774
  142.4 0.6 collective-permute-start.11
  143.0 2.7 collective-permute-start.12
  145.7 0.9 collective-permute-start.13
  146.6 2.4 collective-permute-start.14
  149.0 3.2 %collective-permute-start.10 = (bf16[128,3072]{1,0:T(8,128)(2,1)S(1)}, bf16[128,3072]{1,0:T(8,128)(2,1)S(1)}, u32[]{:S(2)}, u32[]{:S(2)}) collective-permute-start(bf16[128,3072]{1,0:T(8,128)(2,1)S(1)} %copy-done.4), channel_id=1, source_target_pairs={{0,2},{2,0},{1,3},{3,1},{4,6},{6,4},{5,7},{7,5},{8,10},{10,8},{9,1... | collective-permute-start | bytes 2359304 | tf_op jit(solution)/shard_map/ppermute | solution.py:1503
  152.2 27.4 %attend_back.1 = (bf16[32,128,128]{2,1,0:T(8,128)(2,1)}, bf16[16,64,128]{2,1,0:T(8,128)(2,1)}) custom-call(s32[64]{0:T(128)} %reshape.40.blk, s32[1,64,64]{2,1,0:T(8,128)} %mask.3, bf16[32,128,128]{2,1,0:T(8,128)(2,1)} %get-tuple-element.72.kvr, bf16[16,64,128]{2,1,0:T(8,128)(2,1)} %get-tuple-element.73.qr, bf16[16,64,128]{2,1,0:T(8,128)(2,1)} %get-tuple-element.97.dor, ...), custom_call_target="tpu_custom_call" | custom-call | flops 1073741824 | bytes 4194304 | tf_op jit(solution)/shard_map/attend_back/pallas_call | solution.py:546
  179.7 0.8 copy-done.5
  180.5 0.3 copy-done
  180.8 0.3 copy-done.1
  181.1 0.3 copy-done.2
  181.4 0.3 copy-done.3
  181.8 95.5 %finish.1 = (f32[128,1024]{1,0:T(8,128)}, bf16[1280,1024]{1,0:T(8,128)(2,1)}, bf16[1024,1024]{1,0:T(8,128)(2,1)}, bf16[768,1024]{1,0:T(8,128)(2,1)}, f32[8,256]{1,0:T(8,128)}) custom-call(bf16[32,128,128]{2,1,0:T(8,128)(2,1)} %get-tuple-element.101.refs_0_, bf16[16,64,128]{2,1,0:T(8,128)(2,1)} %get-tuple-element.102.refs_1_, ...), custom_call_target="tpu_custom_call" | custom-call | tf_op jit(solution)/shard_map/finish/pallas_call | solution.py:1422
  277.3 1.4 fusion
  278.7 8.4 %scaled.1 = (f32[256,1024]{1,0:T(8,128)}, f32[256,1024]{1,0:T(8,128)}, f32[256,1024]{1,0:T(8,128)}, f32[256,1024]{1,0:T(8,128)}, f32[256,4096]{1,0:T(8,128)}, /*index=5*/f32[1024,1024]{1,0:T(8,128)}) custom-call(bf16[1280,1024]{1,0:T(8,128)(2,1)} %get-tuple-element.116.o.i0.i1.i2.i3, bf16[1280,1024]{1,0:T(8,128)(2,1)} %get-tuple-element.116.o.i0.i1.i2.i3, ...), custom_call_target="tpu_custom_call" | custom-call | tf_op jit(solution)/shard_map/scaled/pallas_call | solution.py:1458
  287.1 0.8 copy.25
  (43 shorter events, 0.4 us)
Async XLA Ops:
  2.1 69.8 %copy-start.7 = (s32[32,2]{0,1:T(2,128)S(1)}, s32[32,2]{0,1:T(2,128)}, u32[]{:S(2)}) copy-start(s32[32,2]{0,1:T(2,128)} %param.22) | copy-start | bytes 772
  67.1 29.8 %collective-permute-start.1 = (bf16[9,32,1024]{2,1,0:T(8,128)(2,1)}, bf16[9,32,1024]{2,1,0:T(8,128)(2,1)S(1)}, u32[]{:S(2)}, u32[]{:S(2)}) collective-permute-start(bf16[9,32,1024]{2,1,0:T(8,128)(2,1)} %get-tuple-element.68.refs_11_), channel_id=1, source_target_pairs={{0,48},{4,52},{8,56},{12,60},{16,0},{20,4},{24,8},{28,12},{32,16},... | collective-permute-start | bytes 1769480 | tf_op jit(solution)/shard_map/ppermute | solution.py:1492
  69.9 27.1 %collective-permute-start = (bf16[9,32,1024]{2,1,0:T(8,128)(2,1)}, bf16[9,32,1024]{2,1,0:T(8,128)(2,1)S(1)}, u32[]{:S(2)}, u32[]{:S(2)}) collective-permute-start(bf16[9,32,1024]{2,1,0:T(8,128)(2,1)} %get-tuple-element.68.refs_11_), channel_id=1, source_target_pairs={{0,16},{4,20},{8,24},{12,28},{16,32},{20,36},{24,40},{28,44},{32,4... | collective-permute-start | bytes 1769480 | tf_op jit(solution)/shard_map/ppermute | solution.py:1492
  69.9 27.1 %collective-permute-start.3 = (bf16[9,32,1024]{2,1,0:T(8,128)(2,1)}, bf16[9,32,1024]{2,1,0:T(8,128)(2,1)S(1)}, u32[]{:S(2)}, u32[]{:S(2)}) collective-permute-start(bf16[9,32,1024]{2,1,0:T(8,128)(2,1)} %get-tuple-element.70.refs_15_), channel_id=1, source_target_pairs={{0,12},{4,0},{8,4},{12,8},{16,28},{20,16},{24,20},{28,24},{32,44},... | collective-permute-start | bytes 1769480 | tf_op jit(solution)/shard_map/ppermute | solution.py:1493
  71.3 25.7 %collective-permute-start.2 = (bf16[9,32,1024]{2,1,0:T(8,128)(2,1)}, bf16[9,32,1024]{2,1,0:T(8,128)(2,1)S(1)}, u32[]{:S(2)}, u32[]{:S(2)}) collective-permute-start(bf16[9,32,1024]{2,1,0:T(8,128)(2,1)} %get-tuple-element.70.refs_15_), channel_id=1, source_target_pairs={{0,4},{4,8},{8,12},{12,0},{16,20},{20,24},{24,28},{28,16},{32,36},... | collective-permute-start | bytes 1769480 | tf_op jit(solution)/shard_map/ppermute | solution.py:1493
  72.6 24.5 %copy-start.8 = (bf16[9,32,1024]{2,1,0:T(8,128)(2,1)S(1)}, bf16[9,32,1024]{2,1,0:T(8,128)(2,1)}, u32[]{:S(2)}) copy-start(bf16[9,32,1024]{2,1,0:T(8,128)(2,1)} %get-tuple-element.81.refs_13_) | copy-start | bytes 1769476
  72.6 25.5 %copy-start.9 = (bf16[9,32,1024]{2,1,0:T(8,128)(2,1)S(1)}, bf16[9,32,1024]{2,1,0:T(8,128)(2,1)}, u32[]{:S(2)}) copy-start(bf16[9,32,1024]{2,1,0:T(8,128)(2,1)} %get-tuple-element.84.refs_17_) | copy-start | bytes 1769476
  96.9 14.3 %copy-start.10 = (bf16[9,32,1024]{2,1,0:T(8,128)(2,1)}, bf16[9,32,1024]{2,1,0:T(8,128)(2,1)S(1)}, u32[]{:S(2)}) copy-start(bf16[9,32,1024]{2,1,0:T(8,128)(2,1)S(1)} %collective-permute-done.1.refs_14_) | copy-start | bytes 1769476
  96.9 14.3 %copy-start.11 = (bf16[9,32,1024]{2,1,0:T(8,128)(2,1)}, bf16[9,32,1024]{2,1,0:T(8,128)(2,1)S(1)}, u32[]{:S(2)}) copy-start(bf16[9,32,1024]{2,1,0:T(8,128)(2,1)S(1)} %collective-permute-done.refs_12_) | copy-start | bytes 1769476
  97.0 14.3 %copy-start.12 = (bf16[9,32,1024]{2,1,0:T(8,128)(2,1)}, bf16[9,32,1024]{2,1,0:T(8,128)(2,1)S(1)}, u32[]{:S(2)}) copy-start(bf16[9,32,1024]{2,1,0:T(8,128)(2,1)S(1)} %collective-permute-done.3.refs_18_) | copy-start | bytes 1769476
  97.0 14.3 %copy-start.13 = (bf16[9,32,1024]{2,1,0:T(8,128)(2,1)}, bf16[9,32,1024]{2,1,0:T(8,128)(2,1)S(1)}, u32[]{:S(2)}) copy-start(bf16[9,32,1024]{2,1,0:T(8,128)(2,1)S(1)} %collective-permute-done.2.refs_16_) | copy-start | bytes 1769476
  97.0 2.1 collective-permute-start.4
  97.1 14.2 %collective-permute-start.5 = (bf16[9,32,1024]{2,1,0:T(8,128)(2,1)S(1)}, bf16[9,32,1024]{2,1,0:T(8,128)(2,1)}, u32[]{:S(2)}, u32[]{:S(2)}) collective-permute-start(bf16[9,32,1024]{2,1,0:T(8,128)(2,1)S(1)} %copy-done.8), channel_id=1, source_target_pairs={{0,1},{1,0},{2,3},{3,2},{4,5},{5,4},{6,7},{7,6},{8,9},{9,8},{10,11... | collective-permute-start | bytes 1769480 | tf_op jit(solution)/shard_map/ppermute | solution.py:1497
  97.6 13.7 %collective-permute-start.6 = (bf16[9,32,1024]{2,1,0:T(8,128)(2,1)S(1)}, bf16[9,32,1024]{2,1,0:T(8,128)(2,1)}, u32[]{:S(2)}, u32[]{:S(2)}) collective-permute-start(bf16[9,32,1024]{2,1,0:T(8,128)(2,1)S(1)} %collective-permute-done.1.refs_14_), channel_id=1, source_target_pairs={{0,1},{1,0},{2,3},{3,2},{4,5},{5,4},{6,7},{7,6},{8,9},{9,8},{10,11... | collective-permute-start | bytes 1769480 | tf_op jit(solution)/shard_map/ppermute | solution.py:1497
  97.7 13.6 %collective-permute-start.7 = (bf16[9,32,1024]{2,1,0:T(8,128)(2,1)S(1)}, bf16[9,32,1024]{2,1,0:T(8,128)(2,1)}, u32[]{:S(2)}, u32[]{:S(2)}) collective-permute-start(bf16[9,32,1024]{2,1,0:T(8,128)(2,1)S(1)} %collective-permute-done.2.refs_16_), channel_id=1, source_target_pairs={{0,1},{1,0},{2,3},{3,2},{4,5},{5,4},{6,7},{7,6},{8,9},{9,8},{10,11... | collective-permute-start | bytes 1769480 | tf_op jit(solution)/shard_map/ppermute | solution.py:1497
  98.1 13.2 %collective-permute-start.8 = (bf16[9,32,1024]{2,1,0:T(8,128)(2,1)S(1)}, bf16[9,32,1024]{2,1,0:T(8,128)(2,1)}, u32[]{:S(2)}, u32[]{:S(2)}) collective-permute-start(bf16[9,32,1024]{2,1,0:T(8,128)(2,1)S(1)} %copy-done.9), channel_id=1, source_target_pairs={{0,1},{1,0},{2,3},{3,2},{4,5},{5,4},{6,7},{7,6},{8,9},{9,8},{10,11... | collective-permute-start | bytes 1769480 | tf_op jit(solution)/shard_map/ppermute | solution.py:1497
  99.1 0.8 copy-start.14
  99.9 11.4 %collective-permute-start.9 = (bf16[9,32,1024]{2,1,0:T(8,128)(2,1)S(1)}, bf16[9,32,1024]{2,1,0:T(8,128)(2,1)}, u32[]{:S(2)}, u32[]{:S(2)}) collective-permute-start(bf16[9,32,1024]{2,1,0:T(8,128)(2,1)S(1)} %collective-permute-done.3.refs_18_), channel_id=1, source_target_pairs={{0,1},{1,0},{2,3},{3,2},{4,5},{5,4},{6,7},{7,6},{8,9},{9,8},{10,11... | collective-permute-start | bytes 1769480 | tf_op jit(solution)/shard_map/ppermute | solution.py:1497
  131.2 17.8 %copy-start.4 = (bf16[128,3072]{1,0:T(8,128)(2,1)S(1)}, bf16[128,3072]{1,0:T(8,128)(2,1)}, u32[]{:S(2)}) copy-start(bf16[128,3072]{1,0:T(8,128)(2,1)} %get-tuple-element.89.refs_6_) | copy-start | bytes 2359300
  142.4 37.2 %collective-permute-start.11 = (bf16[2,240,1024]{2,1,0:T(8,128)(2,1)}, bf16[2,240,1024]{2,1,0:T(8,128)(2,1)S(1)}, u32[]{:S(2)}, u32[]{:S(2)}) collective-permute-start(bf16[2,240,1024]{2,1,0:T(8,128)(2,1)} %get-tuple-element.93), channel_id=1, source_target_pairs={{0,16},{4,20},{8,24},{12,28},{16,32},{20,36},{24,40},{28,44},{32,4... | collective-permute-start | bytes 2949128 | tf_op jit(solution)/shard_map/ppermute | solution.py:1505
  143.0 36.6 %collective-permute-start.12 = (bf16[2,240,1024]{2,1,0:T(8,128)(2,1)}, bf16[2,240,1024]{2,1,0:T(8,128)(2,1)S(1)}, u32[]{:S(2)}, u32[]{:S(2)}) collective-permute-start(bf16[2,240,1024]{2,1,0:T(8,128)(2,1)} %get-tuple-element.94), channel_id=1, source_target_pairs={{0,48},{4,52},{8,56},{12,60},{16,0},{20,4},{24,8},{28,12},{32,16},... | collective-permute-start | bytes 2949128 | tf_op jit(solution)/shard_map/ppermute | solution.py:1506
  145.7 33.9 %collective-permute-start.13 = (bf16[2,240,1024]{2,1,0:T(8,128)(2,1)}, bf16[2,240,1024]{2,1,0:T(8,128)(2,1)S(1)}, u32[]{:S(2)}, u32[]{:S(2)}) collective-permute-start(bf16[2,240,1024]{2,1,0:T(8,128)(2,1)} %get-tuple-element.95), channel_id=1, source_target_pairs={{0,4},{4,8},{8,12},{12,0},{16,20},{20,24},{24,28},{28,16},{32,36},... | collective-permute-start | bytes 2949128 | tf_op jit(solution)/shard_map/ppermute | solution.py:1507
  146.6 33.1 %collective-permute-start.14 = (bf16[2,240,1024]{2,1,0:T(8,128)(2,1)}, bf16[2,240,1024]{2,1,0:T(8,128)(2,1)S(1)}, u32[]{:S(2)}, u32[]{:S(2)}) collective-permute-start(bf16[2,240,1024]{2,1,0:T(8,128)(2,1)} %get-tuple-element.96), channel_id=1, source_target_pairs={{0,12},{4,0},{8,4},{12,8},{16,28},{20,16},{24,20},{28,24},{32,44},... | collective-permute-start | bytes 2949128 | tf_op jit(solution)/shard_map/ppermute | solution.py:1508
  149.0 30.6 %collective-permute-start.10 = (bf16[128,3072]{1,0:T(8,128)(2,1)S(1)}, bf16[128,3072]{1,0:T(8,128)(2,1)S(1)}, u32[]{:S(2)}, u32[]{:S(2)}) collective-permute-start(bf16[128,3072]{1,0:T(8,128)(2,1)S(1)} %copy-done.4), channel_id=1, source_target_pairs={{0,2},{2,0},{1,3},{3,1},{4,6},{6,4},{5,7},{7,5},{8,10},{10,8},{9,1... | collective-permute-start | bytes 2359304 | tf_op jit(solution)/shard_map/ppermute | solution.py:1503
  179.6 0.9 copy-start.5
  179.6 1.2 copy-start
  179.6 1.5 copy-start.1
  179.7 1.8 copy-start.2
  179.7 2.1 copy-start.3
  278.6 8.4 %copy-start.6 = (f32[128,1024]{1,0:T(8,128)S(1)}, f32[128,1024]{1,0:T(8,128)}, u32[]{:S(2)}) copy-start(f32[128,1024]{1,0:T(8,128)} %get-tuple-element.115) | copy-start | bytes 1572868

commit v7 on v6

--- a/solution.py
+++ b/solution.py
@@ -255,89 +255,6 @@
     )(tok, *own, tok, lnp, wo, wi, wu)
 
 
-def exchange(wide, narrow, collective):
-    has = wide is not None
-    n = 32 if has else 16
-
-    def kernel(*refs):
-        if has:
-            wi, na, wo, no, sw, rw, sn, rn, ls = refs
-        else:
-            na, no, sn, rn, ls = refs
-        me = lax.axis_index("ctx")
-        zl = me // 16
-        flat = me % 16
-        bar = pltpu.get_barrier_semaphore()
-
-        def peer(i):
-            if has:
-                return (me + i) % 32
-            return zl * 16 + (flat + i) % 16
-
-        def greet_one(i, carry):
-            pl.semaphore_signal(bar, inc=1, device_id={"ctx": peer(i)}, device_id_type=MESH)
-            return carry
-
-        lax.fori_loop(1, n, greet_one, 0)
-        pl.semaphore_wait(bar, n - 1)
-
-        def narrow_copy(i):
-            p = (flat + i) % 16
-            return pltpu.make_async_remote_copy(
-                src_ref=na.at[p], dst_ref=no.at[flat], send_sem=sn.at[i], recv_sem=rn.at[i],
-                device_id={"ctx": zl * 16 + p}, device_id_type=MESH,
-            )
-
-        def wide_copy(i):
-            p = (me + i) % 32
-            src = p if wide.shape[0] == 32 else p % 16
-            return pltpu.make_async_remote_copy(
-                src_ref=wi.at[src], dst_ref=wo.at[me], send_sem=sw.at[i], recv_sem=rw.at[i],
-                device_id={"ctx": p}, device_id_type=MESH,
-            )
-
-        def start(make):
-            def one(i, carry):
-                make(i).start()
-                return carry
-            return one
-
-        def wait(make):
-            def one(i, carry):
-                make(i).wait()
-                return carry
-            return one
-
-        if has:
-            lax.fori_loop(1, 32, start(wide_copy), 0)
-        lax.fori_loop(1, 16, start(narrow_copy), 0)
-        local = [pltpu.make_async_copy(na.at[flat], no.at[flat], ls.at[0])]
-        if has:
-            own = me if wide.shape[0] == 32 else flat
-            local.append(pltpu.make_async_copy(wi.at[own], wo.at[me], ls.at[1]))
-        for c in local:
-            c.start()
-        for c in local:
-            c.wait()
-        if has:
-            lax.fori_loop(1, 32, wait(wide_copy), 0)
-        lax.fori_loop(1, 16, wait(narrow_copy), 0)
-
-    sems = ([DMA((32,)), DMA((32,))] if has else []) + [DMA((16,)), DMA((16,)), DMA((2,))]
-    outs = ([shp((32,) + wide.shape[1:], wide.dtype)] if has else []) + [shp(narrow.shape, narrow.dtype)]
-    args = ([wide] if has else []) + [narrow]
-    return pl.pallas_call(
-        kernel,
-        out_shape=outs,
-        in_specs=[ANY] * len(args),
-        out_specs=[ANY] * len(outs),
-        scratch_shapes=sems,
-        compiler_params=pltpu.CompilerParams(collective_id=collective, has_side_effects=True),
-        cost_estimate=pl.CostEstimate(flops=16 << 30, bytes_accessed=32 << 20, transcendentals=0),
-        name=f"exchange_{collective}",
-    )(*args)
-
-
 def attention_setup(blk, mask, kvr, qr, kvs, kaug, kvt, bias, qs, inv, order, oblk):
     first = (lax.axis_index("ctx") // 16) * 32
 
@@ -572,15 +489,30 @@
     return r * (g - jnp.mean(g, axis=1, keepdims=True) - z * jnp.mean(g * z, axis=1, keepdims=True))
 
 
-def middle_kernel(*refs):
+def heart_kernel(*refs):
     o_ref, x_ref, e_ref, ln_ref, ln_own = refs[:5]
     shards = (refs[5:8], refs[8:11])
-    pieces = (refs[11:19], refs[19:27])
-    y_ref, dr_ref, do_ref, zpay, gpay, cpay, lown, gb_ref = refs[27:35]
-    wo, wi, wu, us, gs, nl, ob, sw, sp = refs[35:]
+    parts, diag_a, diag_b = refs[11:19], refs[19], refs[20]
+    y_ref, dr_ref, zpay, gpay, gb_ref, dor = refs[21:27]
+    cuts = (refs[27:30], refs[30:33])
+    (wo, wi, wu, us, gs, nl, ob, orx, dos, rr, ll, cl, lt, mid,
+     sw, sp, ss, rs, send_o, recv_o, send_do, recv_do, ls, lo) = refs[33:]
     zl, x, y, zh, co = place()
     w = zh * 2 + co
+    flat = lax.axis_index("ctx") % 16
     where = [w, zh * 2 + 1 - co, (1 - zh) * 2 + co, (1 - zh) * 2 + 1 - co]
+    core = device(zl, x, y, zh, 1 - co)
+    bar = pltpu.get_barrier_semaphore()
+
+    def plane(i):
+        return {"ctx": zl * 16 + (flat + i) % 16}
+
+    def greet_one(i, carry):
+        pl.semaphore_signal(bar, inc=1, device_id=plane(i), device_id_type=MESH)
+        return carry
+
+    pl.semaphore_signal(bar, inc=1, device_id=core, device_id_type=MESH)
+    lax.fori_loop(1, 16, greet_one, 0)
     copies = [[], [], []]
     for r, (a, b, c) in enumerate(shards):
         rows = pl.ds(pl.multiple_of(where[r] * 256, 256), 256)
@@ -590,32 +522,71 @@
             copies[1].append(pltpu.make_async_copy(b.at[:, cols], wi.at[k, rows], sw.at[r, 1 + k]))
         groups = pl.ds(where[r] * 8, 8)
         copies[2].append(pltpu.make_async_copy(c, wu.at[groups], sw.at[r, 5]))
-    for r, parts in enumerate(pieces):
-        t = where[2 + r]
-        quarters = [(parts[s], 0, (x + 4 - s) % 4) for s in range(4)]
-        quarters += [(parts[4 + s], 1, (y + 4 - s) % 4) for s in range(4)]
-        for n, (ref, h, q) in enumerate(quarters):
-            rows = pl.ds(pl.multiple_of(t * 256 + h * 128 + q * 32, 32), 32)
-            copies[0].append(pltpu.make_async_copy(ref.at[0], wo.at[rows], sp.at[r, n, 0]))
-            copies[1].append(pltpu.make_async_copy(ref.at[1:5], wi.at[:, rows], sp.at[r, n, 1]))
-            copies[2].append(pltpu.make_async_copy(ref.at[5:9], wu.at[t * 8 + h * 4 + q], sp.at[r, n, 2]))
+
+    def spots(t, h, q):
+        rows = pl.ds(pl.multiple_of(t * 256 + h * 128 + q * 32, 32), 32)
+        return wo.at[rows], wi.at[:, rows], wu.at[t * 8 + h * 4 + q]
+
+    quarters = [(parts[s], 0, (x + 4 - s) % 4) for s in range(4)]
+    quarters += [(parts[4 + s], 1, (y + 4 - s) % 4) for s in range(4)]
+    held = [(where[2],) + q for q in quarters] + [(where[3], diag_a, 0, x), (where[3], diag_b, 1, y)]
+    for n, (t, ref, h, q) in enumerate(held):
+        to = spots(t, h, q)
+        for k, src in enumerate((ref.at[0], ref.at[1:5], ref.at[5:9])):
+            copies[k].append(pltpu.make_async_copy(src, to[k], sp.at[n, k]))
     for group in copies:
         for c in group:
             c.start()
-
+    pl.semaphore_wait(bar, 16)
+    wire = Wire(ss, rs)
+
+    def over(src, dst, send, recv):
+        def copy(i):
+            return pltpu.make_async_remote_copy(
+                src_ref=src.at[(flat + i) % 16], dst_ref=dst.at[flat], send_sem=send.at[i], recv_sem=recv.at[i],
+                device_id=plane(i), device_id_type=MESH,
+            )
+
+        def start_one(i, carry):
+            copy(i).start()
+            return carry
+
+        def wait_one(i, carry):
+            copy(i).wait()
+            return carry
+
+        return start_one, wait_one
+
+    start_o, wait_o = over(o_ref, orx, send_o, recv_o)
+    lax.fori_loop(1, 16, start_o, 0)
+    home = pltpu.make_async_copy(o_ref.at[flat], orx.at[flat], ls.at[0])
+    home.start()
+    shared = [[], [], []]
+    for k in range(3):
+        for n in (1, 2, 3, 5, 6, 7):
+            ref, h, q = quarters[n]
+            src = (ref.at[0], ref.at[1:5], ref.at[5:9])[k]
+            shared[k].append(wire(src, spots(where[2], h, q)[k], core))
+
+    def loaded(k):
+        for c in copies[k]:
+            c.wait()
+        for c in shared[k]:
+            c.wait_recv()
+
+    home.wait()
+    lax.fori_loop(1, 16, wait_o, 0)
     ln = jnp.concatenate([jnp.where(w == k, ln_own[...], ln_ref[k]) for k in range(4)], axis=1)
     gain0, gain1, bias0, bias1 = (ln[k:k + 1, :] for k in range(4))
     for h in range(16):
-        pair = o_ref[h]
+        pair = orx[h]
         ob[:64, 64 * h:64 * h + 64] = pair[:, :64]
         ob[64:, 64 * h:64 * h + 64] = pair[:, 64:]
-    for c in copies[0]:
-        c.wait()
+    loaded(0)
     z0, r0 = norm_parts(x_ref[...].astype(F32) + dot(ob[...], wo[...]))
     n1 = z0 * gain0 + bias0
     nl[...] = n1.astype(BF)
-    for c in copies[1]:
-        c.wait()
+    loaded(1)
 
     half = math.sqrt(0.5)
 
@@ -626,8 +597,7 @@
         return carry
 
     lax.fori_loop(0, 4, up, 0)
-    for c in copies[2]:
-        c.wait()
+    loaded(2)
 
     def down(c, total):
         cols = pl.ds(pl.multiple_of(c * 1024, 1024), 1024)
@@ -643,115 +613,54 @@
     gb_ref[3:4, :] = jnp.sum(e, axis=0, keepdims=True)
 
     def back(c, total):
-        rows = pl.ds(pl.multiple_of(c * 1024, 1024), 1024)
         u = us[c]
         dg = dot(dm, wu[pl.ds(c * 8, 8)].reshape(1024, 1024), NT)
         slope = 0.5 * (1.0 + lax.erf(u * half)) + u * (jnp.exp(-0.5 * u * u) * (1.0 / math.sqrt(2 * math.pi)))
         du = (dg * slope).astype(BF)
-        cpay[:, rows] = du
+        rr[0:128, 1024 * c:1024 * c + 1024] = du
         return total + dot(du, wi[c], NT)
 
-    dn1 = lax.fori_loop(0, 4, back, dr2)
+    few = [pl.ds(pl.multiple_of(where[r] * 256, 256), 256) for r in range(4)]
+    many = [pl.ds(pl.multiple_of(where[r] * 1024, 1024), 1024) for r in range(4)]
+    for ref, rows, at, r in ((ll, 128, 0, 0), (ll, 128, 512, 2), (cl, 128, 0, 1), (cl, 128, 512, 3)):
+        ref[:rows, at:at + 256] = nl[:, few[r]]
+        ref[:rows, at + 256:at + 512] = ob[:, few[r]]
+    near = [wire(cl, ll.at[128:256, :], core)]
+    dn1 = dr2
+    for c in range(4):
+        dn1 = back(c, dn1)
+        cols = slice(1024 * c, 1024 * c + 1024)
+        near.append(wire(rr.at[0:128, cols], rr.at[128:256, cols], core))
     gb_ref[0:1, :] = jnp.sum(dn1 * z0, axis=0, keepdims=True)
     gb_ref[2:3, :] = jnp.sum(dn1, axis=0, keepdims=True)
     gb_ref[4:8, :] = jnp.zeros((4, 1024), F32)
     dr1 = norm_back(dn1, gain0, z0, r0)
     dr_ref[...] = dr1
     da = dr1.astype(BF)
+    rr[0:128, 4096:5120] = da
+    near.append(wire(rr.at[0:128, 4096:5120], rr.at[128:256, 4096:5120], core))
     do = dot(da, wo[...], NT).astype(BF)
     for h in range(16):
         lanes = slice(64 * h, 64 * h + 64)
-        do_ref[h] = jnp.concatenate([do[:64, lanes], do[64:, lanes]], axis=1)
-    cpay[:, 4096:5120] = da
+        dos[h] = jnp.concatenate([do[:64, lanes], do[64:, lanes]], axis=1)
+    start_do, wait_do = over(dos, dor, send_do, recv_do)
+    lax.fori_loop(1, 16, start_do, 0)
+    home = pltpu.make_async_copy(dos.at[flat], dor.at[flat], ls.at[1])
+    home.start()
     zpay[:, 1024:2048] = dm
-    for r, (ref, at, gref, gat) in enumerate((
-        (lown, 0, gpay, 0), (cpay, 5120, gpay, 1024), (lown, 512, zpay, 0), (cpay, 5632, zpay, 2048)
-    )):
-        few = pl.ds(pl.multiple_of(where[r] * 256, 256), 256)
-        many = pl.ds(pl.multiple_of(where[r] * 1024, 1024), 1024)
-        ref[:, at:at + 256] = nl[:, few]
-        ref[:, at + 256:at + 512] = ob[:, few]
-        gref[:, gat:gat + 1024] = gs[:, many]
-
-
-def middle(o, tok, cot, lnf, lnp, shards, pieces):
-    return pl.pallas_call(
-        middle_kernel,
-        out_shape=[
-            shp((128, 1024), F32), shp((128, 1024), F32), shp((16, 64, 128), BF),
-            shp((128, 3072), BF), shp((128, 2048), BF), shp((128, 6144), BF), shp((128, 1024), BF), shp((8, 1024), F32),
-        ],
-        in_specs=[VM] * 5 + [ANY] * 22,
-        out_specs=[VM] * 8,
-        scratch_shapes=[
-            pltpu.VMEM((1024, 1024), BF),
-            pltpu.VMEM((4, 1024, 1024), BF),
-            pltpu.VMEM((32, 4, 32, 1024), BF),
-            pltpu.VMEM((4, 128, 1024), F32),
-            pltpu.VMEM((128, 4096), BF),
-            pltpu.VMEM((128, 1024), BF),
-            pltpu.VMEM((128, 1024), BF),
-            DMA((2, 6)), DMA((2, 8, 3)),
-        ],
-        compiler_params=pltpu.CompilerParams(vmem_limit_bytes=LIMIT),
-        cost_estimate=pl.CostEstimate(flops=10 << 30, bytes_accessed=32 << 20, transcendentals=2 << 20),
-        name="middle",
-    )(o, tok, cot, lnf, lnp, *shards[0], *shards[1], *pieces[0], *pieces[1])
-
-
-def turn_kernel(do, cpay, lown, dor, own_a, plus_a, minus_a, own_b, plus_b, minus_b, rr, ll, lt, mid, sn, rn, ss, rs, ls, lo):
-    zl, x, y, zh, co = place()
-    flat = lax.axis_index("ctx") % 16
-    core = device(zl, x, y, zh, 1 - co)
-    bar = pltpu.get_barrier_semaphore()
-
-    def greet_one(i, carry):
-        pl.semaphore_signal(bar, inc=1, device_id={"ctx": zl * 16 + (flat + i) % 16}, device_id_type=MESH)
-        return carry
-
-    pl.semaphore_signal(bar, inc=1, device_id=core, device_id_type=MESH)
-    lax.fori_loop(1, 16, greet_one, 0)
-    local = [
-        pltpu.make_async_copy(cpay.at[:, :5120], rr.at[0:128, :], ls.at[0]),
-        pltpu.make_async_copy(lown, ll.at[0:128, :], ls.at[1]),
-    ]
-    for c in local:
-        c.start()
-    pl.semaphore_wait(bar, 16)
-
-    def narrow_copy(i):
-        p = (flat + i) % 16
-        return pltpu.make_async_remote_copy(
-            src_ref=do.at[p], dst_ref=dor.at[flat], send_sem=sn.at[i], recv_sem=rn.at[i],
-            device_id={"ctx": zl * 16 + p}, device_id_type=MESH,
-        )
-
-    def start_one(i, carry):
-        narrow_copy(i).start()
-        return carry
-
-    def wait_one(i, carry):
-        narrow_copy(i).wait()
-        return carry
-
-    wire = Wire(ss, rs)
-    near = [wire(cpay.at[:, 5120:], ll.at[128:256, :], core), wire(cpay.at[:, :5120], rr.at[128:256, :], core)]
-    lax.fori_loop(1, 16, start_one, 0)
-    home = pltpu.make_async_copy(do.at[flat], dor.at[flat], ls.at[2])
-    home.start()
-    for c in local:
-        c.wait()
+    for r, (ref, at) in enumerate(((gpay, 0), (gpay, 1024), (zpay, 0), (zpay, 2048))):
+        ref[:, at:at + 1024] = gs[:, many[r]]
     for c in near:
-        c.wait()
+        c.wait_recv()
     for k in range(4):
         lt[256 * k:256 * k + 256, :] = ll[:, 256 * k:256 * k + 256].astype(F32).T.astype(BF)
+    out = []
     for z in range(2):
         mid[z, 0:256, :] = dot(lt[512 * z + 256:512 * z + 512, :], rr[:, 4096:5120]).astype(BF)
         for k in range(4):
             rows = slice(256 + 256 * k, 512 + 256 * k)
             mid[z, rows, :] = dot(lt[512 * z:512 * z + 256, :], rr[:, 1024 * k:1024 * k + 1024]).astype(BF)
-    out = []
-    for h, (at, own, plus, minus) in enumerate(((x, own_a, plus_a, minus_a), (y, own_b, plus_b, minus_b))):
+    for h, (at, (own, plus, minus)) in enumerate(zip((x, y), cuts)):
 
         def rows(s, first, size):
             return pl.ds(pl.multiple_of(h * 640 + (at + s) % 4 * 160 + first, 16), size)
@@ -765,26 +674,49 @@
     for c in out:
         c.start()
     home.wait()
-    lax.fori_loop(1, 16, wait_one, 0)
+    lax.fori_loop(1, 16, wait_do, 0)
+    for c in near:
+        c.wait_send()
+    for group in shared:
+        for c in group:
+            c.wait_send()
     for c in out:
         c.wait()
 
 
-def turn(do, cpay, lown):
+def heart(o, tok, cot, lnf, lnp, shards, parts, diag_a, diag_b):
+    cut = [shp((2, 160, 1024), BF), shp((2, 240, 1024), BF), shp((2, 240, 1024), BF)]
+    n = 18 + 6
     return pl.pallas_call(
-        turn_kernel,
-        out_shape=[shp(do.shape, BF)] + [shp((2, 160, 1024), BF), shp((2, 240, 1024), BF), shp((2, 240, 1024), BF)] * 2,
-        in_specs=[ANY] * 3,
-        out_specs=[ANY] * 7,
+        heart_kernel,
+        out_shape=[
+            shp((128, 1024), F32), shp((128, 1024), F32),
+            shp((128, 3072), BF), shp((128, 2048), BF), shp((8, 1024), F32), shp((16, 64, 128), BF),
+        ] + cut + cut,
+        in_specs=[ANY] + [VM] * 4 + [ANY] * 16,
+        out_specs=[VM] * 5 + [ANY] * 7,
         scratch_shapes=[
-            pltpu.VMEM((256, 5120), BF), pltpu.VMEM((256, 1024), BF), pltpu.VMEM((1024, 256), BF),
+            pltpu.VMEM((1024, 1024), BF),
+            pltpu.VMEM((4, 1024, 1024), BF),
+            pltpu.VMEM((32, 4, 32, 1024), BF),
+            pltpu.VMEM((4, 128, 1024), F32),
+            pltpu.VMEM((128, 4096), BF),
+            pltpu.VMEM((128, 1024), BF),
+            pltpu.VMEM((128, 1024), BF),
+            pltpu.VMEM((16, 64, 128), BF),
+            pltpu.VMEM((16, 64, 128), BF),
+            pltpu.VMEM((256, 5120), BF),
+            pltpu.VMEM((256, 1024), BF),
+            pltpu.VMEM((128, 1024), BF),
+            pltpu.VMEM((1024, 256), BF),
             pltpu.VMEM((2, 1280, 1024), BF),
-            DMA((16,)), DMA((16,)), DMA((2,)), DMA((2,)), DMA((3,)), DMA((10,)),
+            DMA((2, 6)), DMA((10, 3)), DMA((n,)), DMA((n,)), DMA((16,)), DMA((16,)), DMA((16,)), DMA((16,)),
+            DMA((2,)), DMA((10,)),
         ],
         compiler_params=pltpu.CompilerParams(collective_id=5, has_side_effects=True, vmem_limit_bytes=LIMIT),
-        cost_estimate=pl.CostEstimate(flops=16 << 30, bytes_accessed=32 << 20, transcendentals=0),
-        name="turn",
-    )(do, cpay, lown)
+        cost_estimate=pl.CostEstimate(flops=16 << 30, bytes_accessed=32 << 20, transcendentals=2 << 20),
+        name="heart",
+    )(o, tok, cot, lnf, lnp, *shards[0], *shards[1], *parts, diag_a, diag_b)
 
 
 class Spread:
@@ -1494,14 +1426,10 @@
     o, ot, lse = attend(blk, block_mask, kvr, qr)
     x1, x2, x3, y1, y2, y3, o = lax.optimization_barrier((x1, x2, x3, y1, y2, y3, o))
     far = [qa, x1, x2, x3, qb, y1, y2, y3]
-    d1, d2, d3, e1, e2, e3 = (lax.ppermute(p, "wsh", FLIP_CORE) for p in (x1, x2, x3, y1, y2, y3))
-    diag = [diag_a, d1, d2, d3, diag_b, e1, e2, e3]
-    (o_back,) = exchange(None, o, 3)
-    y_out, dr1, do, zpay, gpay, cpay, lown, gb = middle(
-        o_back, tok, cot, lnf, lnp, ((w_output, w_inner, outer), core_shard), (far, diag)
+    y_out, dr1, zpay, gpay, gb, dor, own_a, plus_a, minus_a, own_b, plus_b, minus_b = heart(
+        o, tok, cot, lnf, lnp, ((w_output, w_inner, outer), core_shard), far, diag_a, diag_b
     )
     zr = lax.ppermute(zpay, "wsh", FLIP_FAR)
-    dor, own_a, plus_a, minus_a, own_b, plus_b, minus_b = turn(do, cpay, lown)
     plus_a = lax.ppermute(plus_a, "ctx", along_x(1))
     minus_a = lax.ppermute(minus_a, "ctx", along_x(3))
     plus_b = lax.ppermute(plus_b, "ctx", along_y(1))

time: 288 us -> 276 us (0.958)
  Pallas kernels: 263 us -> 252 us
    pallas_call x3 -> x1, Pallas kernels: 42.3 us -> 32.1 us  [heart(): pl.pallas_call(heart_kernel, out_shape=[shp((128, 1024), F32), shp((128,...]
  transfers between devices with their start and end apart: 15 -> 9, of which waited for: 1 -> 0; matrix products, arithmetic and copies ran while one was open for 0% -> 0% of each run, Pallas kernels for 22% -> 19%
where the time goes in v7:
time: 276 us; the launch traced here: 275 us
  Pallas kernels  252 us (91%)
  starting transfers between devices  14.6 us (5%)
  local copies, waits for them, and re-layouts  7.17 us (3%)
    pallas_call x1, Pallas kernels, finish(): pl.pallas_call(finish_kernel, out_shape=[shp((128, 1024), F32), shp((1280...  93.7 us
    pallas_call x1, Pallas kernels, front(): pl.pallas_call(front_kernel, out_shape=[shp((4, 3, 256, 1024), BF), shp((...  65 us
    pallas_call x1, Pallas kernels, heart(): pl.pallas_call(heart_kernel, out_shape=[shp((128, 1024), F32), shp((128,...  32.1 us
    pallas_call x1, Pallas kernels, attend_back(): pl.pallas_call(attend_back_kernel, out_shape=[shp((32, 128, 128), BF), sh...  27.8 us
    pallas_call x1, Pallas kernels, attend(): pl.pallas_call(attend_kernel, out_shape=[shp((16, 64, 128), BF), shp((8,...  24.5 us
    pallas_call x1, Pallas kernels, scaled(): pl.pallas_call(scale_kernel, grid=(8,), out_shape=[shp((256, 1024), F32)]...  8.45 us
  transfers between devices with their start and end apart: 9, of which 0 were waited for; matrix products, arithmetic and copies ran while one was open for 0% of the time, Pallas kernels for 19%

profile of v7, /device:TPU:0, one launch (start us, length us, event | category | flops | bytes accessed | tf_op | source)
XLA Modules:
  0.0 275.5 jit_solution(14628896136435414725)
XLA Ops:
  0.7 0.1 pad.2.clone
  0.7 1.4 maximum_maximum_fusion.refs_5_.refs_4_
  2.1 65.0 %front.1 = (bf16[4,3,256,1024]{3,2,1,0:T(8,128)(2,1)}, bf16[2,128,256]{2,1,0:T(8,128)(2,1)}, f32[4,8,256]{2,1,0:T(8,128)}, bf16[256,1024]{1,0:T(8,128)(2,1)}, bf...) custom-call(bf16[128,1024]{1,0:T(8,128)(2,1)} %bitcast.7, ...), custom_call_target="tpu_custom_call" | custom-call | flops 17179869184 | bytes 33554432 | tf_op jit(solution)/shard_map/front/pallas_call | solution.py:240
  67.1 2.8 %collective-permute-start.1 = (bf16[9,32,1024]{2,1,0:T(8,128)(2,1)}, bf16[9,32,1024]{2,1,0:T(8,128)(2,1)S(1)}, u32[]{:S(2)}, u32[]{:S(2)}) collective-permute-start(bf16[9,32,1024]{2,1,0:T(8,128)(2,1)} %get-tuple-element.65.refs_11_), channel_id=1, source_target_pairs={{0,48},{4,52},{8,56},{12,60},{16,0},{20,4},{24,8},{28,12},{32,16},... | collective-permute-start | bytes 1769480 | tf_op jit(solution)/shard_map/ppermute | solution.py:1424
  69.9 1.4 collective-permute-start.3
  71.3 0.6 collective-permute-start.2
  71.9 0.1 copy.23
  72.0 0.6 reshape.40.blk
  72.6 24.5 %attend.1 = (bf16[16,64,128]{2,1,0:T(8,128)(2,1)}, f32[8,64,256]{2,1,0:T(8,128)}, f32[8,1,256]{2,1,0:T(1,128)}) custom-call(s32[64]{0:T(128)} %reshape.40.blk, s32[1,64,64]{2,1,0:T(8,128)} %mask.3, bf16[32,128,128]{2,1,0:T(8,128)(2,1)} %get-tuple-element.69.kvr, bf16[16,64,128]{2,1,0:T(8,128)(2,1)} %get-tuple-element.70.qr), custom_call_target="tpu_custom_call" | custom-call | flops 10737418240 | bytes 33554432 | tf_op jit(solution)/shard_map/attend/pallas_call | solution.py:378
  97.1 0.0 copy-start.10
  97.2 0.7 copy-done.8
  97.9 0.2 copy-done.9
  98.1 0.2 copy-done.10
  98.3 0.2 copy-done.11
  98.5 32.1 %heart.1 = (f32[128,1024]{1,0:T(8,128)}, f32[128,1024]{1,0:T(8,128)}, bf16[128,3072]{1,0:T(8,128)(2,1)}, bf16[128,2048]{1,0:T(8,128)(2,1)}, f32[8,1024]{1,0:T(8,...) custom-call(bf16[16,64,128]{2,1,0:T(8,128)(2,1)} %get-tuple-element., ...), custom_call_target="tpu_custom_call" | custom-call | flops 17179869184 | bytes 33554432 | tf_op jit(solution)/shard_map/heart/pallas_call | solution.py:690
  130.6 0.1 collective-permute-start.5
  130.7 3.2 %collective-permute-start.6 = (bf16[2,240,1024]{2,1,0:T(8,128)(2,1)}, bf16[2,240,1024]{2,1,0:T(8,128)(2,1)S(1)}, u32[]{:S(2)}, u32[]{:S(2)}) collective-permute-start(bf16[2,240,1024]{2,1,0:T(8,128)(2,1)} %get-tuple-element.88), channel_id=1, source_target_pairs={{0,48},{4,52},{8,56},{12,60},{16,0},{20,4},{24,8},{28,12},{32,16},... | collective-permute-start | bytes 2949128 | tf_op jit(solution)/shard_map/ppermute | solution.py:1434
  133.9 1.0 collective-permute-start.7
  134.9 2.3 collective-permute-start.8
  137.1 3.2 %collective-permute-start.4 = (bf16[128,3072]{1,0:T(8,128)(2,1)}, bf16[128,3072]{1,0:T(8,128)(2,1)S(1)}, u32[]{:S(2)}, u32[]{:S(2)}) collective-permute-start(bf16[128,3072]{1,0:T(8,128)(2,1)} %get-tuple-element.86.refs_6_), channel_id=1, source_target_pairs={{0,2},{2,0},{1,3},{3,1},{4,6},{6,4},{5,7},{7,5},{8,10},{10,8},{9,1... | collective-permute-start | bytes 2359304 | tf_op jit(solution)/shard_map/ppermute | solution.py:1432
  140.3 27.8 %attend_back.1 = (bf16[32,128,128]{2,1,0:T(8,128)(2,1)}, bf16[16,64,128]{2,1,0:T(8,128)(2,1)}) custom-call(s32[64]{0:T(128)} %reshape.40.blk, s32[1,64,64]{2,1,0:T(8,128)} %mask.3, bf16[32,128,128]{2,1,0:T(8,128)(2,1)} %get-tuple-element.69.kvr, bf16[16,64,128]{2,1,0:T(8,128)(2,1)} %get-tuple-element.70.qr, bf16[16,64,128]{2,1,0:T(8,128)(2,1)} %get-tuple-element.91.dor, ...), custom_call_target="tpu_custom_call" | custom-call | flops 1073741824 | bytes 4194304 | tf_op jit(solution)/shard_map/attend_back/pallas_call | solution.py:463
  168.2 0.0 copy-start
  168.3 0.8 copy-done.4
  169.0 0.3 copy-done
  169.4 0.3 copy-done.1
  169.7 0.3 copy-done.2
  170.0 0.3 copy-done.3
  170.3 93.7 %finish.1 = (f32[128,1024]{1,0:T(8,128)}, bf16[1280,1024]{1,0:T(8,128)(2,1)}, bf16[1024,1024]{1,0:T(8,128)(2,1)}, bf16[768,1024]{1,0:T(8,128)(2,1)}, f32[8,256]{1,0:T(8,128)}) custom-call(bf16[32,128,128]{2,1,0:T(8,128)(2,1)} %get-tuple-element.95.refs_0_, bf16[16,64,128]{2,1,0:T(8,128)(2,1)} %get-tuple-element.96.refs_1_, ...), custom_call_target="tpu_custom_call" | custom-call | tf_op jit(solution)/shard_map/finish/pallas_call | solution.py:1354
  264.0 1.4 fusion
  265.4 8.4 %scaled.1 = (f32[256,1024]{1,0:T(8,128)}, f32[256,1024]{1,0:T(8,128)}, f32[256,1024]{1,0:T(8,128)}, f32[256,1024]{1,0:T(8,128)}, f32[256,4096]{1,0:T(8,128)}, /*index=5*/f32[1024,1024]{1,0:T(8,128)}) custom-call(bf16[1280,1024]{1,0:T(8,128)(2,1)} %get-tuple-element.110.o.i0.i1.i2.i3, bf16[1280,1024]{1,0:T(8,128)(2,1)} %get-tuple-element.110.o.i0.i1.i2.i3, ...), custom_call_target="tpu_custom_call" | custom-call | tf_op jit(solution)/shard_map/scaled/pallas_call | solution.py:1390
  273.9 0.8 copy.26
  274.7 0.8 copy.27
  (24 shorter events, 0.1 us)
Async XLA Ops:
  2.1 69.8 %copy-start.7 = (s32[32,2]{0,1:T(2,128)S(1)}, s32[32,2]{0,1:T(2,128)}, u32[]{:S(2)}) copy-start(s32[32,2]{0,1:T(2,128)} %param.22) | copy-start | bytes 772
  67.1 30.0 %collective-permute-start.1 = (bf16[9,32,1024]{2,1,0:T(8,128)(2,1)}, bf16[9,32,1024]{2,1,0:T(8,128)(2,1)S(1)}, u32[]{:S(2)}, u32[]{:S(2)}) collective-permute-start(bf16[9,32,1024]{2,1,0:T(8,128)(2,1)} %get-tuple-element.65.refs_11_), channel_id=1, source_target_pairs={{0,48},{4,52},{8,56},{12,60},{16,0},{20,4},{24,8},{28,12},{32,16},... | collective-permute-start | bytes 1769480 | tf_op jit(solution)/shard_map/ppermute | solution.py:1424
  69.9 27.2 %collective-permute-start = (bf16[9,32,1024]{2,1,0:T(8,128)(2,1)}, bf16[9,32,1024]{2,1,0:T(8,128)(2,1)S(1)}, u32[]{:S(2)}, u32[]{:S(2)}) collective-permute-start(bf16[9,32,1024]{2,1,0:T(8,128)(2,1)} %get-tuple-element.65.refs_11_), channel_id=1, source_target_pairs={{0,16},{4,20},{8,24},{12,28},{16,32},{20,36},{24,40},{28,44},{32,4... | collective-permute-start | bytes 1769480 | tf_op jit(solution)/shard_map/ppermute | solution.py:1424
  69.9 27.3 %collective-permute-start.3 = (bf16[9,32,1024]{2,1,0:T(8,128)(2,1)}, bf16[9,32,1024]{2,1,0:T(8,128)(2,1)S(1)}, u32[]{:S(2)}, u32[]{:S(2)}) collective-permute-start(bf16[9,32,1024]{2,1,0:T(8,128)(2,1)} %get-tuple-element.67.refs_15_), channel_id=1, source_target_pairs={{0,12},{4,0},{8,4},{12,8},{16,28},{20,16},{24,20},{28,24},{32,44},... | collective-permute-start | bytes 1769480 | tf_op jit(solution)/shard_map/ppermute | solution.py:1425
  71.3 25.9 %collective-permute-start.2 = (bf16[9,32,1024]{2,1,0:T(8,128)(2,1)}, bf16[9,32,1024]{2,1,0:T(8,128)(2,1)S(1)}, u32[]{:S(2)}, u32[]{:S(2)}) collective-permute-start(bf16[9,32,1024]{2,1,0:T(8,128)(2,1)} %get-tuple-element.67.refs_15_), channel_id=1, source_target_pairs={{0,4},{4,8},{8,12},{12,0},{16,20},{20,24},{24,28},{28,16},{32,36},... | collective-permute-start | bytes 1769480 | tf_op jit(solution)/shard_map/ppermute | solution.py:1425
  97.1 0.8 copy-start.8
  97.1 1.0 copy-start.9
  97.1 1.2 copy-start.10
  97.2 1.3 copy-start.11
  130.6 37.6 %collective-permute-start.5 = (bf16[2,240,1024]{2,1,0:T(8,128)(2,1)}, bf16[2,240,1024]{2,1,0:T(8,128)(2,1)S(1)}, u32[]{:S(2)}, u32[]{:S(2)}) collective-permute-start(bf16[2,240,1024]{2,1,0:T(8,128)(2,1)} %get-tuple-element.87), channel_id=1, source_target_pairs={{0,16},{4,20},{8,24},{12,28},{16,32},{20,36},{24,40},{28,44},{32,4... | collective-permute-start | bytes 2949128 | tf_op jit(solution)/shard_map/ppermute | solution.py:1433
  130.7 37.5 %collective-permute-start.6 = (bf16[2,240,1024]{2,1,0:T(8,128)(2,1)}, bf16[2,240,1024]{2,1,0:T(8,128)(2,1)S(1)}, u32[]{:S(2)}, u32[]{:S(2)}) collective-permute-start(bf16[2,240,1024]{2,1,0:T(8,128)(2,1)} %get-tuple-element.88), channel_id=1, source_target_pairs={{0,48},{4,52},{8,56},{12,60},{16,0},{20,4},{24,8},{28,12},{32,16},... | collective-permute-start | bytes 2949128 | tf_op jit(solution)/shard_map/ppermute | solution.py:1434
  133.9 34.3 %collective-permute-start.7 = (bf16[2,240,1024]{2,1,0:T(8,128)(2,1)}, bf16[2,240,1024]{2,1,0:T(8,128)(2,1)S(1)}, u32[]{:S(2)}, u32[]{:S(2)}) collective-permute-start(bf16[2,240,1024]{2,1,0:T(8,128)(2,1)} %get-tuple-element.89), channel_id=1, source_target_pairs={{0,4},{4,8},{8,12},{12,0},{16,20},{20,24},{24,28},{28,16},{32,36},... | collective-permute-start | bytes 2949128 | tf_op jit(solution)/shard_map/ppermute | solution.py:1435
  134.9 33.4 %collective-permute-start.8 = (bf16[2,240,1024]{2,1,0:T(8,128)(2,1)}, bf16[2,240,1024]{2,1,0:T(8,128)(2,1)S(1)}, u32[]{:S(2)}, u32[]{:S(2)}) collective-permute-start(bf16[2,240,1024]{2,1,0:T(8,128)(2,1)} %get-tuple-element.90), channel_id=1, source_target_pairs={{0,12},{4,0},{8,4},{12,8},{16,28},{20,16},{24,20},{28,24},{32,44},... | collective-permute-start | bytes 2949128 | tf_op jit(solution)/shard_map/ppermute | solution.py:1436
  137.1 31.0 %collective-permute-start.4 = (bf16[128,3072]{1,0:T(8,128)(2,1)}, bf16[128,3072]{1,0:T(8,128)(2,1)S(1)}, u32[]{:S(2)}, u32[]{:S(2)}) collective-permute-start(bf16[128,3072]{1,0:T(8,128)(2,1)} %get-tuple-element.86.refs_6_), channel_id=1, source_target_pairs={{0,2},{2,0},{1,3},{3,1},{4,6},{6,4},{5,7},{7,5},{8,10},{10,8},{9,1... | collective-permute-start | bytes 2359304 | tf_op jit(solution)/shard_map/ppermute | solution.py:1432
  168.2 0.9 copy-start.4
  168.2 1.2 copy-start
  168.2 1.5 copy-start.1
  168.2 1.8 copy-start.2
  168.2 2.1 copy-start.3
  265.4 8.5 %copy-start.5 = (f32[128,1024]{1,0:T(8,128)S(1)}, f32[128,1024]{1,0:T(8,128)}, u32[]{:S(2)}) copy-start(f32[128,1024]{1,0:T(8,128)} %get-tuple-element.85) | copy-start | bytes 1572868
  265.4 9.3 %copy-start.6 = (f32[128,1024]{1,0:T(8,128)S(1)}, f32[128,1024]{1,0:T(8,128)}, u32[]{:S(2)}) copy-start(f32[128,1024]{1,0:T(8,128)} %get-tuple-element.109) | copy-start | bytes 1572868

commit v8 on v7

--- a/solution.py
+++ b/solution.py
@@ -66,8 +66,8 @@
 
 def front_kernel(*refs):
     x_ref, wq, wk, wv, x_any, ln_ref, wo, wi, wu = refs[:9]
-    wall, xs, lnf, co_ref, ci_ref, cu_ref, qa_ref, qb_ref, x2_ref, y2_ref, da_ref, db_ref, kvr, qr = refs[9:23]
-    weights, acc, kvp, qp, ss, rs, sw, rw, sf, rf, sn, rn, ls = refs[23:]
+    wall, xs, lnf, co_ref, ci_ref, cu_ref, qa_ref, qb_ref, da_ref, db_ref, kvr, qr = refs[9:21]
+    weights, acc, kvp, qp, ss, rs, sw, rw, sf, rf, sn, rn, ls = refs[21:]
     zl, x, y, zh, co = place()
     me = zh * 2 + co
     slots = [me, zh * 2 + 1 - co, (1 - zh) * 2 + co, (1 - zh) * 2 + 1 - co]
@@ -141,6 +141,13 @@
     for c in near:
         c.wait_recv()
     add(1, False)
+    for c in quarters:
+        c.wait_recv()
+    subs = []
+    for ref, n, peers in ((qa_ref, y, yp), (qb_ref, x, xp)):
+        spot = ref.at[:, :, pl.ds(pl.multiple_of(n * 256, 256), 256)]
+        for p in peers:
+            subs.append(wire(spot, spot, p))
     for c in second:
         c.wait_recv()
     last = [wire(weights.at[slots[2], m], weights.at[slots[2], m], core) for m in range(3)]
@@ -209,20 +216,13 @@
     ]
     for c in home:
         c.start()
-    for c in quarters:
-        c.wait_recv()
-    subs = []
-    for ref, n, peers in ((qa_ref, y, yp), (qb_ref, x, xp)):
-        spot = ref.at[:, :, pl.ds(pl.multiple_of(n * 256, 256), 256)]
-        for p in peers:
-            subs.append(wire(spot, spot, p))
     for src, dst in ((wo, co_ref), (wi, ci_ref), (wu, cu_ref)):
         rest.append(wire(src, dst, core))
     lax.fori_loop(1, 16, pass_on, 0)
     for c in subs:
         c.wait_recv()
-    for src, dst, p in ((qa_ref, x2_ref, xp[1]), (qb_ref, y2_ref, yp[1]), (qa_ref, da_ref, core), (qb_ref, db_ref, core)):
-        rest.append(wire(src, dst, p))
+    for src, dst in ((qa_ref, da_ref), (qb_ref, db_ref)):
+        rest.append(wire(src, dst, core))
     for c in home:
         c.wait()
     keep.wait()
@@ -235,15 +235,15 @@
 
 
 def front(tok, own, lnp, wo, wi, wu):
-    n = 6 + 3 + 12 + 3 + 2 + 18 + 3 + 1 + 6 + 3 + 4
+    n = 6 + 3 + 12 + 3 + 2 + 18 + 3 + 1 + 6 + 3 + 2
     piece = shp((9, 32, 1024), BF)
     return pl.pallas_call(
         front_kernel,
         out_shape=[shp((4, 3, 256, 1024), BF), shp((2, 128, 256), BF), shp((4, 8, 256), F32)]
-        + [shp(wo.shape, BF), shp(wi.shape, BF), shp(wu.shape, BF)] + [piece] * 6
+        + [shp(wo.shape, BF), shp(wi.shape, BF), shp(wu.shape, BF)] + [piece] * 4
         + [shp((32, 128, 128), BF), shp((16, 64, 128), BF)],
         in_specs=[VM] + [ANY] * 8,
-        out_specs=[ANY] * 14,
+        out_specs=[ANY] * 12,
         scratch_shapes=[
             pltpu.VMEM((4, 3, 256, 1024), BF), pltpu.VMEM((3, 128, 1024), F32),
             pltpu.VMEM((16, 128, 128), BF), pltpu.VMEM((16, 64, 128), BF),
@@ -492,11 +492,11 @@
 def heart_kernel(*refs):
     o_ref, x_ref, e_ref, ln_ref, ln_own = refs[:5]
     shards = (refs[5:8], refs[8:11])
-    parts, diag_a, diag_b = refs[11:19], refs[19], refs[20]
-    y_ref, dr_ref, zpay, gpay, gb_ref, dor = refs[21:27]
-    cuts = (refs[27:30], refs[30:33])
+    qa, x1, x3, qb, y1, y3, diag_a, diag_b = refs[11:19]
+    y_ref, dr_ref, zpay, gpay, gb_ref, dor = refs[19:25]
+    cuts = (refs[25:28], refs[28:31])
     (wo, wi, wu, us, gs, nl, ob, orx, dos, rr, ll, cl, lt, mid,
-     sw, sp, ss, rs, send_o, recv_o, send_do, recv_do, ls, lo) = refs[33:]
+     sw, sp, ss, rs, send_o, recv_o, send_do, recv_do, ls, lo) = refs[31:]
     zl, x, y, zh, co = place()
     w = zh * 2 + co
     flat = lax.axis_index("ctx") % 16
@@ -527,8 +527,8 @@
         rows = pl.ds(pl.multiple_of(t * 256 + h * 128 + q * 32, 32), 32)
         return wo.at[rows], wi.at[:, rows], wu.at[t * 8 + h * 4 + q]
 
-    quarters = [(parts[s], 0, (x + 4 - s) % 4) for s in range(4)]
-    quarters += [(parts[4 + s], 1, (y + 4 - s) % 4) for s in range(4)]
+    quarters = [(qa, 0, x), (x1, 0, (x + 3) % 4), (x3, 0, (x + 1) % 4)]
+    quarters += [(qb, 1, y), (y1, 1, (y + 3) % 4), (y3, 1, (y + 1) % 4)]
     held = [(where[2],) + q for q in quarters] + [(where[3], diag_a, 0, x), (where[3], diag_b, 1, y)]
     for n, (t, ref, h, q) in enumerate(held):
         to = spots(t, h, q)
@@ -562,8 +562,18 @@
     home = pltpu.make_async_copy(o_ref.at[flat], orx.at[flat], ls.at[0])
     home.start()
     shared = [[], [], []]
+    passed = [[], [], []]
+    ends = (
+        (device(zl, (x + 1) % 4, y, zh, co), device(zl, (x + 3) % 4, y, zh, co)),
+        (device(zl, x, (y + 1) % 4, zh, co), device(zl, x, (y + 3) % 4, zh, co)),
+    )
     for k in range(3):
-        for n in (1, 2, 3, 5, 6, 7):
+        for h in range(2):
+            ref, _, q = quarters[3 * h + (2 if k == 2 else 1)]
+            src = (ref.at[0], ref.at[1:5], ref.at[5:9])[k]
+            passed[k].append(wire(src, spots(where[2], h, q)[k], ends[h][1 if k == 2 else 0]))
+    for k in range(3):
+        for n in (1, 2, 4, 5):
             ref, h, q = quarters[n]
             src = (ref.at[0], ref.at[1:5], ref.at[5:9])[k]
             shared[k].append(wire(src, spots(where[2], h, q)[k], core))
@@ -576,6 +586,11 @@
 
     home.wait()
     lax.fori_loop(1, 16, wait_o, 0)
+    for k in range(3):
+        for h, at in enumerate((x, y)):
+            passed[k][h].wait_recv()
+            spot = spots(where[2], h, (at + 2) % 4)[k]
+            shared[k].append(wire(spot, spot, core))
     ln = jnp.concatenate([jnp.where(w == k, ln_own[...], ln_ref[k]) for k in range(4)], axis=1)
     gain0, gain1, bias0, bias1 = (ln[k:k + 1, :] for k in range(4))
     for h in range(16):
@@ -677,23 +692,23 @@
     lax.fori_loop(1, 16, wait_do, 0)
     for c in near:
         c.wait_send()
-    for group in shared:
+    for group in shared + passed:
         for c in group:
             c.wait_send()
     for c in out:
         c.wait()
 
 
-def heart(o, tok, cot, lnf, lnp, shards, parts, diag_a, diag_b):
+def heart(o, tok, cot, lnf, lnp, shards, parts):
     cut = [shp((2, 160, 1024), BF), shp((2, 240, 1024), BF), shp((2, 240, 1024), BF)]
-    n = 18 + 6
+    n = 12 + 6 + 6 + 6
     return pl.pallas_call(
         heart_kernel,
         out_shape=[
             shp((128, 1024), F32), shp((128, 1024), F32),
             shp((128, 3072), BF), shp((128, 2048), BF), shp((8, 1024), F32), shp((16, 64, 128), BF),
         ] + cut + cut,
-        in_specs=[ANY] + [VM] * 4 + [ANY] * 16,
+        in_specs=[ANY] + [VM] * 4 + [ANY] * 14,
         out_specs=[VM] * 5 + [ANY] * 7,
         scratch_shapes=[
             pltpu.VMEM((1024, 1024), BF),
@@ -710,13 +725,13 @@
             pltpu.VMEM((128, 1024), BF),
             pltpu.VMEM((1024, 256), BF),
             pltpu.VMEM((2, 1280, 1024), BF),
-            DMA((2, 6)), DMA((10, 3)), DMA((n,)), DMA((n,)), DMA((16,)), DMA((16,)), DMA((16,)), DMA((16,)),
+            DMA((2, 6)), DMA((8, 3)), DMA((n,)), DMA((n,)), DMA((16,)), DMA((16,)), DMA((16,)), DMA((16,)),
             DMA((2,)), DMA((10,)),
         ],
         compiler_params=pltpu.CompilerParams(collective_id=5, has_side_effects=True, vmem_limit_bytes=LIMIT),
         cost_estimate=pl.CostEstimate(flops=16 << 30, bytes_accessed=32 << 20, transcendentals=2 << 20),
         name="heart",
-    )(o, tok, cot, lnf, lnp, *shards[0], *shards[1], *parts, diag_a, diag_b)
+    )(o, tok, cot, lnf, lnp, *shards[0], *shards[1], *parts)
 
 
 class Spread:
@@ -1261,9 +1276,9 @@
     for k in range(4):
         rows = slice(256 * k, 256 * k + 256)
         mid[rows, :] = dot(lt2[rows, :], rr2[...]).astype(BF)
-    next(big)
     lax.fori_loop(1, 16, pass_on, 0)
     dkv[flat] = both(0)
+    next(big)
     for c in parts:
         c.wait()
     next(io)
@@ -1420,14 +1435,13 @@
     own = (w_query, w_key, w_value)
     outer = w_outer.reshape(8, 4, 32, 1024)
     wall, xs, lnf, *rest = front(tok, own, lnp, w_output, w_inner, outer)
-    core_shard, (qa, qb, x2, y2, diag_a, diag_b, kvr, qr) = rest[:3], rest[3:]
+    core_shard, (qa, qb, diag_a, diag_b, kvr, qr) = rest[:3], rest[3:]
     x1, x3 = (lax.ppermute(qa, "ctx", along_x(s)) for s in (1, 3))
     y1, y3 = (lax.ppermute(qb, "ctx", along_y(s)) for s in (1, 3))
     o, ot, lse = attend(blk, block_mask, kvr, qr)
-    x1, x2, x3, y1, y2, y3, o = lax.optimization_barrier((x1, x2, x3, y1, y2, y3, o))
-    far = [qa, x1, x2, x3, qb, y1, y2, y3]
+    x1, x3, y1, y3, o = lax.optimization_barrier((x1, x3, y1, y3, o))
     y_out, dr1, zpay, gpay, gb, dor, own_a, plus_a, minus_a, own_b, plus_b, minus_b = heart(
-        o, tok, cot, lnf, lnp, ((w_output, w_inner, outer), core_shard), far, diag_a, diag_b
+        o, tok, cot, lnf, lnp, ((w_output, w_inner, outer), core_shard), (qa, x1, x3, qb, y1, y3, diag_a, diag_b)
     )
     zr = lax.ppermute(zpay, "wsh", FLIP_FAR)
     plus_a = lax.ppermute(plus_a, "ctx", along_x(1))

time: 276 us -> 272 us (0.986)
  Pallas kernels: 252 us -> 245 us
    pallas_call x1, Pallas kernels: 65 us -> 50.7 us  [front(): pl.pallas_call(front_kernel, out_shape=[shp((4, 3, 256, 1024), BF), shp((...]
    pallas_call x1, Pallas kernels: 32.1 us -> 38.9 us  [heart(): pl.pallas_call(heart_kernel, out_shape=[shp((128, 1024), F32), shp((128,...]
    ppermute x2, starting transfers between devices: 2.03 us -> 5.37 us  [body(): y1, y3 = (lax.ppermute(qb, 'ctx', along_y(s)) for s in (1, 3))]
where the time goes in v8:
time: 272 us
  Pallas kernels  245 us (90%)
  starting transfers between devices  17.3 us (6%)
  local copies, waits for them, and re-layouts  7.17 us (3%)
    pallas_call x1, Pallas kernels, finish(): pl.pallas_call(finish_kernel, out_shape=[shp((128, 1024), F32), shp((1280...  96.2 us
    pallas_call x1, Pallas kernels, front(): pl.pallas_call(front_kernel, out_shape=[shp((4, 3, 256, 1024), BF), shp((...  50.7 us
    pallas_call x1, Pallas kernels, heart(): pl.pallas_call(heart_kernel, out_shape=[shp((128, 1024), F32), shp((128,...  38.9 us
    pallas_call x1, Pallas kernels, attend_back(): pl.pallas_call(attend_back_kernel, out_shape=[shp((32, 128, 128), BF), sh...  27 us
    pallas_call x1, Pallas kernels, attend(): pl.pallas_call(attend_kernel, out_shape=[shp((16, 64, 128), BF), shp((8,...  23.9 us
    pallas_call x1, Pallas kernels, scaled(): pl.pallas_call(scale_kernel, grid=(8,), out_shape=[shp((256, 1024), F32)]...  8.45 us
  transfers between devices with their start and end apart: 9, of which 0 were waited for; matrix products, arithmetic and copies ran while one was open for 0% of the time, Pallas kernels for 19%

profile of v8, /device:TPU:0, one launch (start us, length us, event | category | flops | bytes accessed | tf_op | source)
XLA Modules:
  0.0 271.9 jit_solution(2384034043265251347)
XLA Ops:
  0.7 0.1 pad.2.clone
  0.7 1.4 maximum_maximum_fusion.refs_5_.refs_4_
  2.1 50.7 %front.1 = (bf16[4,3,256,1024]{3,2,1,0:T(8,128)(2,1)}, bf16[2,128,256]{2,1,0:T(8,128)(2,1)}, f32[4,8,256]{2,1,0:T(8,128)}, bf16[256,1024]{1,0:T(8,128)(2,1)}, bf...) custom-call(bf16[128,1024]{1,0:T(8,128)(2,1)} %bitcast.7, ...), custom_call_target="tpu_custom_call" | custom-call | flops 17179869184 | bytes 33554432 | tf_op jit(solution)/shard_map/front/pallas_call | solution.py:240
  52.8 0.5 collective-permute-start.1
  53.4 1.6 collective-permute-start
  54.9 5.4 %collective-permute-start.3 = (bf16[9,32,1024]{2,1,0:T(8,128)(2,1)}, bf16[9,32,1024]{2,1,0:T(8,128)(2,1)S(1)}, u32[]{:S(2)}, u32[]{:S(2)}) collective-permute-start(bf16[9,32,1024]{2,1,0:T(8,128)(2,1)} %get-tuple-element.62.refs_14_), channel_id=1, source_target_pairs={{0,12},{4,0},{8,4},{12,8},{16,28},{20,16},{24,20},{28,24},{32,44},... | collective-permute-start | bytes 1769480 | tf_op jit(solution)/shard_map/ppermute | solution.py:1440
  60.3 0.1 copy.23
  60.4 0.6 reshape.40.blk
  61.0 23.9 %attend.1 = (bf16[16,64,128]{2,1,0:T(8,128)(2,1)}, f32[8,64,256]{2,1,0:T(8,128)}, f32[8,1,256]{2,1,0:T(1,128)}) custom-call(s32[64]{0:T(128)} %reshape.40.blk, s32[1,64,64]{2,1,0:T(8,128)} %mask.3, bf16[32,128,128]{2,1,0:T(8,128)(2,1)} %get-tuple-element.63.kvr, bf16[16,64,128]{2,1,0:T(8,128)(2,1)} %get-tuple-element.64.qr), custom_call_target="tpu_custom_call" | custom-call | flops 10737418240 | bytes 33554432 | tf_op jit(solution)/shard_map/attend/pallas_call | solution.py:378
  85.0 0.0 copy-start.9
  85.0 0.0 copy-start.11
  85.0 0.7 copy-done.8
  85.8 0.2 copy-done.9
  86.0 0.2 copy-done.10
  86.2 0.2 copy-done.11
  86.4 38.9 %heart.1 = (f32[128,1024]{1,0:T(8,128)}, f32[128,1024]{1,0:T(8,128)}, bf16[128,3072]{1,0:T(8,128)(2,1)}, bf16[128,2048]{1,0:T(8,128)(2,1)}, f32[8,1024]{1,0:T(8,...) custom-call(bf16[16,64,128]{2,1,0:T(8,128)(2,1)} %get-tuple-element., ...), custom_call_target="tpu_custom_call" | custom-call | flops 17179869184 | bytes 33554432 | tf_op jit(solution)/shard_map/heart/pallas_call | solution.py:705
  125.2 0.1 collective-permute-start.5
  125.3 3.2 %collective-permute-start.6 = (bf16[2,240,1024]{2,1,0:T(8,128)(2,1)}, bf16[2,240,1024]{2,1,0:T(8,128)(2,1)S(1)}, u32[]{:S(2)}, u32[]{:S(2)}) collective-permute-start(bf16[2,240,1024]{2,1,0:T(8,128)(2,1)} %get-tuple-element.80), channel_id=1, source_target_pairs={{0,48},{4,52},{8,56},{12,60},{16,0},{20,4},{24,8},{28,12},{32,16},... | collective-permute-start | bytes 2949128 | tf_op jit(solution)/shard_map/ppermute | solution.py:1448
  128.5 0.6 collective-permute-start.7
  129.1 2.7 collective-permute-start.8
  131.8 3.3 %collective-permute-start.4 = (bf16[128,3072]{1,0:T(8,128)(2,1)}, bf16[128,3072]{1,0:T(8,128)(2,1)S(1)}, u32[]{:S(2)}, u32[]{:S(2)}) collective-permute-start(bf16[128,3072]{1,0:T(8,128)(2,1)} %get-tuple-element.78.refs_6_), channel_id=1, source_target_pairs={{0,2},{2,0},{1,3},{3,1},{4,6},{6,4},{5,7},{7,5},{8,10},{10,8},{9,1... | collective-permute-start | bytes 2359304 | tf_op jit(solution)/shard_map/ppermute | solution.py:1446
  135.1 27.0 %attend_back.1 = (bf16[32,128,128]{2,1,0:T(8,128)(2,1)}, bf16[16,64,128]{2,1,0:T(8,128)(2,1)}) custom-call(s32[64]{0:T(128)} %reshape.40.blk, s32[1,64,64]{2,1,0:T(8,128)} %mask.3, bf16[32,128,128]{2,1,0:T(8,128)(2,1)} %get-tuple-element.63.kvr, bf16[16,64,128]{2,1,0:T(8,128)(2,1)} %get-tuple-element.64.qr, bf16[16,64,128]{2,1,0:T(8,128)(2,1)} %get-tuple-element.83.dor, ...), custom_call_target="tpu_custom_call" | custom-call | flops 1073741824 | bytes 4194304 | tf_op jit(solution)/shard_map/attend_back/pallas_call | solution.py:463
  162.2 0.8 copy-done.4
  163.0 0.3 copy-done
  163.3 0.3 copy-done.1
  163.6 0.3 copy-done.2
  164.0 0.3 copy-done.3
  164.3 96.2 %finish.1 = (f32[128,1024]{1,0:T(8,128)}, bf16[1280,1024]{1,0:T(8,128)(2,1)}, bf16[1024,1024]{1,0:T(8,128)(2,1)}, bf16[768,1024]{1,0:T(8,128)(2,1)}, f32[8,256]{1,0:T(8,128)}) custom-call(bf16[32,128,128]{2,1,0:T(8,128)(2,1)} %get-tuple-element.87.refs_0_, bf16[16,64,128]{2,1,0:T(8,128)(2,1)} %get-tuple-element.88.refs_1_, ...), custom_call_target="tpu_custom_call" | custom-call | tf_op jit(solution)/shard_map/finish/pallas_call | solution.py:1369
  260.5 1.4 fusion
  261.9 8.4 %scaled.1 = (f32[256,1024]{1,0:T(8,128)}, f32[256,1024]{1,0:T(8,128)}, f32[256,1024]{1,0:T(8,128)}, f32[256,1024]{1,0:T(8,128)}, f32[256,4096]{1,0:T(8,128)}, /*index=5*/f32[1024,1024]{1,0:T(8,128)}) custom-call(bf16[1280,1024]{1,0:T(8,128)(2,1)} %get-tuple-element.102.o.i0.i1.i2.i3, bf16[1280,1024]{1,0:T(8,128)(2,1)} %get-tuple-element.102.o.i0.i1.i2.i3, ...), custom_call_target="tpu_custom_call" | custom-call | tf_op jit(solution)/shard_map/scaled/pallas_call | solution.py:1405
  270.3 0.8 copy.26
  271.1 0.8 copy.27
  (24 shorter events, 0.1 us)
Async XLA Ops:
  2.1 58.2 %copy-start.7 = (s32[32,2]{0,1:T(2,128)S(1)}, s32[32,2]{0,1:T(2,128)}, u32[]{:S(2)}) copy-start(s32[32,2]{0,1:T(2,128)} %param.22) | copy-start | bytes 772
  52.8 32.1 %collective-permute-start.1 = (bf16[9,32,1024]{2,1,0:T(8,128)(2,1)}, bf16[9,32,1024]{2,1,0:T(8,128)(2,1)S(1)}, u32[]{:S(2)}, u32[]{:S(2)}) collective-permute-start(bf16[9,32,1024]{2,1,0:T(8,128)(2,1)} %get-tuple-element.61.refs_11_), channel_id=1, source_target_pairs={{0,48},{4,52},{8,56},{12,60},{16,0},{20,4},{24,8},{28,12},{32,16},... | collective-permute-start | bytes 1769480 | tf_op jit(solution)/shard_map/ppermute | solution.py:1439
  53.4 31.6 %collective-permute-start = (bf16[9,32,1024]{2,1,0:T(8,128)(2,1)}, bf16[9,32,1024]{2,1,0:T(8,128)(2,1)S(1)}, u32[]{:S(2)}, u32[]{:S(2)}) collective-permute-start(bf16[9,32,1024]{2,1,0:T(8,128)(2,1)} %get-tuple-element.61.refs_11_), channel_id=1, source_target_pairs={{0,16},{4,20},{8,24},{12,28},{16,32},{20,36},{24,40},{28,44},{32,4... | collective-permute-start | bytes 1769480 | tf_op jit(solution)/shard_map/ppermute | solution.py:1439
  54.9 30.1 %collective-permute-start.3 = (bf16[9,32,1024]{2,1,0:T(8,128)(2,1)}, bf16[9,32,1024]{2,1,0:T(8,128)(2,1)S(1)}, u32[]{:S(2)}, u32[]{:S(2)}) collective-permute-start(bf16[9,32,1024]{2,1,0:T(8,128)(2,1)} %get-tuple-element.62.refs_14_), channel_id=1, source_target_pairs={{0,12},{4,0},{8,4},{12,8},{16,28},{20,16},{24,20},{28,24},{32,44},... | collective-permute-start | bytes 1769480 | tf_op jit(solution)/shard_map/ppermute | solution.py:1440
  60.3 24.7 %collective-permute-start.2 = (bf16[9,32,1024]{2,1,0:T(8,128)(2,1)}, bf16[9,32,1024]{2,1,0:T(8,128)(2,1)S(1)}, u32[]{:S(2)}, u32[]{:S(2)}) collective-permute-start(bf16[9,32,1024]{2,1,0:T(8,128)(2,1)} %get-tuple-element.62.refs_14_), channel_id=1, source_target_pairs={{0,4},{4,8},{8,12},{12,0},{16,20},{20,24},{24,28},{28,16},{32,36},... | collective-permute-start | bytes 1769480 | tf_op jit(solution)/shard_map/ppermute | solution.py:1440
  85.0 0.8 copy-start.8
  85.0 1.0 copy-start.9
  85.0 1.2 copy-start.10
  85.0 1.3 copy-start.11
  125.2 36.9 %collective-permute-start.5 = (bf16[2,240,1024]{2,1,0:T(8,128)(2,1)}, bf16[2,240,1024]{2,1,0:T(8,128)(2,1)S(1)}, u32[]{:S(2)}, u32[]{:S(2)}) collective-permute-start(bf16[2,240,1024]{2,1,0:T(8,128)(2,1)} %get-tuple-element.79), channel_id=1, source_target_pairs={{0,16},{4,20},{8,24},{12,28},{16,32},{20,36},{24,40},{28,44},{32,4... | collective-permute-start | bytes 2949128 | tf_op jit(solution)/shard_map/ppermute | solution.py:1447
  125.3 36.8 %collective-permute-start.6 = (bf16[2,240,1024]{2,1,0:T(8,128)(2,1)}, bf16[2,240,1024]{2,1,0:T(8,128)(2,1)S(1)}, u32[]{:S(2)}, u32[]{:S(2)}) collective-permute-start(bf16[2,240,1024]{2,1,0:T(8,128)(2,1)} %get-tuple-element.80), channel_id=1, source_target_pairs={{0,48},{4,52},{8,56},{12,60},{16,0},{20,4},{24,8},{28,12},{32,16},... | collective-permute-start | bytes 2949128 | tf_op jit(solution)/shard_map/ppermute | solution.py:1448
  128.5 33.6 %collective-permute-start.7 = (bf16[2,240,1024]{2,1,0:T(8,128)(2,1)}, bf16[2,240,1024]{2,1,0:T(8,128)(2,1)S(1)}, u32[]{:S(2)}, u32[]{:S(2)}) collective-permute-start(bf16[2,240,1024]{2,1,0:T(8,128)(2,1)} %get-tuple-element.81), channel_id=1, source_target_pairs={{0,4},{4,8},{8,12},{12,0},{16,20},{20,24},{24,28},{28,16},{32,36},... | collective-permute-start | bytes 2949128 | tf_op jit(solution)/shard_map/ppermute | solution.py:1449
  129.1 33.1 %collective-permute-start.8 = (bf16[2,240,1024]{2,1,0:T(8,128)(2,1)}, bf16[2,240,1024]{2,1,0:T(8,128)(2,1)S(1)}, u32[]{:S(2)}, u32[]{:S(2)}) collective-permute-start(bf16[2,240,1024]{2,1,0:T(8,128)(2,1)} %get-tuple-element.82), channel_id=1, source_target_pairs={{0,12},{4,0},{8,4},{12,8},{16,28},{20,16},{24,20},{28,24},{32,44},... | collective-permute-start | bytes 2949128 | tf_op jit(solution)/shard_map/ppermute | solution.py:1450
  131.8 30.3 %collective-permute-start.4 = (bf16[128,3072]{1,0:T(8,128)(2,1)}, bf16[128,3072]{1,0:T(8,128)(2,1)S(1)}, u32[]{:S(2)}, u32[]{:S(2)}) collective-permute-start(bf16[128,3072]{1,0:T(8,128)(2,1)} %get-tuple-element.78.refs_6_), channel_id=1, source_target_pairs={{0,2},{2,0},{1,3},{3,1},{4,6},{6,4},{5,7},{7,5},{8,10},{10,8},{9,1... | collective-permute-start | bytes 2359304 | tf_op jit(solution)/shard_map/ppermute | solution.py:1446
  162.1 0.9 copy-start.4
  162.1 1.2 copy-start
  162.1 1.5 copy-start.1
  162.2 1.8 copy-start.2
  162.2 2.1 copy-start.3
  261.9 8.5 %copy-start.5 = (f32[128,1024]{1,0:T(8,128)S(1)}, f32[128,1024]{1,0:T(8,128)}, u32[]{:S(2)}) copy-start(f32[128,1024]{1,0:T(8,128)} %get-tuple-element.77) | copy-start | bytes 1572868
  261.9 9.3 %copy-start.6 = (f32[128,1024]{1,0:T(8,128)S(1)}, f32[128,1024]{1,0:T(8,128)}, u32[]{:S(2)}) copy-start(f32[128,1024]{1,0:T(8,128)} %get-tuple-element.101) | copy-start | bytes 1572868

commit v9 on v8

--- a/solution.py
+++ b/solution.py
@@ -297,16 +297,18 @@
     return key <= query
 
 
-def attend_kernel(blk, mask, kvr, qr, o_ref, ot_ref, lse_ref, kvs, kaug, kvt, bias, qs, qa, os, inv, order, oblk):
+def attend_kernel(
+    blk, mask, kvr, qr, o_ref, ot_ref, lse_ref, kvs, kaug, kvt, bias, qs, qa, os, inv, order, oblk, tops, totals, mixes
+):
     attention_setup(blk, mask, kvr, qr, kvs, kaug, kvt, bias, qs, inv, order, oblk)
 
-    def tile(g, carry):
+    def diagonal(g):
         score, vals = [], []
         for u in range(4):
             i = oblk[4 * g + u]
             q = qs[order[4 * g + u]]
             row = jnp.broadcast_to(bias[pl.ds(i, 1), :], (64, 64)).astype(BF)
-            qa[64 * u:64 * u + 64, :] = jnp.concatenate([q, row], axis=1)
+            qa[g, 64 * u:64 * u + 64, :] = jnp.concatenate([q, row], axis=1)
             kv = kvs[pl.ds(pl.multiple_of(i * 64, 64), 64), :]
             score.append(dot(kv[:, :64], q, NT))
             vals.append(kv[:, 64:])
@@ -316,7 +318,18 @@
         total = jnp.sum(p, axis=0, keepdims=True)
         pb = p.astype(BF)
         mix = jnp.concatenate([dot(vals[u], pb[:, 64 * u:64 * u + 64], TN) for u in range(4)], axis=1)
-        queries = qa[...]
+        tops[g], totals[g], mixes[g] = top, total, mix
+
+    def diagonals(k, carry):
+        for j in range(4):
+            diagonal(4 * k + j)
+        return carry
+
+    lax.fori_loop(0, 2, diagonals, 0)
+
+    def tile(g, carry):
+        top, total, mix = tops[g], totals[g], mixes[g]
+        queries = qa[g]
 
         def chunk(c, state):
             top, total, mix = state
@@ -366,7 +379,7 @@
         pltpu.VMEM((8, 128, 512), BF),
         pltpu.VMEM((64, 64), F32),
         pltpu.VMEM((32, 64, 64), BF),
-        pltpu.VMEM((256, 128), BF),
+        pltpu.VMEM((8, 256, 128), BF),
         pltpu.VMEM((32, 64, 64), BF),
         pltpu.SMEM((64,), jnp.int32),
         pltpu.SMEM((72,), jnp.int32),
@@ -380,7 +393,8 @@
         out_shape=[shp((16, 64, 128), BF), shp((8, 64, 256), F32), shp((8, 1, 256), F32)],
         in_specs=[SM, VM, VM, VM],
         out_specs=[VM] * 3,
-        scratch_shapes=attention_scratch(),
+        scratch_shapes=attention_scratch()
+        + [pltpu.VMEM((8, 1, 256), F32), pltpu.VMEM((8, 1, 256), F32), pltpu.VMEM((8, 64, 256), F32)],
         compiler_params=pltpu.CompilerParams(vmem_limit_bytes=LIMIT),
         cost_estimate=pl.CostEstimate(flops=10 << 30, bytes_accessed=32 << 20, transcendentals=4 << 20),
         name="attend",
@@ -389,7 +403,7 @@
 
 def attend_back_kernel(
     blk, mask, kvr, qr, dor, ot_ref, lse_ref, dkv_ref, dq_ref,
-    kvs, kaug, kvt, bias, qs, qa, dqs, inv, order, oblk, dos, qz, dz, dkv,
+    kvs, kaug, kvt, bias, qs, qa, dqs, inv, order, oblk, dos, qz, dz, dkv, deltas, dqt,
 ):
     attention_setup(blk, mask, kvr, qr, kvs, kaug, kvt, bias, qs, inv, order, oblk)
     for j in range(16):
@@ -399,7 +413,7 @@
     dkv[...] = jnp.zeros_like(dkv)
     zero = jnp.zeros((64, 64), BF)
 
-    def tile(g, carry):
+    def diagonal(g):
         score, dprob, places, keys_own, q_own, d_own = [], [], [], [], [], []
         for u in range(4):
             i = oblk[4 * g + u]
@@ -407,9 +421,9 @@
             do = dos[order[4 * g + u]]
             rows = slice(64 * u, 64 * u + 64)
             row = jnp.broadcast_to(bias[pl.ds(i, 1), :], (64, 64)).astype(BF)
-            qa[rows, :] = jnp.concatenate([q, row], axis=1)
-            qz[rows, :] = jnp.concatenate([q, zero], axis=1)
-            dz[rows, :] = jnp.concatenate([zero, do], axis=1)
+            qa[g, rows, :] = jnp.concatenate([q, row], axis=1)
+            qz[g, rows, :] = jnp.concatenate([q, zero], axis=1)
+            dz[g, rows, :] = jnp.concatenate([zero, do], axis=1)
             at = pl.ds(pl.multiple_of(i * 64, 64), 64)
             kv = kvs[at, :]
             score.append(dot(kv[:, :64], q, NT))
@@ -419,10 +433,7 @@
             q_own.append(q)
             d_own.append(do)
         lse = lse_ref[g]
-        queries = qa[...]
-        qpad = qz[...]
-        dpad = dz[...]
-        dot_t = dpad[:, 64:].astype(F32).T
+        dot_t = dz[g][:, 64:].astype(F32).T
         delta = jnp.sum(ot_ref[g] * dot_t, axis=0, keepdims=True)
         s = jnp.where(triangle(), jnp.concatenate(score, axis=1), NEG)
         p = jnp.exp(s - lse)
@@ -434,6 +445,19 @@
             grad = jnp.concatenate([dot(ds[:, lanes], q_own[u]), dot(pb[:, lanes], d_own[u])], axis=1)
             dkv[places[u], :] += grad
             dq.append(dot(keys_own[u], ds[:, lanes], TN))
+        deltas[g] = delta
+        dqt[g] = jnp.concatenate(dq, axis=1)
+
+    def diagonals(k, carry):
+        for j in range(4):
+            diagonal(4 * k + j)
+        return carry
+
+    lax.fori_loop(0, 2, diagonals, 0)
+
+    def tile(g, carry):
+        lse, delta = lse_ref[g], deltas[g]
+        queries, qpad, dpad = qa[g], qz[g], dz[g]
 
         def chunk(c, dq):
             at = pl.ds(pl.multiple_of(c * 512, 512), 512)
@@ -444,7 +468,7 @@
             return dq + dot(kvt[c, :64, :], ds)
 
         chunks = (oblk[4 * g + 3] + 7) // 8
-        dq = lax.fori_loop(0, chunks // 2, lambda c, dq: chunk(2 * c + 1, chunk(2 * c, dq)), jnp.concatenate(dq, axis=1))
+        dq = lax.fori_loop(0, chunks // 2, lambda c, dq: chunk(2 * c + 1, chunk(2 * c, dq)), dqt[g])
         dq = lax.fori_loop(chunks // 2 * 2, chunks, chunk, dq)
         back = (dq * 0.125).T.astype(BF)
         for u in range(4):
@@ -468,9 +492,11 @@
         scratch_shapes=attention_scratch()
         + [
             pltpu.VMEM((32, 64, 64), BF),
-            pltpu.VMEM((256, 128), BF),
-            pltpu.VMEM((256, 128), BF),
+            pltpu.VMEM((8, 256, 128), BF),
+            pltpu.VMEM((8, 256, 128), BF),
             pltpu.VMEM((4096, 128), F32),
+            pltpu.VMEM((8, 1, 256), F32),
+            pltpu.VMEM((8, 64, 256), F32),
         ],
         compiler_params=pltpu.CompilerParams(vmem_limit_bytes=LIMIT),
         cost_estimate=pl.CostEstimate(flops=1 << 30, bytes_accessed=4 << 20, transcendentals=0),
@@ -569,9 +595,16 @@
     )
     for k in range(3):
         for h in range(2):
-            ref, _, q = quarters[3 * h + (2 if k == 2 else 1)]
-            src = (ref.at[0], ref.at[1:5], ref.at[5:9])[k]
-            passed[k].append(wire(src, spots(where[2], h, q)[k], ends[h][1 if k == 2 else 0]))
+            (one, _, q1), (three, _, q3) = quarters[3 * h + 1], quarters[3 * h + 2]
+            up_to, down_to = spots(where[2], h, q1)[k], spots(where[2], h, q3)[k]
+            if k == 0:
+                passed[k].append([wire(one.at[0], up_to, ends[h][0])])
+            else:
+                first = 4 * k - 3
+                passed[k].append([
+                    wire(one.at[first:first + 2], up_to.at[0:2], ends[h][0]),
+                    wire(three.at[first + 2:first + 4], down_to.at[2:4], ends[h][1]),
+                ])
     for k in range(3):
         for n in (1, 2, 4, 5):
             ref, h, q = quarters[n]
@@ -586,11 +619,15 @@
 
     home.wait()
     lax.fori_loop(1, 16, wait_o, 0)
-    for k in range(3):
+
+    def pass_on(k):
         for h, at in enumerate((x, y)):
-            passed[k][h].wait_recv()
+            for c in passed[k][h]:
+                c.wait_recv()
             spot = spots(where[2], h, (at + 2) % 4)[k]
             shared[k].append(wire(spot, spot, core))
+
+    pass_on(0)
     ln = jnp.concatenate([jnp.where(w == k, ln_own[...], ln_ref[k]) for k in range(4)], axis=1)
     gain0, gain1, bias0, bias1 = (ln[k:k + 1, :] for k in range(4))
     for h in range(16):
@@ -601,7 +638,9 @@
     z0, r0 = norm_parts(x_ref[...].astype(F32) + dot(ob[...], wo[...]))
     n1 = z0 * gain0 + bias0
     nl[...] = n1.astype(BF)
+    pass_on(1)
     loaded(1)
+    pass_on(2)
 
     half = math.sqrt(0.5)
 
@@ -692,7 +731,7 @@
     lax.fori_loop(1, 16, wait_do, 0)
     for c in near:
         c.wait_send()
-    for group in shared + passed:
+    for group in shared + [c for k in range(3) for c in passed[k]]:
         for c in group:
             c.wait_send()
     for c in out:
@@ -701,7 +740,7 @@
 
 def heart(o, tok, cot, lnf, lnp, shards, parts):
     cut = [shp((2, 160, 1024), BF), shp((2, 240, 1024), BF), shp((2, 240, 1024), BF)]
-    n = 12 + 6 + 6 + 6
+    n = 12 + 10 + 6 + 6
     return pl.pallas_call(
         heart_kernel,
         out_shape=[

time: 272 us -> 272 us (level)
  transfers between devices with their start and end apart: 9 -> 9, of which waited for: 0 -> 0; matrix products, arithmetic and copies ran while one was open for 0% -> 0% of each run, Pallas kernels for 19% -> 18%
where the time goes in v9:
time: 272 us; the launch traced here: 273 us
  Pallas kernels  246 us (90%)
  starting transfers between devices  17.8 us (7%)
  local copies, waits for them, and re-layouts  7.17 us (3%)
    pallas_call x1, Pallas kernels, finish(): pl.pallas_call(finish_kernel, out_shape=[shp((128, 1024), F32), shp((1280...  98.1 us
    pallas_call x1, Pallas kernels, front(): pl.pallas_call(front_kernel, out_shape=[shp((4, 3, 256, 1024), BF), shp((...  50.7 us
    pallas_call x1, Pallas kernels, heart(): pl.pallas_call(heart_kernel, out_shape=[shp((128, 1024), F32), shp((128,...  38.4 us
    pallas_call x1, Pallas kernels, attend_back(): pl.pallas_call(attend_back_kernel, out_shape=[shp((32, 128, 128), BF), sh...  26.4 us
    pallas_call x1, Pallas kernels, attend(): pl.pallas_call(attend_kernel, out_shape=[shp((16, 64, 128), BF), shp((8,...  23.5 us
    pallas_call x1, Pallas kernels, scaled(): pl.pallas_call(scale_kernel, grid=(8,), out_shape=[shp((256, 1024), F32)]...  8.45 us
  transfers between devices with their start and end apart: 9, of which 0 were waited for; matrix products, arithmetic and copies ran while one was open for 0% of the time, Pallas kernels for 18%

profile of v9, /device:TPU:0, one launch (start us, length us, event | category | flops | bytes accessed | tf_op | source)
XLA Modules:
  0.0 272.8 jit_solution(12841464223302106292)
XLA Ops:
  0.7 0.1 pad.2.clone
  0.7 1.4 maximum_maximum_fusion.refs_5_.refs_4_
  2.1 50.7 %front.1 = (bf16[4,3,256,1024]{3,2,1,0:T(8,128)(2,1)}, bf16[2,128,256]{2,1,0:T(8,128)(2,1)}, f32[4,8,256]{2,1,0:T(8,128)}, bf16[256,1024]{1,0:T(8,128)(2,1)}, bf...) custom-call(bf16[128,1024]{1,0:T(8,128)(2,1)} %bitcast.7, ...), custom_call_target="tpu_custom_call" | custom-call | flops 17179869184 | bytes 33554432 | tf_op jit(solution)/shard_map/front/pallas_call | solution.py:240
  52.8 0.5 collective-permute-start.1
  53.4 1.6 collective-permute-start
  54.9 5.4 %collective-permute-start.3 = (bf16[9,32,1024]{2,1,0:T(8,128)(2,1)}, bf16[9,32,1024]{2,1,0:T(8,128)(2,1)S(1)}, u32[]{:S(2)}, u32[]{:S(2)}) collective-permute-start(bf16[9,32,1024]{2,1,0:T(8,128)(2,1)} %get-tuple-element.62.refs_14_), channel_id=1, source_target_pairs={{0,12},{4,0},{8,4},{12,8},{16,28},{20,16},{24,20},{28,24},{32,44},... | collective-permute-start | bytes 1769480 | tf_op jit(solution)/shard_map/ppermute | solution.py:1479
  60.3 0.1 copy.23
  60.4 0.6 reshape.40.blk
  61.0 23.5 %attend.1 = (bf16[16,64,128]{2,1,0:T(8,128)(2,1)}, f32[8,64,256]{2,1,0:T(8,128)}, f32[8,1,256]{2,1,0:T(1,128)}) custom-call(s32[64]{0:T(128)} %reshape.40.blk, s32[1,64,64]{2,1,0:T(8,128)} %mask.3, bf16[32,128,128]{2,1,0:T(8,128)(2,1)} %get-tuple-element.63.kvr, bf16[16,64,128]{2,1,0:T(8,128)(2,1)} %get-tuple-element.64.qr), custom_call_target="tpu_custom_call" | custom-call | flops 10737418240 | bytes 33554432 | tf_op jit(solution)/shard_map/attend/pallas_call | solution.py:391
  84.5 0.0 copy-start.10
  84.5 0.7 copy-done.8
  85.3 0.2 copy-done.9
  85.5 0.2 copy-done.10
  85.7 0.2 copy-done.11
  85.9 38.4 %heart.1 = (f32[128,1024]{1,0:T(8,128)}, f32[128,1024]{1,0:T(8,128)}, bf16[128,3072]{1,0:T(8,128)(2,1)}, bf16[128,2048]{1,0:T(8,128)(2,1)}, f32[8,1024]{1,0:T(8,...) custom-call(bf16[16,64,128]{2,1,0:T(8,128)(2,1)} %get-tuple-element., ...), custom_call_target="tpu_custom_call" | custom-call | flops 17179869184 | bytes 33554432 | tf_op jit(solution)/shard_map/heart/pallas_call | solution.py:744
  124.3 0.3 collective-permute-start.5
  124.6 3.2 %collective-permute-start.6 = (bf16[2,240,1024]{2,1,0:T(8,128)(2,1)}, bf16[2,240,1024]{2,1,0:T(8,128)(2,1)S(1)}, u32[]{:S(2)}, u32[]{:S(2)}) collective-permute-start(bf16[2,240,1024]{2,1,0:T(8,128)(2,1)} %get-tuple-element.80), channel_id=1, source_target_pairs={{0,48},{4,52},{8,56},{12,60},{16,0},{20,4},{24,8},{28,12},{32,16},... | collective-permute-start | bytes 2949128 | tf_op jit(solution)/shard_map/ppermute | solution.py:1487
  127.8 0.9 collective-permute-start.7
  128.7 2.4 collective-permute-start.8
  131.0 3.6 %collective-permute-start.4 = (bf16[128,3072]{1,0:T(8,128)(2,1)}, bf16[128,3072]{1,0:T(8,128)(2,1)S(1)}, u32[]{:S(2)}, u32[]{:S(2)}) collective-permute-start(bf16[128,3072]{1,0:T(8,128)(2,1)} %get-tuple-element.78.refs_6_), channel_id=1, source_target_pairs={{0,2},{2,0},{1,3},{3,1},{4,6},{6,4},{5,7},{7,5},{8,10},{10,8},{9,1... | collective-permute-start | bytes 2359304 | tf_op jit(solution)/shard_map/ppermute | solution.py:1485
  134.6 26.4 %attend_back.1 = (bf16[32,128,128]{2,1,0:T(8,128)(2,1)}, bf16[16,64,128]{2,1,0:T(8,128)(2,1)}) custom-call(s32[64]{0:T(128)} %reshape.40.blk, s32[1,64,64]{2,1,0:T(8,128)} %mask.3, bf16[32,128,128]{2,1,0:T(8,128)(2,1)} %get-tuple-element.63.kvr, bf16[16,64,128]{2,1,0:T(8,128)(2,1)} %get-tuple-element.64.qr, bf16[16,64,128]{2,1,0:T(8,128)(2,1)} %get-tuple-element.83.dor, ...), custom_call_target="tpu_custom_call" | custom-call | flops 1073741824 | bytes 4194304 | tf_op jit(solution)/shard_map/attend_back/pallas_call | solution.py:487
  161.1 0.0 copy-start.1
  161.1 0.8 copy-done.4
  161.9 0.3 copy-done
  162.2 0.3 copy-done.1
  162.5 0.3 copy-done.2
  162.9 0.3 copy-done.3
  163.2 98.1 %finish.1 = (f32[128,1024]{1,0:T(8,128)}, bf16[1280,1024]{1,0:T(8,128)(2,1)}, bf16[1024,1024]{1,0:T(8,128)(2,1)}, bf16[768,1024]{1,0:T(8,128)(2,1)}, f32[8,256]{1,0:T(8,128)}) custom-call(bf16[32,128,128]{2,1,0:T(8,128)(2,1)} %get-tuple-element.87.refs_0_, bf16[16,64,128]{2,1,0:T(8,128)(2,1)} %get-tuple-element.88.refs_1_, ...), custom_call_target="tpu_custom_call" | custom-call | tf_op jit(solution)/shard_map/finish/pallas_call | solution.py:1408
  261.3 1.4 fusion
  262.7 8.4 %scaled.1 = (f32[256,1024]{1,0:T(8,128)}, f32[256,1024]{1,0:T(8,128)}, f32[256,1024]{1,0:T(8,128)}, f32[256,1024]{1,0:T(8,128)}, f32[256,4096]{1,0:T(8,128)}, /*index=5*/f32[1024,1024]{1,0:T(8,128)}) custom-call(bf16[1280,1024]{1,0:T(8,128)(2,1)} %get-tuple-element.102.o.i0.i1.i2.i3, bf16[1280,1024]{1,0:T(8,128)(2,1)} %get-tuple-element.102.o.i0.i1.i2.i3, ...), custom_call_target="tpu_custom_call" | custom-call | tf_op jit(solution)/shard_map/scaled/pallas_call | solution.py:1444
  271.2 0.8 copy.26
  272.0 0.8 copy.27
  (24 shorter events, 0.1 us)
Async XLA Ops:
  2.1 58.2 %copy-start.7 = (s32[32,2]{0,1:T(2,128)S(1)}, s32[32,2]{0,1:T(2,128)}, u32[]{:S(2)}) copy-start(s32[32,2]{0,1:T(2,128)} %param.22) | copy-start | bytes 772
  52.8 31.6 %collective-permute-start.1 = (bf16[9,32,1024]{2,1,0:T(8,128)(2,1)}, bf16[9,32,1024]{2,1,0:T(8,128)(2,1)S(1)}, u32[]{:S(2)}, u32[]{:S(2)}) collective-permute-start(bf16[9,32,1024]{2,1,0:T(8,128)(2,1)} %get-tuple-element.61.refs_11_), channel_id=1, source_target_pairs={{0,48},{4,52},{8,56},{12,60},{16,0},{20,4},{24,8},{28,12},{32,16},... | collective-permute-start | bytes 1769480 | tf_op jit(solution)/shard_map/ppermute | solution.py:1478
  53.4 31.1 %collective-permute-start = (bf16[9,32,1024]{2,1,0:T(8,128)(2,1)}, bf16[9,32,1024]{2,1,0:T(8,128)(2,1)S(1)}, u32[]{:S(2)}, u32[]{:S(2)}) collective-permute-start(bf16[9,32,1024]{2,1,0:T(8,128)(2,1)} %get-tuple-element.61.refs_11_), channel_id=1, source_target_pairs={{0,16},{4,20},{8,24},{12,28},{16,32},{20,36},{24,40},{28,44},{32,4... | collective-permute-start | bytes 1769480 | tf_op jit(solution)/shard_map/ppermute | solution.py:1478
  54.9 29.6 %collective-permute-start.3 = (bf16[9,32,1024]{2,1,0:T(8,128)(2,1)}, bf16[9,32,1024]{2,1,0:T(8,128)(2,1)S(1)}, u32[]{:S(2)}, u32[]{:S(2)}) collective-permute-start(bf16[9,32,1024]{2,1,0:T(8,128)(2,1)} %get-tuple-element.62.refs_14_), channel_id=1, source_target_pairs={{0,12},{4,0},{8,4},{12,8},{16,28},{20,16},{24,20},{28,24},{32,44},... | collective-permute-start | bytes 1769480 | tf_op jit(solution)/shard_map/ppermute | solution.py:1479
  60.3 24.2 %collective-permute-start.2 = (bf16[9,32,1024]{2,1,0:T(8,128)(2,1)}, bf16[9,32,1024]{2,1,0:T(8,128)(2,1)S(1)}, u32[]{:S(2)}, u32[]{:S(2)}) collective-permute-start(bf16[9,32,1024]{2,1,0:T(8,128)(2,1)} %get-tuple-element.62.refs_14_), channel_id=1, source_target_pairs={{0,4},{4,8},{8,12},{12,0},{16,20},{20,24},{24,28},{28,16},{32,36},... | collective-permute-start | bytes 1769480 | tf_op jit(solution)/shard_map/ppermute | solution.py:1479
  84.5 0.8 copy-start.8
  84.5 1.0 copy-start.9
  84.5 1.2 copy-start.10
  84.5 1.3 copy-start.11
  124.3 36.8 %collective-permute-start.5 = (bf16[2,240,1024]{2,1,0:T(8,128)(2,1)}, bf16[2,240,1024]{2,1,0:T(8,128)(2,1)S(1)}, u32[]{:S(2)}, u32[]{:S(2)}) collective-permute-start(bf16[2,240,1024]{2,1,0:T(8,128)(2,1)} %get-tuple-element.79), channel_id=1, source_target_pairs={{0,16},{4,20},{8,24},{12,28},{16,32},{20,36},{24,40},{28,44},{32,4... | collective-permute-start | bytes 2949128 | tf_op jit(solution)/shard_map/ppermute | solution.py:1486
  124.6 36.5 %collective-permute-start.6 = (bf16[2,240,1024]{2,1,0:T(8,128)(2,1)}, bf16[2,240,1024]{2,1,0:T(8,128)(2,1)S(1)}, u32[]{:S(2)}, u32[]{:S(2)}) collective-permute-start(bf16[2,240,1024]{2,1,0:T(8,128)(2,1)} %get-tuple-element.80), channel_id=1, source_target_pairs={{0,48},{4,52},{8,56},{12,60},{16,0},{20,4},{24,8},{28,12},{32,16},... | collective-permute-start | bytes 2949128 | tf_op jit(solution)/shard_map/ppermute | solution.py:1487
  127.8 33.3 %collective-permute-start.7 = (bf16[2,240,1024]{2,1,0:T(8,128)(2,1)}, bf16[2,240,1024]{2,1,0:T(8,128)(2,1)S(1)}, u32[]{:S(2)}, u32[]{:S(2)}) collective-permute-start(bf16[2,240,1024]{2,1,0:T(8,128)(2,1)} %get-tuple-element.81), channel_id=1, source_target_pairs={{0,4},{4,8},{8,12},{12,0},{16,20},{20,24},{24,28},{28,16},{32,36},... | collective-permute-start | bytes 2949128 | tf_op jit(solution)/shard_map/ppermute | solution.py:1488
  128.7 32.4 %collective-permute-start.8 = (bf16[2,240,1024]{2,1,0:T(8,128)(2,1)}, bf16[2,240,1024]{2,1,0:T(8,128)(2,1)S(1)}, u32[]{:S(2)}, u32[]{:S(2)}) collective-permute-start(bf16[2,240,1024]{2,1,0:T(8,128)(2,1)} %get-tuple-element.82), channel_id=1, source_target_pairs={{0,12},{4,0},{8,4},{12,8},{16,28},{20,16},{24,20},{28,24},{32,44},... | collective-permute-start | bytes 2949128 | tf_op jit(solution)/shard_map/ppermute | solution.py:1489
  131.0 30.0 %collective-permute-start.4 = (bf16[128,3072]{1,0:T(8,128)(2,1)}, bf16[128,3072]{1,0:T(8,128)(2,1)S(1)}, u32[]{:S(2)}, u32[]{:S(2)}) collective-permute-start(bf16[128,3072]{1,0:T(8,128)(2,1)} %get-tuple-element.78.refs_6_), channel_id=1, source_target_pairs={{0,2},{2,0},{1,3},{3,1},{4,6},{6,4},{5,7},{7,5},{8,10},{10,8},{9,1... | collective-permute-start | bytes 2359304 | tf_op jit(solution)/shard_map/ppermute | solution.py:1485
  161.0 0.9 copy-start.4
  161.0 1.2 copy-start
  161.1 1.5 copy-start.1
  161.1 1.8 copy-start.2
  161.1 2.1 copy-start.3
  262.7 8.5 %copy-start.5 = (f32[128,1024]{1,0:T(8,128)S(1)}, f32[128,1024]{1,0:T(8,128)}, u32[]{:S(2)}) copy-start(f32[128,1024]{1,0:T(8,128)} %get-tuple-element.77) | copy-start | bytes 1572868
  262.7 9.3 %copy-start.6 = (f32[128,1024]{1,0:T(8,128)S(1)}, f32[128,1024]{1,0:T(8,128)}, u32[]{:S(2)}) copy-start(f32[128,1024]{1,0:T(8,128)} %get-tuple-element.101) | copy-start | bytes 1572868

commit v10 on v9

--- a/solution.py
+++ b/solution.py
@@ -115,6 +115,8 @@
         rest.append(wire(ln_ref, lnf.at[me], p))
     for n, idx in enumerate((slots[1], slots[3])):
         rest.append(wire(x_any.at[:, pl.ds(pl.multiple_of(idx * 256, 256), 256)], xs.at[n], core))
+    for src, dst in ((wo, co_ref), (wi, ci_ref), (wu, cu_ref)):
+        rest.append(wire(src, dst, core))
 
     def add(k, fresh):
         cols = x_ref[:, pl.ds(pl.multiple_of(slots[k] * 256, 256), 256)]
@@ -216,8 +218,6 @@
     ]
     for c in home:
         c.start()
-    for src, dst in ((wo, co_ref), (wi, ci_ref), (wu, cu_ref)):
-        rest.append(wire(src, dst, core))
     lax.fori_loop(1, 16, pass_on, 0)
     for c in subs:
         c.wait_recv()
@@ -1347,7 +1347,6 @@
         for m in range(3):
             total += dot(pay[:128, 1024 * m:1024 * m + 1024], weights[k, m], NT)
         gt[:, cols] = total
-    next(io)
     to_core.wait_recv()
     for z in range(2):
         for m in range(3):
@@ -1356,6 +1355,7 @@
             total += dot(lt[256 * z:256 * z + 256, 128:], rr[:128, cols])
             tail[z, 256 * m:256 * m + 256, :] = total.astype(BF)
     next(small)
+    next(io)
     for z in range(2):
         v0[z] = (pay[128:144, mine[z]].astype(F32) + rr[128:144, mine[z]].astype(F32))[:8]
     vfar = wire(v0.at[1], vf, far)

time: 272 us -> 274 us (level)
  no operation moved by 1% of the time
where the time goes in v10:
time: 274 us; the launch traced here: 273 us
  Pallas kernels  245 us (89%)
  starting transfers between devices  18.9 us (7%)
  local copies, waits for them, and re-layouts  7.17 us (3%)
    pallas_call x1, Pallas kernels, finish(): pl.pallas_call(finish_kernel, out_shape=[shp((128, 1024), F32), shp((1280...  97.5 us
    pallas_call x1, Pallas kernels, front(): pl.pallas_call(front_kernel, out_shape=[shp((4, 3, 256, 1024), BF), shp((...  50.9 us
    pallas_call x1, Pallas kernels, heart(): pl.pallas_call(heart_kernel, out_shape=[shp((128, 1024), F32), shp((128,...  38.6 us
    pallas_call x1, Pallas kernels, attend_back(): pl.pallas_call(attend_back_kernel, out_shape=[shp((32, 128, 128), BF), sh...  26.1 us
    pallas_call x1, Pallas kernels, attend(): pl.pallas_call(attend_kernel, out_shape=[shp((16, 64, 128), BF), shp((8,...  23.4 us
    pallas_call x1, Pallas kernels, scaled(): pl.pallas_call(scale_kernel, grid=(8,), out_shape=[shp((256, 1024), F32)]...  8.45 us
  transfers between devices with their start and end apart: 9, of which 0 were waited for; matrix products, arithmetic and copies ran while one was open for 0% of the time, Pallas kernels for 18%

profile of v10, /device:TPU:0, one launch (start us, length us, event | category | flops | bytes accessed | tf_op | source)
XLA Modules:
  0.0 273.2 jit_solution(12629252344047943484)
XLA Ops:
  0.7 0.1 pad.2.clone
  0.7 1.4 maximum_maximum_fusion.refs_5_.refs_4_
  2.1 50.9 %front.1 = (bf16[4,3,256,1024]{3,2,1,0:T(8,128)(2,1)}, bf16[2,128,256]{2,1,0:T(8,128)(2,1)}, f32[4,8,256]{2,1,0:T(8,128)}, bf16[256,1024]{1,0:T(8,128)(2,1)}, bf...) custom-call(bf16[128,1024]{1,0:T(8,128)(2,1)} %bitcast.7, ...), custom_call_target="tpu_custom_call" | custom-call | flops 17179869184 | bytes 33554432 | tf_op jit(solution)/shard_map/front/pallas_call | solution.py:240
  53.0 1.4 collective-permute-start.1
  54.4 0.7 collective-permute-start
  55.1 4.7 %collective-permute-start.3 = (bf16[9,32,1024]{2,1,0:T(8,128)(2,1)}, bf16[9,32,1024]{2,1,0:T(8,128)(2,1)S(1)}, u32[]{:S(2)}, u32[]{:S(2)}) collective-permute-start(bf16[9,32,1024]{2,1,0:T(8,128)(2,1)} %get-tuple-element.62.refs_14_), channel_id=1, source_target_pairs={{0,12},{4,0},{8,4},{12,8},{16,28},{20,16},{24,20},{28,24},{32,44},... | collective-permute-start | bytes 1769480 | tf_op jit(solution)/shard_map/ppermute | solution.py:1479
  59.8 0.1 copy.23
  59.9 0.6 reshape.40.blk
  60.6 23.4 %attend.1 = (bf16[16,64,128]{2,1,0:T(8,128)(2,1)}, f32[8,64,256]{2,1,0:T(8,128)}, f32[8,1,256]{2,1,0:T(1,128)}) custom-call(s32[64]{0:T(128)} %reshape.40.blk, s32[1,64,64]{2,1,0:T(8,128)} %mask.3, bf16[32,128,128]{2,1,0:T(8,128)(2,1)} %get-tuple-element.63.kvr, bf16[16,64,128]{2,1,0:T(8,128)(2,1)} %get-tuple-element.64.qr), custom_call_target="tpu_custom_call" | custom-call | flops 10737418240 | bytes 33554432 | tf_op jit(solution)/shard_map/attend/pallas_call | solution.py:391
  84.1 0.0 copy-start.11
  84.1 0.7 copy-done.8
  84.8 0.2 copy-done.9
  85.0 0.2 copy-done.10
  85.2 0.2 copy-done.11
  85.4 38.6 %heart.1 = (f32[128,1024]{1,0:T(8,128)}, f32[128,1024]{1,0:T(8,128)}, bf16[128,3072]{1,0:T(8,128)(2,1)}, bf16[128,2048]{1,0:T(8,128)(2,1)}, f32[8,1024]{1,0:T(8,...) custom-call(bf16[16,64,128]{2,1,0:T(8,128)(2,1)} %get-tuple-element., ...), custom_call_target="tpu_custom_call" | custom-call | flops 17179869184 | bytes 33554432 | tf_op jit(solution)/shard_map/heart/pallas_call | solution.py:744
  124.0 0.3 collective-permute-start.5
  124.3 3.2 %collective-permute-start.6 = (bf16[2,240,1024]{2,1,0:T(8,128)(2,1)}, bf16[2,240,1024]{2,1,0:T(8,128)(2,1)S(1)}, u32[]{:S(2)}, u32[]{:S(2)}) collective-permute-start(bf16[2,240,1024]{2,1,0:T(8,128)(2,1)} %get-tuple-element.80), channel_id=1, source_target_pairs={{0,48},{4,52},{8,56},{12,60},{16,0},{20,4},{24,8},{28,12},{32,16},... | collective-permute-start | bytes 2949128 | tf_op jit(solution)/shard_map/ppermute | solution.py:1487
  127.5 0.9 collective-permute-start.7
  128.4 2.3 collective-permute-start.8
  130.7 5.3 %collective-permute-start.4 = (bf16[128,3072]{1,0:T(8,128)(2,1)}, bf16[128,3072]{1,0:T(8,128)(2,1)S(1)}, u32[]{:S(2)}, u32[]{:S(2)}) collective-permute-start(bf16[128,3072]{1,0:T(8,128)(2,1)} %get-tuple-element.78.refs_6_), channel_id=1, source_target_pairs={{0,2},{2,0},{1,3},{3,1},{4,6},{6,4},{5,7},{7,5},{8,10},{10,8},{9,1... | collective-permute-start | bytes 2359304 | tf_op jit(solution)/shard_map/ppermute | solution.py:1485
  136.1 26.1 %attend_back.1 = (bf16[32,128,128]{2,1,0:T(8,128)(2,1)}, bf16[16,64,128]{2,1,0:T(8,128)(2,1)}) custom-call(s32[64]{0:T(128)} %reshape.40.blk, s32[1,64,64]{2,1,0:T(8,128)} %mask.3, bf16[32,128,128]{2,1,0:T(8,128)(2,1)} %get-tuple-element.63.kvr, bf16[16,64,128]{2,1,0:T(8,128)(2,1)} %get-tuple-element.64.qr, bf16[16,64,128]{2,1,0:T(8,128)(2,1)} %get-tuple-element.83.dor, ...), custom_call_target="tpu_custom_call" | custom-call | flops 1073741824 | bytes 4194304 | tf_op jit(solution)/shard_map/attend_back/pallas_call | solution.py:487
  162.2 0.0 copy-start.1
  162.2 0.8 copy-done.4
  163.0 0.3 copy-done
  163.4 0.3 copy-done.1
  163.7 0.3 copy-done.2
  164.0 0.3 copy-done.3
  164.3 97.5 %finish.1 = (f32[128,1024]{1,0:T(8,128)}, bf16[1280,1024]{1,0:T(8,128)(2,1)}, bf16[1024,1024]{1,0:T(8,128)(2,1)}, bf16[768,1024]{1,0:T(8,128)(2,1)}, f32[8,256]{1,0:T(8,128)}) custom-call(bf16[32,128,128]{2,1,0:T(8,128)(2,1)} %get-tuple-element.87.refs_0_, bf16[16,64,128]{2,1,0:T(8,128)(2,1)} %get-tuple-element.88.refs_1_, ...), custom_call_target="tpu_custom_call" | custom-call | tf_op jit(solution)/shard_map/finish/pallas_call | solution.py:1408
  261.8 1.4 fusion
  263.2 8.4 %scaled.1 = (f32[256,1024]{1,0:T(8,128)}, f32[256,1024]{1,0:T(8,128)}, f32[256,1024]{1,0:T(8,128)}, f32[256,1024]{1,0:T(8,128)}, f32[256,4096]{1,0:T(8,128)}, /*index=5*/f32[1024,1024]{1,0:T(8,128)}) custom-call(bf16[1280,1024]{1,0:T(8,128)(2,1)} %get-tuple-element.102.o.i0.i1.i2.i3, bf16[1280,1024]{1,0:T(8,128)(2,1)} %get-tuple-element.102.o.i0.i1.i2.i3, ...), custom_call_target="tpu_custom_call" | custom-call | tf_op jit(solution)/shard_map/scaled/pallas_call | solution.py:1444
  271.6 0.8 copy.26
  272.4 0.8 copy.27
  (24 shorter events, 0.1 us)
Async XLA Ops:
  2.1 57.8 %copy-start.7 = (s32[32,2]{0,1:T(2,128)S(1)}, s32[32,2]{0,1:T(2,128)}, u32[]{:S(2)}) copy-start(s32[32,2]{0,1:T(2,128)} %param.22) | copy-start | bytes 772
  53.0 30.9 %collective-permute-start.1 = (bf16[9,32,1024]{2,1,0:T(8,128)(2,1)}, bf16[9,32,1024]{2,1,0:T(8,128)(2,1)S(1)}, u32[]{:S(2)}, u32[]{:S(2)}) collective-permute-start(bf16[9,32,1024]{2,1,0:T(8,128)(2,1)} %get-tuple-element.61.refs_11_), channel_id=1, source_target_pairs={{0,48},{4,52},{8,56},{12,60},{16,0},{20,4},{24,8},{28,12},{32,16},... | collective-permute-start | bytes 1769480 | tf_op jit(solution)/shard_map/ppermute | solution.py:1478
  54.4 29.6 %collective-permute-start = (bf16[9,32,1024]{2,1,0:T(8,128)(2,1)}, bf16[9,32,1024]{2,1,0:T(8,128)(2,1)S(1)}, u32[]{:S(2)}, u32[]{:S(2)}) collective-permute-start(bf16[9,32,1024]{2,1,0:T(8,128)(2,1)} %get-tuple-element.61.refs_11_), channel_id=1, source_target_pairs={{0,16},{4,20},{8,24},{12,28},{16,32},{20,36},{24,40},{28,44},{32,4... | collective-permute-start | bytes 1769480 | tf_op jit(solution)/shard_map/ppermute | solution.py:1478
  55.1 28.9 %collective-permute-start.3 = (bf16[9,32,1024]{2,1,0:T(8,128)(2,1)}, bf16[9,32,1024]{2,1,0:T(8,128)(2,1)S(1)}, u32[]{:S(2)}, u32[]{:S(2)}) collective-permute-start(bf16[9,32,1024]{2,1,0:T(8,128)(2,1)} %get-tuple-element.62.refs_14_), channel_id=1, source_target_pairs={{0,12},{4,0},{8,4},{12,8},{16,28},{20,16},{24,20},{28,24},{32,44},... | collective-permute-start | bytes 1769480 | tf_op jit(solution)/shard_map/ppermute | solution.py:1479
  59.8 24.2 %collective-permute-start.2 = (bf16[9,32,1024]{2,1,0:T(8,128)(2,1)}, bf16[9,32,1024]{2,1,0:T(8,128)(2,1)S(1)}, u32[]{:S(2)}, u32[]{:S(2)}) collective-permute-start(bf16[9,32,1024]{2,1,0:T(8,128)(2,1)} %get-tuple-element.62.refs_14_), channel_id=1, source_target_pairs={{0,4},{4,8},{8,12},{12,0},{16,20},{20,24},{24,28},{28,16},{32,36},... | collective-permute-start | bytes 1769480 | tf_op jit(solution)/shard_map/ppermute | solution.py:1479
  84.0 0.8 copy-start.8
  84.0 1.0 copy-start.9
  84.0 1.2 copy-start.10
  84.1 1.3 copy-start.11
  124.0 38.2 %collective-permute-start.5 = (bf16[2,240,1024]{2,1,0:T(8,128)(2,1)}, bf16[2,240,1024]{2,1,0:T(8,128)(2,1)S(1)}, u32[]{:S(2)}, u32[]{:S(2)}) collective-permute-start(bf16[2,240,1024]{2,1,0:T(8,128)(2,1)} %get-tuple-element.79), channel_id=1, source_target_pairs={{0,16},{4,20},{8,24},{12,28},{16,32},{20,36},{24,40},{28,44},{32,4... | collective-permute-start | bytes 2949128 | tf_op jit(solution)/shard_map/ppermute | solution.py:1486
  124.3 37.9 %collective-permute-start.6 = (bf16[2,240,1024]{2,1,0:T(8,128)(2,1)}, bf16[2,240,1024]{2,1,0:T(8,128)(2,1)S(1)}, u32[]{:S(2)}, u32[]{:S(2)}) collective-permute-start(bf16[2,240,1024]{2,1,0:T(8,128)(2,1)} %get-tuple-element.80), channel_id=1, source_target_pairs={{0,48},{4,52},{8,56},{12,60},{16,0},{20,4},{24,8},{28,12},{32,16},... | collective-permute-start | bytes 2949128 | tf_op jit(solution)/shard_map/ppermute | solution.py:1487
  127.5 34.7 %collective-permute-start.7 = (bf16[2,240,1024]{2,1,0:T(8,128)(2,1)}, bf16[2,240,1024]{2,1,0:T(8,128)(2,1)S(1)}, u32[]{:S(2)}, u32[]{:S(2)}) collective-permute-start(bf16[2,240,1024]{2,1,0:T(8,128)(2,1)} %get-tuple-element.81), channel_id=1, source_target_pairs={{0,4},{4,8},{8,12},{12,0},{16,20},{20,24},{24,28},{28,16},{32,36},... | collective-permute-start | bytes 2949128 | tf_op jit(solution)/shard_map/ppermute | solution.py:1488
  128.4 33.8 %collective-permute-start.8 = (bf16[2,240,1024]{2,1,0:T(8,128)(2,1)}, bf16[2,240,1024]{2,1,0:T(8,128)(2,1)S(1)}, u32[]{:S(2)}, u32[]{:S(2)}) collective-permute-start(bf16[2,240,1024]{2,1,0:T(8,128)(2,1)} %get-tuple-element.82), channel_id=1, source_target_pairs={{0,12},{4,0},{8,4},{12,8},{16,28},{20,16},{24,20},{28,24},{32,44},... | collective-permute-start | bytes 2949128 | tf_op jit(solution)/shard_map/ppermute | solution.py:1489
  130.7 31.4 %collective-permute-start.4 = (bf16[128,3072]{1,0:T(8,128)(2,1)}, bf16[128,3072]{1,0:T(8,128)(2,1)S(1)}, u32[]{:S(2)}, u32[]{:S(2)}) collective-permute-start(bf16[128,3072]{1,0:T(8,128)(2,1)} %get-tuple-element.78.refs_6_), channel_id=1, source_target_pairs={{0,2},{2,0},{1,3},{3,1},{4,6},{6,4},{5,7},{7,5},{8,10},{10,8},{9,1... | collective-permute-start | bytes 2359304 | tf_op jit(solution)/shard_map/ppermute | solution.py:1485
  162.1 0.9 copy-start.4
  162.2 1.2 copy-start
  162.2 1.5 copy-start.1
  162.2 1.8 copy-start.2
  162.2 2.1 copy-start.3
  263.2 8.5 %copy-start.5 = (f32[128,1024]{1,0:T(8,128)S(1)}, f32[128,1024]{1,0:T(8,128)}, u32[]{:S(2)}) copy-start(f32[128,1024]{1,0:T(8,128)} %get-tuple-element.77) | copy-start | bytes 1572868
  263.2 9.3 %copy-start.6 = (f32[128,1024]{1,0:T(8,128)S(1)}, f32[128,1024]{1,0:T(8,128)}, u32[]{:S(2)}) copy-start(f32[128,1024]{1,0:T(8,128)} %get-tuple-element.101) | copy-start | bytes 1572868
